TPU v7x, 32 devices: a whole 2x2x4 slice. The times are simulated.
32 devices in a mesh: grp: 2 (over y), store: 4 (over z), layer: 4 (over x, core).
Axes of the slice: x: 2, y: 2, z: 4, core: 2. Of those that a mesh axis runs over, the one named last changes fastest.
Arguments:
- hidden: bfloat16 [4, 288, 8, 8192], P('layer', ('grp', 'store')), parts along dimension 1, may hold values from -6 to 6
- cotangent: bfloat16 [4, 288, 8, 1024], P('layer', ('grp', 'store')), parts along dimension 1, may hold values from -6 to 6
- lengths: int32 [288], P(('grp', 'store')), parts along dimension 0, may hold values from 1 to 8, as said below
- norm_gain: bfloat16 [4, 8192], P('layer'), may hold values from 0.25 to 1.75
- in_projection: bfloat16 [4, 64, 8192], P('layer'), may hold values from -0.0625 to 0.0625
- out_projection: bfloat16 [4, 64, 1024], P('layer'), may hold values from -0.1875 to 0.1875
- store_slab: bfloat16 [4, 7680, 4096], P('layer', ('grp', 'store')), parts along dimension 1, may hold values from -0.0625 to 0.0625
Outputs:
- scores: float32 [7680, 144], P(('grp', 'store', 'layer')), parts along dimension 0
There are 2 independent parts, one for each index of `grp`. A program takes and returns all parts, laid end to end along the dimension named above; an argument that names none is the same for every part. Nothing has to cross between parts.
Inputs may be any that keep to these rules, and one draw needn't show every extreme that they name: Positions s < lengths[q] of query q count; some query has 8 tokens and some has 1.
All inputs are finite; a program needn't handle non-finite values.
Results may differ from a plain program's by a relative error of at most 0.0057.
Values may be sent and summed in bfloat16 or wider, within the bound.
No kernel may reach another device: no remote copies, remote signals or barrier semaphores. Data moves between devices by JAX's collectives and lax.ppermute only.
A program may use at most 64 MiB of HBM per device.

v0:
```python
import jax
import jax.numpy as jnp
from jax import lax
from jax.sharding import PartitionSpec as P

norm_epsilon = 1e-05


def contract_last(left, right):
    return lax.dot_general(
        left, right, (((1,), (1,)), ((), ())), preferred_element_type=jnp.float32
    )


def outer_grads(out_factor, in_factor):
    grads = jnp.einsum("qsi,qsj->qij", out_factor, in_factor, preferred_element_type=jnp.float32)
    return grads.astype(jnp.bfloat16).reshape(grads.shape[0], -1)


def on_device(hidden, cotangent, lengths, norm_gain, in_projection, out_projection, store_slab):
    queries, positions, width = (hidden.shape[1], hidden.shape[2], hidden.shape[3])
    flat = hidden[0].reshape(queries * positions, width).astype(jnp.float32)
    mean_square = jnp.mean(flat * flat, axis=-1, keepdims=True)
    normed = (
        flat * lax.rsqrt(mean_square + norm_epsilon) * norm_gain[0].astype(jnp.float32)
    ).astype(jnp.bfloat16)
    in_factor = (
        contract_last(normed, in_projection[0]).astype(jnp.bfloat16).reshape(queries, positions, -1)
    )
    flat_cot = cotangent[0].reshape(queries * positions, cotangent.shape[3])
    out_factor = contract_last(flat_cot, out_projection[0]).astype(jnp.bfloat16)
    live_mask = lax.broadcasted_iota(jnp.int32, (queries, positions), 1) < lengths[:, None]
    out_factor = out_factor.reshape(queries, positions, -1) * live_mask[:, :, None].astype(
        jnp.bfloat16
    )
    store_rows = store_slab[0]
    query_grads = outer_grads(out_factor, in_factor)
    partial_scores = contract_last(
        store_rows, lax.all_gather(query_grads, "store", axis=0, tiled=True)
    )
    return lax.psum_scatter(partial_scores, "layer", scatter_dimension=0, tiled=True)


def solution(mesh):
    placed = (
        P("layer", ("grp", "store"), None, None),
        P("layer", ("grp", "store"), None, None),
        P(("grp", "store")),
        P("layer", None),
        P("layer", None, None),
        P("layer", None, None),
        P("layer", ("grp", "store"), None),
    )
    return jax.shard_map(
        on_device,
        mesh=mesh,
        in_specs=placed,
        out_specs=P(("grp", "store", "layer"), None),
        check_vma=False,
    )
```

profile of v0, /device:TPU:0, one launch (start us, length us, event | category | flops | bytes accessed | tf_op | source)
XLA Modules:
  0.0 91.7 jit_solution(6837549071141438674)
XLA Ops:
  6.5 0.0 copy-start
  6.5 0.0 copy-start.4
  6.5 0.0 all-gather.3.cloned.1.call-start
  6.5 0.0 copy-start.1
  6.5 0.9 fusion.21
  7.4 3.8 %fusion = f32[36,8]{1,0:T(8,128)S(1)} fusion(bf16[1,36,8,8192]{3,2,1,0:T(8,128)(2,1)} %param.7), kind=kLoop, calls=%fused_computation.2 | loop fusion | flops 7077600 | bytes 4719744 | tf_op jit(solution)/shard_map/reduce_sum | solution.py:23
  11.2 0.0 copy-done.4
  11.3 0.0 copy-done
  11.3 0.0 copy-done.1
  11.3 0.0 copy-start.2
  11.3 0.0 copy-start.3
  11.3 1.7 %fusion.13 = bf16[288,64]{0,1:T(8,128)(2,1)S(1)} fusion(bf16[1,36,8,8192]{3,2,1,0:T(8,128)(2,1)S(1)} %copy-done.1, f32[8192]{0:T(1024)S(1)} %bitcast.30, f32[36,8]{1,0:T(8,128)S(1)} %add_rsqrt_fusion, bf16[1,64,8192]{2,1,0:T(8,128)(2,1)S(1)} %copy-done), kind=kOutput, calls=%fused_computation.13 | convolution fusion | flops 311445504 | bytes 5837952 | tf_op jit(solution)/shard_map/dot_general | solution.py:10
  13.0 0.1 copy.13
  13.2 0.0 copy-done.2
  13.2 0.0 copy-done.3
  13.2 0.3 convolution_convert_fusion.1
  13.5 0.1 copy.12
  13.7 0.5 convolution_convert_fusion
  14.1 1.2 %reshape.59 = bf16[1,36,4096]{2,1,0:T(8,128)(2,1)} reshape(bf16[36,64,64]{2,1,0:T(8,128)(2,1)S(1)} %convolution_convert_fusion) | data formatting | bytes 589824
  15.4 0.0 all-gather.3.cloned.1.call-update
  15.4 0.0 reduce-scatter.4.cloned.1.call-start
  15.4 35.5 %all-gather.3.cloned.1.call-done = bf16[4,36,4096]{2,1,0:T(8,128)(2,1)} async-done(((bf16[1,36,4096]{2,1,0:T(8,128)(2,1)}), bf16[4,36,4096]{2,1,0:T(8,128)(2,1)}) %all-gather.3.cloned.1.call-update) | async-done | bytes 1179664 | tf_op jit(solution)/shard_map/all_gather | solution.py:39
  50.9 1.4 %reshape.60 = bf16[144,4096]{1,0:T(8,128)(2,1)S(1)} reshape(bf16[4,36,4096]{2,1,0:T(8,128)(2,1)} %all-gather.3.cloned.1.call-done) | data formatting | bytes 2359296
  52.4 5.8 %fusion.10 = f32[960,144]{0,1:T(8,128)S(1)} fusion(bf16[144,4096]{1,0:T(8,128)(2,1)S(1)} %reshape.60, bf16[1,960,4096]{2,1,0:T(8,128)(2,1)} %param.13), kind=kOutput, calls=%fused_computation.12 | convolution fusion | flops 1132462080 | bytes 9596928 | tf_op jit(solution)/shard_map/dot_general | solution.py:10
  58.2 1.3 %copy.14 = f32[960,144]{1,0:T(8,128)} copy(f32[960,144]{0,1:T(8,128)S(1)} %fusion.10) | data formatting | bytes 1105920
  59.5 0.0 reduce-scatter.4.cloned.1.call-update
  59.5 23.6 %reduce-scatter.4.cloned.1.call-done = f32[240,144]{1,0:T(8,128)} async-done(((f32[960,144]{1,0:T(8,128)}), f32[240,144]{1,0:T(8,128)}) %reduce-scatter.4.cloned.1.call-update) | async-done | bytes 138256
  83.1 1.7 %copy.15 = f32[240,144]{0,1:T(8,128)} copy(f32[240,144]{1,0:T(8,128)} %reduce-scatter.4.cloned.1.call-done) | data formatting | bytes 276480
  (2 shorter events, 0.0 us)
Async XLA Ops:
  6.5 4.8 %copy-start = (bf16[1,64,8192]{2,1,0:T(8,128)(2,1)S(1)}, bf16[1,64,8192]{2,1,0:T(8,128)(2,1)}, u32[]{:S(2)}) copy-start(bf16[1,64,8192]{2,1,0:T(8,128)(2,1)} %param.11) | copy-start | bytes 3145732
  6.5 4.7 %copy-start.4 = (bf16[1,8192]{1,0:T(2,128)(2,1)S(1)}, bf16[1,8192]{1,0:T(2,128)(2,1)}, u32[]{:S(2)}) copy-start(bf16[1,8192]{1,0:T(2,128)(2,1)} %param.10) | copy-start | bytes 49156
  6.5 44.4 %all-gather.3.cloned.1.call-start = ((), (), s32[]{:S(2)}) async-start(), calls=%async_computation.1 | async-start | bytes 1638400 | tf_op jit(solution)/shard_map/all_gather | solution.py:39
  6.5 4.8 %copy-start.1 = (bf16[1,36,8,8192]{3,2,1,0:T(8,128)(2,1)S(1)}, bf16[1,36,8,8192]{3,2,1,0:T(8,128)(2,1)}, u32[]{:S(2)}) copy-start(bf16[1,36,8,8192]{3,2,1,0:T(8,128)(2,1)} %param.7) | copy-start | bytes 14155780
  11.3 1.9 %copy-start.2 = (bf16[1,36,8,1024]{3,2,1,0:T(8,128)(2,1)S(1)}, bf16[1,36,8,1024]{3,2,1,0:T(8,128)(2,1)}, u32[]{:S(2)}) copy-start(bf16[1,36,8,1024]{3,2,1,0:T(8,128)(2,1)} %param.8) | copy-start | bytes 1769476
  11.3 1.9 %copy-start.3 = (bf16[1,64,1024]{2,1,0:T(8,128)(2,1)S(1)}, bf16[1,64,1024]{2,1,0:T(8,128)(2,1)}, u32[]{:S(2)}) copy-start(bf16[1,64,1024]{2,1,0:T(8,128)(2,1)} %param.12) | copy-start | bytes 393220
  15.4 67.7 %reduce-scatter.4.cloned.1.call-start = ((), (), s32[]{:S(2)}) async-start(), calls=%async_computation.2 | async-start | bytes 1228800
Sparse Core Ops, SparseCore 0:
  15.5 35.3 all-gather.2
  59.6 23.4 reduce-scatter.3
where the time goes:
time: 91.9 us; the launch traced here: 91.7 us
  waiting for transfers between devices  59.1 us (64%)
  between operations  13.5 us (15%)
  matrix products  8.34 us (9%)
  local copies, waits for them, and re-layouts  5.91 us (6%)
  other arithmetic  4.72 us (5%)
    all_gather x1, waiting for transfers between devices, on_device(): lax.all_gather(query_grads, 'store', axis=0, tiled=True)  35.5 us
    unnamed x3, waiting for transfers between devices  23.6 us
    dot_general x3, matrix products, contract_last(): lax.dot_general(left, right, (((1,), (1,)), ((), ())), preferred_element_...  7.87 us
    unnamed x14, local copies, waits for them, and re-layouts  5.66 us
    reduce_sum x1, other arithmetic, on_device(): mean_square = jnp.mean(flat * flat, axis=-1, keepdims=True)  3.8 us
  transfers between devices with their start and end apart: 2, of which 2 were waited for; matrix products, arithmetic and copies ran while one was open for 0% of the time, Pallas kernels for 0%

commit v1 on v0

v1 whole, which is shorter than its diff:
```python
import functools

import jax
import jax.numpy as jnp
from jax import lax
from jax.experimental import pallas as pl
from jax.experimental.pallas import tpu as pltpu
from jax.sharding import PartitionSpec as P

norm_epsilon = 1e-05
f32 = jnp.float32
bf16 = jnp.bfloat16
S = 8
R = 64
B = 4
A = R // B
G = 8
H = 4


def dot_nt(left, right):
    return lax.dot_general(left, right, (((1,), (1,)), ((), ())), preferred_element_type=f32)


def iota(shape, dim):
    return lax.broadcasted_iota(jnp.int32, shape, dim)


def factors_kernel(
    steps, width, lengths, hidden, cot, gain, inp, outp, packed, in_acc, out_acc, sq_acc, out_t
):
    step = pl.program_id(0)
    queries = lengths.shape[0]
    rows = queries * S
    full = queries // G * G * S
    half = rows - full

    @pl.when(step == 0)
    def _():
        in_acc[...] = jnp.zeros_like(in_acc)
        out_acc[...] = jnp.zeros_like(out_acc)
        sq_acc[...] = jnp.zeros_like(sq_acc)

    block = hidden[...]
    wide = block.astype(f32)
    square = wide * wide
    lanes = sq_acc.shape[1]
    total = square[:, :lanes]
    for at in range(lanes, block.shape[1], lanes):
        total += square[:, at : at + lanes]
    sq_acc[...] += total
    scaled = (inp[...].astype(f32) * gain[...].astype(f32)).astype(bf16)
    in_acc[...] += dot_nt(block, scaled)
    out_acc[...] += dot_nt(cot[...], outp[...])

    @pl.when(step == steps - 1)
    def _():
        mean_square = jnp.sum(sq_acc[...], axis=1, keepdims=True) * (1.0 / width)
        factor = in_acc[...] * lax.rsqrt(mean_square + norm_epsilon)
        position = iota((S, R), 0)
        for q in range(queries):
            in_acc[q * S : (q + 1) * S, :] = jnp.where(
                position < lengths[q], factor[q * S : (q + 1) * S], 0.0
            )
        odd = lax.rem(lax.axis_index("store"), 2)
        at_full = pl.multiple_of(odd * half, half)
        at_half = pl.multiple_of((1 - odd) * full, half)
        in_full = in_acc[pl.ds(at_full, full), :]
        in_half = in_acc[pl.ds(at_half, half), :]
        mid, low = full // 2, half // 2
        packed[:mid, :] = jnp.concatenate([in_full[:mid], in_full[mid:]], axis=1).astype(bf16)
        packed[mid : mid + low, :] = jnp.concatenate(
            [in_half[:low], in_half[low:]], axis=1
        ).astype(bf16)
        turned = out_acc[pl.ds(at_full, full), :].T
        for t in range(full // 128):
            out_t[t * R : (t + 1) * R, :] = turned[:, t * 128 : (t + 1) * 128]
        out_t[full // 128 * R :, :half] = out_acc[pl.ds(at_half, half), :].T

        def part(t, b):
            return out_t[pl.ds(t * R + b, A, stride=B), :]

        row = mid + low
        for m in range(full // (G * S)):
            t, at = divmod(m * G * S, 128)
            for b in range(0, B, 2):
                both = [part(t, b + c)[:, at : at + G * S] for c in range(2)]
                packed[row : row + A, :] = jnp.concatenate(both, axis=1).astype(bf16)
                row += A
        packed[row : row + A, :] = jnp.concatenate(
            [part(full // 128, b)[:, :half] for b in range(B)], axis=1
        ).astype(bf16)


def factors(lengths, hidden, cotangent, gain, in_projection, out_projection):
    rows, width = hidden.shape
    steps = 8
    k_in, k_out = width // steps, cotangent.shape[1] // steps
    column = lambda step: (0, step)
    return pl.pallas_call(
        functools.partial(factors_kernel, steps, width),
        grid=(steps,),
        out_shape=jax.ShapeDtypeStruct((rows, 2 * R), bf16),
        in_specs=[
            pl.BlockSpec(memory_space=pltpu.SMEM),
            pl.BlockSpec((rows, k_in), column),
            pl.BlockSpec((rows, k_out), column),
            pl.BlockSpec((1, k_in), column),
            pl.BlockSpec((R, k_in), column),
            pl.BlockSpec((R, k_out), column),
        ],
        out_specs=pl.BlockSpec((rows, 2 * R), lambda step: (0, 0)),
        scratch_shapes=[
            pltpu.VMEM((rows, R), f32),
            pltpu.VMEM((rows, R), f32),
            pltpu.VMEM((rows, 128), f32),
            pltpu.VMEM((-(-rows // 128) * R, 128), f32),
        ],
        compiler_params=pltpu.CompilerParams(vmem_limit_bytes=16 * 2**20),
        name="factors",
    )(lengths, hidden, cotangent, gain, in_projection, out_projection)


def spread_out(tile, owner):
    lanes = tile.shape[1]
    mine = (owner == iota((G, lanes), 0))[None]
    wide = jnp.where(mine, tile.astype(f32)[:, None, :], 0.0)
    return wide.reshape(A * G, lanes).astype(bf16)


def halves(tile):
    wide = tile.astype(f32)
    turned = jnp.concatenate([wide[:, R:], wide[:, :R]], axis=1)
    low = iota(wide.shape, 1) < R
    return [
        jnp.where(mask, x, 0.0).astype(bf16)
        for x in (wide, turned)
        for mask in (low, jnp.logical_not(low))
    ]


def diagonal(low, high):
    zero = jnp.zeros_like(low)
    left = jnp.concatenate([low, high, zero, zero], axis=0)
    right = jnp.concatenate([zero, zero, low, high], axis=0)
    return jnp.concatenate([left, right], axis=1)


def build_grads(shards, base, row0, full_groups, grads):
    mid = full_groups * G * S // 2
    low = H * S // 2
    lane = iota((G, 2 * 128), 1)
    whole_owner = lax.rem(lane, G * S) // S
    half_owner = lax.rem(lane, H * S) // S + H * (lane // 128)

    def whole(shard):
        found = []
        pairs = {}
        for m in range(full_groups):
            first = m % (full_groups // 2)
            if first not in pairs:
                pairs[first] = halves(
                    shards[base + shard, first * G * S : (first + 1) * G * S, :]
                )
            plain_low, plain_high, turned_low, turned_high = pairs[first]
            weights = (
                diagonal(plain_low, turned_high)
                if m < full_groups // 2
                else diagonal(turned_low, plain_high)
            )
            at = mid + low + m * 2 * A
            tile = jnp.concatenate(
                [shards[base + shard, at : at + A, :], shards[base + shard, at + A : at + 2 * A, :]],
                axis=1,
            )
            found.append((spread_out(tile, whole_owner), weights))
        return found

    def joined(shard):
        tiles, weights = [], []
        for s in (shard, shard + 1):
            plain_low, plain_high, turned_low, turned_high = halves(
                shards[base + s, mid : mid + low, :]
            )
            weights.append(
                diagonal(
                    jnp.concatenate([plain_low, turned_low], axis=0),
                    jnp.concatenate([turned_high, plain_high], axis=0),
                )
            )
            at = mid + low + full_groups * 2 * A
            tiles.append(shards[base + s, at : at + A, :])
        return [
            (
                spread_out(jnp.concatenate(tiles, axis=1), half_owner),
                jnp.concatenate(weights, axis=0),
            )
        ]

    groups = []
    for shard in (0, 2):
        groups += whole(shard) + joined(shard) + whole(shard + 1)
    for at in range(0, len(groups), 2):
        first, second = [jnp.dot(x, w, preferred_element_type=f32) for x, w in groups[at : at + 2]]
        for a in range(A):
            pair = [x[a * G : (a + 1) * G] for x in (first, second)]
            grads[pl.ds(row0 + at * G, 2 * G), a * 256 : (a + 1) * 256] = jnp.concatenate(
                pair, axis=0
            ).astype(bf16)


def scores_kernel(n_store, n_layer, full_groups, *refs):
    gathered = refs[:n_store]
    store = refs[n_store]
    outs = refs[n_store + 1 : n_store + 1 + n_layer]
    shards, grads, slab, sems = refs[n_store + 1 + n_layer :]
    block = slab.shape[1]
    me_layer = lax.axis_index("layer")
    me_store = lax.axis_index("store")
    rows = 16 if block % 16 == 0 else 8
    copies = []
    for place, k in enumerate(reversed(range(n_layer))):
        copies.append(
            pltpu.make_async_copy(
                store.at[pl.ds(pl.multiple_of(partner(me_layer, k, n_layer) * block, rows), block)],
                slab.at[place],
                sems.at[place],
            )
        )
        copies[-1].start()
    for k in range(n_store):
        shards[partner(me_store, k, n_store)] = gathered[k][...]
    four = 4 * (full_groups * G + H)
    if n_store == 4:
        build_grads(shards, 0, 0, full_groups, grads)
    else:

        @pl.loop(0, n_store // 4)
        def _(at):
            build_grads(shards, at * 4, pl.multiple_of(at * four, 16), full_groups, grads)

    for place, k in enumerate(reversed(range(n_layer))):
        copies[place].wait()
        outs[k][...] = dot_nt(grads[...], slab[place]).astype(outs[k].dtype)


def partner(me, k, n):
    return jnp.bitwise_xor(me, k) if n & (n - 1) == 0 else lax.rem(n + k - me, n)


def swap(x, axis, n, k):
    pairs = [(i, i ^ k if n & (n - 1) == 0 else (n + k - i) % n) for i in range(n)]
    return lax.ppermute(x, axis, pairs)


def scores(gathered, store, n_store, n_layer):
    rows, features = store.shape
    queries = gathered[0].shape[0] // S
    block = rows // n_layer
    vmem = pl.BlockSpec(memory_space=pltpu.VMEM)
    return pl.pallas_call(
        functools.partial(scores_kernel, n_store, n_layer, queries // G),
        out_shape=[
            jax.ShapeDtypeStruct((n_store * queries, block), f32 if k == 0 else bf16)
            for k in range(n_layer)
        ],
        in_specs=[vmem] * n_store + [pl.BlockSpec(memory_space=pl.ANY)],
        out_specs=[vmem] * n_layer,
        scratch_shapes=[
            pltpu.VMEM((n_store,) + gathered[0].shape, bf16),
            pltpu.VMEM((n_store * queries, features), bf16),
            pltpu.VMEM((n_layer, block, features), bf16),
            pltpu.SemaphoreType.DMA((n_layer,)),
        ],
        compiler_params=pltpu.CompilerParams(vmem_limit_bytes=32 * 2**20),
        name="scores",
    )(*gathered, store)


def on_device(n_store, n_layer, hidden, cotangent, lengths, norm_gain, in_proj, out_proj, store):
    queries, positions, width = hidden.shape[1:]
    packed = factors(
        lengths,
        hidden.reshape(queries * positions, width),
        cotangent.reshape(queries * positions, cotangent.shape[3]),
        norm_gain,
        in_proj[0],
        out_proj[0],
    )
    gathered = [packed] + [swap(packed, "store", n_store, k) for k in range(1, n_store)]
    partial = scores(gathered, store[0], n_store, n_layer)
    total = partial[0]
    for k in range(1, n_layer):
        total = total + swap(partial[k], "layer", n_layer, k).astype(f32)
    return total.T


def solution(mesh):
    placed = (
        P("layer", ("grp", "store"), None, None),
        P("layer", ("grp", "store"), None, None),
        P(("grp", "store")),
        P("layer", None),
        P("layer", None, None),
        P("layer", None, None),
        P("layer", ("grp", "store"), None),
    )
    return jax.shard_map(
        functools.partial(on_device, mesh.shape["store"], mesh.shape["layer"]),
        mesh=mesh,
        in_specs=placed,
        out_specs=P(("grp", "store", "layer"), None),
        check_vma=False,
    )
```

time: 91.9 us -> 39.7 us (0.43)
  waiting for transfers between devices: 59.1 us -> 9.81 us
  between operations: 13.5 us -> 0.04 us
  Pallas kernels: 0 us -> 10.9 us
  matrix products: 8.34 us -> 0 us
  starting transfers between devices: 0.04 us -> 7.69 us
  local copies, waits for them, and re-layouts: 5.91 us -> 10.2 us
  other arithmetic: 4.72 us -> 0.7 us
    all_gather x1 -> x0, waiting for transfers between devices: 35.5 us -> none  [on_device(): lax.all_gather(query_grads, 'store', axis=0, tiled=True)]
    unnamed x3 -> x0, waiting for transfers between devices: 23.6 us -> none
    pallas_call x0 -> x2, Pallas kernels: none -> 10.9 us  [the longest x1 6.63 us: scores(): pl.pallas_call(functools.partial(scores_kernel, n_store, n_layer, queries...]
    ppermute x0 -> x6, waiting for transfers between devices: none -> 9.81 us  [swap(): return lax.ppermute(x, axis, pairs)]
    dot_general x4 -> x0, matrix products: 8.34 us -> none  [the longest x3 7.87 us: contract_last(): lax.dot_general(left, right, (((1,), (1,)), ((), ())), preferred_element_...]
    ppermute x0 -> x6, starting transfers between devices: none -> 7.69 us  [swap(): return lax.ppermute(x, axis, pairs)]
    unnamed x14, local copies, waits for them, and re-layouts: 5.66 us -> 10.2 us
    reduce_sum x1 -> x0, other arithmetic: 3.8 us -> none  [on_device(): mean_square = jnp.mean(flat * flat, axis=-1, keepdims=True)]
  transfers between devices with their start and end apart: 2 -> 6, of which waited for: 2 -> 4; matrix products, arithmetic and copies ran while one was open for 0% -> 0% of each run, Pallas kernels for 0% -> 0%
where the time goes in v1:
time: 39.7 us; the launch traced here: 39.3 us
  Pallas kernels  10.9 us (27%)
  local copies, waits for them, and re-layouts  10.2 us (26%)
  waiting for transfers between devices  9.81 us (25%)
  starting transfers between devices  7.69 us (19%)
  other arithmetic  0.7 us (2%)
    unnamed x14, local copies, waits for them, and re-layouts  10.2 us
    ppermute x6, waiting for transfers between devices, swap(): return lax.ppermute(x, axis, pairs)  9.81 us
    ppermute x6, starting transfers between devices, swap(): return lax.ppermute(x, axis, pairs)  7.69 us
    pallas_call x1, Pallas kernels, scores(): pl.pallas_call(functools.partial(scores_kernel, n_store, n_layer, queries...  6.63 us
    pallas_call x1, Pallas kernels, factors(): pl.pallas_call(functools.partial(factors_kernel, steps, width), grid=(ste...  4.28 us
  transfers between devices with their start and end apart: 6, of which 4 were waited for; matrix products, arithmetic and copies ran while one was open for 0% of the time, Pallas kernels for 0%

profile of v1, /device:TPU:0, one launch (start us, length us, event | category | flops | bytes accessed | tf_op | source)
XLA Modules:
  0.0 39.3 jit_solution(13839370932074561734)
XLA Ops:
  0.0 0.0 copy-start.1
  0.0 2.3 %copy-done.1 = bf16[1,36,8,8192]{3,2,1,0:T(8,128)(2,1)S(1)} copy-done((bf16[1,36,8,8192]{3,2,1,0:T(8,128)(2,1)S(1)}, bf16[1,36,8,8192]{3,2,1,0:T(8,128)(2,1)}, u32[]{:S(2)}) %copy-start.1) | copy-done | bytes 4718616
  2.3 0.0 copy-start.2
  2.3 1.2 %copy-done.2 = bf16[1,64,8192]{2,1,0:T(8,128)(2,1)S(1)} copy-done((bf16[1,64,8192]{2,1,0:T(8,128)(2,1)S(1)}, bf16[1,64,8192]{2,1,0:T(8,128)(2,1)}, u32[]{:S(2)}) %copy-start.2) | copy-done | bytes 1048600
  3.6 0.0 copy-start.3
  3.6 1.1 %copy-done.3 = bf16[1,36,8,1024]{3,2,1,0:T(8,128)(2,1)S(1)} copy-done((bf16[1,36,8,1024]{3,2,1,0:T(8,128)(2,1)S(1)}, bf16[1,36,8,1024]{3,2,1,0:T(8,128)(2,1)}, u32[]{:S(2)}) %copy-start.3) | copy-done | bytes 589848
  4.6 0.0 copy-start.4
  4.6 0.9 %copy-done.4 = bf16[1,64,1024]{2,1,0:T(8,128)(2,1)S(1)} copy-done((bf16[1,64,1024]{2,1,0:T(8,128)(2,1)S(1)}, bf16[1,64,1024]{2,1,0:T(8,128)(2,1)}, u32[]{:S(2)}) %copy-start.4) | copy-done | bytes 131096
  5.5 0.0 copy-start.5
  5.5 0.8 %copy-done.5 = bf16[1,8192]{1,0:T(2,128)(2,1)S(1)} copy-done((bf16[1,8192]{1,0:T(2,128)(2,1)S(1)}, bf16[1,8192]{1,0:T(2,128)(2,1)}, u32[]{:S(2)}) %copy-start.5) | copy-done | bytes 16408
  6.3 0.0 copy-start.6
  6.3 0.7 %copy-done.6 = s32[36]{0:T(128)S(1)} copy-done((s32[36]{0:T(128)S(1)}, s32[36]{0:T(128)}, u32[]{:S(2)}) %copy-start.6) | copy-done | bytes 168
  6.9 4.3 %factors.1.refs_0_ = bf16[288,128]{1,0:T(8,128)(2,1)S(1)} custom-call(s32[36]{0:T(128)S(1)} %copy-done.6, bf16[288,8192]{1,0:T(8,128)(2,1)S(1)} %bitcast.8, bf16[288,1024]{1,0:T(8,128)(2,1)S(1)} %bitcast.10, bf16[1,8192]{1,0:T(2,128)(2,1)S(1)} %copy-done.5, bf16[64,8192]{1,0:T(8,128)(2,1)S(1)} %bitcast.9, bf16[64,1024]{1,0:T(8,128)(2,1)S(1)} %bitcast.11), custom_call_target="tpu_custom_call" | custom-call | tf_op jit(solution)/shard_map/factors/pallas_call | solution.py:100
  11.2 5.1 %collective-permute-start.2 = (bf16[288,128]{1,0:T(8,128)(2,1)S(1)}, bf16[288,128]{1,0:T(8,128)(2,1)S(1)}, u32[]{:S(2)}, u32[]{:S(2)}) collective-permute-start(bf16[288,128]{1,0:T(8,128)(2,1)S(1)} %factors.1.refs_0_), channel_id=1, source_target_pairs={{0,12},{4,8},{8,4},{12,0},{1,13},{5,9},{9,5},{13,1},{2,14},{6,10},... | collective-permute-start | bytes 221192 | tf_op jit(solution)/shard_map/ppermute | solution.py:253
  16.3 0.0 collective-permute-start.1
  16.3 0.6 %collective-permute-start = (bf16[288,128]{1,0:T(8,128)(2,1)S(1)}, bf16[288,128]{1,0:T(8,128)(2,1)S(1)}, u32[]{:S(2)}, u32[]{:S(2)}) collective-permute-start(bf16[288,128]{1,0:T(8,128)(2,1)S(1)} %factors.1.refs_0_), channel_id=1, source_target_pairs={{0,4},{4,0},{8,12},{12,8},{1,5},{5,1},{9,13},{13,9},{2,6},{6,2},{1... | collective-permute-start | bytes 221192 | tf_op jit(solution)/shard_map/ppermute | solution.py:253
  17.0 2.1 %collective-permute-done.2.refs_3_ = bf16[288,128]{1,0:T(8,128)(2,1)S(1)} collective-permute-done((bf16[288,128]{1,0:T(8,128)(2,1)S(1)}, bf16[288,128]{1,0:T(8,128)(2,1)S(1)}, u32[]{:S(2)}, u32[]{:S(2)}) %collective-permute-start.2) | collective-permute-done | bytes 73760 | tf_op jit(solution)/shard_map/ppermute | solution.py:253
  19.1 3.5 %collective-permute-done.1.refs_2_ = bf16[288,128]{1,0:T(8,128)(2,1)S(1)} collective-permute-done((bf16[288,128]{1,0:T(8,128)(2,1)S(1)}, bf16[288,128]{1,0:T(8,128)(2,1)S(1)}, u32[]{:S(2)}, u32[]{:S(2)}) %collective-permute-start.1) | collective-permute-done | bytes 73760 | tf_op jit(solution)/shard_map/ppermute | solution.py:253
  22.6 0.0 collective-permute-done.refs_1_
  22.6 0.0 copy-start
  22.6 3.2 %copy-done = bf16[1,960,4096]{2,1,0:T(8,128)(2,1)S(1)} copy-done((bf16[1,960,4096]{2,1,0:T(8,128)(2,1)S(1)}, bf16[1,960,4096]{2,1,0:T(8,128)(2,1)}, u32[]{:S(2)}) %copy-start) | copy-done | bytes 7864344
  25.8 6.6 %scores.1 = (f32[144,240]{1,0:T(8,128)S(1)}, bf16[144,240]{1,0:T(8,128)(2,1)S(1)}, bf16[144,240]{1,0:T(8,128)(2,1)S(1)}, bf16[144,240]{1,0:T(8,128)(2,1)S(1)}) custom-call(bf16[288,128]{1,0:T(8,128)(2,1)S(1)} %factors.1.refs_0_, bf16[288,128]{1,0:T(8,128)(2,1)S(1)} %collective-permute-done.refs_1_, bf16[288,128]{1,0:T(8,128)(2,1)S(1)} %collective-permute-done.1.refs_2_, ...), custom_call_target="tpu_custom_call" | custom-call | tf_op jit(solution)/shard_map/scores/pallas_call | solution.py:261
  32.5 0.1 collective-permute-start.3
  32.5 1.5 %collective-permute-start.4 = (bf16[144,240]{1,0:T(8,128)(2,1)S(1)}, bf16[144,240]{1,0:T(8,128)(2,1)S(1)}, u32[]{:S(2)}, u32[]{:S(2)}) collective-permute-start(bf16[144,240]{1,0:T(8,128)(2,1)S(1)} %get-tuple-element.11), channel_id=1, source_target_pairs={{0,2},{1,3},{2,0},{3,1},{4,6},{5,7},{6,4},{7,5},{8,10},{9,11},{10,... | collective-permute-start | bytes 207368 | tf_op jit(solution)/shard_map/ppermute | solution.py:253
  34.1 0.3 collective-permute-start.5
  34.4 0.0 collective-permute-done.3
  34.4 3.0 %collective-permute-done.4 = bf16[144,240]{1,0:T(8,128)(2,1)S(1)} collective-permute-done((bf16[144,240]{1,0:T(8,128)(2,1)S(1)}, bf16[144,240]{1,0:T(8,128)(2,1)S(1)}, u32[]{:S(2)}, u32[]{:S(2)}) %collective-permute-start.4) | collective-permute-done | bytes 69152 | tf_op jit(solution)/shard_map/ppermute | solution.py:253
  37.4 1.2 %collective-permute-done.5 = bf16[144,240]{1,0:T(8,128)(2,1)S(1)} collective-permute-done((bf16[144,240]{1,0:T(8,128)(2,1)S(1)}, bf16[144,240]{1,0:T(8,128)(2,1)S(1)}, u32[]{:S(2)}, u32[]{:S(2)}) %collective-permute-start.5) | collective-permute-done | bytes 69152 | tf_op jit(solution)/shard_map/ppermute | solution.py:253
  38.6 0.7 %add_bitcast_fusion = f32[240,144]{0,1:T(8,128)} fusion(bf16[144,240]{1,0:T(8,128)(2,1)S(1)} %collective-permute-done.5, bf16[144,240]{1,0:T(8,128)(2,1)S(1)} %collective-permute-done.4, f32[144,240]{1,0:T(8,128)S(1)} %get-tuple-element.9, bf16[144,240]{1,0:T(8,128)(2,1)S(1)} %collective-permute-done.3), kind=kLoop, calls=%fused_computation | loop fusion | flops 207360 | bytes 483840 | tf_op jit(solution)/shard_map/transpose | solution.py:295
Async XLA Ops:
  0.0 2.3 %copy-start.1 = (bf16[1,36,8,8192]{3,2,1,0:T(8,128)(2,1)S(1)}, bf16[1,36,8,8192]{3,2,1,0:T(8,128)(2,1)}, u32[]{:S(2)}) copy-start(bf16[1,36,8,8192]{3,2,1,0:T(8,128)(2,1)} %param.7) | copy-start | bytes 14155780
  2.3 1.2 %copy-start.2 = (bf16[1,64,8192]{2,1,0:T(8,128)(2,1)S(1)}, bf16[1,64,8192]{2,1,0:T(8,128)(2,1)}, u32[]{:S(2)}) copy-start(bf16[1,64,8192]{2,1,0:T(8,128)(2,1)} %param.11) | copy-start | bytes 3145732
  3.6 1.1 %copy-start.3 = (bf16[1,36,8,1024]{3,2,1,0:T(8,128)(2,1)S(1)}, bf16[1,36,8,1024]{3,2,1,0:T(8,128)(2,1)}, u32[]{:S(2)}) copy-start(bf16[1,36,8,1024]{3,2,1,0:T(8,128)(2,1)} %param.8) | copy-start | bytes 1769476
  4.6 0.9 %copy-start.4 = (bf16[1,64,1024]{2,1,0:T(8,128)(2,1)S(1)}, bf16[1,64,1024]{2,1,0:T(8,128)(2,1)}, u32[]{:S(2)}) copy-start(bf16[1,64,1024]{2,1,0:T(8,128)(2,1)} %param.12) | copy-start | bytes 393220
  5.5 0.8 %copy-start.5 = (bf16[1,8192]{1,0:T(2,128)(2,1)S(1)}, bf16[1,8192]{1,0:T(2,128)(2,1)}, u32[]{:S(2)}) copy-start(bf16[1,8192]{1,0:T(2,128)(2,1)} %gain.1) | copy-start | bytes 49156
  6.3 0.7 %copy-start.6 = (s32[36]{0:T(128)S(1)}, s32[36]{0:T(128)}, u32[]{:S(2)}) copy-start(s32[36]{0:T(128)} %lengths.1) | copy-start | bytes 436
  11.2 7.9 %collective-permute-start.2 = (bf16[288,128]{1,0:T(8,128)(2,1)S(1)}, bf16[288,128]{1,0:T(8,128)(2,1)S(1)}, u32[]{:S(2)}, u32[]{:S(2)}) collective-permute-start(bf16[288,128]{1,0:T(8,128)(2,1)S(1)} %factors.1.refs_0_), channel_id=1, source_target_pairs={{0,12},{4,8},{8,4},{12,0},{1,13},{5,9},{9,5},{13,1},{2,14},{6,10},... | collective-permute-start | bytes 221192 | tf_op jit(solution)/shard_map/ppermute | solution.py:253
  16.3 6.2 %collective-permute-start.1 = (bf16[288,128]{1,0:T(8,128)(2,1)S(1)}, bf16[288,128]{1,0:T(8,128)(2,1)S(1)}, u32[]{:S(2)}, u32[]{:S(2)}) collective-permute-start(bf16[288,128]{1,0:T(8,128)(2,1)S(1)} %factors.1.refs_0_), channel_id=1, source_target_pairs={{0,8},{4,12},{8,0},{12,4},{1,9},{5,13},{9,1},{13,5},{2,10},{6,14},... | collective-permute-start | bytes 221192 | tf_op jit(solution)/shard_map/ppermute | solution.py:253
  16.3 6.2 %collective-permute-start = (bf16[288,128]{1,0:T(8,128)(2,1)S(1)}, bf16[288,128]{1,0:T(8,128)(2,1)S(1)}, u32[]{:S(2)}, u32[]{:S(2)}) collective-permute-start(bf16[288,128]{1,0:T(8,128)(2,1)S(1)} %factors.1.refs_0_), channel_id=1, source_target_pairs={{0,4},{4,0},{8,12},{12,8},{1,5},{5,1},{9,13},{13,9},{2,6},{6,2},{1... | collective-permute-start | bytes 221192 | tf_op jit(solution)/shard_map/ppermute | solution.py:253
  22.6 3.2 %copy-start = (bf16[1,960,4096]{2,1,0:T(8,128)(2,1)S(1)}, bf16[1,960,4096]{2,1,0:T(8,128)(2,1)}, u32[]{:S(2)}) copy-start(bf16[1,960,4096]{2,1,0:T(8,128)(2,1)} %param.13) | copy-start | bytes 23592964
  32.5 1.9 %collective-permute-start.3 = (bf16[144,240]{1,0:T(8,128)(2,1)S(1)}, bf16[144,240]{1,0:T(8,128)(2,1)S(1)}, u32[]{:S(2)}, u32[]{:S(2)}) collective-permute-start(bf16[144,240]{1,0:T(8,128)(2,1)S(1)} %get-tuple-element.10), channel_id=1, source_target_pairs={{0,1},{1,0},{2,3},{3,2},{4,5},{5,4},{6,7},{7,6},{8,9},{9,8},{10,11... | collective-permute-start | bytes 207368 | tf_op jit(solution)/shard_map/ppermute | solution.py:253
  32.5 4.9 %collective-permute-start.4 = (bf16[144,240]{1,0:T(8,128)(2,1)S(1)}, bf16[144,240]{1,0:T(8,128)(2,1)S(1)}, u32[]{:S(2)}, u32[]{:S(2)}) collective-permute-start(bf16[144,240]{1,0:T(8,128)(2,1)S(1)} %get-tuple-element.11), channel_id=1, source_target_pairs={{0,2},{1,3},{2,0},{3,1},{4,6},{5,7},{6,4},{7,5},{8,10},{9,11},{10,... | collective-permute-start | bytes 207368 | tf_op jit(solution)/shard_map/ppermute | solution.py:253
  34.1 4.5 %collective-permute-start.5 = (bf16[144,240]{1,0:T(8,128)(2,1)S(1)}, bf16[144,240]{1,0:T(8,128)(2,1)S(1)}, u32[]{:S(2)}, u32[]{:S(2)}) collective-permute-start(bf16[144,240]{1,0:T(8,128)(2,1)S(1)} %get-tuple-element.12), channel_id=1, source_target_pairs={{0,3},{1,2},{2,1},{3,0},{4,7},{5,6},{6,5},{7,4},{8,11},{9,10},{10,... | collective-permute-start | bytes 207368 | tf_op jit(solution)/shard_map/ppermute | solution.py:253

commit v2 on v1

v2 whole, which is shorter than its diff:
```python
import functools

import jax
import jax.numpy as jnp
from jax import lax
from jax.experimental import pallas as pl
from jax.experimental.pallas import tpu as pltpu
from jax.sharding import PartitionSpec as P

norm_epsilon = 1e-05
f32 = jnp.float32
bf16 = jnp.bfloat16
S = 8
R = 64
B = 4
A = R // B
G = 8
H = 4


def dot_nt(left, right):
    return lax.dot_general(left, right, (((1,), (1,)), ((), ())), preferred_element_type=f32)


def iota(shape, dim):
    return lax.broadcasted_iota(jnp.int32, shape, dim)


def factors_kernel(
    columns,
    width,
    hbm_lengths,
    hbm_hidden,
    hbm_cot,
    hbm_gain,
    hbm_inp,
    hbm_outp,
    packed,
    lengths,
    hidden,
    cot,
    gain,
    inp,
    outp,
    in_acc,
    out_acc,
    sq_acc,
    out_t,
    sems,
):
    chunks = width // columns
    queries = lengths.shape[0]
    rows = queries * S
    full = queries // G * G * S
    half = rows - full
    mid, low = full // 2, half // 2

    def start(source, target, at):
        copy = pltpu.make_async_copy(source, target, sems.at[at])
        copy.start()
        return copy

    head = [
        start(hbm_cot, cot, 0),
        start(hbm_outp, outp, 1),
        start(hbm_gain, gain, 2),
        start(hbm_lengths, lengths, 3),
    ]
    body = []
    for c in range(chunks):
        cut = pl.ds(c * columns, columns)
        body.append(
            [
                start(hbm_inp.at[:, cut], inp.at[c], 4 + 2 * c),
                start(hbm_hidden.at[:, cut], hidden.at[c], 5 + 2 * c),
            ]
        )
    for copy in head:
        copy.wait()
    odd = lax.rem(lax.axis_index("store"), 2)
    at_full = pl.multiple_of(odd * half, half)
    at_half = pl.multiple_of((1 - odd) * full, half)

    out_acc[...] = dot_nt(cot[...], outp[...])
    turned = out_acc[pl.ds(at_full, full), :].T
    for t in range(full // 128):
        out_t[t * R : (t + 1) * R, :] = turned[:, t * 128 : (t + 1) * 128]
    out_t[full // 128 * R :, :half] = out_acc[pl.ds(at_half, half), :].T

    def part(t, b):
        return out_t[pl.ds(t * R + b, A, stride=B), :]

    row = mid + low
    for m in range(full // (G * S)):
        t, at = divmod(m * G * S, 128)
        for b in range(0, B, 2):
            both = [part(t, b + c)[:, at : at + G * S] for c in range(2)]
            packed[row : row + A, :] = jnp.concatenate(both, axis=1).astype(bf16)
            row += A
    packed[row : row + A, :] = jnp.concatenate(
        [part(full // 128, b)[:, :half] for b in range(B)], axis=1
    ).astype(bf16)

    for c in range(chunks):
        for copy in body[c]:
            copy.wait()
        scaled = inp[c].astype(f32) * gain[:, c * columns : (c + 1) * columns].astype(f32)
        high = scaled.astype(bf16)
        rest = (scaled - high.astype(f32)).astype(bf16)
        product = dot_nt(hidden[c], jnp.concatenate([high, rest], axis=0))
        in_acc[...] = product if c == 0 else in_acc[...] + product
        for r in range(0, rows, 16):
            total = None if c == 0 else sq_acc[r : r + 16, :]
            for at in range(0, columns, 128):
                wide = hidden[c, r : r + 16, at : at + 128].astype(f32)
                total = wide * wide if total is None else total + wide * wide
            sq_acc[r : r + 16, :] = total

    mean_square = jnp.sum(sq_acc[...], axis=1, keepdims=True) * (1.0 / width)
    factor = in_acc[:, :R] + in_acc[:, R:]
    factor = factor * lax.rsqrt(mean_square + norm_epsilon)
    position = iota((S, R), 0)
    for q in range(queries):
        out_acc[q * S : (q + 1) * S, :] = jnp.where(
            position < lengths[q], factor[q * S : (q + 1) * S], 0.0
        )
    in_full = out_acc[pl.ds(at_full, full), :]
    in_half = out_acc[pl.ds(at_half, half), :]
    packed[:mid, :] = jnp.concatenate([in_full[:mid], in_full[mid:]], axis=1).astype(bf16)
    packed[mid : mid + low, :] = jnp.concatenate([in_half[:low], in_half[low:]], axis=1).astype(
        bf16
    )


def in_hbm(x):
    return pltpu.with_memory_space_constraint(x, pltpu.HBM)


def factors(lengths, hidden, cotangent, gain, in_projection, out_projection):
    rows, width = hidden.shape
    columns = 1024
    chunks = width // columns
    return pl.pallas_call(
        functools.partial(factors_kernel, columns, width),
        out_shape=jax.ShapeDtypeStruct((rows, 2 * R), bf16),
        in_specs=[pl.BlockSpec(memory_space=pl.ANY)] * 6,
        out_specs=pl.BlockSpec(memory_space=pltpu.VMEM),
        scratch_shapes=[
            pltpu.SMEM(lengths.shape, jnp.int32),
            pltpu.VMEM((chunks, rows, columns), bf16),
            pltpu.VMEM(cotangent.shape, bf16),
            pltpu.VMEM(gain.shape, bf16),
            pltpu.VMEM((chunks, R, columns), bf16),
            pltpu.VMEM(out_projection.shape, bf16),
            pltpu.VMEM((rows, 2 * R), f32),
            pltpu.VMEM((rows, R), f32),
            pltpu.VMEM((rows, 128), f32),
            pltpu.VMEM((-(-rows // 128) * R, 128), f32),
            pltpu.SemaphoreType.DMA((4 + 2 * chunks,)),
        ],
        compiler_params=pltpu.CompilerParams(vmem_limit_bytes=24 * 2**20),
        name="factors",
    )(*[in_hbm(x) for x in (lengths, hidden, cotangent, gain, in_projection, out_projection)])


def fetch_kernel(n_layer, after, store, slab, sems):
    block = slab.shape[1]
    rows = 16 if block % 16 == 0 else 8
    me = lax.axis_index("layer")
    copies = []
    for k in range(n_layer):
        at = pl.multiple_of(partner(me, k, n_layer) * block, rows)
        copies.append(pltpu.make_async_copy(store.at[pl.ds(at, block)], slab.at[k], sems.at[k]))
        copies[-1].start()
    for copy in copies:
        copy.wait()


def fetch(after, store, n_layer):
    rows, features = store.shape
    return pl.pallas_call(
        functools.partial(fetch_kernel, n_layer),
        out_shape=jax.ShapeDtypeStruct((n_layer, rows // n_layer, features), bf16),
        in_specs=[pl.BlockSpec(memory_space=pl.ANY)] * 2,
        out_specs=pl.BlockSpec(memory_space=pltpu.VMEM),
        scratch_shapes=[pltpu.SemaphoreType.DMA((n_layer,))],
        compiler_params=pltpu.CompilerParams(vmem_limit_bytes=12 * 2**20),
        cost_estimate=pl.CostEstimate(
            flops=0, bytes_accessed=2 * rows * features, transcendentals=0
        ),
        name="fetch",
    )(after, in_hbm(store))


def spread_out(tile, owner):
    lanes = tile.shape[1]
    mine = (owner == iota((G, lanes), 0))[None]
    wide = jnp.where(mine, tile.astype(f32)[:, None, :], 0.0)
    return wide.reshape(A * G, lanes).astype(bf16)


def halves(tile):
    wide = tile.astype(f32)
    turned = jnp.concatenate([wide[:, R:], wide[:, :R]], axis=1)
    low = iota(wide.shape, 1) < R
    return [
        jnp.where(mask, x, 0.0).astype(bf16)
        for x in (wide, turned)
        for mask in (low, jnp.logical_not(low))
    ]


def diagonal(low, high):
    zero = jnp.zeros_like(low)
    left = jnp.concatenate([low, high, zero, zero], axis=0)
    right = jnp.concatenate([zero, zero, low, high], axis=0)
    return jnp.concatenate([left, right], axis=1)


def build_grads(shards, base, row0, full_groups, grads):
    mid = full_groups * G * S // 2
    low = H * S // 2
    lane = iota((G, 2 * 128), 1)
    whole_owner = lax.rem(lane, G * S) // S
    half_owner = lax.rem(lane, H * S) // S + H * (lane // 128)

    def whole(shard):
        found = []
        pairs = {}
        for m in range(full_groups):
            first = m % (full_groups // 2)
            if first not in pairs:
                pairs[first] = halves(
                    shards[base + shard, first * G * S : (first + 1) * G * S, :]
                )
            plain_low, plain_high, turned_low, turned_high = pairs[first]
            weights = (
                diagonal(plain_low, turned_high)
                if m < full_groups // 2
                else diagonal(turned_low, plain_high)
            )
            at = mid + low + m * 2 * A
            tile = jnp.concatenate(
                [shards[base + shard, at : at + A, :], shards[base + shard, at + A : at + 2 * A, :]],
                axis=1,
            )
            found.append((spread_out(tile, whole_owner), weights))
        return found

    def joined(shard):
        tiles, weights = [], []
        for s in (shard, shard + 1):
            plain_low, plain_high, turned_low, turned_high = halves(
                shards[base + s, mid : mid + low, :]
            )
            weights.append(
                diagonal(
                    jnp.concatenate([plain_low, turned_low], axis=0),
                    jnp.concatenate([turned_high, plain_high], axis=0),
                )
            )
            at = mid + low + full_groups * 2 * A
            tiles.append(shards[base + s, at : at + A, :])
        return [
            (
                spread_out(jnp.concatenate(tiles, axis=1), half_owner),
                jnp.concatenate(weights, axis=0),
            )
        ]

    groups = []
    for shard in (0, 2):
        groups += whole(shard) + joined(shard) + whole(shard + 1)
    for at in range(0, len(groups), 2):
        first, second = [jnp.dot(x, w, preferred_element_type=f32) for x, w in groups[at : at + 2]]
        for a in range(A):
            pair = [x[a * G : (a + 1) * G] for x in (first, second)]
            grads[pl.ds(row0 + at * G, 2 * G), a * 256 : (a + 1) * 256] = jnp.concatenate(
                pair, axis=0
            ).astype(bf16)


def scores_kernel(n_store, n_layer, full_groups, *refs):
    gathered = refs[:n_store]
    slab = refs[n_store]
    outs = refs[n_store + 1 : n_store + 1 + n_layer]
    shards, grads = refs[n_store + 1 + n_layer :]
    me_store = lax.axis_index("store")
    for k in range(n_store):
        shards[partner(me_store, k, n_store)] = gathered[k][...]
    four = 4 * (full_groups * G + H)
    if n_store == 4:
        build_grads(shards, 0, 0, full_groups, grads)
    else:

        @pl.loop(0, n_store // 4)
        def _(at):
            build_grads(shards, at * 4, pl.multiple_of(at * four, 16), full_groups, grads)

    for k in reversed(range(n_layer)):
        outs[k][...] = dot_nt(grads[...], slab[k]).astype(outs[k].dtype)


def partner(me, k, n):
    return jnp.bitwise_xor(me, k) if n & (n - 1) == 0 else lax.rem(n + k - me, n)


def swap(x, axis, n, k):
    pairs = [(i, i ^ k if n & (n - 1) == 0 else (n + k - i) % n) for i in range(n)]
    return lax.ppermute(x, axis, pairs)


def scores(gathered, slab, n_store, n_layer):
    block, features = slab.shape[1:]
    queries = gathered[0].shape[0] // S
    vmem = pl.BlockSpec(memory_space=pltpu.VMEM)
    return pl.pallas_call(
        functools.partial(scores_kernel, n_store, n_layer, queries // G),
        out_shape=[
            jax.ShapeDtypeStruct((n_store * queries, block), f32 if k == 0 else bf16)
            for k in range(n_layer)
        ],
        in_specs=[vmem] * (n_store + 1),
        out_specs=[vmem] * n_layer,
        scratch_shapes=[
            pltpu.VMEM((n_store,) + gathered[0].shape, bf16),
            pltpu.VMEM((n_store * queries, features), bf16),
        ],
        compiler_params=pltpu.CompilerParams(vmem_limit_bytes=24 * 2**20),
        name="scores",
    )(*gathered, slab)


def on_device(n_store, n_layer, hidden, cotangent, lengths, norm_gain, in_proj, out_proj, store):
    queries, positions, width = hidden.shape[1:]
    packed = factors(
        lengths,
        hidden.reshape(queries * positions, width),
        cotangent.reshape(queries * positions, cotangent.shape[3]),
        norm_gain,
        in_proj[0],
        out_proj[0],
    )
    gathered = [packed] + [swap(packed, "store", n_store, k) for k in range(1, n_store)]
    slab = fetch(packed, store[0], n_layer)
    partial = scores(gathered, slab, n_store, n_layer)
    total = partial[0]
    for k in range(1, n_layer):
        total = total + swap(partial[k], "layer", n_layer, k).astype(f32)
    return total.T


def solution(mesh):
    placed = (
        P("layer", ("grp", "store"), None, None),
        P("layer", ("grp", "store"), None, None),
        P(("grp", "store")),
        P("layer", None),
        P("layer", None, None),
        P("layer", None, None),
        P("layer", ("grp", "store"), None),
    )
    return jax.shard_map(
        functools.partial(on_device, mesh.shape["store"], mesh.shape["layer"]),
        mesh=mesh,
        in_specs=placed,
        out_specs=P(("grp", "store", "layer"), None),
        check_vma=False,
    )
```

time: 39.7 us -> 27.2 us (0.69)
  local copies, waits for them, and re-layouts: 10.2 us -> 0 us
  waiting for transfers between devices: 9.81 us -> 6.4 us
  Pallas kernels: 10.9 us -> 12.2 us
    unnamed x14 -> x0, local copies, waits for them, and re-layouts: 10.2 us -> none
    pallas_call x1 -> x2, Pallas kernels: 4.28 us -> 9.02 us  [the longest x1 5.68 us: factors(): pl.pallas_call(functools.partial(factors_kernel, columns, width), out_sha...]
    ppermute x6, waiting for transfers between devices: 9.81 us -> 6.4 us  [swap(): return lax.ppermute(x, axis, pairs)]
    pallas_call x1, Pallas kernels: 6.63 us -> 3.22 us  [scores(): pl.pallas_call(functools.partial(scores_kernel, n_store, n_layer, queries...]
  transfers between devices with their start and end apart: 6 -> 6, of which waited for: 4 -> 3; matrix products, arithmetic and copies ran while one was open for 0% -> 0% of each run, Pallas kernels for 0% -> 12%
where the time goes in v2:
time: 27.2 us; the launch traced here: 27.1 us
  Pallas kernels  12.2 us (45%)
  starting transfers between devices  7.71 us (28%)
  waiting for transfers between devices  6.4 us (24%)
  other arithmetic  0.7 us (3%)
    ppermute x6, starting transfers between devices, swap(): return lax.ppermute(x, axis, pairs)  7.71 us
    ppermute x6, waiting for transfers between devices, swap(): return lax.ppermute(x, axis, pairs)  6.4 us
    pallas_call x1, Pallas kernels, factors(): pl.pallas_call(functools.partial(factors_kernel, columns, width), out_sha...  5.68 us
    pallas_call x1, Pallas kernels, fetch(): pl.pallas_call(functools.partial(fetch_kernel, n_layer), out_shape=jax.Sh...  3.34 us
    pallas_call x1, Pallas kernels, scores(): pl.pallas_call(functools.partial(scores_kernel, n_store, n_layer, queries...  3.22 us
    transpose x1, other arithmetic, on_device(): return total.T  0.7 us
  transfers between devices with their start and end apart: 6, of which 3 were waited for; matrix products, arithmetic and copies ran while one was open for 0% of the time, Pallas kernels for 12%

profile of v2, /device:TPU:0, one launch (start us, length us, event | category | flops | bytes accessed | tf_op | source)
XLA Modules:
  0.0 27.1 jit_solution(8258810961825409758)
XLA Ops:
  0.0 5.7 %factors.1.after.refs_0_ = bf16[288,128]{1,0:T(8,128)(2,1)S(1)} custom-call(s32[36]{0:T(128)} %hbm_lengths.1, bf16[288,8192]{1,0:T(8,128)(2,1)} %bitcast.8, bf16[288,1024]{1,0:T(8,128)(2,1)} %bitcast.10, bf16[1,8192]{1,0:T(2,128)(2,1)} %hbm_gain.1, bf16[64,8192]{1,0:T(8,128)(2,1)} %bitcast.9, bf16[64,1024]{1,0:T(8,128)(2,1)} %bitcast.11), custom_call_target="tpu_custom_call" | custom-call | tf_op jit(solution)/shard_map/factors/pallas_call | solution.py:143
  5.7 5.1 %collective-permute-start.2 = (bf16[288,128]{1,0:T(8,128)(2,1)S(1)}, bf16[288,128]{1,0:T(8,128)(2,1)S(1)}, u32[]{:S(2)}, u32[]{:S(2)}) collective-permute-start(bf16[288,128]{1,0:T(8,128)(2,1)S(1)} %factors.1.after.refs_0_), channel_id=1, source_target_pairs={{0,12},{4,8},{8,4},{12,0},{1,13},{5,9},{9,5},{13,1},{2,14},{6,10},... | collective-permute-start | bytes 221192 | tf_op jit(solution)/shard_map/ppermute | solution.py:310
  10.8 0.0 collective-permute-start.1
  10.8 0.6 %collective-permute-start = (bf16[288,128]{1,0:T(8,128)(2,1)S(1)}, bf16[288,128]{1,0:T(8,128)(2,1)S(1)}, u32[]{:S(2)}, u32[]{:S(2)}) collective-permute-start(bf16[288,128]{1,0:T(8,128)(2,1)S(1)} %factors.1.after.refs_0_), channel_id=1, source_target_pairs={{0,4},{4,0},{8,12},{12,8},{1,5},{5,1},{9,13},{13,9},{2,6},{6,2},{1... | collective-permute-start | bytes 221192 | tf_op jit(solution)/shard_map/ppermute | solution.py:310
  11.5 3.3 %fetch.1.refs_4_ = bf16[4,240,4096]{2,1,0:T(8,128)(2,1)S(1)} custom-call(bf16[288,128]{1,0:T(8,128)(2,1)S(1)} %factors.1.after.refs_0_, bf16[960,4096]{1,0:T(8,128)(2,1)} %bitcast.7), custom_call_target="tpu_custom_call" | custom-call | bytes 7864320 | tf_op jit(solution)/shard_map/fetch/pallas_call | solution.py:181
  14.8 0.0 collective-permute-done.2.refs_3_
  14.8 2.2 %collective-permute-done.1.refs_2_ = bf16[288,128]{1,0:T(8,128)(2,1)S(1)} collective-permute-done((bf16[288,128]{1,0:T(8,128)(2,1)S(1)}, bf16[288,128]{1,0:T(8,128)(2,1)S(1)}, u32[]{:S(2)}, u32[]{:S(2)}) %collective-permute-start.1) | collective-permute-done | bytes 73760 | tf_op jit(solution)/shard_map/ppermute | solution.py:310
  17.0 0.0 collective-permute-done.refs_1_
  17.0 3.2 %scores.1 = (f32[144,240]{1,0:T(8,128)S(1)}, bf16[144,240]{1,0:T(8,128)(2,1)S(1)}, bf16[144,240]{1,0:T(8,128)(2,1)S(1)}, bf16[144,240]{1,0:T(8,128)(2,1)S(1)}) custom-call(bf16[288,128]{1,0:T(8,128)(2,1)S(1)} %factors.1.after.refs_0_, bf16[288,128]{1,0:T(8,128)(2,1)S(1)} %collective-permute-done.refs_1_, ...), custom_call_target="tpu_custom_call" | custom-call | tf_op jit(solution)/shard_map/scores/pallas_call | solution.py:317
  20.3 0.1 collective-permute-start.3
  20.3 1.6 %collective-permute-start.4 = (bf16[144,240]{1,0:T(8,128)(2,1)S(1)}, bf16[144,240]{1,0:T(8,128)(2,1)S(1)}, u32[]{:S(2)}, u32[]{:S(2)}) collective-permute-start(bf16[144,240]{1,0:T(8,128)(2,1)S(1)} %get-tuple-element.11), channel_id=1, source_target_pairs={{0,2},{1,3},{2,0},{3,1},{4,6},{5,7},{6,4},{7,5},{8,10},{9,11},{10,... | collective-permute-start | bytes 207368 | tf_op jit(solution)/shard_map/ppermute | solution.py:310
  21.9 0.3 %collective-permute-start.5 = (bf16[144,240]{1,0:T(8,128)(2,1)S(1)}, bf16[144,240]{1,0:T(8,128)(2,1)S(1)}, u32[]{:S(2)}, u32[]{:S(2)}) collective-permute-start(bf16[144,240]{1,0:T(8,128)(2,1)S(1)} %get-tuple-element.12), channel_id=1, source_target_pairs={{0,3},{1,2},{2,1},{3,0},{4,7},{5,6},{6,5},{7,4},{8,11},{9,10},{10,... | collective-permute-start | bytes 207368 | tf_op jit(solution)/shard_map/ppermute | solution.py:310
  22.2 0.0 collective-permute-done.3
  22.2 3.0 %collective-permute-done.4 = bf16[144,240]{1,0:T(8,128)(2,1)S(1)} collective-permute-done((bf16[144,240]{1,0:T(8,128)(2,1)S(1)}, bf16[144,240]{1,0:T(8,128)(2,1)S(1)}, u32[]{:S(2)}, u32[]{:S(2)}) %collective-permute-start.4) | collective-permute-done | bytes 69152 | tf_op jit(solution)/shard_map/ppermute | solution.py:310
  25.2 1.2 %collective-permute-done.5 = bf16[144,240]{1,0:T(8,128)(2,1)S(1)} collective-permute-done((bf16[144,240]{1,0:T(8,128)(2,1)S(1)}, bf16[144,240]{1,0:T(8,128)(2,1)S(1)}, u32[]{:S(2)}, u32[]{:S(2)}) %collective-permute-start.5) | collective-permute-done | bytes 69152 | tf_op jit(solution)/shard_map/ppermute | solution.py:310
  26.4 0.7 %add_bitcast_fusion = f32[240,144]{0,1:T(8,128)} fusion(bf16[144,240]{1,0:T(8,128)(2,1)S(1)} %collective-permute-done.5, bf16[144,240]{1,0:T(8,128)(2,1)S(1)} %collective-permute-done.4, f32[144,240]{1,0:T(8,128)S(1)} %get-tuple-element.9, bf16[144,240]{1,0:T(8,128)(2,1)S(1)} %collective-permute-done.3), kind=kLoop, calls=%fused_computation | loop fusion | flops 207360 | bytes 483840 | tf_op jit(solution)/shard_map/transpose | solution.py:350
Async XLA Ops:
  5.7 9.1 %collective-permute-start.2 = (bf16[288,128]{1,0:T(8,128)(2,1)S(1)}, bf16[288,128]{1,0:T(8,128)(2,1)S(1)}, u32[]{:S(2)}, u32[]{:S(2)}) collective-permute-start(bf16[288,128]{1,0:T(8,128)(2,1)S(1)} %factors.1.after.refs_0_), channel_id=1, source_target_pairs={{0,12},{4,8},{8,4},{12,0},{1,13},{5,9},{9,5},{13,1},{2,14},{6,10},... | collective-permute-start | bytes 221192 | tf_op jit(solution)/shard_map/ppermute | solution.py:310
  10.8 6.2 %collective-permute-start.1 = (bf16[288,128]{1,0:T(8,128)(2,1)S(1)}, bf16[288,128]{1,0:T(8,128)(2,1)S(1)}, u32[]{:S(2)}, u32[]{:S(2)}) collective-permute-start(bf16[288,128]{1,0:T(8,128)(2,1)S(1)} %factors.1.after.refs_0_), channel_id=1, source_target_pairs={{0,8},{4,12},{8,0},{12,4},{1,9},{5,13},{9,1},{13,5},{2,10},{6,14},... | collective-permute-start | bytes 221192 | tf_op jit(solution)/shard_map/ppermute | solution.py:310
  10.8 6.2 %collective-permute-start = (bf16[288,128]{1,0:T(8,128)(2,1)S(1)}, bf16[288,128]{1,0:T(8,128)(2,1)S(1)}, u32[]{:S(2)}, u32[]{:S(2)}) collective-permute-start(bf16[288,128]{1,0:T(8,128)(2,1)S(1)} %factors.1.after.refs_0_), channel_id=1, source_target_pairs={{0,4},{4,0},{8,12},{12,8},{1,5},{5,1},{9,13},{13,9},{2,6},{6,2},{1... | collective-permute-start | bytes 221192 | tf_op jit(solution)/shard_map/ppermute | solution.py:310
  20.3 1.9 %collective-permute-start.3 = (bf16[144,240]{1,0:T(8,128)(2,1)S(1)}, bf16[144,240]{1,0:T(8,128)(2,1)S(1)}, u32[]{:S(2)}, u32[]{:S(2)}) collective-permute-start(bf16[144,240]{1,0:T(8,128)(2,1)S(1)} %get-tuple-element.10), channel_id=1, source_target_pairs={{0,1},{1,0},{2,3},{3,2},{4,5},{5,4},{6,7},{7,6},{8,9},{9,8},{10,11... | collective-permute-start | bytes 207368 | tf_op jit(solution)/shard_map/ppermute | solution.py:310
  20.3 4.8 %collective-permute-start.4 = (bf16[144,240]{1,0:T(8,128)(2,1)S(1)}, bf16[144,240]{1,0:T(8,128)(2,1)S(1)}, u32[]{:S(2)}, u32[]{:S(2)}) collective-permute-start(bf16[144,240]{1,0:T(8,128)(2,1)S(1)} %get-tuple-element.11), channel_id=1, source_target_pairs={{0,2},{1,3},{2,0},{3,1},{4,6},{5,7},{6,4},{7,5},{8,10},{9,11},{10,... | collective-permute-start | bytes 207368 | tf_op jit(solution)/shard_map/ppermute | solution.py:310
  21.9 4.5 %collective-permute-start.5 = (bf16[144,240]{1,0:T(8,128)(2,1)S(1)}, bf16[144,240]{1,0:T(8,128)(2,1)S(1)}, u32[]{:S(2)}, u32[]{:S(2)}) collective-permute-start(bf16[144,240]{1,0:T(8,128)(2,1)S(1)} %get-tuple-element.12), channel_id=1, source_target_pairs={{0,3},{1,2},{2,1},{3,0},{4,7},{5,6},{6,5},{7,4},{8,11},{9,10},{10,... | collective-permute-start | bytes 207368 | tf_op jit(solution)/shard_map/ppermute | solution.py:310

commit v3 on v2

--- a/solution.py
+++ b/solution.py
@@ -27,8 +27,7 @@
 
 
 def factors_kernel(
-    columns,
-    width,
+    cuts,
     hbm_lengths,
     hbm_hidden,
     hbm_cot,
@@ -42,13 +41,14 @@
     gain,
     inp,
     outp,
+    weights,
     in_acc,
     out_acc,
     sq_acc,
     out_t,
     sems,
 ):
-    chunks = width // columns
+    width = hidden.shape[1]
     queries = lengths.shape[0]
     rows = queries * S
     full = queries // G * G * S
@@ -60,27 +60,31 @@
         copy.start()
         return copy
 
-    head = [
-        start(hbm_cot, cot, 0),
-        start(hbm_outp, outp, 1),
-        start(hbm_gain, gain, 2),
-        start(hbm_lengths, lengths, 3),
-    ]
-    body = []
-    for c in range(chunks):
-        cut = pl.ds(c * columns, columns)
-        body.append(
-            [
-                start(hbm_inp.at[:, cut], inp.at[c], 4 + 2 * c),
-                start(hbm_hidden.at[:, cut], hidden.at[c], 5 + 2 * c),
-            ]
-        )
-    for copy in head:
-        copy.wait()
+    copy_gain = start(hbm_gain, gain, 0)
+    copy_inp = start(hbm_inp, inp, 1)
+    copy_outp = start(hbm_outp, outp, 2)
+    copy_cot = start(hbm_cot, cot, 3)
+    copy_lengths = start(hbm_lengths, lengths, 4)
+    copies = []
+    for c in range(len(cuts) - 1):
+        cut = pl.ds(cuts[c], cuts[c + 1] - cuts[c])
+        copies.append(start(hbm_hidden.at[:, cut], hidden.at[:, cut], 5 + c))
     odd = lax.rem(lax.axis_index("store"), 2)
     at_full = pl.multiple_of(odd * half, half)
     at_half = pl.multiple_of((1 - odd) * full, half)
 
+    copy_gain.wait()
+    copy_inp.wait()
+    for at in range(0, width, 512):
+        cut = slice(at, at + 512)
+        scaled = inp[:, cut].astype(f32) * gain[:, cut].astype(f32)
+        high = scaled.astype(bf16)
+        weights[:R, cut] = high
+        weights[R:, cut] = (scaled - high.astype(f32)).astype(bf16)
+
+    copy_outp.wait()
+    copy_cot.wait()
+    copy_lengths.wait()
     out_acc[...] = dot_nt(cot[...], outp[...])
     turned = out_acc[pl.ds(at_full, full), :].T
     for t in range(full // 128):
@@ -101,18 +105,15 @@
         [part(full // 128, b)[:, :half] for b in range(B)], axis=1
     ).astype(bf16)
 
-    for c in range(chunks):
-        for copy in body[c]:
-            copy.wait()
-        scaled = inp[c].astype(f32) * gain[:, c * columns : (c + 1) * columns].astype(f32)
-        high = scaled.astype(bf16)
-        rest = (scaled - high.astype(f32)).astype(bf16)
-        product = dot_nt(hidden[c], jnp.concatenate([high, rest], axis=0))
+    for c, copy in enumerate(copies):
+        copy.wait()
+        cut = slice(cuts[c], cuts[c + 1])
+        product = dot_nt(hidden[:, cut], weights[:, cut])
         in_acc[...] = product if c == 0 else in_acc[...] + product
         for r in range(0, rows, 16):
             total = None if c == 0 else sq_acc[r : r + 16, :]
-            for at in range(0, columns, 128):
-                wide = hidden[c, r : r + 16, at : at + 128].astype(f32)
+            for at in range(cuts[c], cuts[c + 1], 128):
+                wide = hidden[r : r + 16, at : at + 128].astype(f32)
                 total = wide * wide if total is None else total + wide * wide
             sq_acc[r : r + 16, :] = total
 
@@ -138,25 +139,25 @@
 
 def factors(lengths, hidden, cotangent, gain, in_projection, out_projection):
     rows, width = hidden.shape
-    columns = 1024
-    chunks = width // columns
+    cuts = [width * part // 8 for part in (0, 2, 4, 6, 7, 8)]
     return pl.pallas_call(
-        functools.partial(factors_kernel, columns, width),
+        functools.partial(factors_kernel, cuts),
         out_shape=jax.ShapeDtypeStruct((rows, 2 * R), bf16),
         in_specs=[pl.BlockSpec(memory_space=pl.ANY)] * 6,
         out_specs=pl.BlockSpec(memory_space=pltpu.VMEM),
         scratch_shapes=[
             pltpu.SMEM(lengths.shape, jnp.int32),
-            pltpu.VMEM((chunks, rows, columns), bf16),
+            pltpu.VMEM(hidden.shape, bf16),
             pltpu.VMEM(cotangent.shape, bf16),
             pltpu.VMEM(gain.shape, bf16),
-            pltpu.VMEM((chunks, R, columns), bf16),
+            pltpu.VMEM(in_projection.shape, bf16),
             pltpu.VMEM(out_projection.shape, bf16),
+            pltpu.VMEM((2 * R, width), bf16),
             pltpu.VMEM((rows, 2 * R), f32),
             pltpu.VMEM((rows, R), f32),
             pltpu.VMEM((rows, 128), f32),
             pltpu.VMEM((-(-rows // 128) * R, 128), f32),
-            pltpu.SemaphoreType.DMA((4 + 2 * chunks,)),
+            pltpu.SemaphoreType.DMA((4 + len(cuts),)),
         ],
         compiler_params=pltpu.CompilerParams(vmem_limit_bytes=24 * 2**20),
         name="factors",
@@ -280,11 +281,11 @@
             ).astype(bf16)
 
 
-def scores_kernel(n_store, n_layer, full_groups, *refs):
+def far_kernel(n_store, full_groups, *refs):
     gathered = refs[:n_store]
-    slab = refs[n_store]
-    outs = refs[n_store + 1 : n_store + 1 + n_layer]
-    shards, grads = refs[n_store + 1 + n_layer :]
+    slab, grads = refs[n_store : n_store + 2]
+    outs = refs[n_store + 2 : -1]
+    shards = refs[-1]
     me_store = lax.axis_index("store")
     for k in range(n_store):
         shards[partner(me_store, k, n_store)] = gathered[k][...]
@@ -297,8 +298,13 @@
         def _(at):
             build_grads(shards, at * 4, pl.multiple_of(at * four, 16), full_groups, grads)
 
-    for k in reversed(range(n_layer)):
-        outs[k][...] = dot_nt(grads[...], slab[k]).astype(outs[k].dtype)
+    for at, out in enumerate(outs):
+        out[...] = dot_nt(grads[...], slab[2 + at]).astype(out.dtype)
+
+
+def near_kernel(grads, slab, *outs):
+    for k, out in enumerate(outs):
+        out[...] = dot_nt(grads[...], slab[k]).astype(out.dtype)
 
 
 def partner(me, k, n):
@@ -310,25 +316,45 @@
     return lax.ppermute(x, axis, pairs)
 
 
-def scores(gathered, slab, n_store, n_layer):
-    block, features = slab.shape[1:]
+def far_scores(gathered, slab, n_store):
+    n_layer, block, features = slab.shape
     queries = gathered[0].shape[0] // S
     vmem = pl.BlockSpec(memory_space=pltpu.VMEM)
     return pl.pallas_call(
-        functools.partial(scores_kernel, n_store, n_layer, queries // G),
-        out_shape=[
-            jax.ShapeDtypeStruct((n_store * queries, block), f32 if k == 0 else bf16)
-            for k in range(n_layer)
+        functools.partial(far_kernel, n_store, queries // G),
+        out_shape=[jax.ShapeDtypeStruct((n_store * queries, features), bf16)]
+        + [
+            jax.ShapeDtypeStruct((n_store * queries, block), f32 if k % 2 == 0 else bf16)
+            for k in range(2, n_layer)
         ],
         in_specs=[vmem] * (n_store + 1),
-        out_specs=[vmem] * n_layer,
-        scratch_shapes=[
-            pltpu.VMEM((n_store,) + gathered[0].shape, bf16),
-            pltpu.VMEM((n_store * queries, features), bf16),
+        out_specs=[vmem] * (n_layer - 1),
+        scratch_shapes=[pltpu.VMEM((n_store,) + gathered[0].shape, bf16)],
+        compiler_params=pltpu.CompilerParams(vmem_limit_bytes=24 * 2**20),
+        name="far_scores",
+    )(*gathered, slab)
+
+
+def near_scores(grads, slab):
+    block, features = slab.shape[1:]
+    queries = grads.shape[0]
+    vmem = pl.BlockSpec(memory_space=pltpu.VMEM)
+    return pl.pallas_call(
+        near_kernel,
+        out_shape=[
+            jax.ShapeDtypeStruct((queries, block), f32),
+            jax.ShapeDtypeStruct((queries, block), bf16),
         ],
+        in_specs=[vmem] * 2,
+        out_specs=[vmem] * 2,
         compiler_params=pltpu.CompilerParams(vmem_limit_bytes=24 * 2**20),
-        name="scores",
-    )(*gathered, slab)
+        cost_estimate=pl.CostEstimate(
+            flops=4 * queries * block * features,
+            bytes_accessed=4 * block * features,
+            transcendentals=0,
+        ),
+        name="near_scores",
+    )(grads, slab)
 
 
 def on_device(n_store, n_layer, hidden, cotangent, lengths, norm_gain, in_proj, out_proj, store):
@@ -343,10 +369,13 @@
     )
     gathered = [packed] + [swap(packed, "store", n_store, k) for k in range(1, n_store)]
     slab = fetch(packed, store[0], n_layer)
-    partial = scores(gathered, slab, n_store, n_layer)
-    total = partial[0]
-    for k in range(1, n_layer):
-        total = total + swap(partial[k], "layer", n_layer, k).astype(f32)
+    grads, *far = far_scores(gathered, slab, n_store)
+    crossed = [swap(x, "layer", n_layer, 1) for x in far[1::2]]
+    own, other = near_scores(grads, slab)
+    joined = [(x + y.astype(f32)).astype(bf16) for x, y in zip(far[::2], crossed)]
+    total = own + swap(other, "layer", n_layer, 1).astype(f32)
+    for at, x in enumerate(joined):
+        total = total + swap(x, "layer", n_layer, 2 + 2 * at).astype(f32)
     return total.T
 
 

time: 27.2 us -> 26.5 us (0.974)
  waiting for transfers between devices: 6.4 us -> 5.07 us
  Pallas kernels: 12.2 us -> 12.6 us
    ppermute x6, waiting for transfers between devices: 6.4 us -> 5.07 us  [swap(): return lax.ppermute(x, axis, pairs)]
    pallas_call x2 -> x3, Pallas kernels: 8.89 us -> 9.21 us  [the longest x1 5.82 us: factors(): pl.pallas_call(functools.partial(factors_kernel, cuts), out_shape=jax.Sha...]
  transfers between devices with their start and end apart: 6 -> 6, of which waited for: 3 -> 2; matrix products, arithmetic and copies ran while one was open for 0% -> 0% of each run, Pallas kernels for 12% -> 18%
where the time goes in v3:
time: 26.5 us; the launch traced here: 26.4 us
  Pallas kernels  12.6 us (48%)
  starting transfers between devices  7.97 us (30%)
  waiting for transfers between devices  5.07 us (19%)
  other arithmetic  0.71 us (3%)
    ppermute x6, starting transfers between devices, swap(): return lax.ppermute(x, axis, pairs)  7.97 us
    pallas_call x1, Pallas kernels, factors(): pl.pallas_call(functools.partial(factors_kernel, cuts), out_shape=jax.Sha...  5.82 us
    ppermute x6, waiting for transfers between devices, swap(): return lax.ppermute(x, axis, pairs)  5.07 us
    pallas_call x1, Pallas kernels, fetch(): pl.pallas_call(functools.partial(fetch_kernel, n_layer), out_shape=jax.Sh...  3.34 us
    pallas_call x1, Pallas kernels, far_scores(): pl.pallas_call(functools.partial(far_kernel, n_store, queries // G), out_...  1.91 us
    pallas_call x1, Pallas kernels, near_scores(): pl.pallas_call(near_kernel, out_shape=[jax.ShapeDtypeStruct((queries, blo...  1.48 us
    transpose x1, other arithmetic, on_device(): return total.T  0.69 us
  transfers between devices with their start and end apart: 6, of which 2 were waited for; matrix products, arithmetic and copies ran while one was open for 0% of the time, Pallas kernels for 18%

profile of v3, /device:TPU:0, one launch (start us, length us, event | category | flops | bytes accessed | tf_op | source)
XLA Modules:
  0.0 26.4 jit_solution(4551281008353082806)
XLA Ops:
  0.0 5.8 %factors.1.after.refs_0_ = bf16[288,128]{1,0:T(8,128)(2,1)S(1)} custom-call(s32[36]{0:T(128)} %hbm_lengths.1, bf16[288,8192]{1,0:T(8,128)(2,1)} %bitcast.8, bf16[288,1024]{1,0:T(8,128)(2,1)} %bitcast.10, bf16[1,8192]{1,0:T(2,128)(2,1)} %hbm_gain.1, bf16[64,8192]{1,0:T(8,128)(2,1)} %bitcast.9, bf16[64,1024]{1,0:T(8,128)(2,1)} %bitcast.11), custom_call_target="tpu_custom_call" | custom-call | tf_op jit(solution)/shard_map/factors/pallas_call | solution.py:143
  5.8 5.1 %collective-permute-start.2 = (bf16[288,128]{1,0:T(8,128)(2,1)S(1)}, bf16[288,128]{1,0:T(8,128)(2,1)S(1)}, u32[]{:S(2)}, u32[]{:S(2)}) collective-permute-start(bf16[288,128]{1,0:T(8,128)(2,1)S(1)} %factors.1.after.refs_0_), channel_id=1, source_target_pairs={{0,12},{4,8},{8,4},{12,0},{1,13},{5,9},{9,5},{13,1},{2,14},{6,10},... | collective-permute-start | bytes 221192 | tf_op jit(solution)/shard_map/ppermute | solution.py:316
  11.0 0.0 collective-permute-start.1
  11.0 0.6 %collective-permute-start = (bf16[288,128]{1,0:T(8,128)(2,1)S(1)}, bf16[288,128]{1,0:T(8,128)(2,1)S(1)}, u32[]{:S(2)}, u32[]{:S(2)}) collective-permute-start(bf16[288,128]{1,0:T(8,128)(2,1)S(1)} %factors.1.after.refs_0_), channel_id=1, source_target_pairs={{0,4},{4,0},{8,12},{12,8},{1,5},{5,1},{9,13},{13,9},{2,6},{6,2},{1... | collective-permute-start | bytes 221192 | tf_op jit(solution)/shard_map/ppermute | solution.py:316
  11.6 3.3 %fetch.1.refs_4_.slab = bf16[4,240,4096]{2,1,0:T(8,128)(2,1)S(1)} custom-call(bf16[288,128]{1,0:T(8,128)(2,1)S(1)} %factors.1.after.refs_0_, bf16[960,4096]{1,0:T(8,128)(2,1)} %bitcast.7), custom_call_target="tpu_custom_call" | custom-call | bytes 7864320 | tf_op jit(solution)/shard_map/fetch/pallas_call | solution.py:182
  15.0 0.0 collective-permute-done.2.refs_3_
  15.0 2.2 %collective-permute-done.1.refs_2_ = bf16[288,128]{1,0:T(8,128)(2,1)S(1)} collective-permute-done((bf16[288,128]{1,0:T(8,128)(2,1)S(1)}, bf16[288,128]{1,0:T(8,128)(2,1)S(1)}, u32[]{:S(2)}, u32[]{:S(2)}) %collective-permute-start.1) | collective-permute-done | bytes 73760 | tf_op jit(solution)/shard_map/ppermute | solution.py:316
  17.2 0.0 collective-permute-done.refs_1_
  17.2 1.9 %far_scores.1 = (bf16[144,4096]{1,0:T(8,128)(2,1)S(1)}, f32[144,240]{1,0:T(8,128)S(1)}, bf16[144,240]{1,0:T(8,128)(2,1)S(1)}) custom-call(bf16[288,128]{1,0:T(8,128)(2,1)S(1)} %factors.1.after.refs_0_, bf16[288,128]{1,0:T(8,128)(2,1)S(1)} %collective-permute-done.refs_1_, bf16[288,128]{1,0:T(8,128)(2,1)S(1)} %collective-permute-done.1.refs_2_, ...), custom_call_target="tpu_custom_call" | custom-call | tf_op jit(solution)/shard_map/far_scores/pallas_call | solution.py:323
  19.1 0.1 collective-permute-start.4
  19.2 1.5 %near_scores.1 = (f32[144,240]{1,0:T(8,128)S(1)}, bf16[144,240]{1,0:T(8,128)(2,1)S(1)}) custom-call(bf16[144,4096]{1,0:T(8,128)(2,1)S(1)} %get-tuple-element.10.grads, bf16[4,240,4096]{2,1,0:T(8,128)(2,1)S(1)} %fetch.1.refs_4_.slab), custom_call_target="tpu_custom_call" | custom-call | flops 566231040 | bytes 3932160 | tf_op jit(solution)/shard_map/near_scores/pallas_call | solution.py:342
  20.7 0.6 %collective-permute-start.3 = (bf16[144,240]{1,0:T(8,128)(2,1)S(1)}, bf16[144,240]{1,0:T(8,128)(2,1)S(1)}, u32[]{:S(2)}, u32[]{:S(2)}) collective-permute-start(bf16[144,240]{1,0:T(8,128)(2,1)S(1)} %get-tuple-element.12), channel_id=1, source_target_pairs={{0,1},{1,0},{2,3},{3,2},{4,5},{5,4},{6,7},{7,6},{8,9},{9,8},{10,11... | collective-permute-start | bytes 207368 | tf_op jit(solution)/shard_map/ppermute | solution.py:316
  21.2 0.0 collective-permute-done.4
  21.2 1.6 %collective-permute-start.5 = (bf16[144,240]{1,0:T(8,128)(2,1)S(1)}, bf16[144,240]{1,0:T(8,128)(2,1)S(1)}, u32[]{:S(2)}, u32[]{:S(2)}) collective-permute-start(bf16[144,240]{1,0:T(8,128)(2,1)S(1)} %add_convert_fusion), channel_id=1, source_target_pairs={{0,2},{1,3},{2,0},{3,1},{4,6},{5,7},{6,4},{7,5},{8,10},{9,11},{10,... | collective-permute-start | bytes 207368 | tf_op jit(solution)/shard_map/ppermute | solution.py:316
  22.8 0.0 collective-permute-done.3
  22.8 2.9 %collective-permute-done.5 = bf16[144,240]{1,0:T(8,128)(2,1)S(1)} collective-permute-done((bf16[144,240]{1,0:T(8,128)(2,1)S(1)}, bf16[144,240]{1,0:T(8,128)(2,1)S(1)}, u32[]{:S(2)}, u32[]{:S(2)}) %collective-permute-start.5) | collective-permute-done | bytes 69152 | tf_op jit(solution)/shard_map/ppermute | solution.py:316
  25.7 0.7 %add_bitcast_fusion = f32[240,144]{0,1:T(8,128)} fusion(bf16[144,240]{1,0:T(8,128)(2,1)S(1)} %collective-permute-done.5, f32[144,240]{1,0:T(8,128)S(1)} %get-tuple-element.11, bf16[144,240]{1,0:T(8,128)(2,1)S(1)} %collective-permute-done.3), kind=kLoop, calls=%fused_computation | loop fusion | flops 138240 | bytes 414720 | tf_op jit(solution)/shard_map/transpose | solution.py:379
  (1 shorter events, 0.0 us)
Async XLA Ops:
  5.8 9.1 %collective-permute-start.2 = (bf16[288,128]{1,0:T(8,128)(2,1)S(1)}, bf16[288,128]{1,0:T(8,128)(2,1)S(1)}, u32[]{:S(2)}, u32[]{:S(2)}) collective-permute-start(bf16[288,128]{1,0:T(8,128)(2,1)S(1)} %factors.1.after.refs_0_), channel_id=1, source_target_pairs={{0,12},{4,8},{8,4},{12,0},{1,13},{5,9},{9,5},{13,1},{2,14},{6,10},... | collective-permute-start | bytes 221192 | tf_op jit(solution)/shard_map/ppermute | solution.py:316
  11.0 6.2 %collective-permute-start.1 = (bf16[288,128]{1,0:T(8,128)(2,1)S(1)}, bf16[288,128]{1,0:T(8,128)(2,1)S(1)}, u32[]{:S(2)}, u32[]{:S(2)}) collective-permute-start(bf16[288,128]{1,0:T(8,128)(2,1)S(1)} %factors.1.after.refs_0_), channel_id=1, source_target_pairs={{0,8},{4,12},{8,0},{12,4},{1,9},{5,13},{9,1},{13,5},{2,10},{6,14},... | collective-permute-start | bytes 221192 | tf_op jit(solution)/shard_map/ppermute | solution.py:316
  11.0 6.2 %collective-permute-start = (bf16[288,128]{1,0:T(8,128)(2,1)S(1)}, bf16[288,128]{1,0:T(8,128)(2,1)S(1)}, u32[]{:S(2)}, u32[]{:S(2)}) collective-permute-start(bf16[288,128]{1,0:T(8,128)(2,1)S(1)} %factors.1.after.refs_0_), channel_id=1, source_target_pairs={{0,4},{4,0},{8,12},{12,8},{1,5},{5,1},{9,13},{13,9},{2,6},{6,2},{1... | collective-permute-start | bytes 221192 | tf_op jit(solution)/shard_map/ppermute | solution.py:316
  19.1 2.1 %collective-permute-start.4 = (bf16[144,240]{1,0:T(8,128)(2,1)S(1)}, bf16[144,240]{1,0:T(8,128)(2,1)S(1)}, u32[]{:S(2)}, u32[]{:S(2)}) collective-permute-start(bf16[144,240]{1,0:T(8,128)(2,1)S(1)} %get-tuple-element.14), channel_id=1, source_target_pairs={{0,1},{1,0},{2,3},{3,2},{4,5},{5,4},{6,7},{7,6},{8,9},{9,8},{10,11... | collective-permute-start | bytes 207368 | tf_op jit(solution)/shard_map/ppermute | solution.py:316
  20.7 2.1 %collective-permute-start.3 = (bf16[144,240]{1,0:T(8,128)(2,1)S(1)}, bf16[144,240]{1,0:T(8,128)(2,1)S(1)}, u32[]{:S(2)}, u32[]{:S(2)}) collective-permute-start(bf16[144,240]{1,0:T(8,128)(2,1)S(1)} %get-tuple-element.12), channel_id=1, source_target_pairs={{0,1},{1,0},{2,3},{3,2},{4,5},{5,4},{6,7},{7,6},{8,9},{9,8},{10,11... | collective-permute-start | bytes 207368 | tf_op jit(solution)/shard_map/ppermute | solution.py:316
  21.2 4.4 %collective-permute-start.5 = (bf16[144,240]{1,0:T(8,128)(2,1)S(1)}, bf16[144,240]{1,0:T(8,128)(2,1)S(1)}, u32[]{:S(2)}, u32[]{:S(2)}) collective-permute-start(bf16[144,240]{1,0:T(8,128)(2,1)S(1)} %add_convert_fusion), channel_id=1, source_target_pairs={{0,2},{1,3},{2,0},{3,1},{4,6},{5,7},{6,4},{7,5},{8,10},{9,11},{10,... | collective-permute-start | bytes 207368 | tf_op jit(solution)/shard_map/ppermute | solution.py:316

commit v4 on v3

--- a/solution.py
+++ b/solution.py
@@ -16,6 +16,7 @@
 A = R // B
 G = 8
 H = 4
+LANES = 128
 
 
 def dot_nt(left, right):
@@ -48,7 +49,7 @@
     out_t,
     sems,
 ):
-    width = hidden.shape[1]
+    width = hbm_hidden.shape[1]
     queries = lengths.shape[0]
     rows = queries * S
     full = queries // G * G * S
@@ -65,10 +66,10 @@
     copy_outp = start(hbm_outp, outp, 2)
     copy_cot = start(hbm_cot, cot, 3)
     copy_lengths = start(hbm_lengths, lengths, 4)
-    copies = []
-    for c in range(len(cuts) - 1):
-        cut = pl.ds(cuts[c], cuts[c + 1] - cuts[c])
-        copies.append(start(hbm_hidden.at[:, cut], hidden.at[:, cut], 5 + c))
+    tiles = hidden.shape[0]
+    copies = [
+        start(hbm_hidden.at[:, pl.ds(t * LANES, LANES)], hidden.at[t], 5 + t) for t in range(tiles)
+    ]
     odd = lax.rem(lax.axis_index("store"), 2)
     at_full = pl.multiple_of(odd * half, half)
     at_half = pl.multiple_of((1 - odd) * full, half)
@@ -105,15 +106,19 @@
         [part(full // 128, b)[:, :half] for b in range(B)], axis=1
     ).astype(bf16)
 
-    for c, copy in enumerate(copies):
-        copy.wait()
-        cut = slice(cuts[c], cuts[c + 1])
-        product = dot_nt(hidden[:, cut], weights[:, cut])
+    for c in range(len(cuts) - 1):
+        held = range(cuts[c], cuts[c + 1])
+        for t in held:
+            copies[t].wait()
+        product = dot_nt(
+            jnp.concatenate([hidden[t] for t in held], axis=1),
+            weights[:, cuts[c] * LANES : cuts[c + 1] * LANES],
+        )
         in_acc[...] = product if c == 0 else in_acc[...] + product
         for r in range(0, rows, 16):
             total = None if c == 0 else sq_acc[r : r + 16, :]
-            for at in range(cuts[c], cuts[c + 1], 128):
-                wide = hidden[r : r + 16, at : at + 128].astype(f32)
+            for t in held:
+                wide = hidden[t, r : r + 16, :].astype(f32)
                 total = wide * wide if total is None else total + wide * wide
             sq_acc[r : r + 16, :] = total
 
@@ -139,7 +144,8 @@
 
 def factors(lengths, hidden, cotangent, gain, in_projection, out_projection):
     rows, width = hidden.shape
-    cuts = [width * part // 8 for part in (0, 2, 4, 6, 7, 8)]
+    tiles = width // LANES
+    cuts = [tiles * part // 8 for part in (0, 2, 4, 6, 7, 8)]
     return pl.pallas_call(
         functools.partial(factors_kernel, cuts),
         out_shape=jax.ShapeDtypeStruct((rows, 2 * R), bf16),
@@ -147,7 +153,7 @@
         out_specs=pl.BlockSpec(memory_space=pltpu.VMEM),
         scratch_shapes=[
             pltpu.SMEM(lengths.shape, jnp.int32),
-            pltpu.VMEM(hidden.shape, bf16),
+            pltpu.VMEM((tiles, rows, LANES), bf16),
             pltpu.VMEM(cotangent.shape, bf16),
             pltpu.VMEM(gain.shape, bf16),
             pltpu.VMEM(in_projection.shape, bf16),
@@ -157,7 +163,7 @@
             pltpu.VMEM((rows, R), f32),
             pltpu.VMEM((rows, 128), f32),
             pltpu.VMEM((-(-rows // 128) * R, 128), f32),
-            pltpu.SemaphoreType.DMA((4 + len(cuts),)),
+            pltpu.SemaphoreType.DMA((5 + tiles,)),
         ],
         compiler_params=pltpu.CompilerParams(vmem_limit_bytes=24 * 2**20),
         name="factors",
@@ -165,13 +171,14 @@
 
 
 def fetch_kernel(n_layer, after, store, slab, sems):
-    block = slab.shape[1]
+    block = slab.shape[0] // n_layer
     rows = 16 if block % 16 == 0 else 8
     me = lax.axis_index("layer")
     copies = []
     for k in range(n_layer):
         at = pl.multiple_of(partner(me, k, n_layer) * block, rows)
-        copies.append(pltpu.make_async_copy(store.at[pl.ds(at, block)], slab.at[k], sems.at[k]))
+        to = slab.at[pl.ds(k * block, block)]
+        copies.append(pltpu.make_async_copy(store.at[pl.ds(at, block)], to, sems.at[k]))
         copies[-1].start()
     for copy in copies:
         copy.wait()
@@ -181,7 +188,7 @@
     rows, features = store.shape
     return pl.pallas_call(
         functools.partial(fetch_kernel, n_layer),
-        out_shape=jax.ShapeDtypeStruct((n_layer, rows // n_layer, features), bf16),
+        out_shape=jax.ShapeDtypeStruct((rows, features), bf16),
         in_specs=[pl.BlockSpec(memory_space=pl.ANY)] * 2,
         out_specs=pl.BlockSpec(memory_space=pltpu.VMEM),
         scratch_shapes=[pltpu.SemaphoreType.DMA((n_layer,))],
@@ -298,13 +305,19 @@
         def _(at):
             build_grads(shards, at * 4, pl.multiple_of(at * four, 16), full_groups, grads)
 
+    score(slab, 2, grads, outs)
+
+
+def score(slab, first, grads, outs):
+    block = outs[0].shape[1]
+    rows = slab[first * block : (first + len(outs)) * block, :]
+    product = dot_nt(rows, grads[...])
     for at, out in enumerate(outs):
-        out[...] = dot_nt(grads[...], slab[2 + at]).astype(out.dtype)
+        out[...] = product[at * block : (at + 1) * block].T.astype(out.dtype)
 
 
 def near_kernel(grads, slab, *outs):
-    for k, out in enumerate(outs):
-        out[...] = dot_nt(grads[...], slab[k]).astype(out.dtype)
+    score(slab, 0, grads, outs)
 
 
 def partner(me, k, n):
@@ -316,8 +329,9 @@
     return lax.ppermute(x, axis, pairs)
 
 
-def far_scores(gathered, slab, n_store):
-    n_layer, block, features = slab.shape
+def far_scores(gathered, slab, n_store, n_layer):
+    rows, features = slab.shape
+    block = rows // n_layer
     queries = gathered[0].shape[0] // S
     vmem = pl.BlockSpec(memory_space=pltpu.VMEM)
     return pl.pallas_call(
@@ -335,8 +349,9 @@
     )(*gathered, slab)
 
 
-def near_scores(grads, slab):
-    block, features = slab.shape[1:]
+def near_scores(grads, slab, n_layer):
+    rows, features = slab.shape
+    block = rows // n_layer
     queries = grads.shape[0]
     vmem = pl.BlockSpec(memory_space=pltpu.VMEM)
     return pl.pallas_call(
@@ -369,9 +384,9 @@
     )
     gathered = [packed] + [swap(packed, "store", n_store, k) for k in range(1, n_store)]
     slab = fetch(packed, store[0], n_layer)
-    grads, *far = far_scores(gathered, slab, n_store)
+    grads, *far = far_scores(gathered, slab, n_store, n_layer)
     crossed = [swap(x, "layer", n_layer, 1) for x in far[1::2]]
-    own, other = near_scores(grads, slab)
+    own, other = near_scores(grads, slab, n_layer)
     joined = [(x + y.astype(f32)).astype(bf16) for x, y in zip(far[::2], crossed)]
     total = own + swap(other, "layer", n_layer, 1).astype(f32)
     for at, x in enumerate(joined):

time: 26.5 us -> 26.4 us (level)
  transfers between devices with their start and end apart: 6 -> 6, of which waited for: 2 -> 2; matrix products, arithmetic and copies ran while one was open for 0% -> 0% of each run, Pallas kernels for 18% -> 17%
where the time goes in v4:
time: 26.4 us; the launch traced here: 26.3 us
  Pallas kernels  12.4 us (47%)
  starting transfers between devices  7.97 us (30%)
  waiting for transfers between devices  5.09 us (19%)
  other arithmetic  0.71 us (3%)
    ppermute x6, starting transfers between devices, swap(): return lax.ppermute(x, axis, pairs)  7.97 us
    pallas_call x1, Pallas kernels, factors(): pl.pallas_call(functools.partial(factors_kernel, cuts), out_shape=jax.Sha...  6.05 us
    ppermute x6, waiting for transfers between devices, swap(): return lax.ppermute(x, axis, pairs)  5.09 us
    pallas_call x1, Pallas kernels, fetch(): pl.pallas_call(functools.partial(fetch_kernel, n_layer), out_shape=jax.Sh...  3.34 us
    pallas_call x1, Pallas kernels, far_scores(): pl.pallas_call(functools.partial(far_kernel, n_store, queries // G), out_...  1.79 us
    pallas_call x1, Pallas kernels, near_scores(): pl.pallas_call(near_kernel, out_shape=[jax.ShapeDtypeStruct((queries, blo...  1.26 us
    transpose x1, other arithmetic, on_device(): return total.T  0.69 us
  transfers between devices with their start and end apart: 6, of which 2 were waited for; matrix products, arithmetic and copies ran while one was open for 0% of the time, Pallas kernels for 17%

profile of v4, /device:TPU:0, one launch (start us, length us, event | category | flops | bytes accessed | tf_op | source)
XLA Modules:
  0.0 26.3 jit_solution(3344028646959560409)
XLA Ops:
  0.0 6.1 %factors.1.after.refs_0_ = bf16[288,128]{1,0:T(8,128)(2,1)S(1)} custom-call(s32[36]{0:T(128)} %hbm_lengths.1, bf16[288,8192]{1,0:T(8,128)(2,1)} %bitcast.8, bf16[288,1024]{1,0:T(8,128)(2,1)} %bitcast.10, bf16[1,8192]{1,0:T(2,128)(2,1)} %hbm_gain.1, bf16[64,8192]{1,0:T(8,128)(2,1)} %bitcast.9, bf16[64,1024]{1,0:T(8,128)(2,1)} %bitcast.11), custom_call_target="tpu_custom_call" | custom-call | tf_op jit(solution)/shard_map/factors/pallas_call | solution.py:149
  6.1 5.1 %collective-permute-start.2 = (bf16[288,128]{1,0:T(8,128)(2,1)S(1)}, bf16[288,128]{1,0:T(8,128)(2,1)S(1)}, u32[]{:S(2)}, u32[]{:S(2)}) collective-permute-start(bf16[288,128]{1,0:T(8,128)(2,1)S(1)} %factors.1.after.refs_0_), channel_id=1, source_target_pairs={{0,12},{4,8},{8,4},{12,0},{1,13},{5,9},{9,5},{13,1},{2,14},{6,10},... | collective-permute-start | bytes 221192 | tf_op jit(solution)/shard_map/ppermute | solution.py:329
  11.2 0.0 collective-permute-start.1
  11.2 0.6 %collective-permute-start = (bf16[288,128]{1,0:T(8,128)(2,1)S(1)}, bf16[288,128]{1,0:T(8,128)(2,1)S(1)}, u32[]{:S(2)}, u32[]{:S(2)}) collective-permute-start(bf16[288,128]{1,0:T(8,128)(2,1)S(1)} %factors.1.after.refs_0_), channel_id=1, source_target_pairs={{0,4},{4,0},{8,12},{12,8},{1,5},{5,1},{9,13},{13,9},{2,6},{6,2},{1... | collective-permute-start | bytes 221192 | tf_op jit(solution)/shard_map/ppermute | solution.py:329
  11.8 3.3 %fetch.1.refs_4_.slab = bf16[960,4096]{1,0:T(8,128)(2,1)S(1)} custom-call(bf16[288,128]{1,0:T(8,128)(2,1)S(1)} %factors.1.after.refs_0_, bf16[960,4096]{1,0:T(8,128)(2,1)} %bitcast.7), custom_call_target="tpu_custom_call" | custom-call | bytes 7864320 | tf_op jit(solution)/shard_map/fetch/pallas_call | solution.py:189
  15.2 0.0 collective-permute-done.2.refs_3_
  15.2 2.2 %collective-permute-done.1.refs_2_ = bf16[288,128]{1,0:T(8,128)(2,1)S(1)} collective-permute-done((bf16[288,128]{1,0:T(8,128)(2,1)S(1)}, bf16[288,128]{1,0:T(8,128)(2,1)S(1)}, u32[]{:S(2)}, u32[]{:S(2)}) %collective-permute-start.1) | collective-permute-done | bytes 73760 | tf_op jit(solution)/shard_map/ppermute | solution.py:329
  17.4 0.0 collective-permute-done.refs_1_
  17.4 1.8 %far_scores.1 = (bf16[144,4096]{1,0:T(8,128)(2,1)S(1)}, f32[144,240]{1,0:T(8,128)S(1)}, bf16[144,240]{1,0:T(8,128)(2,1)S(1)}) custom-call(bf16[288,128]{1,0:T(8,128)(2,1)S(1)} %factors.1.after.refs_0_, bf16[288,128]{1,0:T(8,128)(2,1)S(1)} %collective-permute-done.refs_1_, bf16[288,128]{1,0:T(8,128)(2,1)S(1)} %collective-permute-done.1.refs_2_, ...), custom_call_target="tpu_custom_call" | custom-call | tf_op jit(solution)/shard_map/far_scores/pallas_call | solution.py:337
  19.2 0.1 collective-permute-start.4
  19.3 1.3 %near_scores.1 = (f32[144,240]{1,0:T(8,128)S(1)}, bf16[144,240]{1,0:T(8,128)(2,1)S(1)}) custom-call(bf16[144,4096]{1,0:T(8,128)(2,1)S(1)} %get-tuple-element.10.grads, bf16[960,4096]{1,0:T(8,128)(2,1)S(1)} %fetch.1.refs_4_.slab), custom_call_target="tpu_custom_call" | custom-call | flops 566231040 | bytes 3932160 | tf_op jit(solution)/shard_map/near_scores/pallas_call | solution.py:357
  20.6 0.6 %collective-permute-start.3 = (bf16[144,240]{1,0:T(8,128)(2,1)S(1)}, bf16[144,240]{1,0:T(8,128)(2,1)S(1)}, u32[]{:S(2)}, u32[]{:S(2)}) collective-permute-start(bf16[144,240]{1,0:T(8,128)(2,1)S(1)} %get-tuple-element.12), channel_id=1, source_target_pairs={{0,1},{1,0},{2,3},{3,2},{4,5},{5,4},{6,7},{7,6},{8,9},{9,8},{10,11... | collective-permute-start | bytes 207368 | tf_op jit(solution)/shard_map/ppermute | solution.py:329
  21.1 0.0 collective-permute-done.4
  21.2 1.6 %collective-permute-start.5 = (bf16[144,240]{1,0:T(8,128)(2,1)S(1)}, bf16[144,240]{1,0:T(8,128)(2,1)S(1)}, u32[]{:S(2)}, u32[]{:S(2)}) collective-permute-start(bf16[144,240]{1,0:T(8,128)(2,1)S(1)} %add_convert_fusion), channel_id=1, source_target_pairs={{0,2},{1,3},{2,0},{3,1},{4,6},{5,7},{6,4},{7,5},{8,10},{9,11},{10,... | collective-permute-start | bytes 207368 | tf_op jit(solution)/shard_map/ppermute | solution.py:329
  22.7 0.0 collective-permute-done.3
  22.7 2.9 %collective-permute-done.5 = bf16[144,240]{1,0:T(8,128)(2,1)S(1)} collective-permute-done((bf16[144,240]{1,0:T(8,128)(2,1)S(1)}, bf16[144,240]{1,0:T(8,128)(2,1)S(1)}, u32[]{:S(2)}, u32[]{:S(2)}) %collective-permute-start.5) | collective-permute-done | bytes 69152 | tf_op jit(solution)/shard_map/ppermute | solution.py:329
  25.6 0.7 %add_bitcast_fusion = f32[240,144]{0,1:T(8,128)} fusion(bf16[144,240]{1,0:T(8,128)(2,1)S(1)} %collective-permute-done.5, f32[144,240]{1,0:T(8,128)S(1)} %get-tuple-element.11, bf16[144,240]{1,0:T(8,128)(2,1)S(1)} %collective-permute-done.3), kind=kLoop, calls=%fused_computation | loop fusion | flops 138240 | bytes 414720 | tf_op jit(solution)/shard_map/transpose | solution.py:394
  (1 shorter events, 0.0 us)
Async XLA Ops:
  6.1 9.1 %collective-permute-start.2 = (bf16[288,128]{1,0:T(8,128)(2,1)S(1)}, bf16[288,128]{1,0:T(8,128)(2,1)S(1)}, u32[]{:S(2)}, u32[]{:S(2)}) collective-permute-start(bf16[288,128]{1,0:T(8,128)(2,1)S(1)} %factors.1.after.refs_0_), channel_id=1, source_target_pairs={{0,12},{4,8},{8,4},{12,0},{1,13},{5,9},{9,5},{13,1},{2,14},{6,10},... | collective-permute-start | bytes 221192 | tf_op jit(solution)/shard_map/ppermute | solution.py:329
  11.2 6.2 %collective-permute-start.1 = (bf16[288,128]{1,0:T(8,128)(2,1)S(1)}, bf16[288,128]{1,0:T(8,128)(2,1)S(1)}, u32[]{:S(2)}, u32[]{:S(2)}) collective-permute-start(bf16[288,128]{1,0:T(8,128)(2,1)S(1)} %factors.1.after.refs_0_), channel_id=1, source_target_pairs={{0,8},{4,12},{8,0},{12,4},{1,9},{5,13},{9,1},{13,5},{2,10},{6,14},... | collective-permute-start | bytes 221192 | tf_op jit(solution)/shard_map/ppermute | solution.py:329
  11.2 6.2 %collective-permute-start = (bf16[288,128]{1,0:T(8,128)(2,1)S(1)}, bf16[288,128]{1,0:T(8,128)(2,1)S(1)}, u32[]{:S(2)}, u32[]{:S(2)}) collective-permute-start(bf16[288,128]{1,0:T(8,128)(2,1)S(1)} %factors.1.after.refs_0_), channel_id=1, source_target_pairs={{0,4},{4,0},{8,12},{12,8},{1,5},{5,1},{9,13},{13,9},{2,6},{6,2},{1... | collective-permute-start | bytes 221192 | tf_op jit(solution)/shard_map/ppermute | solution.py:329
  19.2 1.9 %collective-permute-start.4 = (bf16[144,240]{1,0:T(8,128)(2,1)S(1)}, bf16[144,240]{1,0:T(8,128)(2,1)S(1)}, u32[]{:S(2)}, u32[]{:S(2)}) collective-permute-start(bf16[144,240]{1,0:T(8,128)(2,1)S(1)} %get-tuple-element.14), channel_id=1, source_target_pairs={{0,1},{1,0},{2,3},{3,2},{4,5},{5,4},{6,7},{7,6},{8,9},{9,8},{10,11... | collective-permute-start | bytes 207368 | tf_op jit(solution)/shard_map/ppermute | solution.py:329
  20.6 2.1 %collective-permute-start.3 = (bf16[144,240]{1,0:T(8,128)(2,1)S(1)}, bf16[144,240]{1,0:T(8,128)(2,1)S(1)}, u32[]{:S(2)}, u32[]{:S(2)}) collective-permute-start(bf16[144,240]{1,0:T(8,128)(2,1)S(1)} %get-tuple-element.12), channel_id=1, source_target_pairs={{0,1},{1,0},{2,3},{3,2},{4,5},{5,4},{6,7},{7,6},{8,9},{9,8},{10,11... | collective-permute-start | bytes 207368 | tf_op jit(solution)/shard_map/ppermute | solution.py:329
  21.2 4.4 %collective-permute-start.5 = (bf16[144,240]{1,0:T(8,128)(2,1)S(1)}, bf16[144,240]{1,0:T(8,128)(2,1)S(1)}, u32[]{:S(2)}, u32[]{:S(2)}) collective-permute-start(bf16[144,240]{1,0:T(8,128)(2,1)S(1)} %add_convert_fusion), channel_id=1, source_target_pairs={{0,2},{1,3},{2,0},{3,1},{4,6},{5,7},{6,4},{7,5},{8,10},{9,11},{10,... | collective-permute-start | bytes 207368 | tf_op jit(solution)/shard_map/ppermute | solution.py:329

commit v5 on v2

--- a/solution.py
+++ b/solution.py
@@ -16,6 +16,7 @@
 A = R // B
 G = 8
 H = 4
+LANES = 128
 
 
 def dot_nt(left, right):
@@ -27,8 +28,7 @@
 
 
 def factors_kernel(
-    columns,
-    width,
+    window,
     hbm_lengths,
     hbm_hidden,
     hbm_cot,
@@ -48,9 +48,8 @@
     out_t,
     sems,
 ):
-    chunks = width // columns
+    chunks, rows, columns = hidden.shape
     queries = lengths.shape[0]
-    rows = queries * S
     full = queries // G * G * S
     half = rows - full
     mid, low = full // 2, half // 2
@@ -60,50 +59,28 @@
         copy.start()
         return copy
 
-    head = [
-        start(hbm_cot, cot, 0),
-        start(hbm_outp, outp, 1),
-        start(hbm_gain, gain, 2),
-        start(hbm_lengths, lengths, 3),
-    ]
-    body = []
+    def start_chunk(c):
+        cut = pl.ds(c * columns, columns)
+        return [
+            start(hbm_inp.at[:, cut], inp.at[c], 4 + 2 * c),
+            start(hbm_hidden.at[:, cut], hidden.at[c], 5 + 2 * c),
+        ]
+
+    copy_gain = start(hbm_gain, gain, 0)
+    copies = [start_chunk(c) for c in range(window)]
+    copy_gain.wait()
+    tail = []
     for c in range(chunks):
-        cut = pl.ds(c * columns, columns)
-        body.append(
-            [
-                start(hbm_inp.at[:, cut], inp.at[c], 4 + 2 * c),
-                start(hbm_hidden.at[:, cut], hidden.at[c], 5 + 2 * c),
+        for copy in copies[c]:
+            copy.wait()
+        if c + window < chunks:
+            copies.append(start_chunk(c + window))
+        elif not tail:
+            tail = [
+                start(hbm_outp, outp, 1),
+                start(hbm_cot, cot, 2),
+                start(hbm_lengths, lengths, 3),
             ]
-        )
-    for copy in head:
-        copy.wait()
-    odd = lax.rem(lax.axis_index("store"), 2)
-    at_full = pl.multiple_of(odd * half, half)
-    at_half = pl.multiple_of((1 - odd) * full, half)
-
-    out_acc[...] = dot_nt(cot[...], outp[...])
-    turned = out_acc[pl.ds(at_full, full), :].T
-    for t in range(full // 128):
-        out_t[t * R : (t + 1) * R, :] = turned[:, t * 128 : (t + 1) * 128]
-    out_t[full // 128 * R :, :half] = out_acc[pl.ds(at_half, half), :].T
-
-    def part(t, b):
-        return out_t[pl.ds(t * R + b, A, stride=B), :]
-
-    row = mid + low
-    for m in range(full // (G * S)):
-        t, at = divmod(m * G * S, 128)
-        for b in range(0, B, 2):
-            both = [part(t, b + c)[:, at : at + G * S] for c in range(2)]
-            packed[row : row + A, :] = jnp.concatenate(both, axis=1).astype(bf16)
-            row += A
-    packed[row : row + A, :] = jnp.concatenate(
-        [part(full // 128, b)[:, :half] for b in range(B)], axis=1
-    ).astype(bf16)
-
-    for c in range(chunks):
-        for copy in body[c]:
-            copy.wait()
         scaled = inp[c].astype(f32) * gain[:, c * columns : (c + 1) * columns].astype(f32)
         high = scaled.astype(bf16)
         rest = (scaled - high.astype(f32)).astype(bf16)
@@ -111,25 +88,50 @@
         in_acc[...] = product if c == 0 else in_acc[...] + product
         for r in range(0, rows, 16):
             total = None if c == 0 else sq_acc[r : r + 16, :]
-            for at in range(0, columns, 128):
-                wide = hidden[c, r : r + 16, at : at + 128].astype(f32)
+            for at in range(0, columns, LANES):
+                wide = hidden[c, r : r + 16, at : at + LANES].astype(f32)
                 total = wide * wide if total is None else total + wide * wide
             sq_acc[r : r + 16, :] = total
 
-    mean_square = jnp.sum(sq_acc[...], axis=1, keepdims=True) * (1.0 / width)
+    for copy in tail:
+        copy.wait()
+    odd = lax.rem(lax.axis_index("store"), 2)
+    at_full = pl.multiple_of(odd * half, half)
+    at_half = pl.multiple_of((1 - odd) * full, half)
+
+    mean_square = jnp.sum(sq_acc[...], axis=1, keepdims=True) * (1.0 / (chunks * columns))
     factor = in_acc[:, :R] + in_acc[:, R:]
     factor = factor * lax.rsqrt(mean_square + norm_epsilon)
     position = iota((S, R), 0)
     for q in range(queries):
-        out_acc[q * S : (q + 1) * S, :] = jnp.where(
+        in_acc[q * S : (q + 1) * S, :R] = jnp.where(
             position < lengths[q], factor[q * S : (q + 1) * S], 0.0
         )
-    in_full = out_acc[pl.ds(at_full, full), :]
-    in_half = out_acc[pl.ds(at_half, half), :]
+    out_acc[...] = dot_nt(cot[...], outp[...])
+    in_full = in_acc[pl.ds(at_full, full), :R]
+    in_half = in_acc[pl.ds(at_half, half), :R]
     packed[:mid, :] = jnp.concatenate([in_full[:mid], in_full[mid:]], axis=1).astype(bf16)
     packed[mid : mid + low, :] = jnp.concatenate([in_half[:low], in_half[low:]], axis=1).astype(
         bf16
     )
+    turned = out_acc[pl.ds(at_full, full), :].T
+    for t in range(full // LANES):
+        out_t[t * R : (t + 1) * R, :] = turned[:, t * LANES : (t + 1) * LANES]
+    out_t[full // LANES * R :, :half] = out_acc[pl.ds(at_half, half), :].T
+
+    def part(t, b):
+        return out_t[pl.ds(t * R + b, A, stride=B), :]
+
+    row = mid + low
+    for m in range(full // (G * S)):
+        t, at = divmod(m * G * S, LANES)
+        for b in range(0, B, 2):
+            both = [part(t, b + c)[:, at : at + G * S] for c in range(2)]
+            packed[row : row + A, :] = jnp.concatenate(both, axis=1).astype(bf16)
+            row += A
+    packed[row : row + A, :] = jnp.concatenate(
+        [part(full // LANES, b)[:, :half] for b in range(B)], axis=1
+    ).astype(bf16)
 
 
 def in_hbm(x):
@@ -141,7 +143,7 @@
     columns = 1024
     chunks = width // columns
     return pl.pallas_call(
-        functools.partial(factors_kernel, columns, width),
+        functools.partial(factors_kernel, 3),
         out_shape=jax.ShapeDtypeStruct((rows, 2 * R), bf16),
         in_specs=[pl.BlockSpec(memory_space=pl.ANY)] * 6,
         out_specs=pl.BlockSpec(memory_space=pltpu.VMEM),
@@ -154,8 +156,8 @@
             pltpu.VMEM(out_projection.shape, bf16),
             pltpu.VMEM((rows, 2 * R), f32),
             pltpu.VMEM((rows, R), f32),
-            pltpu.VMEM((rows, 128), f32),
-            pltpu.VMEM((-(-rows // 128) * R, 128), f32),
+            pltpu.VMEM((rows, LANES), f32),
+            pltpu.VMEM((-(-rows // LANES) * R, LANES), f32),
             pltpu.SemaphoreType.DMA((4 + 2 * chunks,)),
         ],
         compiler_params=pltpu.CompilerParams(vmem_limit_bytes=24 * 2**20),
@@ -164,13 +166,14 @@
 
 
 def fetch_kernel(n_layer, after, store, slab, sems):
-    block = slab.shape[1]
+    block = slab.shape[0] // n_layer
     rows = 16 if block % 16 == 0 else 8
     me = lax.axis_index("layer")
     copies = []
     for k in range(n_layer):
         at = pl.multiple_of(partner(me, k, n_layer) * block, rows)
-        copies.append(pltpu.make_async_copy(store.at[pl.ds(at, block)], slab.at[k], sems.at[k]))
+        to = slab.at[pl.ds(k * block, block)]
+        copies.append(pltpu.make_async_copy(store.at[pl.ds(at, block)], to, sems.at[k]))
         copies[-1].start()
     for copy in copies:
         copy.wait()
@@ -180,7 +183,7 @@
     rows, features = store.shape
     return pl.pallas_call(
         functools.partial(fetch_kernel, n_layer),
-        out_shape=jax.ShapeDtypeStruct((n_layer, rows // n_layer, features), bf16),
+        out_shape=jax.ShapeDtypeStruct((rows, features), bf16),
         in_specs=[pl.BlockSpec(memory_space=pl.ANY)] * 2,
         out_specs=pl.BlockSpec(memory_space=pltpu.VMEM),
         scratch_shapes=[pltpu.SemaphoreType.DMA((n_layer,))],
@@ -280,14 +283,12 @@
             ).astype(bf16)
 
 
-def scores_kernel(n_store, n_layer, full_groups, *refs):
+def grads_kernel(n_store, full_groups, k, *refs):
     gathered = refs[:n_store]
-    slab = refs[n_store]
-    outs = refs[n_store + 1 : n_store + 1 + n_layer]
-    shards, grads = refs[n_store + 1 + n_layer :]
+    slab, grads, out, shards = refs[n_store:]
     me_store = lax.axis_index("store")
-    for k in range(n_store):
-        shards[partner(me_store, k, n_store)] = gathered[k][...]
+    for at in range(n_store):
+        shards[partner(me_store, at, n_store)] = gathered[at][...]
     four = 4 * (full_groups * G + H)
     if n_store == 4:
         build_grads(shards, 0, 0, full_groups, grads)
@@ -297,8 +298,16 @@
         def _(at):
             build_grads(shards, at * 4, pl.multiple_of(at * four, 16), full_groups, grads)
 
-    for k in reversed(range(n_layer)):
-        outs[k][...] = dot_nt(grads[...], slab[k]).astype(outs[k].dtype)
+    scores_kernel(k, grads, slab, out)
+
+
+def scores_kernel(k, grads, slab, *refs):
+    *terms, out = refs
+    block = out.shape[1]
+    total = dot_nt(slab[k * block : (k + 1) * block, :], grads[...]).T
+    for term in terms:
+        total += term[...].astype(f32)
+    out[...] = total.astype(out.dtype)
 
 
 def partner(me, k, n):
@@ -310,25 +319,42 @@
     return lax.ppermute(x, axis, pairs)
 
 
-def scores(gathered, slab, n_store, n_layer):
-    block, features = slab.shape[1:]
-    queries = gathered[0].shape[0] // S
+def grads_and_scores(gathered, slab, n_store, n_layer, k):
+    rows, features = slab.shape
+    queries = n_store * gathered[0].shape[0] // S
     vmem = pl.BlockSpec(memory_space=pltpu.VMEM)
     return pl.pallas_call(
-        functools.partial(scores_kernel, n_store, n_layer, queries // G),
+        functools.partial(grads_kernel, n_store, queries // n_store // G, k),
         out_shape=[
-            jax.ShapeDtypeStruct((n_store * queries, block), f32 if k == 0 else bf16)
-            for k in range(n_layer)
+            jax.ShapeDtypeStruct((queries, features), bf16),
+            jax.ShapeDtypeStruct((queries, rows // n_layer), bf16),
         ],
         in_specs=[vmem] * (n_store + 1),
-        out_specs=[vmem] * n_layer,
-        scratch_shapes=[
-            pltpu.VMEM((n_store,) + gathered[0].shape, bf16),
-            pltpu.VMEM((n_store * queries, features), bf16),
-        ],
+        out_specs=[vmem] * 2,
+        scratch_shapes=[pltpu.VMEM((n_store,) + gathered[0].shape, bf16)],
         compiler_params=pltpu.CompilerParams(vmem_limit_bytes=24 * 2**20),
+        name="grads",
+    )(*gathered, slab)
+
+
+def scores(grads, slab, n_layer, k, terms=()):
+    rows, features = slab.shape
+    block = rows // n_layer
+    queries = grads.shape[0]
+    vmem = pl.BlockSpec(memory_space=pltpu.VMEM)
+    return pl.pallas_call(
+        functools.partial(scores_kernel, k),
+        out_shape=jax.ShapeDtypeStruct((queries, block), bf16 if k else f32),
+        in_specs=[vmem] * (2 + len(terms)),
+        out_specs=vmem,
+        compiler_params=pltpu.CompilerParams(vmem_limit_bytes=24 * 2**20),
+        cost_estimate=pl.CostEstimate(
+            flops=2 * queries * block * features,
+            bytes_accessed=2 * (queries + block) * features,
+            transcendentals=0,
+        ),
         name="scores",
-    )(*gathered, slab)
+    )(grads, slab, *terms)
 
 
 def on_device(n_store, n_layer, hidden, cotangent, lengths, norm_gain, in_proj, out_proj, store):
@@ -343,10 +369,13 @@
     )
     gathered = [packed] + [swap(packed, "store", n_store, k) for k in range(1, n_store)]
     slab = fetch(packed, store[0], n_layer)
-    partial = scores(gathered, slab, n_store, n_layer)
-    total = partial[0]
-    for k in range(1, n_layer):
-        total = total + swap(partial[k], "layer", n_layer, k).astype(f32)
+    grads, partial = grads_and_scores(gathered, slab, n_store, n_layer, n_layer - 1)
+    crossed = [swap(partial, "layer", n_layer, n_layer - 1)]
+    for k in reversed(range(1, n_layer - 1)):
+        crossed.append(swap(scores(grads, slab, n_layer, k), "layer", n_layer, k))
+    total = scores(grads, slab, n_layer, 0, crossed[:1])
+    for x in crossed[1:]:
+        total = total + x.astype(f32)
     return total.T
 
 

time: 27.2 us -> 26.5 us (0.974)
  waiting for transfers between devices: 6.4 us -> 5.38 us
  Pallas kernels: 12.2 us -> 12.5 us
    ppermute x6, waiting for transfers between devices: 6.4 us -> 5.38 us  [swap(): return lax.ppermute(x, axis, pairs)]
    pallas_call x2 -> x5, Pallas kernels: 8.89 us -> 9.12 us  [the longest x1 5.6 us: factors(): pl.pallas_call(functools.partial(factors_kernel, 3), out_shape=jax.ShapeD...]
  transfers between devices with their start and end apart: 6 -> 6, of which waited for: 3 -> 3; matrix products, arithmetic and copies ran while one was open for 0% -> 0% of each run, Pallas kernels for 12% -> 21%
where the time goes in v5:
time: 26.5 us; the launch traced here: 26.3 us
  Pallas kernels  12.5 us (47%)
  starting transfers between devices  7.76 us (29%)
  waiting for transfers between devices  5.38 us (20%)
  other arithmetic  0.69 us (3%)
    ppermute x6, starting transfers between devices, swap(): return lax.ppermute(x, axis, pairs)  7.76 us
    pallas_call x1, Pallas kernels, factors(): pl.pallas_call(functools.partial(factors_kernel, 3), out_shape=jax.ShapeD...  5.6 us
    ppermute x6, waiting for transfers between devices, swap(): return lax.ppermute(x, axis, pairs)  5.38 us
    pallas_call x1, Pallas kernels, fetch(): pl.pallas_call(functools.partial(fetch_kernel, n_layer), out_shape=jax.Sh...  3.34 us
    pallas_call x3, Pallas kernels, scores(): pl.pallas_call(functools.partial(scores_kernel, k), out_shape=jax.ShapeDt...  2.24 us
    pallas_call x1, Pallas kernels, grads_and_scores(): pl.pallas_call(functools.partial(grads_kernel, n_store, queries // n_stor...  1.28 us
    transpose x1, other arithmetic, on_device(): return total.T  0.69 us
  transfers between devices with their start and end apart: 6, of which 3 were waited for; matrix products, arithmetic and copies ran while one was open for 0% of the time, Pallas kernels for 21%

profile of v5, /device:TPU:0, one launch (start us, length us, event | category | flops | bytes accessed | tf_op | source)
XLA Modules:
  0.0 26.3 jit_solution(11122218344648556451)
XLA Ops:
  0.0 5.6 %factors.1.after.refs_0_ = bf16[288,128]{1,0:T(8,128)(2,1)S(1)} custom-call(s32[36]{0:T(128)} %hbm_lengths.1, bf16[288,8192]{1,0:T(8,128)(2,1)} %bitcast.8, bf16[288,1024]{1,0:T(8,128)(2,1)} %bitcast.10, bf16[1,8192]{1,0:T(2,128)(2,1)} %hbm_gain.1, bf16[64,8192]{1,0:T(8,128)(2,1)} %bitcast.9, bf16[64,1024]{1,0:T(8,128)(2,1)} %bitcast.11), custom_call_target="tpu_custom_call" | custom-call | tf_op jit(solution)/shard_map/factors/pallas_call | solution.py:145
  5.6 5.1 %collective-permute-start.2 = (bf16[288,128]{1,0:T(8,128)(2,1)S(1)}, bf16[288,128]{1,0:T(8,128)(2,1)S(1)}, u32[]{:S(2)}, u32[]{:S(2)}) collective-permute-start(bf16[288,128]{1,0:T(8,128)(2,1)S(1)} %factors.1.after.refs_0_), channel_id=1, source_target_pairs={{0,12},{4,8},{8,4},{12,0},{1,13},{5,9},{9,5},{13,1},{2,14},{6,10},... | collective-permute-start | bytes 221192 | tf_op jit(solution)/shard_map/ppermute | solution.py:319
  10.7 0.0 collective-permute-start.1
  10.7 0.6 %collective-permute-start = (bf16[288,128]{1,0:T(8,128)(2,1)S(1)}, bf16[288,128]{1,0:T(8,128)(2,1)S(1)}, u32[]{:S(2)}, u32[]{:S(2)}) collective-permute-start(bf16[288,128]{1,0:T(8,128)(2,1)S(1)} %factors.1.after.refs_0_), channel_id=1, source_target_pairs={{0,4},{4,0},{8,12},{12,8},{1,5},{5,1},{9,13},{13,9},{2,6},{6,2},{1... | collective-permute-start | bytes 221192 | tf_op jit(solution)/shard_map/ppermute | solution.py:319
  11.4 3.3 %fetch.1.refs_4_.slab = bf16[960,4096]{1,0:T(8,128)(2,1)S(1)} custom-call(bf16[288,128]{1,0:T(8,128)(2,1)S(1)} %factors.1.after.refs_0_, bf16[960,4096]{1,0:T(8,128)(2,1)} %bitcast.7), custom_call_target="tpu_custom_call" | custom-call | bytes 7864320 | tf_op jit(solution)/shard_map/fetch/pallas_call | solution.py:184
  14.7 0.0 collective-permute-done.2.refs_3_
  14.7 2.2 %collective-permute-done.1.refs_2_ = bf16[288,128]{1,0:T(8,128)(2,1)S(1)} collective-permute-done((bf16[288,128]{1,0:T(8,128)(2,1)S(1)}, bf16[288,128]{1,0:T(8,128)(2,1)S(1)}, u32[]{:S(2)}, u32[]{:S(2)}) %collective-permute-start.1) | collective-permute-done | bytes 73760 | tf_op jit(solution)/shard_map/ppermute | solution.py:319
  17.0 0.0 collective-permute-done.refs_1_
  17.0 1.3 %grads.1 = (bf16[144,4096]{1,0:T(8,128)(2,1)S(1)}, bf16[144,240]{1,0:T(8,128)(2,1)S(1)}) custom-call(bf16[288,128]{1,0:T(8,128)(2,1)S(1)} %factors.1.after.refs_0_, bf16[288,128]{1,0:T(8,128)(2,1)S(1)} %collective-permute-done.refs_1_, bf16[288,128]{1,0:T(8,128)(2,1)S(1)} %collective-permute-done.1.refs_2_, ...), custom_call_target="tpu_custom_call" | custom-call | tf_op jit(solution)/shard_map/grads/pallas_call | solution.py:326
  18.2 0.8 %collective-permute-start.3 = (bf16[144,240]{1,0:T(8,128)(2,1)S(1)}, bf16[144,240]{1,0:T(8,128)(2,1)S(1)}, u32[]{:S(2)}, u32[]{:S(2)}) collective-permute-start(bf16[144,240]{1,0:T(8,128)(2,1)S(1)} %get-tuple-element.8), channel_id=1, source_target_pairs={{0,3},{1,2},{2,1},{3,0},{4,7},{5,6},{6,5},{7,4},{8,11},{9,10},{10,... | collective-permute-start | bytes 207368 | tf_op jit(solution)/shard_map/ppermute | solution.py:319
  19.0 0.7 %scores.5 = bf16[144,240]{1,0:T(8,128)(2,1)S(1)} custom-call(bf16[144,4096]{1,0:T(8,128)(2,1)S(1)} %get-tuple-element.7.grads, bf16[960,4096]{1,0:T(8,128)(2,1)S(1)} %fetch.1.refs_4_.slab), custom_call_target="tpu_custom_call" | custom-call | flops 283115520 | bytes 3145728 | tf_op jit(solution)/shard_map/scores/pallas_call | solution.py:345
  19.8 0.8 %scores.4 = bf16[144,240]{1,0:T(8,128)(2,1)S(1)} custom-call(bf16[144,4096]{1,0:T(8,128)(2,1)S(1)} %get-tuple-element.7.grads, bf16[960,4096]{1,0:T(8,128)(2,1)S(1)} %fetch.1.refs_4_.slab), custom_call_target="tpu_custom_call" | custom-call | flops 283115520 | bytes 3145728 | tf_op jit(solution)/shard_map/scores/pallas_call | solution.py:345
  20.6 0.8 %collective-permute-start.4 = (bf16[144,240]{1,0:T(8,128)(2,1)S(1)}, bf16[144,240]{1,0:T(8,128)(2,1)S(1)}, u32[]{:S(2)}, u32[]{:S(2)}) collective-permute-start(bf16[144,240]{1,0:T(8,128)(2,1)S(1)} %scores.4), channel_id=1, source_target_pairs={{0,2},{1,3},{2,0},{3,1},{4,6},{5,7},{6,4},{7,5},{8,10},{9,11},{10,... | collective-permute-start | bytes 207368 | tf_op jit(solution)/shard_map/ppermute | solution.py:319
  21.4 0.4 %collective-permute-start.5 = (bf16[144,240]{1,0:T(8,128)(2,1)S(1)}, bf16[144,240]{1,0:T(8,128)(2,1)S(1)}, u32[]{:S(2)}, u32[]{:S(2)}) collective-permute-start(bf16[144,240]{1,0:T(8,128)(2,1)S(1)} %scores.5), channel_id=1, source_target_pairs={{0,1},{1,0},{2,3},{3,2},{4,5},{5,4},{6,7},{7,6},{8,9},{9,8},{10,11... | collective-permute-start | bytes 207368 | tf_op jit(solution)/shard_map/ppermute | solution.py:319
  21.7 1.1 %collective-permute-done.3.refs_0_ = bf16[144,240]{1,0:T(8,128)(2,1)S(1)} collective-permute-done((bf16[144,240]{1,0:T(8,128)(2,1)S(1)}, bf16[144,240]{1,0:T(8,128)(2,1)S(1)}, u32[]{:S(2)}, u32[]{:S(2)}) %collective-permute-start.3) | collective-permute-done | bytes 69152 | tf_op jit(solution)/shard_map/ppermute | solution.py:319
  22.8 0.7 %scores.3 = f32[144,240]{1,0:T(8,128)S(1)} custom-call(bf16[144,4096]{1,0:T(8,128)(2,1)S(1)} %get-tuple-element.7.grads, bf16[960,4096]{1,0:T(8,128)(2,1)S(1)} %fetch.1.refs_4_.slab, bf16[144,240]{1,0:T(8,128)(2,1)S(1)} %collective-permute-done.3.refs_0_), custom_call_target="tpu_custom_call" | custom-call | flops 283115520 | bytes 3145728 | tf_op jit(solution)/shard_map/scores/pallas_call | solution.py:345
  23.6 2.1 %collective-permute-done.4 = bf16[144,240]{1,0:T(8,128)(2,1)S(1)} collective-permute-done((bf16[144,240]{1,0:T(8,128)(2,1)S(1)}, bf16[144,240]{1,0:T(8,128)(2,1)S(1)}, u32[]{:S(2)}, u32[]{:S(2)}) %collective-permute-start.4) | collective-permute-done | bytes 69152 | tf_op jit(solution)/shard_map/ppermute | solution.py:319
  25.7 0.0 collective-permute-done.5
  25.7 0.7 %add_bitcast_fusion = f32[240,144]{0,1:T(8,128)} fusion(bf16[144,240]{1,0:T(8,128)(2,1)S(1)} %collective-permute-done.5, f32[144,240]{1,0:T(8,128)S(1)} %scores.3, bf16[144,240]{1,0:T(8,128)(2,1)S(1)} %collective-permute-done.4), kind=kLoop, calls=%fused_computation | loop fusion | flops 138240 | bytes 414720 | tf_op jit(solution)/shard_map/transpose | solution.py:379
Async XLA Ops:
  5.6 9.1 %collective-permute-start.2 = (bf16[288,128]{1,0:T(8,128)(2,1)S(1)}, bf16[288,128]{1,0:T(8,128)(2,1)S(1)}, u32[]{:S(2)}, u32[]{:S(2)}) collective-permute-start(bf16[288,128]{1,0:T(8,128)(2,1)S(1)} %factors.1.after.refs_0_), channel_id=1, source_target_pairs={{0,12},{4,8},{8,4},{12,0},{1,13},{5,9},{9,5},{13,1},{2,14},{6,10},... | collective-permute-start | bytes 221192 | tf_op jit(solution)/shard_map/ppermute | solution.py:319
  10.7 6.2 %collective-permute-start.1 = (bf16[288,128]{1,0:T(8,128)(2,1)S(1)}, bf16[288,128]{1,0:T(8,128)(2,1)S(1)}, u32[]{:S(2)}, u32[]{:S(2)}) collective-permute-start(bf16[288,128]{1,0:T(8,128)(2,1)S(1)} %factors.1.after.refs_0_), channel_id=1, source_target_pairs={{0,8},{4,12},{8,0},{12,4},{1,9},{5,13},{9,1},{13,5},{2,10},{6,14},... | collective-permute-start | bytes 221192 | tf_op jit(solution)/shard_map/ppermute | solution.py:319
  10.7 6.2 %collective-permute-start = (bf16[288,128]{1,0:T(8,128)(2,1)S(1)}, bf16[288,128]{1,0:T(8,128)(2,1)S(1)}, u32[]{:S(2)}, u32[]{:S(2)}) collective-permute-start(bf16[288,128]{1,0:T(8,128)(2,1)S(1)} %factors.1.after.refs_0_), channel_id=1, source_target_pairs={{0,4},{4,0},{8,12},{12,8},{1,5},{5,1},{9,13},{13,9},{2,6},{6,2},{1... | collective-permute-start | bytes 221192 | tf_op jit(solution)/shard_map/ppermute | solution.py:319
  18.2 4.6 %collective-permute-start.3 = (bf16[144,240]{1,0:T(8,128)(2,1)S(1)}, bf16[144,240]{1,0:T(8,128)(2,1)S(1)}, u32[]{:S(2)}, u32[]{:S(2)}) collective-permute-start(bf16[144,240]{1,0:T(8,128)(2,1)S(1)} %get-tuple-element.8), channel_id=1, source_target_pairs={{0,3},{1,2},{2,1},{3,0},{4,7},{5,6},{6,5},{7,4},{8,11},{9,10},{10,... | collective-permute-start | bytes 207368 | tf_op jit(solution)/shard_map/ppermute | solution.py:319
  20.6 5.1 %collective-permute-start.4 = (bf16[144,240]{1,0:T(8,128)(2,1)S(1)}, bf16[144,240]{1,0:T(8,128)(2,1)S(1)}, u32[]{:S(2)}, u32[]{:S(2)}) collective-permute-start(bf16[144,240]{1,0:T(8,128)(2,1)S(1)} %scores.4), channel_id=1, source_target_pairs={{0,2},{1,3},{2,0},{3,1},{4,6},{5,7},{6,4},{7,5},{8,10},{9,11},{10,... | collective-permute-start | bytes 207368 | tf_op jit(solution)/shard_map/ppermute | solution.py:319
  21.4 4.3 %collective-permute-start.5 = (bf16[144,240]{1,0:T(8,128)(2,1)S(1)}, bf16[144,240]{1,0:T(8,128)(2,1)S(1)}, u32[]{:S(2)}, u32[]{:S(2)}) collective-permute-start(bf16[144,240]{1,0:T(8,128)(2,1)S(1)} %scores.5), channel_id=1, source_target_pairs={{0,1},{1,0},{2,3},{3,2},{4,5},{5,4},{6,7},{7,6},{8,9},{9,8},{10,11... | collective-permute-start | bytes 207368 | tf_op jit(solution)/shard_map/ppermute | solution.py:319

commit v6 on v5

--- a/solution.py
+++ b/solution.py
@@ -66,85 +66,84 @@
             start(hbm_hidden.at[:, cut], hidden.at[c], 5 + 2 * c),
         ]
 
-    copy_gain = start(hbm_gain, gain, 0)
+    early = [
+        start(hbm_outp, outp, 1),
+        start(hbm_cot, cot, 2),
+        start(hbm_gain, gain, 0),
+        start(hbm_lengths, lengths, 3),
+    ]
     copies = [start_chunk(c) for c in range(window)]
-    copy_gain.wait()
-    tail = []
+    for copy in early:
+        copy.wait()
+    odd = lax.rem(lax.axis_index("store"), 2)
+    at_full = pl.multiple_of(odd * half, half)
+    at_half = pl.multiple_of((1 - odd) * full, half)
+
+    def pack(row, *parts):
+        piece = jnp.concatenate(parts, axis=1).astype(bf16)
+        for copy in range(packed.shape[0]):
+            packed[copy, row : row + piece.shape[0], :] = piece
+
+    out_acc[...] = dot_nt(cot[...], outp[...])
+    turned = out_acc[pl.ds(at_full, full), :].T
+    for t in range(full // LANES):
+        out_t[t * R : (t + 1) * R, :] = turned[:, t * LANES : (t + 1) * LANES]
+    out_t[full // LANES * R :, :half] = out_acc[pl.ds(at_half, half), :].T
+
+    def part(t, b):
+        return out_t[pl.ds(t * R + b, A, stride=B), :]
+
+    row = mid + low
+    for m in range(full // (G * S)):
+        t, at = divmod(m * G * S, LANES)
+        for b in range(0, B, 2):
+            pack(row, *[part(t, b + c)[:, at : at + G * S] for c in range(2)])
+            row += A
+    pack(row, *[part(full // LANES, b)[:, :half] for b in range(B)])
+
     for c in range(chunks):
         for copy in copies[c]:
             copy.wait()
         if c + window < chunks:
             copies.append(start_chunk(c + window))
-        elif not tail:
-            tail = [
-                start(hbm_outp, outp, 1),
-                start(hbm_cot, cot, 2),
-                start(hbm_lengths, lengths, 3),
-            ]
         scaled = inp[c].astype(f32) * gain[:, c * columns : (c + 1) * columns].astype(f32)
         high = scaled.astype(bf16)
         rest = (scaled - high.astype(f32)).astype(bf16)
         product = dot_nt(hidden[c], jnp.concatenate([high, rest], axis=0))
         in_acc[...] = product if c == 0 else in_acc[...] + product
-        for r in range(0, rows, 16):
-            total = None if c == 0 else sq_acc[r : r + 16, :]
-            for at in range(0, columns, LANES):
-                wide = hidden[c, r : r + 16, at : at + LANES].astype(f32)
-                total = wide * wide if total is None else total + wide * wide
-            sq_acc[r : r + 16, :] = total
-
-    for copy in tail:
-        copy.wait()
-    odd = lax.rem(lax.axis_index("store"), 2)
-    at_full = pl.multiple_of(odd * half, half)
-    at_half = pl.multiple_of((1 - odd) * full, half)
+        for r in range(0, rows, 48):
+            wide = hidden[c, r : r + 48, :].astype(f32)
+            square = wide * wide
+            total = square[:, :LANES]
+            for at in range(LANES, columns, LANES):
+                total += square[:, at : at + LANES]
+            sq_acc[r : r + 48, :] = total if c == 0 else sq_acc[r : r + 48, :] + total
 
     mean_square = jnp.sum(sq_acc[...], axis=1, keepdims=True) * (1.0 / (chunks * columns))
     factor = in_acc[:, :R] + in_acc[:, R:]
     factor = factor * lax.rsqrt(mean_square + norm_epsilon)
     position = iota((S, R), 0)
     for q in range(queries):
-        in_acc[q * S : (q + 1) * S, :R] = jnp.where(
+        out_acc[q * S : (q + 1) * S, :] = jnp.where(
             position < lengths[q], factor[q * S : (q + 1) * S], 0.0
         )
-    out_acc[...] = dot_nt(cot[...], outp[...])
-    in_full = in_acc[pl.ds(at_full, full), :R]
-    in_half = in_acc[pl.ds(at_half, half), :R]
-    packed[:mid, :] = jnp.concatenate([in_full[:mid], in_full[mid:]], axis=1).astype(bf16)
-    packed[mid : mid + low, :] = jnp.concatenate([in_half[:low], in_half[low:]], axis=1).astype(
-        bf16
-    )
-    turned = out_acc[pl.ds(at_full, full), :].T
-    for t in range(full // LANES):
-        out_t[t * R : (t + 1) * R, :] = turned[:, t * LANES : (t + 1) * LANES]
-    out_t[full // LANES * R :, :half] = out_acc[pl.ds(at_half, half), :].T
-
-    def part(t, b):
-        return out_t[pl.ds(t * R + b, A, stride=B), :]
-
-    row = mid + low
-    for m in range(full // (G * S)):
-        t, at = divmod(m * G * S, LANES)
-        for b in range(0, B, 2):
-            both = [part(t, b + c)[:, at : at + G * S] for c in range(2)]
-            packed[row : row + A, :] = jnp.concatenate(both, axis=1).astype(bf16)
-            row += A
-    packed[row : row + A, :] = jnp.concatenate(
-        [part(full // LANES, b)[:, :half] for b in range(B)], axis=1
-    ).astype(bf16)
+    in_full = out_acc[pl.ds(at_full, full), :]
+    in_half = out_acc[pl.ds(at_half, half), :]
+    pack(0, in_full[:mid], in_full[mid:])
+    pack(mid, in_half[:low], in_half[low:])
 
 
 def in_hbm(x):
     return pltpu.with_memory_space_constraint(x, pltpu.HBM)
 
 
-def factors(lengths, hidden, cotangent, gain, in_projection, out_projection):
+def factors(copies, lengths, hidden, cotangent, gain, in_projection, out_projection):
     rows, width = hidden.shape
     columns = 1024
     chunks = width // columns
     return pl.pallas_call(
         functools.partial(factors_kernel, 3),
-        out_shape=jax.ShapeDtypeStruct((rows, 2 * R), bf16),
+        out_shape=jax.ShapeDtypeStruct((copies, rows, 2 * R), bf16),
         in_specs=[pl.BlockSpec(memory_space=pl.ANY)] * 6,
         out_specs=pl.BlockSpec(memory_space=pltpu.VMEM),
         scratch_shapes=[
@@ -283,12 +282,8 @@
             ).astype(bf16)
 
 
-def grads_kernel(n_store, full_groups, k, *refs):
-    gathered = refs[:n_store]
-    slab, grads, out, shards = refs[n_store:]
-    me_store = lax.axis_index("store")
-    for at in range(n_store):
-        shards[partner(me_store, at, n_store)] = gathered[at][...]
+def grads_kernel(full_groups, k, shards, slab, grads, out):
+    n_store = shards.shape[0]
     four = 4 * (full_groups * G + H)
     if n_store == 4:
         build_grads(shards, 0, 0, full_groups, grads)
@@ -301,8 +296,8 @@
     scores_kernel(k, grads, slab, out)
 
 
-def scores_kernel(k, grads, slab, *refs):
-    *terms, out = refs
+def scores_kernel(k, grads, slab, *refs, skip=0):
+    *terms, out = refs[skip:]
     block = out.shape[1]
     total = dot_nt(slab[k * block : (k + 1) * block, :], grads[...]).T
     for term in terms:
@@ -319,33 +314,34 @@
     return lax.ppermute(x, axis, pairs)
 
 
-def grads_and_scores(gathered, slab, n_store, n_layer, k):
+def grads_and_scores(shards, slab, n_layer, k):
     rows, features = slab.shape
-    queries = n_store * gathered[0].shape[0] // S
+    queries = shards.shape[1] // S
     vmem = pl.BlockSpec(memory_space=pltpu.VMEM)
     return pl.pallas_call(
-        functools.partial(grads_kernel, n_store, queries // n_store // G, k),
+        functools.partial(grads_kernel, queries // G, k),
         out_shape=[
-            jax.ShapeDtypeStruct((queries, features), bf16),
-            jax.ShapeDtypeStruct((queries, rows // n_layer), bf16),
+            jax.ShapeDtypeStruct((shards.shape[0] * queries, features), bf16),
+            jax.ShapeDtypeStruct((shards.shape[0] * queries, rows // n_layer), bf16),
         ],
-        in_specs=[vmem] * (n_store + 1),
+        in_specs=[vmem] * 2,
         out_specs=[vmem] * 2,
-        scratch_shapes=[pltpu.VMEM((n_store,) + gathered[0].shape, bf16)],
         compiler_params=pltpu.CompilerParams(vmem_limit_bytes=24 * 2**20),
         name="grads",
-    )(*gathered, slab)
-
-
-def scores(grads, slab, n_layer, k, terms=()):
+    )(shards, slab)
+
+
+def scores(grads, slab, n_layer, k, terms=(), after=()):
     rows, features = slab.shape
     block = rows // n_layer
     queries = grads.shape[0]
     vmem = pl.BlockSpec(memory_space=pltpu.VMEM)
     return pl.pallas_call(
-        functools.partial(scores_kernel, k),
+        functools.partial(scores_kernel, k, skip=len(after)),
         out_shape=jax.ShapeDtypeStruct((queries, block), bf16 if k else f32),
-        in_specs=[vmem] * (2 + len(terms)),
+        in_specs=[vmem] * 2
+        + [pl.BlockSpec(memory_space=pl.ANY)] * len(after)
+        + [vmem] * len(terms),
         out_specs=vmem,
         compiler_params=pltpu.CompilerParams(vmem_limit_bytes=24 * 2**20),
         cost_estimate=pl.CostEstimate(
@@ -354,12 +350,13 @@
             transcendentals=0,
         ),
         name="scores",
-    )(grads, slab, *terms)
+    )(grads, slab, *after, *terms)
 
 
 def on_device(n_store, n_layer, hidden, cotangent, lengths, norm_gain, in_proj, out_proj, store):
     queries, positions, width = hidden.shape[1:]
     packed = factors(
+        n_store,
         lengths,
         hidden.reshape(queries * positions, width),
         cotangent.reshape(queries * positions, cotangent.shape[3]),
@@ -367,13 +364,14 @@
         in_proj[0],
         out_proj[0],
     )
-    gathered = [packed] + [swap(packed, "store", n_store, k) for k in range(1, n_store)]
+    shards = lax.all_to_all(packed, "store", 0, 0)
     slab = fetch(packed, store[0], n_layer)
-    grads, partial = grads_and_scores(gathered, slab, n_store, n_layer, n_layer - 1)
+    grads, partial = grads_and_scores(shards, slab, n_layer, n_layer - 1)
     crossed = [swap(partial, "layer", n_layer, n_layer - 1)]
     for k in reversed(range(1, n_layer - 1)):
-        crossed.append(swap(scores(grads, slab, n_layer, k), "layer", n_layer, k))
-    total = scores(grads, slab, n_layer, 0, crossed[:1])
+        after = crossed[:1] if k == 1 else []
+        crossed.append(swap(scores(grads, slab, n_layer, k, after=after), "layer", n_layer, k))
+    total = scores(grads, slab, n_layer, 0, terms=crossed[:1])
     for x in crossed[1:]:
         total = total + x.astype(f32)
     return total.T

time: 26.5 us -> 34.5 us (1.30)
  local copies, waits for them, and re-layouts: 0 us -> 6.28 us
  Pallas kernels: 12.5 us -> 13.2 us
  starting transfers between devices: 7.76 us -> 8.16 us
  waiting for transfers between devices: 5.38 us -> 5.78 us
    all_to_all x0 -> x1, starting transfers between devices: none -> 6.35 us  [on_device(): shards = lax.all_to_all(packed, 'store', 0, 0)]
    unnamed x0 -> x4, local copies, waits for them, and re-layouts: none -> 6.28 us
    ppermute x6 -> x3, starting transfers between devices: 7.76 us -> 1.81 us  [swap(): return lax.ppermute(x, axis, pairs)]
    all_to_all x0 -> x1, waiting for transfers between devices: none -> 3.21 us  [on_device(): shards = lax.all_to_all(packed, 'store', 0, 0)]
    ppermute x6 -> x3, waiting for transfers between devices: 5.38 us -> 2.58 us  [swap(): return lax.ppermute(x, axis, pairs)]
    pallas_call x1, Pallas kernels: 5.6 us -> 6.38 us  [factors(): pl.pallas_call(functools.partial(factors_kernel, 3), out_shape=jax.ShapeD...]
  transfers between devices with their start and end apart: 6 -> 4, of which waited for: 3 -> 3; matrix products, arithmetic and copies ran while one was open for 0% -> 0% of each run, Pallas kernels for 21% -> 16%
where the time goes in v6:
time: 34.5 us; the launch traced here: 34.2 us
  Pallas kernels  13.2 us (38%)
  starting transfers between devices  8.16 us (24%)
  local copies, waits for them, and re-layouts  6.28 us (18%)
  waiting for transfers between devices  5.78 us (17%)
  other arithmetic  0.69 us (2%)
    pallas_call x1, Pallas kernels, factors(): pl.pallas_call(functools.partial(factors_kernel, 3), out_shape=jax.ShapeD...  6.38 us
    all_to_all x1, starting transfers between devices, on_device(): shards = lax.all_to_all(packed, 'store', 0, 0)  6.35 us
    unnamed x4, local copies, waits for them, and re-layouts  6.28 us
    pallas_call x1, Pallas kernels, fetch(): pl.pallas_call(functools.partial(fetch_kernel, n_layer), out_shape=jax.Sh...  3.34 us
    all_to_all x1, waiting for transfers between devices, on_device(): shards = lax.all_to_all(packed, 'store', 0, 0)  3.21 us
    ppermute x3, waiting for transfers between devices, swap(): return lax.ppermute(x, axis, pairs)  2.58 us
    pallas_call x3, Pallas kernels, scores(): pl.pallas_call(functools.partial(scores_kernel, k, skip=len(after)), out_...  2.24 us
    ppermute x3, starting transfers between devices, swap(): return lax.ppermute(x, axis, pairs)  1.81 us
  transfers between devices with their start and end apart: 4, of which 3 were waited for; matrix products, arithmetic and copies ran while one was open for 0% of the time, Pallas kernels for 16%

profile of v6, /device:TPU:0, one launch (start us, length us, event | category | flops | bytes accessed | tf_op | source)
XLA Modules:
  0.0 34.2 jit_solution(16927538728811050387)
XLA Ops:
  0.0 6.4 %factors.1.after = bf16[4,288,128]{2,1,0:T(8,128)(2,1)} custom-call(s32[36]{0:T(128)} %hbm_lengths.1, bf16[288,8192]{1,0:T(8,128)(2,1)} %bitcast.8, bf16[288,1024]{1,0:T(8,128)(2,1)} %bitcast.10, bf16[1,8192]{1,0:T(2,128)(2,1)} %hbm_gain.1, bf16[64,8192]{1,0:T(8,128)(2,1)} %bitcast.9, bf16[64,1024]{1,0:T(8,128)(2,1)} %bitcast.11), custom_call_target="tpu_custom_call" | custom-call | tf_op jit(solution)/shard_map/factors/pallas_call | solution.py:144
  6.4 6.3 %all-to-all-start = ((bf16[4,288,128]{2,1,0:T(8,128)(2,1)}), bf16[4,288,128]{2,1,0:T(8,128)(2,1)S(1)}, u32[]{:S(2)}, u32[]{:S(2)}) async-start(bf16[4,288,128]{2,1,0:T(8,128)(2,1)} %factors.1.after), calls=%async_computation | async-start | bytes 589824 | tf_op jit(solution)/shard_map/all_to_all | solution.py:367
  12.7 3.3 %fetch.1.slab = bf16[960,4096]{1,0:T(8,128)(2,1)S(1)} custom-call(bf16[4,288,128]{2,1,0:T(8,128)(2,1)} %factors.1.after, bf16[960,4096]{1,0:T(8,128)(2,1)} %bitcast.7), custom_call_target="tpu_custom_call" | custom-call | bytes 7864320 | tf_op jit(solution)/shard_map/fetch/pallas_call | solution.py:183
  16.1 0.0 copy-start
  16.1 3.0 %copy-done = bf16[960,4096]{1,0:T(8,128)(2,1)} copy-done((bf16[960,4096]{1,0:T(8,128)(2,1)}, bf16[960,4096]{1,0:T(8,128)(2,1)S(1)}, u32[]{:S(2)}) %copy-start) | copy-done | bytes 7864344
  19.1 3.2 %all-to-all-done.shards = bf16[4,288,128]{2,1,0:T(8,128)(2,1)S(1)} async-done(((bf16[4,288,128]{2,1,0:T(8,128)(2,1)}), bf16[4,288,128]{2,1,0:T(8,128)(2,1)S(1)}, u32[]{:S(2)}, u32[]{:S(2)}) %all-to-all-start) | async-done | bytes 294944 | tf_op jit(solution)/shard_map/all_to_all | solution.py:367
  22.4 0.0 copy-start.1
  22.4 3.2 %copy-done.1 = bf16[960,4096]{1,0:T(8,128)(2,1)S(1)} copy-done((bf16[960,4096]{1,0:T(8,128)(2,1)S(1)}, bf16[960,4096]{1,0:T(8,128)(2,1)}, u32[]{:S(2)}) %copy-start.1) | copy-done | bytes 7864344
  25.6 1.2 %grads.1 = (bf16[144,4096]{1,0:T(8,128)(2,1)S(1)}, bf16[144,240]{1,0:T(8,128)(2,1)S(1)}) custom-call(bf16[4,288,128]{2,1,0:T(8,128)(2,1)S(1)} %all-to-all-done.shards, bf16[960,4096]{1,0:T(8,128)(2,1)S(1)} %copy-done.1), custom_call_target="tpu_custom_call" | custom-call | tf_op jit(solution)/shard_map/grads/pallas_call | solution.py:321
  26.8 0.1 collective-permute-start
  26.9 0.7 %scores.4 = bf16[144,240]{1,0:T(8,128)(2,1)S(1)} custom-call(bf16[144,4096]{1,0:T(8,128)(2,1)S(1)} %get-tuple-element.7.grads, bf16[960,4096]{1,0:T(8,128)(2,1)S(1)} %copy-done.1), custom_call_target="tpu_custom_call" | custom-call | flops 283115520 | bytes 3145728 | tf_op jit(solution)/shard_map/scores/pallas_call | solution.py:339
  27.7 1.6 %collective-permute-start.1 = (bf16[144,240]{1,0:T(8,128)(2,1)S(1)}, bf16[144,240]{1,0:T(8,128)(2,1)S(1)}, u32[]{:S(2)}, u32[]{:S(2)}) collective-permute-start(bf16[144,240]{1,0:T(8,128)(2,1)S(1)} %scores.4), channel_id=1, source_target_pairs={{0,2},{1,3},{2,0},{3,1},{4,6},{5,7},{6,4},{7,5},{8,10},{9,11},{10,... | collective-permute-start | bytes 207368 | tf_op jit(solution)/shard_map/ppermute | solution.py:314
  29.2 2.2 %collective-permute-done.refs_0_ = bf16[144,240]{1,0:T(8,128)(2,1)S(1)} collective-permute-done((bf16[144,240]{1,0:T(8,128)(2,1)S(1)}, bf16[144,240]{1,0:T(8,128)(2,1)S(1)}, u32[]{:S(2)}, u32[]{:S(2)}) %collective-permute-start) | collective-permute-done | bytes 69152 | tf_op jit(solution)/shard_map/ppermute | solution.py:314
  31.4 0.8 %scores.5 = bf16[144,240]{1,0:T(8,128)(2,1)S(1)} custom-call(bf16[144,4096]{1,0:T(8,128)(2,1)S(1)} %get-tuple-element.7.grads, bf16[960,4096]{1,0:T(8,128)(2,1)S(1)} %copy-done.1, bf16[144,240]{1,0:T(8,128)(2,1)S(1)} %collective-permute-done.refs_0_), custom_call_target="tpu_custom_call" | custom-call | flops 283115520 | bytes 3145728 | tf_op jit(solution)/shard_map/scores/pallas_call | solution.py:339
  32.2 0.2 collective-permute-start.2
  32.4 0.7 %scores.3 = f32[144,240]{1,0:T(8,128)S(1)} custom-call(bf16[144,4096]{1,0:T(8,128)(2,1)S(1)} %get-tuple-element.7.grads, bf16[960,4096]{1,0:T(8,128)(2,1)S(1)} %copy-done.1, bf16[144,240]{1,0:T(8,128)(2,1)S(1)} %collective-permute-done.refs_0_), custom_call_target="tpu_custom_call" | custom-call | flops 283115520 | bytes 3145728 | tf_op jit(solution)/shard_map/scores/pallas_call | solution.py:339
  33.1 0.0 collective-permute-done.1
  33.1 0.4 %collective-permute-done.2 = bf16[144,240]{1,0:T(8,128)(2,1)S(1)} collective-permute-done((bf16[144,240]{1,0:T(8,128)(2,1)S(1)}, bf16[144,240]{1,0:T(8,128)(2,1)S(1)}, u32[]{:S(2)}, u32[]{:S(2)}) %collective-permute-start.2) | collective-permute-done | bytes 69152 | tf_op jit(solution)/shard_map/ppermute | solution.py:314
  33.5 0.7 %add_bitcast_fusion = f32[240,144]{0,1:T(8,128)} fusion(bf16[144,240]{1,0:T(8,128)(2,1)S(1)} %collective-permute-done.2, f32[144,240]{1,0:T(8,128)S(1)} %scores.3, bf16[144,240]{1,0:T(8,128)(2,1)S(1)} %collective-permute-done.1), kind=kLoop, calls=%fused_computation | loop fusion | flops 138240 | bytes 414720 | tf_op jit(solution)/shard_map/transpose | solution.py:377
Async XLA Ops:
  6.4 16.0 %all-to-all-start = ((bf16[4,288,128]{2,1,0:T(8,128)(2,1)}), bf16[4,288,128]{2,1,0:T(8,128)(2,1)S(1)}, u32[]{:S(2)}, u32[]{:S(2)}) async-start(bf16[4,288,128]{2,1,0:T(8,128)(2,1)} %factors.1.after), calls=%async_computation | async-start | bytes 589824 | tf_op jit(solution)/shard_map/all_to_all | solution.py:367
  16.1 3.1 %copy-start = (bf16[960,4096]{1,0:T(8,128)(2,1)}, bf16[960,4096]{1,0:T(8,128)(2,1)S(1)}, u32[]{:S(2)}) copy-start(bf16[960,4096]{1,0:T(8,128)(2,1)S(1)} %fetch.1.slab) | copy-start | bytes 23592964
  22.4 3.2 %copy-start.1 = (bf16[960,4096]{1,0:T(8,128)(2,1)S(1)}, bf16[960,4096]{1,0:T(8,128)(2,1)}, u32[]{:S(2)}) copy-start(bf16[960,4096]{1,0:T(8,128)(2,1)} %copy-done) | copy-start | bytes 23592964
  26.8 4.6 %collective-permute-start = (bf16[144,240]{1,0:T(8,128)(2,1)S(1)}, bf16[144,240]{1,0:T(8,128)(2,1)S(1)}, u32[]{:S(2)}, u32[]{:S(2)}) collective-permute-start(bf16[144,240]{1,0:T(8,128)(2,1)S(1)} %get-tuple-element.8), channel_id=1, source_target_pairs={{0,3},{1,2},{2,1},{3,0},{4,7},{5,6},{6,5},{7,4},{8,11},{9,10},{10,... | collective-permute-start | bytes 207368 | tf_op jit(solution)/shard_map/ppermute | solution.py:314
  27.7 5.4 %collective-permute-start.1 = (bf16[144,240]{1,0:T(8,128)(2,1)S(1)}, bf16[144,240]{1,0:T(8,128)(2,1)S(1)}, u32[]{:S(2)}, u32[]{:S(2)}) collective-permute-start(bf16[144,240]{1,0:T(8,128)(2,1)S(1)} %scores.4), channel_id=1, source_target_pairs={{0,2},{1,3},{2,0},{3,1},{4,6},{5,7},{6,4},{7,5},{8,10},{9,11},{10,... | collective-permute-start | bytes 207368 | tf_op jit(solution)/shard_map/ppermute | solution.py:314
  32.2 1.3 %collective-permute-start.2 = (bf16[144,240]{1,0:T(8,128)(2,1)S(1)}, bf16[144,240]{1,0:T(8,128)(2,1)S(1)}, u32[]{:S(2)}, u32[]{:S(2)}) collective-permute-start(bf16[144,240]{1,0:T(8,128)(2,1)S(1)} %scores.5), channel_id=1, source_target_pairs={{0,1},{1,0},{2,3},{3,2},{4,5},{5,4},{6,7},{7,6},{8,9},{9,8},{10,11... | collective-permute-start | bytes 207368 | tf_op jit(solution)/shard_map/ppermute | solution.py:314

commit v7 on v6

--- a/solution.py
+++ b/solution.py
@@ -28,7 +28,6 @@
 
 
 def factors_kernel(
-    window,
     hbm_lengths,
     hbm_hidden,
     hbm_cot,
@@ -59,30 +58,33 @@
         copy.start()
         return copy
 
-    def start_chunk(c):
-        cut = pl.ds(c * columns, columns)
-        return [
-            start(hbm_inp.at[:, cut], inp.at[c], 4 + 2 * c),
-            start(hbm_hidden.at[:, cut], hidden.at[c], 5 + 2 * c),
-        ]
-
-    early = [
-        start(hbm_outp, outp, 1),
-        start(hbm_cot, cot, 2),
-        start(hbm_gain, gain, 0),
-        start(hbm_lengths, lengths, 3),
-    ]
-    copies = [start_chunk(c) for c in range(window)]
+    copies = []
+
+    def start_chunks(upto):
+        for c in range(len(copies), min(upto, chunks)):
+            cut = pl.ds(c * columns, columns)
+            copies.append(
+                [
+                    start(hbm_inp.at[:, cut], inp.at[c], 4 + 2 * c),
+                    start(hbm_hidden.at[:, cut], hidden.at[c], 5 + 2 * c),
+                ]
+            )
+
+    copy_gain = start(hbm_gain, gain, 0)
+    early = [start(hbm_outp, outp, 1), start(hbm_cot, cot, 2), start(hbm_lengths, lengths, 3)]
+    start_chunks(1)
+    copy_gain.wait()
+    start_chunks(3)
     for copy in early:
         copy.wait()
+    start_chunks(4)
     odd = lax.rem(lax.axis_index("store"), 2)
     at_full = pl.multiple_of(odd * half, half)
     at_half = pl.multiple_of((1 - odd) * full, half)
 
     def pack(row, *parts):
         piece = jnp.concatenate(parts, axis=1).astype(bf16)
-        for copy in range(packed.shape[0]):
-            packed[copy, row : row + piece.shape[0], :] = piece
+        packed[row : row + piece.shape[0], :] = piece
 
     out_acc[...] = dot_nt(cot[...], outp[...])
     turned = out_acc[pl.ds(at_full, full), :].T
@@ -104,8 +106,7 @@
     for c in range(chunks):
         for copy in copies[c]:
             copy.wait()
-        if c + window < chunks:
-            copies.append(start_chunk(c + window))
+        start_chunks(c + 5)
         scaled = inp[c].astype(f32) * gain[:, c * columns : (c + 1) * columns].astype(f32)
         high = scaled.astype(bf16)
         rest = (scaled - high.astype(f32)).astype(bf16)
@@ -137,13 +138,13 @@
     return pltpu.with_memory_space_constraint(x, pltpu.HBM)
 
 
-def factors(copies, lengths, hidden, cotangent, gain, in_projection, out_projection):
+def factors(lengths, hidden, cotangent, gain, in_projection, out_projection):
     rows, width = hidden.shape
     columns = 1024
     chunks = width // columns
     return pl.pallas_call(
-        functools.partial(factors_kernel, 3),
-        out_shape=jax.ShapeDtypeStruct((copies, rows, 2 * R), bf16),
+        factors_kernel,
+        out_shape=jax.ShapeDtypeStruct((rows, 2 * R), bf16),
         in_specs=[pl.BlockSpec(memory_space=pl.ANY)] * 6,
         out_specs=pl.BlockSpec(memory_space=pltpu.VMEM),
         scratch_shapes=[
@@ -282,8 +283,12 @@
             ).astype(bf16)
 
 
-def grads_kernel(full_groups, k, shards, slab, grads, out):
-    n_store = shards.shape[0]
+def grads_kernel(n_store, full_groups, k, *refs):
+    gathered = refs[:n_store]
+    slab, grads, out, shards = refs[n_store:]
+    me_store = lax.axis_index("store")
+    for at in range(n_store):
+        shards[partner(me_store, at, n_store)] = gathered[at][...]
     four = 4 * (full_groups * G + H)
     if n_store == 4:
         build_grads(shards, 0, 0, full_groups, grads)
@@ -296,8 +301,8 @@
     scores_kernel(k, grads, slab, out)
 
 
-def scores_kernel(k, grads, slab, *refs, skip=0):
-    *terms, out = refs[skip:]
+def scores_kernel(k, grads, slab, *refs):
+    *terms, out = refs
     block = out.shape[1]
     total = dot_nt(slab[k * block : (k + 1) * block, :], grads[...]).T
     for term in terms:
@@ -314,34 +319,33 @@
     return lax.ppermute(x, axis, pairs)
 
 
-def grads_and_scores(shards, slab, n_layer, k):
+def grads_and_scores(gathered, slab, n_store, n_layer, k):
     rows, features = slab.shape
-    queries = shards.shape[1] // S
+    queries = n_store * gathered[0].shape[0] // S
     vmem = pl.BlockSpec(memory_space=pltpu.VMEM)
     return pl.pallas_call(
-        functools.partial(grads_kernel, queries // G, k),
+        functools.partial(grads_kernel, n_store, queries // n_store // G, k),
         out_shape=[
-            jax.ShapeDtypeStruct((shards.shape[0] * queries, features), bf16),
-            jax.ShapeDtypeStruct((shards.shape[0] * queries, rows // n_layer), bf16),
+            jax.ShapeDtypeStruct((queries, features), bf16),
+            jax.ShapeDtypeStruct((queries, rows // n_layer), bf16),
         ],
-        in_specs=[vmem] * 2,
+        in_specs=[vmem] * (n_store + 1),
         out_specs=[vmem] * 2,
+        scratch_shapes=[pltpu.VMEM((n_store,) + gathered[0].shape, bf16)],
         compiler_params=pltpu.CompilerParams(vmem_limit_bytes=24 * 2**20),
         name="grads",
-    )(shards, slab)
-
-
-def scores(grads, slab, n_layer, k, terms=(), after=()):
+    )(*gathered, slab)
+
+
+def scores(grads, slab, n_layer, k, terms=()):
     rows, features = slab.shape
     block = rows // n_layer
     queries = grads.shape[0]
     vmem = pl.BlockSpec(memory_space=pltpu.VMEM)
     return pl.pallas_call(
-        functools.partial(scores_kernel, k, skip=len(after)),
+        functools.partial(scores_kernel, k),
         out_shape=jax.ShapeDtypeStruct((queries, block), bf16 if k else f32),
-        in_specs=[vmem] * 2
-        + [pl.BlockSpec(memory_space=pl.ANY)] * len(after)
-        + [vmem] * len(terms),
+        in_specs=[vmem] * (2 + len(terms)),
         out_specs=vmem,
         compiler_params=pltpu.CompilerParams(vmem_limit_bytes=24 * 2**20),
         cost_estimate=pl.CostEstimate(
@@ -350,13 +354,12 @@
             transcendentals=0,
         ),
         name="scores",
-    )(grads, slab, *after, *terms)
+    )(grads, slab, *terms)
 
 
 def on_device(n_store, n_layer, hidden, cotangent, lengths, norm_gain, in_proj, out_proj, store):
     queries, positions, width = hidden.shape[1:]
     packed = factors(
-        n_store,
         lengths,
         hidden.reshape(queries * positions, width),
         cotangent.reshape(queries * positions, cotangent.shape[3]),
@@ -364,14 +367,13 @@
         in_proj[0],
         out_proj[0],
     )
-    shards = lax.all_to_all(packed, "store", 0, 0)
+    gathered = [packed] + [swap(packed, "store", n_store, k) for k in range(1, n_store)]
     slab = fetch(packed, store[0], n_layer)
-    grads, partial = grads_and_scores(shards, slab, n_layer, n_layer - 1)
+    grads, partial = grads_and_scores(gathered, slab, n_store, n_layer, n_layer - 1)
     crossed = [swap(partial, "layer", n_layer, n_layer - 1)]
     for k in reversed(range(1, n_layer - 1)):
-        after = crossed[:1] if k == 1 else []
-        crossed.append(swap(scores(grads, slab, n_layer, k, after=after), "layer", n_layer, k))
-    total = scores(grads, slab, n_layer, 0, terms=crossed[:1])
+        crossed.append(swap(scores(grads, slab, n_layer, k), "layer", n_layer, k))
+    total = scores(grads, slab, n_layer, 0, crossed[:1])
     for x in crossed[1:]:
         total = total + x.astype(f32)
     return total.T

time: 34.5 us -> 26.6 us (0.77)
  local copies, waits for them, and re-layouts: 6.28 us -> 0 us
  Pallas kernels: 13.2 us -> 12.6 us
  starting transfers between devices: 8.16 us -> 7.75 us
  waiting for transfers between devices: 5.78 us -> 5.39 us
    all_to_all x1 -> x0, starting transfers between devices: 6.35 us -> none  [on_device(): shards = lax.all_to_all(packed, 'store', 0, 0)]
    unnamed x4 -> x0, local copies, waits for them, and re-layouts: 6.28 us -> none
    ppermute x3 -> x6, starting transfers between devices: 1.81 us -> 7.75 us  [swap(): return lax.ppermute(x, axis, pairs)]
    all_to_all x1 -> x0, waiting for transfers between devices: 3.21 us -> none  [on_device(): shards = lax.all_to_all(packed, 'store', 0, 0)]
    ppermute x3 -> x6, waiting for transfers between devices: 2.58 us -> 5.39 us  [swap(): return lax.ppermute(x, axis, pairs)]
    pallas_call x5, Pallas kernels: 9.87 us -> 9.23 us  [the longest x1 5.71 us: factors(): pl.pallas_call(factors_kernel, out_shape=jax.ShapeDtypeStruct((rows, 2 *...]
  transfers between devices with their start and end apart: 4 -> 6, of which waited for: 3 -> 3; matrix products, arithmetic and copies ran while one was open for 0% -> 0% of each run, Pallas kernels for 16% -> 21%
where the time goes in v7:
time: 26.6 us; the launch traced here: 26.5 us
  Pallas kernels  12.6 us (47%)
  starting transfers between devices  7.75 us (29%)
  waiting for transfers between devices  5.39 us (20%)
  other arithmetic  0.69 us (3%)
    ppermute x6, starting transfers between devices, swap(): return lax.ppermute(x, axis, pairs)  7.75 us
    pallas_call x1, Pallas kernels, factors(): pl.pallas_call(factors_kernel, out_shape=jax.ShapeDtypeStruct((rows, 2 *...  5.71 us
    ppermute x6, waiting for transfers between devices, swap(): return lax.ppermute(x, axis, pairs)  5.39 us
    pallas_call x1, Pallas kernels, fetch(): pl.pallas_call(functools.partial(fetch_kernel, n_layer), out_shape=jax.Sh...  3.34 us
    pallas_call x3, Pallas kernels, scores(): pl.pallas_call(functools.partial(scores_kernel, k), out_shape=jax.ShapeDt...  2.25 us
    pallas_call x1, Pallas kernels, grads_and_scores(): pl.pallas_call(functools.partial(grads_kernel, n_store, queries // n_stor...  1.28 us
    transpose x1, other arithmetic, on_device(): return total.T  0.69 us
  transfers between devices with their start and end apart: 6, of which 3 were waited for; matrix products, arithmetic and copies ran while one was open for 0% of the time, Pallas kernels for 21%

profile of v7, /device:TPU:0, one launch (start us, length us, event | category | flops | bytes accessed | tf_op | source)
XLA Modules:
  0.0 26.5 jit_solution(18437716421120358790)
XLA Ops:
  0.0 5.7 %factors.1.after.refs_0_ = bf16[288,128]{1,0:T(8,128)(2,1)S(1)} custom-call(s32[36]{0:T(128)} %hbm_lengths.1, bf16[288,8192]{1,0:T(8,128)(2,1)} %bitcast.8, bf16[288,1024]{1,0:T(8,128)(2,1)} %bitcast.10, bf16[1,8192]{1,0:T(2,128)(2,1)} %hbm_gain.1, bf16[64,8192]{1,0:T(8,128)(2,1)} %bitcast.9, bf16[64,1024]{1,0:T(8,128)(2,1)} %bitcast.11), custom_call_target="tpu_custom_call" | custom-call | tf_op jit(solution)/shard_map/factors/pallas_call | solution.py:145
  5.7 5.1 %collective-permute-start.2 = (bf16[288,128]{1,0:T(8,128)(2,1)S(1)}, bf16[288,128]{1,0:T(8,128)(2,1)S(1)}, u32[]{:S(2)}, u32[]{:S(2)}) collective-permute-start(bf16[288,128]{1,0:T(8,128)(2,1)S(1)} %factors.1.after.refs_0_), channel_id=1, source_target_pairs={{0,12},{4,8},{8,4},{12,0},{1,13},{5,9},{9,5},{13,1},{2,14},{6,10},... | collective-permute-start | bytes 221192 | tf_op jit(solution)/shard_map/ppermute | solution.py:319
  10.8 0.0 collective-permute-start.1
  10.8 0.6 %collective-permute-start = (bf16[288,128]{1,0:T(8,128)(2,1)S(1)}, bf16[288,128]{1,0:T(8,128)(2,1)S(1)}, u32[]{:S(2)}, u32[]{:S(2)}) collective-permute-start(bf16[288,128]{1,0:T(8,128)(2,1)S(1)} %factors.1.after.refs_0_), channel_id=1, source_target_pairs={{0,4},{4,0},{8,12},{12,8},{1,5},{5,1},{9,13},{13,9},{2,6},{6,2},{1... | collective-permute-start | bytes 221192 | tf_op jit(solution)/shard_map/ppermute | solution.py:319
  11.5 3.3 %fetch.1.refs_4_.slab = bf16[960,4096]{1,0:T(8,128)(2,1)S(1)} custom-call(bf16[288,128]{1,0:T(8,128)(2,1)S(1)} %factors.1.after.refs_0_, bf16[960,4096]{1,0:T(8,128)(2,1)} %bitcast.7), custom_call_target="tpu_custom_call" | custom-call | bytes 7864320 | tf_op jit(solution)/shard_map/fetch/pallas_call | solution.py:184
  14.8 0.0 collective-permute-done.2.refs_3_
  14.8 2.2 %collective-permute-done.1.refs_2_ = bf16[288,128]{1,0:T(8,128)(2,1)S(1)} collective-permute-done((bf16[288,128]{1,0:T(8,128)(2,1)S(1)}, bf16[288,128]{1,0:T(8,128)(2,1)S(1)}, u32[]{:S(2)}, u32[]{:S(2)}) %collective-permute-start.1) | collective-permute-done | bytes 73760 | tf_op jit(solution)/shard_map/ppermute | solution.py:319
  17.1 0.0 collective-permute-done.refs_1_
  17.1 1.3 %grads.1 = (bf16[144,4096]{1,0:T(8,128)(2,1)S(1)}, bf16[144,240]{1,0:T(8,128)(2,1)S(1)}) custom-call(bf16[288,128]{1,0:T(8,128)(2,1)S(1)} %factors.1.after.refs_0_, bf16[288,128]{1,0:T(8,128)(2,1)S(1)} %collective-permute-done.refs_1_, bf16[288,128]{1,0:T(8,128)(2,1)S(1)} %collective-permute-done.1.refs_2_, ...), custom_call_target="tpu_custom_call" | custom-call | tf_op jit(solution)/shard_map/grads/pallas_call | solution.py:326
  18.4 0.8 %collective-permute-start.3 = (bf16[144,240]{1,0:T(8,128)(2,1)S(1)}, bf16[144,240]{1,0:T(8,128)(2,1)S(1)}, u32[]{:S(2)}, u32[]{:S(2)}) collective-permute-start(bf16[144,240]{1,0:T(8,128)(2,1)S(1)} %get-tuple-element.8), channel_id=1, source_target_pairs={{0,3},{1,2},{2,1},{3,0},{4,7},{5,6},{6,5},{7,4},{8,11},{9,10},{10,... | collective-permute-start | bytes 207368 | tf_op jit(solution)/shard_map/ppermute | solution.py:319
  19.1 0.8 %scores.5 = bf16[144,240]{1,0:T(8,128)(2,1)S(1)} custom-call(bf16[144,4096]{1,0:T(8,128)(2,1)S(1)} %get-tuple-element.7.grads, bf16[960,4096]{1,0:T(8,128)(2,1)S(1)} %fetch.1.refs_4_.slab), custom_call_target="tpu_custom_call" | custom-call | flops 283115520 | bytes 3145728 | tf_op jit(solution)/shard_map/scores/pallas_call | solution.py:345
  19.9 0.7 %scores.4 = bf16[144,240]{1,0:T(8,128)(2,1)S(1)} custom-call(bf16[144,4096]{1,0:T(8,128)(2,1)S(1)} %get-tuple-element.7.grads, bf16[960,4096]{1,0:T(8,128)(2,1)S(1)} %fetch.1.refs_4_.slab), custom_call_target="tpu_custom_call" | custom-call | flops 283115520 | bytes 3145728 | tf_op jit(solution)/shard_map/scores/pallas_call | solution.py:345
  20.7 0.8 %collective-permute-start.4 = (bf16[144,240]{1,0:T(8,128)(2,1)S(1)}, bf16[144,240]{1,0:T(8,128)(2,1)S(1)}, u32[]{:S(2)}, u32[]{:S(2)}) collective-permute-start(bf16[144,240]{1,0:T(8,128)(2,1)S(1)} %scores.4), channel_id=1, source_target_pairs={{0,2},{1,3},{2,0},{3,1},{4,6},{5,7},{6,4},{7,5},{8,10},{9,11},{10,... | collective-permute-start | bytes 207368 | tf_op jit(solution)/shard_map/ppermute | solution.py:319
  21.5 0.4 %collective-permute-start.5 = (bf16[144,240]{1,0:T(8,128)(2,1)S(1)}, bf16[144,240]{1,0:T(8,128)(2,1)S(1)}, u32[]{:S(2)}, u32[]{:S(2)}) collective-permute-start(bf16[144,240]{1,0:T(8,128)(2,1)S(1)} %scores.5), channel_id=1, source_target_pairs={{0,1},{1,0},{2,3},{3,2},{4,5},{5,4},{6,7},{7,6},{8,9},{9,8},{10,11... | collective-permute-start | bytes 207368 | tf_op jit(solution)/shard_map/ppermute | solution.py:319
  21.9 1.1 %collective-permute-done.3.refs_0_ = bf16[144,240]{1,0:T(8,128)(2,1)S(1)} collective-permute-done((bf16[144,240]{1,0:T(8,128)(2,1)S(1)}, bf16[144,240]{1,0:T(8,128)(2,1)S(1)}, u32[]{:S(2)}, u32[]{:S(2)}) %collective-permute-start.3) | collective-permute-done | bytes 69152 | tf_op jit(solution)/shard_map/ppermute | solution.py:319
  22.9 0.7 %scores.3 = f32[144,240]{1,0:T(8,128)S(1)} custom-call(bf16[144,4096]{1,0:T(8,128)(2,1)S(1)} %get-tuple-element.7.grads, bf16[960,4096]{1,0:T(8,128)(2,1)S(1)} %fetch.1.refs_4_.slab, bf16[144,240]{1,0:T(8,128)(2,1)S(1)} %collective-permute-done.3.refs_0_), custom_call_target="tpu_custom_call" | custom-call | flops 283115520 | bytes 3145728 | tf_op jit(solution)/shard_map/scores/pallas_call | solution.py:345
  23.7 2.1 %collective-permute-done.4 = bf16[144,240]{1,0:T(8,128)(2,1)S(1)} collective-permute-done((bf16[144,240]{1,0:T(8,128)(2,1)S(1)}, bf16[144,240]{1,0:T(8,128)(2,1)S(1)}, u32[]{:S(2)}, u32[]{:S(2)}) %collective-permute-start.4) | collective-permute-done | bytes 69152 | tf_op jit(solution)/shard_map/ppermute | solution.py:319
  25.8 0.0 collective-permute-done.5
  25.8 0.7 %add_bitcast_fusion = f32[240,144]{0,1:T(8,128)} fusion(bf16[144,240]{1,0:T(8,128)(2,1)S(1)} %collective-permute-done.5, f32[144,240]{1,0:T(8,128)S(1)} %scores.3, bf16[144,240]{1,0:T(8,128)(2,1)S(1)} %collective-permute-done.4), kind=kLoop, calls=%fused_computation | loop fusion | flops 138240 | bytes 414720 | tf_op jit(solution)/shard_map/transpose | solution.py:379
Async XLA Ops:
  5.7 9.1 %collective-permute-start.2 = (bf16[288,128]{1,0:T(8,128)(2,1)S(1)}, bf16[288,128]{1,0:T(8,128)(2,1)S(1)}, u32[]{:S(2)}, u32[]{:S(2)}) collective-permute-start(bf16[288,128]{1,0:T(8,128)(2,1)S(1)} %factors.1.after.refs_0_), channel_id=1, source_target_pairs={{0,12},{4,8},{8,4},{12,0},{1,13},{5,9},{9,5},{13,1},{2,14},{6,10},... | collective-permute-start | bytes 221192 | tf_op jit(solution)/shard_map/ppermute | solution.py:319
  10.8 6.2 %collective-permute-start.1 = (bf16[288,128]{1,0:T(8,128)(2,1)S(1)}, bf16[288,128]{1,0:T(8,128)(2,1)S(1)}, u32[]{:S(2)}, u32[]{:S(2)}) collective-permute-start(bf16[288,128]{1,0:T(8,128)(2,1)S(1)} %factors.1.after.refs_0_), channel_id=1, source_target_pairs={{0,8},{4,12},{8,0},{12,4},{1,9},{5,13},{9,1},{13,5},{2,10},{6,14},... | collective-permute-start | bytes 221192 | tf_op jit(solution)/shard_map/ppermute | solution.py:319
  10.8 6.2 %collective-permute-start = (bf16[288,128]{1,0:T(8,128)(2,1)S(1)}, bf16[288,128]{1,0:T(8,128)(2,1)S(1)}, u32[]{:S(2)}, u32[]{:S(2)}) collective-permute-start(bf16[288,128]{1,0:T(8,128)(2,1)S(1)} %factors.1.after.refs_0_), channel_id=1, source_target_pairs={{0,4},{4,0},{8,12},{12,8},{1,5},{5,1},{9,13},{13,9},{2,6},{6,2},{1... | collective-permute-start | bytes 221192 | tf_op jit(solution)/shard_map/ppermute | solution.py:319
  18.4 4.6 %collective-permute-start.3 = (bf16[144,240]{1,0:T(8,128)(2,1)S(1)}, bf16[144,240]{1,0:T(8,128)(2,1)S(1)}, u32[]{:S(2)}, u32[]{:S(2)}) collective-permute-start(bf16[144,240]{1,0:T(8,128)(2,1)S(1)} %get-tuple-element.8), channel_id=1, source_target_pairs={{0,3},{1,2},{2,1},{3,0},{4,7},{5,6},{6,5},{7,4},{8,11},{9,10},{10,... | collective-permute-start | bytes 207368 | tf_op jit(solution)/shard_map/ppermute | solution.py:319
  20.7 5.1 %collective-permute-start.4 = (bf16[144,240]{1,0:T(8,128)(2,1)S(1)}, bf16[144,240]{1,0:T(8,128)(2,1)S(1)}, u32[]{:S(2)}, u32[]{:S(2)}) collective-permute-start(bf16[144,240]{1,0:T(8,128)(2,1)S(1)} %scores.4), channel_id=1, source_target_pairs={{0,2},{1,3},{2,0},{3,1},{4,6},{5,7},{6,4},{7,5},{8,10},{9,11},{10,... | collective-permute-start | bytes 207368 | tf_op jit(solution)/shard_map/ppermute | solution.py:319
  21.5 4.3 %collective-permute-start.5 = (bf16[144,240]{1,0:T(8,128)(2,1)S(1)}, bf16[144,240]{1,0:T(8,128)(2,1)S(1)}, u32[]{:S(2)}, u32[]{:S(2)}) collective-permute-start(bf16[144,240]{1,0:T(8,128)(2,1)S(1)} %scores.5), channel_id=1, source_target_pairs={{0,1},{1,0},{2,3},{3,2},{4,5},{5,4},{6,7},{7,6},{8,9},{9,8},{10,11... | collective-permute-start | bytes 207368 | tf_op jit(solution)/shard_map/ppermute | solution.py:319

commit v8 on v7

--- a/solution.py
+++ b/solution.py
@@ -28,6 +28,7 @@
 
 
 def factors_kernel(
+    window,
     hbm_lengths,
     hbm_hidden,
     hbm_cot,
@@ -53,31 +54,30 @@
     half = rows - full
     mid, low = full // 2, half // 2
 
-    def start(source, target, at):
-        copy = pltpu.make_async_copy(source, target, sems.at[at])
-        copy.start()
-        return copy
-
-    copies = []
-
-    def start_chunks(upto):
-        for c in range(len(copies), min(upto, chunks)):
-            cut = pl.ds(c * columns, columns)
-            copies.append(
-                [
-                    start(hbm_inp.at[:, cut], inp.at[c], 4 + 2 * c),
-                    start(hbm_hidden.at[:, cut], hidden.at[c], 5 + 2 * c),
-                ]
-            )
-
-    copy_gain = start(hbm_gain, gain, 0)
-    early = [start(hbm_outp, outp, 1), start(hbm_cot, cot, 2), start(hbm_lengths, lengths, 3)]
-    start_chunks(1)
-    copy_gain.wait()
-    start_chunks(3)
-    for copy in early:
-        copy.wait()
-    start_chunks(4)
+    def copy(source, target, at):
+        return pltpu.make_async_copy(source, target, sems.at[at])
+
+    def chunk(c):
+        cut = pl.ds(pl.multiple_of(c * columns, columns), columns)
+        return [
+            copy(hbm_gain.at[:, cut], gain.at[c], 3 + c),
+            copy(hbm_inp.at[:, cut], inp.at[c], 3 + chunks + c),
+            copy(hbm_hidden.at[:, cut], hidden.at[c], 3 + 2 * chunks + c),
+        ]
+
+    def start_chunk(c):
+        for piece in chunk(c):
+            piece.start()
+
+    early = [copy(hbm_outp, outp, 0), copy(hbm_cot, cot, 1), copy(hbm_lengths, lengths, 2)]
+    for piece in early:
+        piece.start()
+    for c in range(window):
+        start_chunk(c)
+    in_acc[...] = jnp.zeros_like(in_acc)
+    sq_acc[...] = jnp.zeros_like(sq_acc)
+    for piece in early:
+        piece.wait()
     odd = lax.rem(lax.axis_index("store"), 2)
     at_full = pl.multiple_of(odd * half, half)
     at_half = pl.multiple_of((1 - odd) * full, half)
@@ -103,22 +103,26 @@
             row += A
     pack(row, *[part(full // LANES, b)[:, :half] for b in range(B)])
 
-    for c in range(chunks):
-        for copy in copies[c]:
-            copy.wait()
-        start_chunks(c + 5)
-        scaled = inp[c].astype(f32) * gain[:, c * columns : (c + 1) * columns].astype(f32)
+    @pl.loop(0, chunks)
+    def _(c):
+        for piece in chunk(c):
+            piece.wait()
+
+        @pl.when(c + window < chunks)
+        def _():
+            start_chunk(c + window)
+
+        scaled = inp[c].astype(f32) * gain[c].astype(f32)
         high = scaled.astype(bf16)
         rest = (scaled - high.astype(f32)).astype(bf16)
-        product = dot_nt(hidden[c], jnp.concatenate([high, rest], axis=0))
-        in_acc[...] = product if c == 0 else in_acc[...] + product
+        in_acc[...] += dot_nt(hidden[c], jnp.concatenate([high, rest], axis=0))
         for r in range(0, rows, 48):
             wide = hidden[c, r : r + 48, :].astype(f32)
             square = wide * wide
             total = square[:, :LANES]
             for at in range(LANES, columns, LANES):
                 total += square[:, at : at + LANES]
-            sq_acc[r : r + 48, :] = total if c == 0 else sq_acc[r : r + 48, :] + total
+            sq_acc[r : r + 48, :] += total
 
     mean_square = jnp.sum(sq_acc[...], axis=1, keepdims=True) * (1.0 / (chunks * columns))
     factor = in_acc[:, :R] + in_acc[:, R:]
@@ -143,7 +147,7 @@
     columns = 1024
     chunks = width // columns
     return pl.pallas_call(
-        factors_kernel,
+        functools.partial(factors_kernel, 4),
         out_shape=jax.ShapeDtypeStruct((rows, 2 * R), bf16),
         in_specs=[pl.BlockSpec(memory_space=pl.ANY)] * 6,
         out_specs=pl.BlockSpec(memory_space=pltpu.VMEM),
@@ -151,14 +155,14 @@
             pltpu.SMEM(lengths.shape, jnp.int32),
             pltpu.VMEM((chunks, rows, columns), bf16),
             pltpu.VMEM(cotangent.shape, bf16),
-            pltpu.VMEM(gain.shape, bf16),
+            pltpu.VMEM((chunks, 1, columns), bf16),
             pltpu.VMEM((chunks, R, columns), bf16),
             pltpu.VMEM(out_projection.shape, bf16),
             pltpu.VMEM((rows, 2 * R), f32),
             pltpu.VMEM((rows, R), f32),
             pltpu.VMEM((rows, LANES), f32),
             pltpu.VMEM((-(-rows // LANES) * R, LANES), f32),
-            pltpu.SemaphoreType.DMA((4 + 2 * chunks,)),
+            pltpu.SemaphoreType.DMA((3 + 3 * chunks,)),
         ],
         compiler_params=pltpu.CompilerParams(vmem_limit_bytes=24 * 2**20),
         name="factors",

time: 26.6 us -> 26.5 us (level)
  no operation moved by 1% of the time
where the time goes in v8:
time: 26.5 us; the launch traced here: 26.4 us
  Pallas kernels  12.5 us (47%)
  starting transfers between devices  7.75 us (29%)
  waiting for transfers between devices  5.39 us (20%)
  other arithmetic  0.69 us (3%)
    ppermute x6, starting transfers between devices, swap(): return lax.ppermute(x, axis, pairs)  7.75 us
    pallas_call x1, Pallas kernels, factors(): pl.pallas_call(functools.partial(factors_kernel, 4), out_shape=jax.ShapeD...  5.63 us
    ppermute x6, waiting for transfers between devices, swap(): return lax.ppermute(x, axis, pairs)  5.39 us
    pallas_call x1, Pallas kernels, fetch(): pl.pallas_call(functools.partial(fetch_kernel, n_layer), out_shape=jax.Sh...  3.34 us
    pallas_call x3, Pallas kernels, scores(): pl.pallas_call(functools.partial(scores_kernel, k), out_shape=jax.ShapeDt...  2.24 us
    pallas_call x1, Pallas kernels, grads_and_scores(): pl.pallas_call(functools.partial(grads_kernel, n_store, queries // n_stor...  1.28 us
    transpose x1, other arithmetic, on_device(): return total.T  0.69 us
  transfers between devices with their start and end apart: 6, of which 3 were waited for; matrix products, arithmetic and copies ran while one was open for 0% of the time, Pallas kernels for 21%

profile of v8, /device:TPU:0, one launch (start us, length us, event | category | flops | bytes accessed | tf_op | source)
XLA Modules:
  0.0 26.4 jit_solution(8487384280652343480)
XLA Ops:
  0.0 5.6 %factors.1.after.refs_0_ = bf16[288,128]{1,0:T(8,128)(2,1)S(1)} custom-call(s32[36]{0:T(128)} %hbm_lengths.1, bf16[288,8192]{1,0:T(8,128)(2,1)} %bitcast.8, bf16[288,1024]{1,0:T(8,128)(2,1)} %bitcast.10, bf16[1,8192]{1,0:T(2,128)(2,1)} %hbm_gain.1, bf16[64,8192]{1,0:T(8,128)(2,1)} %bitcast.9, bf16[64,1024]{1,0:T(8,128)(2,1)} %bitcast.11), custom_call_target="tpu_custom_call" | custom-call | tf_op jit(solution)/shard_map/factors/pallas_call | solution.py:149
  5.6 5.1 %collective-permute-start.2 = (bf16[288,128]{1,0:T(8,128)(2,1)S(1)}, bf16[288,128]{1,0:T(8,128)(2,1)S(1)}, u32[]{:S(2)}, u32[]{:S(2)}) collective-permute-start(bf16[288,128]{1,0:T(8,128)(2,1)S(1)} %factors.1.after.refs_0_), channel_id=1, source_target_pairs={{0,12},{4,8},{8,4},{12,0},{1,13},{5,9},{9,5},{13,1},{2,14},{6,10},... | collective-permute-start | bytes 221192 | tf_op jit(solution)/shard_map/ppermute | solution.py:323
  10.7 0.0 collective-permute-start.1
  10.8 0.6 %collective-permute-start = (bf16[288,128]{1,0:T(8,128)(2,1)S(1)}, bf16[288,128]{1,0:T(8,128)(2,1)S(1)}, u32[]{:S(2)}, u32[]{:S(2)}) collective-permute-start(bf16[288,128]{1,0:T(8,128)(2,1)S(1)} %factors.1.after.refs_0_), channel_id=1, source_target_pairs={{0,4},{4,0},{8,12},{12,8},{1,5},{5,1},{9,13},{13,9},{2,6},{6,2},{1... | collective-permute-start | bytes 221192 | tf_op jit(solution)/shard_map/ppermute | solution.py:323
  11.4 3.3 %fetch.1.refs_4_.slab = bf16[960,4096]{1,0:T(8,128)(2,1)S(1)} custom-call(bf16[288,128]{1,0:T(8,128)(2,1)S(1)} %factors.1.after.refs_0_, bf16[960,4096]{1,0:T(8,128)(2,1)} %bitcast.7), custom_call_target="tpu_custom_call" | custom-call | bytes 7864320 | tf_op jit(solution)/shard_map/fetch/pallas_call | solution.py:188
  14.7 0.0 collective-permute-done.2.refs_3_
  14.8 2.2 %collective-permute-done.1.refs_2_ = bf16[288,128]{1,0:T(8,128)(2,1)S(1)} collective-permute-done((bf16[288,128]{1,0:T(8,128)(2,1)S(1)}, bf16[288,128]{1,0:T(8,128)(2,1)S(1)}, u32[]{:S(2)}, u32[]{:S(2)}) %collective-permute-start.1) | collective-permute-done | bytes 73760 | tf_op jit(solution)/shard_map/ppermute | solution.py:323
  17.0 0.0 collective-permute-done.refs_1_
  17.0 1.3 %grads.1 = (bf16[144,4096]{1,0:T(8,128)(2,1)S(1)}, bf16[144,240]{1,0:T(8,128)(2,1)S(1)}) custom-call(bf16[288,128]{1,0:T(8,128)(2,1)S(1)} %factors.1.after.refs_0_, bf16[288,128]{1,0:T(8,128)(2,1)S(1)} %collective-permute-done.refs_1_, bf16[288,128]{1,0:T(8,128)(2,1)S(1)} %collective-permute-done.1.refs_2_, ...), custom_call_target="tpu_custom_call" | custom-call | tf_op jit(solution)/shard_map/grads/pallas_call | solution.py:330
  18.3 0.8 %collective-permute-start.3 = (bf16[144,240]{1,0:T(8,128)(2,1)S(1)}, bf16[144,240]{1,0:T(8,128)(2,1)S(1)}, u32[]{:S(2)}, u32[]{:S(2)}) collective-permute-start(bf16[144,240]{1,0:T(8,128)(2,1)S(1)} %get-tuple-element.8), channel_id=1, source_target_pairs={{0,3},{1,2},{2,1},{3,0},{4,7},{5,6},{6,5},{7,4},{8,11},{9,10},{10,... | collective-permute-start | bytes 207368 | tf_op jit(solution)/shard_map/ppermute | solution.py:323
  19.1 0.7 %scores.5 = bf16[144,240]{1,0:T(8,128)(2,1)S(1)} custom-call(bf16[144,4096]{1,0:T(8,128)(2,1)S(1)} %get-tuple-element.7.grads, bf16[960,4096]{1,0:T(8,128)(2,1)S(1)} %fetch.1.refs_4_.slab), custom_call_target="tpu_custom_call" | custom-call | flops 283115520 | bytes 3145728 | tf_op jit(solution)/shard_map/scores/pallas_call | solution.py:349
  19.8 0.7 %scores.4 = bf16[144,240]{1,0:T(8,128)(2,1)S(1)} custom-call(bf16[144,4096]{1,0:T(8,128)(2,1)S(1)} %get-tuple-element.7.grads, bf16[960,4096]{1,0:T(8,128)(2,1)S(1)} %fetch.1.refs_4_.slab), custom_call_target="tpu_custom_call" | custom-call | flops 283115520 | bytes 3145728 | tf_op jit(solution)/shard_map/scores/pallas_call | solution.py:349
  20.6 0.8 %collective-permute-start.4 = (bf16[144,240]{1,0:T(8,128)(2,1)S(1)}, bf16[144,240]{1,0:T(8,128)(2,1)S(1)}, u32[]{:S(2)}, u32[]{:S(2)}) collective-permute-start(bf16[144,240]{1,0:T(8,128)(2,1)S(1)} %scores.4), channel_id=1, source_target_pairs={{0,2},{1,3},{2,0},{3,1},{4,6},{5,7},{6,4},{7,5},{8,10},{9,11},{10,... | collective-permute-start | bytes 207368 | tf_op jit(solution)/shard_map/ppermute | solution.py:323
  21.4 0.4 %collective-permute-start.5 = (bf16[144,240]{1,0:T(8,128)(2,1)S(1)}, bf16[144,240]{1,0:T(8,128)(2,1)S(1)}, u32[]{:S(2)}, u32[]{:S(2)}) collective-permute-start(bf16[144,240]{1,0:T(8,128)(2,1)S(1)} %scores.5), channel_id=1, source_target_pairs={{0,1},{1,0},{2,3},{3,2},{4,5},{5,4},{6,7},{7,6},{8,9},{9,8},{10,11... | collective-permute-start | bytes 207368 | tf_op jit(solution)/shard_map/ppermute | solution.py:323
  21.8 1.1 %collective-permute-done.3.refs_0_ = bf16[144,240]{1,0:T(8,128)(2,1)S(1)} collective-permute-done((bf16[144,240]{1,0:T(8,128)(2,1)S(1)}, bf16[144,240]{1,0:T(8,128)(2,1)S(1)}, u32[]{:S(2)}, u32[]{:S(2)}) %collective-permute-start.3) | collective-permute-done | bytes 69152 | tf_op jit(solution)/shard_map/ppermute | solution.py:323
  22.8 0.7 %scores.3 = f32[144,240]{1,0:T(8,128)S(1)} custom-call(bf16[144,4096]{1,0:T(8,128)(2,1)S(1)} %get-tuple-element.7.grads, bf16[960,4096]{1,0:T(8,128)(2,1)S(1)} %fetch.1.refs_4_.slab, bf16[144,240]{1,0:T(8,128)(2,1)S(1)} %collective-permute-done.3.refs_0_), custom_call_target="tpu_custom_call" | custom-call | flops 283115520 | bytes 3145728 | tf_op jit(solution)/shard_map/scores/pallas_call | solution.py:349
  23.6 2.1 %collective-permute-done.4 = bf16[144,240]{1,0:T(8,128)(2,1)S(1)} collective-permute-done((bf16[144,240]{1,0:T(8,128)(2,1)S(1)}, bf16[144,240]{1,0:T(8,128)(2,1)S(1)}, u32[]{:S(2)}, u32[]{:S(2)}) %collective-permute-start.4) | collective-permute-done | bytes 69152 | tf_op jit(solution)/shard_map/ppermute | solution.py:323
  25.7 0.0 collective-permute-done.5
  25.7 0.7 %add_bitcast_fusion = f32[240,144]{0,1:T(8,128)} fusion(bf16[144,240]{1,0:T(8,128)(2,1)S(1)} %collective-permute-done.5, f32[144,240]{1,0:T(8,128)S(1)} %scores.3, bf16[144,240]{1,0:T(8,128)(2,1)S(1)} %collective-permute-done.4), kind=kLoop, calls=%fused_computation | loop fusion | flops 138240 | bytes 414720 | tf_op jit(solution)/shard_map/transpose | solution.py:383
Async XLA Ops:
  5.6 9.1 %collective-permute-start.2 = (bf16[288,128]{1,0:T(8,128)(2,1)S(1)}, bf16[288,128]{1,0:T(8,128)(2,1)S(1)}, u32[]{:S(2)}, u32[]{:S(2)}) collective-permute-start(bf16[288,128]{1,0:T(8,128)(2,1)S(1)} %factors.1.after.refs_0_), channel_id=1, source_target_pairs={{0,12},{4,8},{8,4},{12,0},{1,13},{5,9},{9,5},{13,1},{2,14},{6,10},... | collective-permute-start | bytes 221192 | tf_op jit(solution)/shard_map/ppermute | solution.py:323
  10.7 6.2 %collective-permute-start.1 = (bf16[288,128]{1,0:T(8,128)(2,1)S(1)}, bf16[288,128]{1,0:T(8,128)(2,1)S(1)}, u32[]{:S(2)}, u32[]{:S(2)}) collective-permute-start(bf16[288,128]{1,0:T(8,128)(2,1)S(1)} %factors.1.after.refs_0_), channel_id=1, source_target_pairs={{0,8},{4,12},{8,0},{12,4},{1,9},{5,13},{9,1},{13,5},{2,10},{6,14},... | collective-permute-start | bytes 221192 | tf_op jit(solution)/shard_map/ppermute | solution.py:323
  10.8 6.2 %collective-permute-start = (bf16[288,128]{1,0:T(8,128)(2,1)S(1)}, bf16[288,128]{1,0:T(8,128)(2,1)S(1)}, u32[]{:S(2)}, u32[]{:S(2)}) collective-permute-start(bf16[288,128]{1,0:T(8,128)(2,1)S(1)} %factors.1.after.refs_0_), channel_id=1, source_target_pairs={{0,4},{4,0},{8,12},{12,8},{1,5},{5,1},{9,13},{13,9},{2,6},{6,2},{1... | collective-permute-start | bytes 221192 | tf_op jit(solution)/shard_map/ppermute | solution.py:323
  18.3 4.6 %collective-permute-start.3 = (bf16[144,240]{1,0:T(8,128)(2,1)S(1)}, bf16[144,240]{1,0:T(8,128)(2,1)S(1)}, u32[]{:S(2)}, u32[]{:S(2)}) collective-permute-start(bf16[144,240]{1,0:T(8,128)(2,1)S(1)} %get-tuple-element.8), channel_id=1, source_target_pairs={{0,3},{1,2},{2,1},{3,0},{4,7},{5,6},{6,5},{7,4},{8,11},{9,10},{10,... | collective-permute-start | bytes 207368 | tf_op jit(solution)/shard_map/ppermute | solution.py:323
  20.6 5.1 %collective-permute-start.4 = (bf16[144,240]{1,0:T(8,128)(2,1)S(1)}, bf16[144,240]{1,0:T(8,128)(2,1)S(1)}, u32[]{:S(2)}, u32[]{:S(2)}) collective-permute-start(bf16[144,240]{1,0:T(8,128)(2,1)S(1)} %scores.4), channel_id=1, source_target_pairs={{0,2},{1,3},{2,0},{3,1},{4,6},{5,7},{6,4},{7,5},{8,10},{9,11},{10,... | collective-permute-start | bytes 207368 | tf_op jit(solution)/shard_map/ppermute | solution.py:323
  21.4 4.3 %collective-permute-start.5 = (bf16[144,240]{1,0:T(8,128)(2,1)S(1)}, bf16[144,240]{1,0:T(8,128)(2,1)S(1)}, u32[]{:S(2)}, u32[]{:S(2)}) collective-permute-start(bf16[144,240]{1,0:T(8,128)(2,1)S(1)} %scores.5), channel_id=1, source_target_pairs={{0,1},{1,0},{2,3},{3,2},{4,5},{5,4},{6,7},{7,6},{8,9},{9,8},{10,11... | collective-permute-start | bytes 207368 | tf_op jit(solution)/shard_map/ppermute | solution.py:323

commit v9 on v8

--- a/solution.py
+++ b/solution.py
@@ -43,7 +43,6 @@
     inp,
     outp,
     in_acc,
-    out_acc,
     sq_acc,
     out_t,
     sems,
@@ -70,38 +69,12 @@
             piece.start()
 
     early = [copy(hbm_outp, outp, 0), copy(hbm_cot, cot, 1), copy(hbm_lengths, lengths, 2)]
+    for c in range(window):
+        start_chunk(c)
     for piece in early:
         piece.start()
-    for c in range(window):
-        start_chunk(c)
     in_acc[...] = jnp.zeros_like(in_acc)
     sq_acc[...] = jnp.zeros_like(sq_acc)
-    for piece in early:
-        piece.wait()
-    odd = lax.rem(lax.axis_index("store"), 2)
-    at_full = pl.multiple_of(odd * half, half)
-    at_half = pl.multiple_of((1 - odd) * full, half)
-
-    def pack(row, *parts):
-        piece = jnp.concatenate(parts, axis=1).astype(bf16)
-        packed[row : row + piece.shape[0], :] = piece
-
-    out_acc[...] = dot_nt(cot[...], outp[...])
-    turned = out_acc[pl.ds(at_full, full), :].T
-    for t in range(full // LANES):
-        out_t[t * R : (t + 1) * R, :] = turned[:, t * LANES : (t + 1) * LANES]
-    out_t[full // LANES * R :, :half] = out_acc[pl.ds(at_half, half), :].T
-
-    def part(t, b):
-        return out_t[pl.ds(t * R + b, A, stride=B), :]
-
-    row = mid + low
-    for m in range(full // (G * S)):
-        t, at = divmod(m * G * S, LANES)
-        for b in range(0, B, 2):
-            pack(row, *[part(t, b + c)[:, at : at + G * S] for c in range(2)])
-            row += A
-    pack(row, *[part(full // LANES, b)[:, :half] for b in range(B)])
 
     @pl.loop(0, chunks)
     def _(c):
@@ -115,7 +88,7 @@
         scaled = inp[c].astype(f32) * gain[c].astype(f32)
         high = scaled.astype(bf16)
         rest = (scaled - high.astype(f32)).astype(bf16)
-        in_acc[...] += dot_nt(hidden[c], jnp.concatenate([high, rest], axis=0))
+        in_acc[...] += dot_nt(hidden[c], jnp.concatenate([high, high, rest, rest], axis=0))
         for r in range(0, rows, 48):
             wide = hidden[c, r : r + 48, :].astype(f32)
             square = wide * wide
@@ -124,18 +97,49 @@
                 total += square[:, at : at + LANES]
             sq_acc[r : r + 48, :] += total
 
-    mean_square = jnp.sum(sq_acc[...], axis=1, keepdims=True) * (1.0 / (chunks * columns))
-    factor = in_acc[:, :R] + in_acc[:, R:]
-    factor = factor * lax.rsqrt(mean_square + norm_epsilon)
-    position = iota((S, R), 0)
-    for q in range(queries):
-        out_acc[q * S : (q + 1) * S, :] = jnp.where(
-            position < lengths[q], factor[q * S : (q + 1) * S], 0.0
-        )
-    in_full = out_acc[pl.ds(at_full, full), :]
-    in_half = out_acc[pl.ds(at_half, half), :]
-    pack(0, in_full[:mid], in_full[mid:])
-    pack(mid, in_half[:low], in_half[low:])
+    for piece in early:
+        piece.wait()
+    odd = lax.rem(lax.axis_index("store"), 2)
+    at_full = pl.multiple_of(odd * half, half)
+    at_half = pl.multiple_of((1 - odd) * full, half)
+    low_lanes = iota((S, LANES), 1) < R
+    position = iota((S, LANES), 0)
+
+    def in_rows(at, count):
+        sums = in_acc[pl.ds(at, count), :]
+        square = jnp.sum(sq_acc[pl.ds(at, count), :], axis=1, keepdims=True)
+        scale = lax.rsqrt(square * (1.0 / (chunks * columns)) + norm_epsilon)
+        factor = (sums[:, :LANES] + sums[:, LANES:]) * scale
+        return [
+            jnp.where(position < lengths[at // S + q], factor[q * S : (q + 1) * S], 0.0)
+            for q in range(count // S)
+        ]
+
+    def side_by_side(tiles):
+        both = zip(tiles[: len(tiles) // 2], tiles[len(tiles) // 2 :])
+        return jnp.concatenate([jnp.where(low_lanes, x, y) for x, y in both], axis=0)
+
+    packed[:mid, :] = side_by_side(in_rows(at_full, full)).astype(bf16)
+    packed[mid : mid + low, :] = side_by_side(in_rows(at_half, half)).astype(bf16)
+
+    whole = dot_nt(outp[...], cot[pl.ds(at_full, full), :])
+    for t in range(full // LANES):
+        out_t[t * R : (t + 1) * R, :] = whole[:, t * LANES : (t + 1) * LANES]
+    out_t[full // LANES * R :, :half] = dot_nt(outp[...], cot[pl.ds(at_half, half), :])
+
+    def part(t, b):
+        return out_t[pl.ds(t * R + b, A, stride=B), :]
+
+    row = mid + low
+    for m in range(full // (G * S)):
+        t, at = divmod(m * G * S, LANES)
+        for b in range(0, B, 2):
+            both = [part(t, b + c)[:, at : at + G * S] for c in range(2)]
+            packed[row : row + A, :] = jnp.concatenate(both, axis=1).astype(bf16)
+            row += A
+    packed[row : row + A, :] = jnp.concatenate(
+        [part(full // LANES, b)[:, :half] for b in range(B)], axis=1
+    ).astype(bf16)
 
 
 def in_hbm(x):
@@ -144,10 +148,10 @@
 
 def factors(lengths, hidden, cotangent, gain, in_projection, out_projection):
     rows, width = hidden.shape
-    columns = 1024
+    columns = 2048
     chunks = width // columns
     return pl.pallas_call(
-        functools.partial(factors_kernel, 4),
+        functools.partial(factors_kernel, 2),
         out_shape=jax.ShapeDtypeStruct((rows, 2 * R), bf16),
         in_specs=[pl.BlockSpec(memory_space=pl.ANY)] * 6,
         out_specs=pl.BlockSpec(memory_space=pltpu.VMEM),
@@ -158,8 +162,7 @@
             pltpu.VMEM((chunks, 1, columns), bf16),
             pltpu.VMEM((chunks, R, columns), bf16),
             pltpu.VMEM(out_projection.shape, bf16),
-            pltpu.VMEM((rows, 2 * R), f32),
-            pltpu.VMEM((rows, R), f32),
+            pltpu.VMEM((rows, 4 * R), f32),
             pltpu.VMEM((rows, LANES), f32),
             pltpu.VMEM((-(-rows // LANES) * R, LANES), f32),
             pltpu.SemaphoreType.DMA((3 + 3 * chunks,)),

time: 26.5 us -> 25.9 us (0.977)
  Pallas kernels: 12.5 us -> 11.8 us
    pallas_call x1, Pallas kernels: 5.63 us -> 4.96 us  [factors(): pl.pallas_call(functools.partial(factors_kernel, 2), out_shape=jax.ShapeD...]
  transfers between devices with their start and end apart: 6 -> 6, of which waited for: 3 -> 3; matrix products, arithmetic and copies ran while one was open for 0% -> 0% of each run, Pallas kernels for 21% -> 22%
where the time goes in v9:
time: 25.9 us; the launch traced here: 25.7 us
  Pallas kernels  11.8 us (46%)
  starting transfers between devices  7.75 us (30%)
  waiting for transfers between devices  5.38 us (21%)
  other arithmetic  0.69 us (3%)
    ppermute x6, starting transfers between devices, swap(): return lax.ppermute(x, axis, pairs)  7.75 us
    ppermute x6, waiting for transfers between devices, swap(): return lax.ppermute(x, axis, pairs)  5.38 us
    pallas_call x1, Pallas kernels, factors(): pl.pallas_call(functools.partial(factors_kernel, 2), out_shape=jax.ShapeD...  4.96 us
    pallas_call x1, Pallas kernels, fetch(): pl.pallas_call(functools.partial(fetch_kernel, n_layer), out_shape=jax.Sh...  3.34 us
    pallas_call x3, Pallas kernels, scores(): pl.pallas_call(functools.partial(scores_kernel, k), out_shape=jax.ShapeDt...  2.24 us
    pallas_call x1, Pallas kernels, grads_and_scores(): pl.pallas_call(functools.partial(grads_kernel, n_store, queries // n_stor...  1.28 us
    transpose x1, other arithmetic, on_device(): return total.T  0.69 us
  transfers between devices with their start and end apart: 6, of which 3 were waited for; matrix products, arithmetic and copies ran while one was open for 0% of the time, Pallas kernels for 22%

profile of v9, /device:TPU:0, one launch (start us, length us, event | category | flops | bytes accessed | tf_op | source)
XLA Modules:
  0.0 25.7 jit_solution(13308913398074349188)
XLA Ops:
  0.0 5.0 %factors.1.after.refs_0_ = bf16[288,128]{1,0:T(8,128)(2,1)S(1)} custom-call(s32[36]{0:T(128)} %hbm_lengths.1, bf16[288,8192]{1,0:T(8,128)(2,1)} %bitcast.8, bf16[288,1024]{1,0:T(8,128)(2,1)} %bitcast.10, bf16[1,8192]{1,0:T(2,128)(2,1)} %hbm_gain.1, bf16[64,8192]{1,0:T(8,128)(2,1)} %bitcast.9, bf16[64,1024]{1,0:T(8,128)(2,1)} %bitcast.11), custom_call_target="tpu_custom_call" | custom-call | tf_op jit(solution)/shard_map/factors/pallas_call | solution.py:153
  5.0 5.1 %collective-permute-start.2 = (bf16[288,128]{1,0:T(8,128)(2,1)S(1)}, bf16[288,128]{1,0:T(8,128)(2,1)S(1)}, u32[]{:S(2)}, u32[]{:S(2)}) collective-permute-start(bf16[288,128]{1,0:T(8,128)(2,1)S(1)} %factors.1.after.refs_0_), channel_id=1, source_target_pairs={{0,12},{4,8},{8,4},{12,0},{1,13},{5,9},{9,5},{13,1},{2,14},{6,10},... | collective-permute-start | bytes 221192 | tf_op jit(solution)/shard_map/ppermute | solution.py:326
  10.1 0.0 collective-permute-start.1
  10.1 0.6 %collective-permute-start = (bf16[288,128]{1,0:T(8,128)(2,1)S(1)}, bf16[288,128]{1,0:T(8,128)(2,1)S(1)}, u32[]{:S(2)}, u32[]{:S(2)}) collective-permute-start(bf16[288,128]{1,0:T(8,128)(2,1)S(1)} %factors.1.after.refs_0_), channel_id=1, source_target_pairs={{0,4},{4,0},{8,12},{12,8},{1,5},{5,1},{9,13},{13,9},{2,6},{6,2},{1... | collective-permute-start | bytes 221192 | tf_op jit(solution)/shard_map/ppermute | solution.py:326
  10.7 3.3 %fetch.1.refs_4_.slab = bf16[960,4096]{1,0:T(8,128)(2,1)S(1)} custom-call(bf16[288,128]{1,0:T(8,128)(2,1)S(1)} %factors.1.after.refs_0_, bf16[960,4096]{1,0:T(8,128)(2,1)} %bitcast.7), custom_call_target="tpu_custom_call" | custom-call | bytes 7864320 | tf_op jit(solution)/shard_map/fetch/pallas_call | solution.py:191
  14.1 0.0 collective-permute-done.2.refs_3_
  14.1 2.2 %collective-permute-done.1.refs_2_ = bf16[288,128]{1,0:T(8,128)(2,1)S(1)} collective-permute-done((bf16[288,128]{1,0:T(8,128)(2,1)S(1)}, bf16[288,128]{1,0:T(8,128)(2,1)S(1)}, u32[]{:S(2)}, u32[]{:S(2)}) %collective-permute-start.1) | collective-permute-done | bytes 73760 | tf_op jit(solution)/shard_map/ppermute | solution.py:326
  16.3 0.0 collective-permute-done.refs_1_
  16.3 1.3 %grads.1 = (bf16[144,4096]{1,0:T(8,128)(2,1)S(1)}, bf16[144,240]{1,0:T(8,128)(2,1)S(1)}) custom-call(bf16[288,128]{1,0:T(8,128)(2,1)S(1)} %factors.1.after.refs_0_, bf16[288,128]{1,0:T(8,128)(2,1)S(1)} %collective-permute-done.refs_1_, bf16[288,128]{1,0:T(8,128)(2,1)S(1)} %collective-permute-done.1.refs_2_, ...), custom_call_target="tpu_custom_call" | custom-call | tf_op jit(solution)/shard_map/grads/pallas_call | solution.py:333
  17.6 0.8 %collective-permute-start.3 = (bf16[144,240]{1,0:T(8,128)(2,1)S(1)}, bf16[144,240]{1,0:T(8,128)(2,1)S(1)}, u32[]{:S(2)}, u32[]{:S(2)}) collective-permute-start(bf16[144,240]{1,0:T(8,128)(2,1)S(1)} %get-tuple-element.8), channel_id=1, source_target_pairs={{0,3},{1,2},{2,1},{3,0},{4,7},{5,6},{6,5},{7,4},{8,11},{9,10},{10,... | collective-permute-start | bytes 207368 | tf_op jit(solution)/shard_map/ppermute | solution.py:326
  18.4 0.7 %scores.5 = bf16[144,240]{1,0:T(8,128)(2,1)S(1)} custom-call(bf16[144,4096]{1,0:T(8,128)(2,1)S(1)} %get-tuple-element.7.grads, bf16[960,4096]{1,0:T(8,128)(2,1)S(1)} %fetch.1.refs_4_.slab), custom_call_target="tpu_custom_call" | custom-call | flops 283115520 | bytes 3145728 | tf_op jit(solution)/shard_map/scores/pallas_call | solution.py:352
  19.2 0.7 %scores.4 = bf16[144,240]{1,0:T(8,128)(2,1)S(1)} custom-call(bf16[144,4096]{1,0:T(8,128)(2,1)S(1)} %get-tuple-element.7.grads, bf16[960,4096]{1,0:T(8,128)(2,1)S(1)} %fetch.1.refs_4_.slab), custom_call_target="tpu_custom_call" | custom-call | flops 283115520 | bytes 3145728 | tf_op jit(solution)/shard_map/scores/pallas_call | solution.py:352
  19.9 0.8 %collective-permute-start.4 = (bf16[144,240]{1,0:T(8,128)(2,1)S(1)}, bf16[144,240]{1,0:T(8,128)(2,1)S(1)}, u32[]{:S(2)}, u32[]{:S(2)}) collective-permute-start(bf16[144,240]{1,0:T(8,128)(2,1)S(1)} %scores.4), channel_id=1, source_target_pairs={{0,2},{1,3},{2,0},{3,1},{4,6},{5,7},{6,4},{7,5},{8,10},{9,11},{10,... | collective-permute-start | bytes 207368 | tf_op jit(solution)/shard_map/ppermute | solution.py:326
  20.7 0.4 %collective-permute-start.5 = (bf16[144,240]{1,0:T(8,128)(2,1)S(1)}, bf16[144,240]{1,0:T(8,128)(2,1)S(1)}, u32[]{:S(2)}, u32[]{:S(2)}) collective-permute-start(bf16[144,240]{1,0:T(8,128)(2,1)S(1)} %scores.5), channel_id=1, source_target_pairs={{0,1},{1,0},{2,3},{3,2},{4,5},{5,4},{6,7},{7,6},{8,9},{9,8},{10,11... | collective-permute-start | bytes 207368 | tf_op jit(solution)/shard_map/ppermute | solution.py:326
  21.1 1.1 %collective-permute-done.3.refs_0_ = bf16[144,240]{1,0:T(8,128)(2,1)S(1)} collective-permute-done((bf16[144,240]{1,0:T(8,128)(2,1)S(1)}, bf16[144,240]{1,0:T(8,128)(2,1)S(1)}, u32[]{:S(2)}, u32[]{:S(2)}) %collective-permute-start.3) | collective-permute-done | bytes 69152 | tf_op jit(solution)/shard_map/ppermute | solution.py:326
  22.2 0.7 %scores.3 = f32[144,240]{1,0:T(8,128)S(1)} custom-call(bf16[144,4096]{1,0:T(8,128)(2,1)S(1)} %get-tuple-element.7.grads, bf16[960,4096]{1,0:T(8,128)(2,1)S(1)} %fetch.1.refs_4_.slab, bf16[144,240]{1,0:T(8,128)(2,1)S(1)} %collective-permute-done.3.refs_0_), custom_call_target="tpu_custom_call" | custom-call | flops 283115520 | bytes 3145728 | tf_op jit(solution)/shard_map/scores/pallas_call | solution.py:352
  22.9 2.1 %collective-permute-done.4 = bf16[144,240]{1,0:T(8,128)(2,1)S(1)} collective-permute-done((bf16[144,240]{1,0:T(8,128)(2,1)S(1)}, bf16[144,240]{1,0:T(8,128)(2,1)S(1)}, u32[]{:S(2)}, u32[]{:S(2)}) %collective-permute-start.4) | collective-permute-done | bytes 69152 | tf_op jit(solution)/shard_map/ppermute | solution.py:326
  25.0 0.0 collective-permute-done.5
  25.0 0.7 %add_bitcast_fusion = f32[240,144]{0,1:T(8,128)} fusion(bf16[144,240]{1,0:T(8,128)(2,1)S(1)} %collective-permute-done.5, f32[144,240]{1,0:T(8,128)S(1)} %scores.3, bf16[144,240]{1,0:T(8,128)(2,1)S(1)} %collective-permute-done.4), kind=kLoop, calls=%fused_computation | loop fusion | flops 138240 | bytes 414720 | tf_op jit(solution)/shard_map/transpose | solution.py:386
Async XLA Ops:
  5.0 9.1 %collective-permute-start.2 = (bf16[288,128]{1,0:T(8,128)(2,1)S(1)}, bf16[288,128]{1,0:T(8,128)(2,1)S(1)}, u32[]{:S(2)}, u32[]{:S(2)}) collective-permute-start(bf16[288,128]{1,0:T(8,128)(2,1)S(1)} %factors.1.after.refs_0_), channel_id=1, source_target_pairs={{0,12},{4,8},{8,4},{12,0},{1,13},{5,9},{9,5},{13,1},{2,14},{6,10},... | collective-permute-start | bytes 221192 | tf_op jit(solution)/shard_map/ppermute | solution.py:326
  10.1 6.2 %collective-permute-start.1 = (bf16[288,128]{1,0:T(8,128)(2,1)S(1)}, bf16[288,128]{1,0:T(8,128)(2,1)S(1)}, u32[]{:S(2)}, u32[]{:S(2)}) collective-permute-start(bf16[288,128]{1,0:T(8,128)(2,1)S(1)} %factors.1.after.refs_0_), channel_id=1, source_target_pairs={{0,8},{4,12},{8,0},{12,4},{1,9},{5,13},{9,1},{13,5},{2,10},{6,14},... | collective-permute-start | bytes 221192 | tf_op jit(solution)/shard_map/ppermute | solution.py:326
  10.1 6.2 %collective-permute-start = (bf16[288,128]{1,0:T(8,128)(2,1)S(1)}, bf16[288,128]{1,0:T(8,128)(2,1)S(1)}, u32[]{:S(2)}, u32[]{:S(2)}) collective-permute-start(bf16[288,128]{1,0:T(8,128)(2,1)S(1)} %factors.1.after.refs_0_), channel_id=1, source_target_pairs={{0,4},{4,0},{8,12},{12,8},{1,5},{5,1},{9,13},{13,9},{2,6},{6,2},{1... | collective-permute-start | bytes 221192 | tf_op jit(solution)/shard_map/ppermute | solution.py:326
  17.6 4.6 %collective-permute-start.3 = (bf16[144,240]{1,0:T(8,128)(2,1)S(1)}, bf16[144,240]{1,0:T(8,128)(2,1)S(1)}, u32[]{:S(2)}, u32[]{:S(2)}) collective-permute-start(bf16[144,240]{1,0:T(8,128)(2,1)S(1)} %get-tuple-element.8), channel_id=1, source_target_pairs={{0,3},{1,2},{2,1},{3,0},{4,7},{5,6},{6,5},{7,4},{8,11},{9,10},{10,... | collective-permute-start | bytes 207368 | tf_op jit(solution)/shard_map/ppermute | solution.py:326
  19.9 5.1 %collective-permute-start.4 = (bf16[144,240]{1,0:T(8,128)(2,1)S(1)}, bf16[144,240]{1,0:T(8,128)(2,1)S(1)}, u32[]{:S(2)}, u32[]{:S(2)}) collective-permute-start(bf16[144,240]{1,0:T(8,128)(2,1)S(1)} %scores.4), channel_id=1, source_target_pairs={{0,2},{1,3},{2,0},{3,1},{4,6},{5,7},{6,4},{7,5},{8,10},{9,11},{10,... | collective-permute-start | bytes 207368 | tf_op jit(solution)/shard_map/ppermute | solution.py:326
  20.7 4.3 %collective-permute-start.5 = (bf16[144,240]{1,0:T(8,128)(2,1)S(1)}, bf16[144,240]{1,0:T(8,128)(2,1)S(1)}, u32[]{:S(2)}, u32[]{:S(2)}) collective-permute-start(bf16[144,240]{1,0:T(8,128)(2,1)S(1)} %scores.5), channel_id=1, source_target_pairs={{0,1},{1,0},{2,3},{3,2},{4,5},{5,4},{6,7},{7,6},{8,9},{9,8},{10,11... | collective-permute-start | bytes 207368 | tf_op jit(solution)/shard_map/ppermute | solution.py:326

commit v10 on v9

--- a/solution.py
+++ b/solution.py
@@ -377,12 +377,14 @@
     gathered = [packed] + [swap(packed, "store", n_store, k) for k in range(1, n_store)]
     slab = fetch(packed, store[0], n_layer)
     grads, partial = grads_and_scores(gathered, slab, n_store, n_layer, n_layer - 1)
-    crossed = [swap(partial, "layer", n_layer, n_layer - 1)]
-    for k in reversed(range(1, n_layer - 1)):
-        crossed.append(swap(scores(grads, slab, n_layer, k), "layer", n_layer, k))
-    total = scores(grads, slab, n_layer, 0, crossed[:1])
-    for x in crossed[1:]:
-        total = total + x.astype(f32)
+    other = swap(partial, "layer", n_layer, 1)
+    near = swap(scores(grads, slab, n_layer, 1), "layer", n_layer, 1)
+    crossed = [near]
+    for k in reversed(range(2, n_layer, 2)):
+        if k < n_layer - 2:
+            other = swap(scores(grads, slab, n_layer, k + 1), "layer", n_layer, 1)
+        crossed.append(swap(scores(grads, slab, n_layer, k, [other]), "layer", n_layer, k))
+    total = scores(grads, slab, n_layer, 0, crossed)
     return total.T
 
 

time: 25.9 us -> 25.8 us (level)
  Pallas kernels: 11.8 us -> 12.5 us
  other arithmetic: 0.69 us -> 0 us
  waiting for transfers between devices: 5.38 us -> 5.08 us
    transpose x1 -> x0, other arithmetic: 0.69 us -> none  [on_device(): return total.T]
    pallas_call x3, Pallas kernels: 2.24 us -> 2.91 us  [scores(): pl.pallas_call(functools.partial(scores_kernel, k), out_shape=jax.ShapeDt...]
    ppermute x6, waiting for transfers between devices: 5.38 us -> 5.08 us  [swap(): return lax.ppermute(x, axis, pairs)]
  transfers between devices with their start and end apart: 6 -> 6, of which waited for: 3 -> 2; matrix products, arithmetic and copies ran while one was open for 0% -> 0% of each run, Pallas kernels for 22% -> 19%
where the time goes in v10:
time: 25.8 us; the launch traced here: 25.6 us
  Pallas kernels  12.5 us (48%)
  starting transfers between devices  7.95 us (31%)
  waiting for transfers between devices  5.08 us (20%)
    ppermute x6, starting transfers between devices, swap(): return lax.ppermute(x, axis, pairs)  7.95 us
    ppermute x6, waiting for transfers between devices, swap(): return lax.ppermute(x, axis, pairs)  5.08 us
    pallas_call x1, Pallas kernels, factors(): pl.pallas_call(functools.partial(factors_kernel, 2), out_shape=jax.ShapeD...  4.96 us
    pallas_call x1, Pallas kernels, fetch(): pl.pallas_call(functools.partial(fetch_kernel, n_layer), out_shape=jax.Sh...  3.34 us
    pallas_call x3, Pallas kernels, scores(): pl.pallas_call(functools.partial(scores_kernel, k), out_shape=jax.ShapeDt...  2.91 us
    pallas_call x1, Pallas kernels, grads_and_scores(): pl.pallas_call(functools.partial(grads_kernel, n_store, queries // n_stor...  1.28 us
  transfers between devices with their start and end apart: 6, of which 2 were waited for; matrix products, arithmetic and copies ran while one was open for 0% of the time, Pallas kernels for 19%

profile of v10, /device:TPU:0, one launch (start us, length us, event | category | flops | bytes accessed | tf_op | source)
XLA Modules:
  0.0 25.6 jit_solution(7382537496178953316)
XLA Ops:
  0.0 5.0 %factors.1.after.refs_0_ = bf16[288,128]{1,0:T(8,128)(2,1)S(1)} custom-call(s32[36]{0:T(128)} %hbm_lengths.1, bf16[288,8192]{1,0:T(8,128)(2,1)} %bitcast.7, bf16[288,1024]{1,0:T(8,128)(2,1)} %bitcast.9, bf16[1,8192]{1,0:T(2,128)(2,1)} %hbm_gain.1, bf16[64,8192]{1,0:T(8,128)(2,1)} %bitcast.8, bf16[64,1024]{1,0:T(8,128)(2,1)} %bitcast.10), custom_call_target="tpu_custom_call" | custom-call | tf_op jit(solution)/shard_map/factors/pallas_call | solution.py:153
  5.0 5.1 %collective-permute-start.2 = (bf16[288,128]{1,0:T(8,128)(2,1)S(1)}, bf16[288,128]{1,0:T(8,128)(2,1)S(1)}, u32[]{:S(2)}, u32[]{:S(2)}) collective-permute-start(bf16[288,128]{1,0:T(8,128)(2,1)S(1)} %factors.1.after.refs_0_), channel_id=1, source_target_pairs={{0,12},{4,8},{8,4},{12,0},{1,13},{5,9},{9,5},{13,1},{2,14},{6,10},... | collective-permute-start | bytes 221192 | tf_op jit(solution)/shard_map/ppermute | solution.py:326
  10.1 0.0 collective-permute-start.1
  10.1 0.6 %collective-permute-start = (bf16[288,128]{1,0:T(8,128)(2,1)S(1)}, bf16[288,128]{1,0:T(8,128)(2,1)S(1)}, u32[]{:S(2)}, u32[]{:S(2)}) collective-permute-start(bf16[288,128]{1,0:T(8,128)(2,1)S(1)} %factors.1.after.refs_0_), channel_id=1, source_target_pairs={{0,4},{4,0},{8,12},{12,8},{1,5},{5,1},{9,13},{13,9},{2,6},{6,2},{1... | collective-permute-start | bytes 221192 | tf_op jit(solution)/shard_map/ppermute | solution.py:326
  10.7 3.3 %fetch.1.refs_4_.slab = bf16[960,4096]{1,0:T(8,128)(2,1)S(1)} custom-call(bf16[288,128]{1,0:T(8,128)(2,1)S(1)} %factors.1.after.refs_0_, bf16[960,4096]{1,0:T(8,128)(2,1)} %bitcast.6), custom_call_target="tpu_custom_call" | custom-call | bytes 7864320 | tf_op jit(solution)/shard_map/fetch/pallas_call | solution.py:191
  14.1 0.0 collective-permute-done.2.refs_3_
  14.1 2.2 %collective-permute-done.1.refs_2_ = bf16[288,128]{1,0:T(8,128)(2,1)S(1)} collective-permute-done((bf16[288,128]{1,0:T(8,128)(2,1)S(1)}, bf16[288,128]{1,0:T(8,128)(2,1)S(1)}, u32[]{:S(2)}, u32[]{:S(2)}) %collective-permute-start.1) | collective-permute-done | bytes 73760 | tf_op jit(solution)/shard_map/ppermute | solution.py:326
  16.3 0.0 collective-permute-done.refs_1_
  16.3 1.3 %grads.1 = (bf16[144,4096]{1,0:T(8,128)(2,1)S(1)}, bf16[144,240]{1,0:T(8,128)(2,1)S(1)}) custom-call(bf16[288,128]{1,0:T(8,128)(2,1)S(1)} %factors.1.after.refs_0_, bf16[288,128]{1,0:T(8,128)(2,1)S(1)} %collective-permute-done.refs_1_, bf16[288,128]{1,0:T(8,128)(2,1)S(1)} %collective-permute-done.1.refs_2_, ...), custom_call_target="tpu_custom_call" | custom-call | tf_op jit(solution)/shard_map/grads/pallas_call | solution.py:333
  17.6 0.1 collective-permute-start.4
  17.7 0.7 %scores.3 = bf16[144,240]{1,0:T(8,128)(2,1)S(1)} custom-call(bf16[144,4096]{1,0:T(8,128)(2,1)S(1)} %get-tuple-element.7.grads, bf16[960,4096]{1,0:T(8,128)(2,1)S(1)} %fetch.1.refs_4_.slab), custom_call_target="tpu_custom_call" | custom-call | flops 283115520 | bytes 3145728 | tf_op jit(solution)/shard_map/scores/pallas_call | solution.py:352
  18.4 0.6 %collective-permute-start.3 = (bf16[144,240]{1,0:T(8,128)(2,1)S(1)}, bf16[144,240]{1,0:T(8,128)(2,1)S(1)}, u32[]{:S(2)}, u32[]{:S(2)}) collective-permute-start(bf16[144,240]{1,0:T(8,128)(2,1)S(1)} %scores.3), channel_id=1, source_target_pairs={{0,1},{1,0},{2,3},{3,2},{4,5},{5,4},{6,7},{7,6},{8,9},{9,8},{10,11... | collective-permute-start | bytes 207368 | tf_op jit(solution)/shard_map/ppermute | solution.py:326
  19.0 0.0 collective-permute-done.4.refs_0_
  19.0 0.7 %scores.4 = bf16[144,240]{1,0:T(8,128)(2,1)S(1)} custom-call(bf16[144,4096]{1,0:T(8,128)(2,1)S(1)} %get-tuple-element.7.grads, bf16[960,4096]{1,0:T(8,128)(2,1)S(1)} %fetch.1.refs_4_.slab, bf16[144,240]{1,0:T(8,128)(2,1)S(1)} %collective-permute-done.4.refs_0_), custom_call_target="tpu_custom_call" | custom-call | flops 283115520 | bytes 3145728 | tf_op jit(solution)/shard_map/scores/pallas_call | solution.py:352
  19.7 1.6 %collective-permute-start.5 = (bf16[144,240]{1,0:T(8,128)(2,1)S(1)}, bf16[144,240]{1,0:T(8,128)(2,1)S(1)}, u32[]{:S(2)}, u32[]{:S(2)}) collective-permute-start(bf16[144,240]{1,0:T(8,128)(2,1)S(1)} %scores.4), channel_id=1, source_target_pairs={{0,2},{1,3},{2,0},{3,1},{4,6},{5,7},{6,4},{7,5},{8,10},{9,11},{10,... | collective-permute-start | bytes 207368 | tf_op jit(solution)/shard_map/ppermute | solution.py:326
  21.3 0.0 collective-permute-done.3.refs_0_
  21.3 2.9 %collective-permute-done.5.refs_1_ = bf16[144,240]{1,0:T(8,128)(2,1)S(1)} collective-permute-done((bf16[144,240]{1,0:T(8,128)(2,1)S(1)}, bf16[144,240]{1,0:T(8,128)(2,1)S(1)}, u32[]{:S(2)}, u32[]{:S(2)}) %collective-permute-start.5) | collective-permute-done | bytes 69152 | tf_op jit(solution)/shard_map/ppermute | solution.py:326
  24.2 1.4 %scores.5 = f32[144,240]{1,0:T(8,128)} custom-call(bf16[144,4096]{1,0:T(8,128)(2,1)S(1)} %get-tuple-element.7.grads, bf16[960,4096]{1,0:T(8,128)(2,1)S(1)} %fetch.1.refs_4_.slab, bf16[144,240]{1,0:T(8,128)(2,1)S(1)} %collective-permute-done.3.refs_0_, bf16[144,240]{1,0:T(8,128)(2,1)S(1)} %collective-permute-done.5.refs_1_), custom_call_target="tpu_custom_call" | custom-call | flops 283115520 | bytes 3145728 | tf_op jit(solution)/shard_map/scores/pallas_call | solution.py:352
Async XLA Ops:
  5.0 9.1 %collective-permute-start.2 = (bf16[288,128]{1,0:T(8,128)(2,1)S(1)}, bf16[288,128]{1,0:T(8,128)(2,1)S(1)}, u32[]{:S(2)}, u32[]{:S(2)}) collective-permute-start(bf16[288,128]{1,0:T(8,128)(2,1)S(1)} %factors.1.after.refs_0_), channel_id=1, source_target_pairs={{0,12},{4,8},{8,4},{12,0},{1,13},{5,9},{9,5},{13,1},{2,14},{6,10},... | collective-permute-start | bytes 221192 | tf_op jit(solution)/shard_map/ppermute | solution.py:326
  10.1 6.2 %collective-permute-start.1 = (bf16[288,128]{1,0:T(8,128)(2,1)S(1)}, bf16[288,128]{1,0:T(8,128)(2,1)S(1)}, u32[]{:S(2)}, u32[]{:S(2)}) collective-permute-start(bf16[288,128]{1,0:T(8,128)(2,1)S(1)} %factors.1.after.refs_0_), channel_id=1, source_target_pairs={{0,8},{4,12},{8,0},{12,4},{1,9},{5,13},{9,1},{13,5},{2,10},{6,14},... | collective-permute-start | bytes 221192 | tf_op jit(solution)/shard_map/ppermute | solution.py:326
  10.1 6.2 %collective-permute-start = (bf16[288,128]{1,0:T(8,128)(2,1)S(1)}, bf16[288,128]{1,0:T(8,128)(2,1)S(1)}, u32[]{:S(2)}, u32[]{:S(2)}) collective-permute-start(bf16[288,128]{1,0:T(8,128)(2,1)S(1)} %factors.1.after.refs_0_), channel_id=1, source_target_pairs={{0,4},{4,0},{8,12},{12,8},{1,5},{5,1},{9,13},{13,9},{2,6},{6,2},{1... | collective-permute-start | bytes 221192 | tf_op jit(solution)/shard_map/ppermute | solution.py:326
  17.6 1.4 %collective-permute-start.4 = (bf16[144,240]{1,0:T(8,128)(2,1)S(1)}, bf16[144,240]{1,0:T(8,128)(2,1)S(1)}, u32[]{:S(2)}, u32[]{:S(2)}) collective-permute-start(bf16[144,240]{1,0:T(8,128)(2,1)S(1)} %get-tuple-element.8), channel_id=1, source_target_pairs={{0,1},{1,0},{2,3},{3,2},{4,5},{5,4},{6,7},{7,6},{8,9},{9,8},{10,11... | collective-permute-start | bytes 207368 | tf_op jit(solution)/shard_map/ppermute | solution.py:326
  18.4 2.9 %collective-permute-start.3 = (bf16[144,240]{1,0:T(8,128)(2,1)S(1)}, bf16[144,240]{1,0:T(8,128)(2,1)S(1)}, u32[]{:S(2)}, u32[]{:S(2)}) collective-permute-start(bf16[144,240]{1,0:T(8,128)(2,1)S(1)} %scores.3), channel_id=1, source_target_pairs={{0,1},{1,0},{2,3},{3,2},{4,5},{5,4},{6,7},{7,6},{8,9},{9,8},{10,11... | collective-permute-start | bytes 207368 | tf_op jit(solution)/shard_map/ppermute | solution.py:326
  19.7 4.4 %collective-permute-start.5 = (bf16[144,240]{1,0:T(8,128)(2,1)S(1)}, bf16[144,240]{1,0:T(8,128)(2,1)S(1)}, u32[]{:S(2)}, u32[]{:S(2)}) collective-permute-start(bf16[144,240]{1,0:T(8,128)(2,1)S(1)} %scores.4), channel_id=1, source_target_pairs={{0,2},{1,3},{2,0},{3,1},{4,6},{5,7},{6,4},{7,5},{8,10},{9,11},{10,... | collective-permute-start | bytes 207368 | tf_op jit(solution)/shard_map/ppermute | solution.py:326

commit v11 on v10

--- a/solution.py
+++ b/solution.py
@@ -290,12 +290,17 @@
             ).astype(bf16)
 
 
-def grads_kernel(n_store, full_groups, k, *refs):
-    gathered = refs[:n_store]
-    slab, grads, out, shards = refs[n_store:]
-    me_store = lax.axis_index("store")
-    for at in range(n_store):
-        shards[partner(me_store, at, n_store)] = gathered[at][...]
+def grads_kernel(shifts, n_store, full_groups, k, packed, *refs):
+    gathered = refs[: len(shifts)]
+    slab, grads, out, shards = refs[len(shifts) :]
+    me = lax.axis_index("store")
+    shards[me] = packed[...]
+    for (away, first, last), block in zip(shifts, gathered):
+
+        @pl.when(jnp.logical_and(me >= first, me <= last))
+        def _():
+            shards[lax.rem(me + away, n_store)] = block[...]
+
     four = 4 * (full_groups * G + H)
     if n_store == 4:
         build_grads(shards, 0, 0, full_groups, grads)
@@ -326,22 +331,33 @@
     return lax.ppermute(x, axis, pairs)
 
 
-def grads_and_scores(gathered, slab, n_store, n_layer, k):
+def store_shifts(n):
+    if n == 4:
+        return [(1, 3, 3), (2, 2, 3), (3, 0, 3), (2, 0, 1), (1, 0, 2)]
+    return [(away, 0, n - 1) for away in range(1, n)]
+
+
+def grads_and_scores(packed, slab, n_store, n_layer, k):
     rows, features = slab.shape
-    queries = n_store * gathered[0].shape[0] // S
+    queries = packed.shape[0] // S
+    shifts = store_shifts(n_store)
+    gathered = []
+    for away, first, last in shifts:
+        pairs = [((to + away) % n_store, to) for to in range(first, last + 1)]
+        gathered.append(lax.ppermute(packed, "store", pairs))
     vmem = pl.BlockSpec(memory_space=pltpu.VMEM)
     return pl.pallas_call(
-        functools.partial(grads_kernel, n_store, queries // n_store // G, k),
+        functools.partial(grads_kernel, shifts, n_store, queries // G, k),
         out_shape=[
-            jax.ShapeDtypeStruct((queries, features), bf16),
-            jax.ShapeDtypeStruct((queries, rows // n_layer), bf16),
+            jax.ShapeDtypeStruct((n_store * queries, features), bf16),
+            jax.ShapeDtypeStruct((n_store * queries, rows // n_layer), bf16),
         ],
-        in_specs=[vmem] * (n_store + 1),
+        in_specs=[vmem] * (len(shifts) + 2),
         out_specs=[vmem] * 2,
-        scratch_shapes=[pltpu.VMEM((n_store,) + gathered[0].shape, bf16)],
+        scratch_shapes=[pltpu.VMEM((n_store,) + packed.shape, bf16)],
         compiler_params=pltpu.CompilerParams(vmem_limit_bytes=24 * 2**20),
         name="grads",
-    )(*gathered, slab)
+    )(packed, *gathered, slab)
 
 
 def scores(grads, slab, n_layer, k, terms=()):
@@ -374,9 +390,8 @@
         in_proj[0],
         out_proj[0],
     )
-    gathered = [packed] + [swap(packed, "store", n_store, k) for k in range(1, n_store)]
     slab = fetch(packed, store[0], n_layer)
-    grads, partial = grads_and_scores(gathered, slab, n_store, n_layer, n_layer - 1)
+    grads, partial = grads_and_scores(packed, slab, n_store, n_layer, n_layer - 1)
     other = swap(partial, "layer", n_layer, 1)
     near = swap(scores(grads, slab, n_layer, 1), "layer", n_layer, 1)
     crossed = [near]
@@ -384,7 +399,9 @@
         if k < n_layer - 2:
             other = swap(scores(grads, slab, n_layer, k + 1), "layer", n_layer, 1)
         crossed.append(swap(scores(grads, slab, n_layer, k, [other]), "layer", n_layer, k))
-    total = scores(grads, slab, n_layer, 0, crossed)
+    total = scores(grads, slab, n_layer, 0)
+    for x in crossed:
+        total = total + x.astype(f32)
     return total.T
 
 

time: 25.8 us -> 30.3 us (1.17)
  starting transfers between devices: 7.95 us -> 15.7 us
  waiting for transfers between devices: 5.08 us -> 1.78 us
  Pallas kernels: 12.5 us -> 11.8 us
  other arithmetic: 0 us -> 0.69 us
    ppermute x0 -> x5, starting transfers between devices: none -> 13 us  [grads_and_scores(): gathered.append(lax.ppermute(packed, 'store', pairs))]
    ppermute x6 -> x3, starting transfers between devices: 7.95 us -> 2.64 us  [swap(): return lax.ppermute(x, axis, pairs)]
    ppermute x6 -> x3, waiting for transfers between devices: 5.08 us -> 1.77 us  [swap(): return lax.ppermute(x, axis, pairs)]
    transpose x0 -> x1, other arithmetic: none -> 0.69 us  [on_device(): return total.T]
    pallas_call x3, Pallas kernels: 2.91 us -> 2.24 us  [scores(): pl.pallas_call(functools.partial(scores_kernel, k), out_shape=jax.ShapeDt...]
  transfers between devices with their start and end apart: 6 -> 8, of which waited for: 2 -> 1; matrix products, arithmetic and copies ran while one was open for 0% -> 0% of each run, Pallas kernels for 19% -> 19%
where the time goes in v11:
time: 30.3 us; the launch traced here: 30.1 us
  starting transfers between devices  15.7 us (52%)
  Pallas kernels  11.8 us (39%)
  waiting for transfers between devices  1.78 us (6%)
  other arithmetic  0.69 us (2%)
    ppermute x5, starting transfers between devices, grads_and_scores(): gathered.append(lax.ppermute(packed, 'store', pairs))  13 us
    pallas_call x1, Pallas kernels, factors(): pl.pallas_call(functools.partial(factors_kernel, 2), out_shape=jax.ShapeD...  4.96 us
    pallas_call x1, Pallas kernels, fetch(): pl.pallas_call(functools.partial(fetch_kernel, n_layer), out_shape=jax.Sh...  3.35 us
    ppermute x3, starting transfers between devices, swap(): return lax.ppermute(x, axis, pairs)  2.64 us
    pallas_call x3, Pallas kernels, scores(): pl.pallas_call(functools.partial(scores_kernel, k), out_shape=jax.ShapeDt...  2.24 us
    ppermute x3, waiting for transfers between devices, swap(): return lax.ppermute(x, axis, pairs)  1.77 us
    pallas_call x1, Pallas kernels, grads_and_scores(): pl.pallas_call(functools.partial(grads_kernel, shifts, n_store, queries /...  1.29 us
    transpose x1, other arithmetic, on_device(): return total.T  0.69 us
  transfers between devices with their start and end apart: 8, of which 1 were waited for; matrix products, arithmetic and copies ran while one was open for 0% of the time, Pallas kernels for 19%

profile of v11, /device:TPU:0, one launch (start us, length us, event | category | flops | bytes accessed | tf_op | source)
XLA Modules:
  0.0 30.1 jit_solution(8348312972280103671)
XLA Ops:
  0.0 5.0 %factors.1.after.packed = bf16[288,128]{1,0:T(8,128)(2,1)S(1)} custom-call(s32[36]{0:T(128)} %hbm_lengths.1, bf16[288,8192]{1,0:T(8,128)(2,1)} %bitcast.8, bf16[288,1024]{1,0:T(8,128)(2,1)} %bitcast.10, bf16[1,8192]{1,0:T(2,128)(2,1)} %hbm_gain.1, bf16[64,8192]{1,0:T(8,128)(2,1)} %bitcast.9, bf16[64,1024]{1,0:T(8,128)(2,1)} %bitcast.11), custom_call_target="tpu_custom_call" | custom-call | tf_op jit(solution)/shard_map/factors/pallas_call | solution.py:153
  5.0 1.3 %collective-permute-start.4 = (bf16[288,128]{1,0:T(8,128)(2,1)S(1)}, bf16[288,128]{1,0:T(8,128)(2,1)S(1)}, u32[]{:S(2)}, u32[]{:S(2)}) collective-permute-start(bf16[288,128]{1,0:T(8,128)(2,1)S(1)} %factors.1.after.packed), channel_id=1, source_target_pairs={{4,0},{8,4},{12,8},{5,1},{9,5},{13,9},{6,2},{10,6},{14,10},{7,3},{... | collective-permute-start | bytes 221192 | tf_op jit(solution)/shard_map/ppermute | solution.py:347
  6.3 1.3 %collective-permute-start.3 = (bf16[288,128]{1,0:T(8,128)(2,1)S(1)}, bf16[288,128]{1,0:T(8,128)(2,1)S(1)}, u32[]{:S(2)}, u32[]{:S(2)}) collective-permute-start(bf16[288,128]{1,0:T(8,128)(2,1)S(1)} %factors.1.after.packed), channel_id=1, source_target_pairs={{8,0},{12,4},{9,1},{13,5},{10,2},{14,6},{11,3},{15,7},{24,16},{28,... | collective-permute-start | bytes 221192 | tf_op jit(solution)/shard_map/ppermute | solution.py:347
  7.6 3.7 %collective-permute-start.2 = (bf16[288,128]{1,0:T(8,128)(2,1)S(1)}, bf16[288,128]{1,0:T(8,128)(2,1)S(1)}, u32[]{:S(2)}, u32[]{:S(2)}) collective-permute-start(bf16[288,128]{1,0:T(8,128)(2,1)S(1)} %factors.1.after.packed), channel_id=1, source_target_pairs={{12,0},{0,4},{4,8},{8,12},{13,1},{1,5},{5,9},{9,13},{14,2},{2,6},{... | collective-permute-start | bytes 221192 | tf_op jit(solution)/shard_map/ppermute | solution.py:347
  11.3 5.4 %collective-permute-start.1 = (bf16[288,128]{1,0:T(8,128)(2,1)S(1)}, bf16[288,128]{1,0:T(8,128)(2,1)S(1)}, u32[]{:S(2)}, u32[]{:S(2)}) collective-permute-start(bf16[288,128]{1,0:T(8,128)(2,1)S(1)} %factors.1.after.packed), channel_id=1, source_target_pairs={{0,8},{4,12},{1,9},{5,13},{2,10},{6,14},{3,11},{7,15},{16,24},{20,... | collective-permute-start | bytes 221192 | tf_op jit(solution)/shard_map/ppermute | solution.py:347
  16.7 1.3 %collective-permute-start = (bf16[288,128]{1,0:T(8,128)(2,1)S(1)}, bf16[288,128]{1,0:T(8,128)(2,1)S(1)}, u32[]{:S(2)}, u32[]{:S(2)}) collective-permute-start(bf16[288,128]{1,0:T(8,128)(2,1)S(1)} %factors.1.after.packed), channel_id=1, source_target_pairs={{0,12},{1,13},{2,14},{3,15},{16,28},{17,29},{18,30},{19,31}} | collective-permute-start | bytes 221192 | tf_op jit(solution)/shard_map/ppermute | solution.py:347
  18.0 3.4 %fetch.1.refs_5_.slab = bf16[960,4096]{1,0:T(8,128)(2,1)S(1)} custom-call(bf16[288,128]{1,0:T(8,128)(2,1)S(1)} %factors.1.after.packed, bf16[960,4096]{1,0:T(8,128)(2,1)} %bitcast.7), custom_call_target="tpu_custom_call" | custom-call | bytes 7864320 | tf_op jit(solution)/shard_map/fetch/pallas_call | solution.py:191
  21.4 0.0 collective-permute-done.4.refs_4_
  21.4 0.0 collective-permute-done.3.refs_3_
  21.4 0.0 collective-permute-done.2.refs_2_
  21.4 0.0 collective-permute-done.1.refs_1_
  21.4 0.0 collective-permute-done.refs_0_
  21.4 1.3 %grads.1 = (bf16[144,4096]{1,0:T(8,128)(2,1)S(1)}, bf16[144,240]{1,0:T(8,128)(2,1)S(1)}) custom-call(bf16[288,128]{1,0:T(8,128)(2,1)S(1)} %factors.1.after.packed, bf16[288,128]{1,0:T(8,128)(2,1)S(1)} %collective-permute-done.refs_0_, bf16[288,128]{1,0:T(8,128)(2,1)S(1)} %collective-permute-done.1.refs_1_, ...), custom_call_target="tpu_custom_call" | custom-call | tf_op jit(solution)/shard_map/grads/pallas_call | solution.py:349
  22.7 0.1 collective-permute-start.6
  22.8 0.7 %scores.4 = bf16[144,240]{1,0:T(8,128)(2,1)S(1)} custom-call(bf16[144,4096]{1,0:T(8,128)(2,1)S(1)} %get-tuple-element.7.grads, bf16[960,4096]{1,0:T(8,128)(2,1)S(1)} %fetch.1.refs_5_.slab), custom_call_target="tpu_custom_call" | custom-call | flops 283115520 | bytes 3145728 | tf_op jit(solution)/shard_map/scores/pallas_call | solution.py:368
  23.6 0.6 %collective-permute-start.5 = (bf16[144,240]{1,0:T(8,128)(2,1)S(1)}, bf16[144,240]{1,0:T(8,128)(2,1)S(1)}, u32[]{:S(2)}, u32[]{:S(2)}) collective-permute-start(bf16[144,240]{1,0:T(8,128)(2,1)S(1)} %scores.4), channel_id=1, source_target_pairs={{0,1},{1,0},{2,3},{3,2},{4,5},{5,4},{6,7},{7,6},{8,9},{9,8},{10,11... | collective-permute-start | bytes 207368 | tf_op jit(solution)/shard_map/ppermute | solution.py:331
  24.1 0.0 collective-permute-done.6.refs_0_
  24.1 0.7 %scores.5 = bf16[144,240]{1,0:T(8,128)(2,1)S(1)} custom-call(bf16[144,4096]{1,0:T(8,128)(2,1)S(1)} %get-tuple-element.7.grads, bf16[960,4096]{1,0:T(8,128)(2,1)S(1)} %fetch.1.refs_5_.slab, bf16[144,240]{1,0:T(8,128)(2,1)S(1)} %collective-permute-done.6.refs_0_), custom_call_target="tpu_custom_call" | custom-call | flops 283115520 | bytes 3145728 | tf_op jit(solution)/shard_map/scores/pallas_call | solution.py:368
  24.9 2.0 %collective-permute-start.7 = (bf16[144,240]{1,0:T(8,128)(2,1)S(1)}, bf16[144,240]{1,0:T(8,128)(2,1)S(1)}, u32[]{:S(2)}, u32[]{:S(2)}) collective-permute-start(bf16[144,240]{1,0:T(8,128)(2,1)S(1)} %scores.5), channel_id=1, source_target_pairs={{0,2},{1,3},{2,0},{3,1},{4,6},{5,7},{6,4},{7,5},{8,10},{9,11},{10,... | collective-permute-start | bytes 207368 | tf_op jit(solution)/shard_map/ppermute | solution.py:331
  26.9 0.7 %scores.3 = f32[144,240]{1,0:T(8,128)S(1)} custom-call(bf16[144,4096]{1,0:T(8,128)(2,1)S(1)} %get-tuple-element.7.grads, bf16[960,4096]{1,0:T(8,128)(2,1)S(1)} %fetch.1.refs_5_.slab), custom_call_target="tpu_custom_call" | custom-call | flops 283115520 | bytes 3145728 | tf_op jit(solution)/shard_map/scores/pallas_call | solution.py:368
  27.6 0.0 collective-permute-done.5
  27.6 1.8 %collective-permute-done.7 = bf16[144,240]{1,0:T(8,128)(2,1)S(1)} collective-permute-done((bf16[144,240]{1,0:T(8,128)(2,1)S(1)}, bf16[144,240]{1,0:T(8,128)(2,1)S(1)}, u32[]{:S(2)}, u32[]{:S(2)}) %collective-permute-start.7) | collective-permute-done | bytes 69152 | tf_op jit(solution)/shard_map/ppermute | solution.py:331
  29.4 0.7 %add_bitcast_fusion = f32[240,144]{0,1:T(8,128)} fusion(bf16[144,240]{1,0:T(8,128)(2,1)S(1)} %collective-permute-done.7, f32[144,240]{1,0:T(8,128)S(1)} %scores.3, bf16[144,240]{1,0:T(8,128)(2,1)S(1)} %collective-permute-done.5), kind=kLoop, calls=%fused_computation | loop fusion | flops 138240 | bytes 414720 | tf_op jit(solution)/shard_map/transpose | solution.py:405
Async XLA Ops:
  5.0 16.4 %collective-permute-start.4 = (bf16[288,128]{1,0:T(8,128)(2,1)S(1)}, bf16[288,128]{1,0:T(8,128)(2,1)S(1)}, u32[]{:S(2)}, u32[]{:S(2)}) collective-permute-start(bf16[288,128]{1,0:T(8,128)(2,1)S(1)} %factors.1.after.packed), channel_id=1, source_target_pairs={{4,0},{8,4},{12,8},{5,1},{9,5},{13,9},{6,2},{10,6},{14,10},{7,3},{... | collective-permute-start | bytes 221192 | tf_op jit(solution)/shard_map/ppermute | solution.py:347
  6.3 15.1 %collective-permute-start.3 = (bf16[288,128]{1,0:T(8,128)(2,1)S(1)}, bf16[288,128]{1,0:T(8,128)(2,1)S(1)}, u32[]{:S(2)}, u32[]{:S(2)}) collective-permute-start(bf16[288,128]{1,0:T(8,128)(2,1)S(1)} %factors.1.after.packed), channel_id=1, source_target_pairs={{8,0},{12,4},{9,1},{13,5},{10,2},{14,6},{11,3},{15,7},{24,16},{28,... | collective-permute-start | bytes 221192 | tf_op jit(solution)/shard_map/ppermute | solution.py:347
  7.6 13.8 %collective-permute-start.2 = (bf16[288,128]{1,0:T(8,128)(2,1)S(1)}, bf16[288,128]{1,0:T(8,128)(2,1)S(1)}, u32[]{:S(2)}, u32[]{:S(2)}) collective-permute-start(bf16[288,128]{1,0:T(8,128)(2,1)S(1)} %factors.1.after.packed), channel_id=1, source_target_pairs={{12,0},{0,4},{4,8},{8,12},{13,1},{1,5},{5,9},{9,13},{14,2},{2,6},{... | collective-permute-start | bytes 221192 | tf_op jit(solution)/shard_map/ppermute | solution.py:347
  11.3 10.1 %collective-permute-start.1 = (bf16[288,128]{1,0:T(8,128)(2,1)S(1)}, bf16[288,128]{1,0:T(8,128)(2,1)S(1)}, u32[]{:S(2)}, u32[]{:S(2)}) collective-permute-start(bf16[288,128]{1,0:T(8,128)(2,1)S(1)} %factors.1.after.packed), channel_id=1, source_target_pairs={{0,8},{4,12},{1,9},{5,13},{2,10},{6,14},{3,11},{7,15},{16,24},{20,... | collective-permute-start | bytes 221192 | tf_op jit(solution)/shard_map/ppermute | solution.py:347
  16.7 4.7 %collective-permute-start = (bf16[288,128]{1,0:T(8,128)(2,1)S(1)}, bf16[288,128]{1,0:T(8,128)(2,1)S(1)}, u32[]{:S(2)}, u32[]{:S(2)}) collective-permute-start(bf16[288,128]{1,0:T(8,128)(2,1)S(1)} %factors.1.after.packed), channel_id=1, source_target_pairs={{0,12},{1,13},{2,14},{3,15},{16,28},{17,29},{18,30},{19,31}} | collective-permute-start | bytes 221192 | tf_op jit(solution)/shard_map/ppermute | solution.py:347
  22.7 1.4 %collective-permute-start.6 = (bf16[144,240]{1,0:T(8,128)(2,1)S(1)}, bf16[144,240]{1,0:T(8,128)(2,1)S(1)}, u32[]{:S(2)}, u32[]{:S(2)}) collective-permute-start(bf16[144,240]{1,0:T(8,128)(2,1)S(1)} %get-tuple-element.8), channel_id=1, source_target_pairs={{0,1},{1,0},{2,3},{3,2},{4,5},{5,4},{6,7},{7,6},{8,9},{9,8},{10,11... | collective-permute-start | bytes 207368 | tf_op jit(solution)/shard_map/ppermute | solution.py:331
  23.6 4.1 %collective-permute-start.5 = (bf16[144,240]{1,0:T(8,128)(2,1)S(1)}, bf16[144,240]{1,0:T(8,128)(2,1)S(1)}, u32[]{:S(2)}, u32[]{:S(2)}) collective-permute-start(bf16[144,240]{1,0:T(8,128)(2,1)S(1)} %scores.4), channel_id=1, source_target_pairs={{0,1},{1,0},{2,3},{3,2},{4,5},{5,4},{6,7},{7,6},{8,9},{9,8},{10,11... | collective-permute-start | bytes 207368 | tf_op jit(solution)/shard_map/ppermute | solution.py:331
  24.9 4.5 %collective-permute-start.7 = (bf16[144,240]{1,0:T(8,128)(2,1)S(1)}, bf16[144,240]{1,0:T(8,128)(2,1)S(1)}, u32[]{:S(2)}, u32[]{:S(2)}) collective-permute-start(bf16[144,240]{1,0:T(8,128)(2,1)S(1)} %scores.5), channel_id=1, source_target_pairs={{0,2},{1,3},{2,0},{3,1},{4,6},{5,7},{6,4},{7,5},{8,10},{9,11},{10,... | collective-permute-start | bytes 207368 | tf_op jit(solution)/shard_map/ppermute | solution.py:331

commit v12 on v10

--- a/solution.py
+++ b/solution.py
@@ -295,7 +295,7 @@
     slab, grads, out, shards = refs[n_store:]
     me_store = lax.axis_index("store")
     for at in range(n_store):
-        shards[partner(me_store, at, n_store)] = gathered[at][...]
+        shards[partner(me_store, n_store - 1 - at, n_store)] = gathered[at][...]
     four = 4 * (full_groups * G + H)
     if n_store == 4:
         build_grads(shards, 0, 0, full_groups, grads)
@@ -374,7 +374,7 @@
         in_proj[0],
         out_proj[0],
     )
-    gathered = [packed] + [swap(packed, "store", n_store, k) for k in range(1, n_store)]
+    gathered = [swap(packed, "store", n_store, k) for k in reversed(range(1, n_store))] + [packed]
     slab = fetch(packed, store[0], n_layer)
     grads, partial = grads_and_scores(gathered, slab, n_store, n_layer, n_layer - 1)
     other = swap(partial, "layer", n_layer, 1)
@@ -384,7 +384,9 @@
         if k < n_layer - 2:
             other = swap(scores(grads, slab, n_layer, k + 1), "layer", n_layer, 1)
         crossed.append(swap(scores(grads, slab, n_layer, k, [other]), "layer", n_layer, k))
-    total = scores(grads, slab, n_layer, 0, crossed)
+    total = scores(grads, slab, n_layer, 0)
+    for x in crossed:
+        total = total + x.astype(f32)
     return total.T
 
 

time: 25.8 us -> 25.6 us (level)
  Pallas kernels: 12.5 us -> 11.8 us
  other arithmetic: 0 us -> 0.69 us
    transpose x0 -> x1, other arithmetic: none -> 0.69 us  [on_device(): return total.T]
    pallas_call x3, Pallas kernels: 2.91 us -> 2.24 us  [scores(): pl.pallas_call(functools.partial(scores_kernel, k), out_shape=jax.ShapeDt...]
  transfers between devices with their start and end apart: 6 -> 6, of which waited for: 2 -> 3; matrix products, arithmetic and copies ran while one was open for 0% -> 0% of each run, Pallas kernels for 19% -> 22%
where the time goes in v12:
time: 25.6 us; the launch traced here: 25.4 us
  Pallas kernels  11.8 us (46%)
  starting transfers between devices  7.87 us (31%)
  waiting for transfers between devices  5.01 us (20%)
  other arithmetic  0.69 us (3%)
    ppermute x6, starting transfers between devices, swap(): return lax.ppermute(x, axis, pairs)  7.87 us
    ppermute x6, waiting for transfers between devices, swap(): return lax.ppermute(x, axis, pairs)  5.01 us
    pallas_call x1, Pallas kernels, factors(): pl.pallas_call(functools.partial(factors_kernel, 2), out_shape=jax.ShapeD...  4.96 us
    pallas_call x1, Pallas kernels, fetch(): pl.pallas_call(functools.partial(fetch_kernel, n_layer), out_shape=jax.Sh...  3.34 us
    pallas_call x3, Pallas kernels, scores(): pl.pallas_call(functools.partial(scores_kernel, k), out_shape=jax.ShapeDt...  2.24 us
    pallas_call x1, Pallas kernels, grads_and_scores(): pl.pallas_call(functools.partial(grads_kernel, n_store, queries // n_stor...  1.27 us
    transpose x1, other arithmetic, on_device(): return total.T  0.69 us
  transfers between devices with their start and end apart: 6, of which 3 were waited for; matrix products, arithmetic and copies ran while one was open for 0% of the time, Pallas kernels for 22%

profile of v12, /device:TPU:0, one launch (start us, length us, event | category | flops | bytes accessed | tf_op | source)
XLA Modules:
  0.0 25.4 jit_solution(5558789679826323533)
XLA Ops:
  0.0 5.0 %factors.1.after.refs_3_ = bf16[288,128]{1,0:T(8,128)(2,1)S(1)} custom-call(s32[36]{0:T(128)} %hbm_lengths.1, bf16[288,8192]{1,0:T(8,128)(2,1)} %bitcast.8, bf16[288,1024]{1,0:T(8,128)(2,1)} %bitcast.10, bf16[1,8192]{1,0:T(2,128)(2,1)} %hbm_gain.1, bf16[64,8192]{1,0:T(8,128)(2,1)} %bitcast.9, bf16[64,1024]{1,0:T(8,128)(2,1)} %bitcast.11), custom_call_target="tpu_custom_call" | custom-call | tf_op jit(solution)/shard_map/factors/pallas_call | solution.py:153
  5.0 3.1 %collective-permute-start.2 = (bf16[288,128]{1,0:T(8,128)(2,1)S(1)}, bf16[288,128]{1,0:T(8,128)(2,1)S(1)}, u32[]{:S(2)}, u32[]{:S(2)}) collective-permute-start(bf16[288,128]{1,0:T(8,128)(2,1)S(1)} %factors.1.after.refs_3_), channel_id=1, source_target_pairs={{0,4},{4,0},{8,12},{12,8},{1,5},{5,1},{9,13},{13,9},{2,6},{6,2},{1... | collective-permute-start | bytes 221192 | tf_op jit(solution)/shard_map/ppermute | solution.py:326
  8.1 2.6 %collective-permute-start.1 = (bf16[288,128]{1,0:T(8,128)(2,1)S(1)}, bf16[288,128]{1,0:T(8,128)(2,1)S(1)}, u32[]{:S(2)}, u32[]{:S(2)}) collective-permute-start(bf16[288,128]{1,0:T(8,128)(2,1)S(1)} %factors.1.after.refs_3_), channel_id=1, source_target_pairs={{0,8},{4,12},{8,0},{12,4},{1,9},{5,13},{9,1},{13,5},{2,10},{6,14},... | collective-permute-start | bytes 221192 | tf_op jit(solution)/shard_map/ppermute | solution.py:326
  10.6 0.0 collective-permute-start
  10.7 3.3 %fetch.1.refs_4_.slab = bf16[960,4096]{1,0:T(8,128)(2,1)S(1)} custom-call(bf16[288,128]{1,0:T(8,128)(2,1)S(1)} %factors.1.after.refs_3_, bf16[960,4096]{1,0:T(8,128)(2,1)} %bitcast.7), custom_call_target="tpu_custom_call" | custom-call | bytes 7864320 | tf_op jit(solution)/shard_map/fetch/pallas_call | solution.py:191
  14.0 0.0 collective-permute-done.2.refs_2_
  14.0 1.8 %collective-permute-done.1.refs_1_ = bf16[288,128]{1,0:T(8,128)(2,1)S(1)} collective-permute-done((bf16[288,128]{1,0:T(8,128)(2,1)S(1)}, bf16[288,128]{1,0:T(8,128)(2,1)S(1)}, u32[]{:S(2)}, u32[]{:S(2)}) %collective-permute-start.1) | collective-permute-done | bytes 73760 | tf_op jit(solution)/shard_map/ppermute | solution.py:326
  15.8 1.1 %collective-permute-done.refs_0_ = bf16[288,128]{1,0:T(8,128)(2,1)S(1)} collective-permute-done((bf16[288,128]{1,0:T(8,128)(2,1)S(1)}, bf16[288,128]{1,0:T(8,128)(2,1)S(1)}, u32[]{:S(2)}, u32[]{:S(2)}) %collective-permute-start) | collective-permute-done | bytes 73760 | tf_op jit(solution)/shard_map/ppermute | solution.py:326
  16.9 1.3 %grads.1 = (bf16[144,4096]{1,0:T(8,128)(2,1)S(1)}, bf16[144,240]{1,0:T(8,128)(2,1)S(1)}) custom-call(bf16[288,128]{1,0:T(8,128)(2,1)S(1)} %collective-permute-done.refs_0_, bf16[288,128]{1,0:T(8,128)(2,1)S(1)} %collective-permute-done.1.refs_1_, bf16[288,128]{1,0:T(8,128)(2,1)S(1)} %collective-permute-done.2.refs_2_, ...), custom_call_target="tpu_custom_call" | custom-call | tf_op jit(solution)/shard_map/grads/pallas_call | solution.py:333
  18.2 0.1 collective-permute-start.4
  18.3 0.7 %scores.4 = bf16[144,240]{1,0:T(8,128)(2,1)S(1)} custom-call(bf16[144,4096]{1,0:T(8,128)(2,1)S(1)} %get-tuple-element.7.grads, bf16[960,4096]{1,0:T(8,128)(2,1)S(1)} %fetch.1.refs_4_.slab), custom_call_target="tpu_custom_call" | custom-call | flops 283115520 | bytes 3145728 | tf_op jit(solution)/shard_map/scores/pallas_call | solution.py:352
  19.0 0.6 %collective-permute-start.3 = (bf16[144,240]{1,0:T(8,128)(2,1)S(1)}, bf16[144,240]{1,0:T(8,128)(2,1)S(1)}, u32[]{:S(2)}, u32[]{:S(2)}) collective-permute-start(bf16[144,240]{1,0:T(8,128)(2,1)S(1)} %scores.4), channel_id=1, source_target_pairs={{0,1},{1,0},{2,3},{3,2},{4,5},{5,4},{6,7},{7,6},{8,9},{9,8},{10,11... | collective-permute-start | bytes 207368 | tf_op jit(solution)/shard_map/ppermute | solution.py:326
  19.6 0.0 collective-permute-done.4.refs_0_
  19.6 0.7 %scores.5 = bf16[144,240]{1,0:T(8,128)(2,1)S(1)} custom-call(bf16[144,4096]{1,0:T(8,128)(2,1)S(1)} %get-tuple-element.7.grads, bf16[960,4096]{1,0:T(8,128)(2,1)S(1)} %fetch.1.refs_4_.slab, bf16[144,240]{1,0:T(8,128)(2,1)S(1)} %collective-permute-done.4.refs_0_), custom_call_target="tpu_custom_call" | custom-call | flops 283115520 | bytes 3145728 | tf_op jit(solution)/shard_map/scores/pallas_call | solution.py:352
  20.3 1.6 %collective-permute-start.5 = (bf16[144,240]{1,0:T(8,128)(2,1)S(1)}, bf16[144,240]{1,0:T(8,128)(2,1)S(1)}, u32[]{:S(2)}, u32[]{:S(2)}) collective-permute-start(bf16[144,240]{1,0:T(8,128)(2,1)S(1)} %scores.5), channel_id=1, source_target_pairs={{0,2},{1,3},{2,0},{3,1},{4,6},{5,7},{6,4},{7,5},{8,10},{9,11},{10,... | collective-permute-start | bytes 207368 | tf_op jit(solution)/shard_map/ppermute | solution.py:326
  21.9 0.7 %scores.3 = f32[144,240]{1,0:T(8,128)S(1)} custom-call(bf16[144,4096]{1,0:T(8,128)(2,1)S(1)} %get-tuple-element.7.grads, bf16[960,4096]{1,0:T(8,128)(2,1)S(1)} %fetch.1.refs_4_.slab), custom_call_target="tpu_custom_call" | custom-call | flops 283115520 | bytes 3145728 | tf_op jit(solution)/shard_map/scores/pallas_call | solution.py:352
  22.6 0.0 collective-permute-done.3
  22.6 2.1 %collective-permute-done.5 = bf16[144,240]{1,0:T(8,128)(2,1)S(1)} collective-permute-done((bf16[144,240]{1,0:T(8,128)(2,1)S(1)}, bf16[144,240]{1,0:T(8,128)(2,1)S(1)}, u32[]{:S(2)}, u32[]{:S(2)}) %collective-permute-start.5) | collective-permute-done | bytes 69152 | tf_op jit(solution)/shard_map/ppermute | solution.py:326
  24.8 0.7 %add_bitcast_fusion = f32[240,144]{0,1:T(8,128)} fusion(bf16[144,240]{1,0:T(8,128)(2,1)S(1)} %collective-permute-done.5, f32[144,240]{1,0:T(8,128)S(1)} %scores.3, bf16[144,240]{1,0:T(8,128)(2,1)S(1)} %collective-permute-done.3), kind=kLoop, calls=%fused_computation | loop fusion | flops 138240 | bytes 414720 | tf_op jit(solution)/shard_map/transpose | solution.py:390
Async XLA Ops:
  5.0 9.0 %collective-permute-start.2 = (bf16[288,128]{1,0:T(8,128)(2,1)S(1)}, bf16[288,128]{1,0:T(8,128)(2,1)S(1)}, u32[]{:S(2)}, u32[]{:S(2)}) collective-permute-start(bf16[288,128]{1,0:T(8,128)(2,1)S(1)} %factors.1.after.refs_3_), channel_id=1, source_target_pairs={{0,4},{4,0},{8,12},{12,8},{1,5},{5,1},{9,13},{13,9},{2,6},{6,2},{1... | collective-permute-start | bytes 221192 | tf_op jit(solution)/shard_map/ppermute | solution.py:326
  8.1 7.8 %collective-permute-start.1 = (bf16[288,128]{1,0:T(8,128)(2,1)S(1)}, bf16[288,128]{1,0:T(8,128)(2,1)S(1)}, u32[]{:S(2)}, u32[]{:S(2)}) collective-permute-start(bf16[288,128]{1,0:T(8,128)(2,1)S(1)} %factors.1.after.refs_3_), channel_id=1, source_target_pairs={{0,8},{4,12},{8,0},{12,4},{1,9},{5,13},{9,1},{13,5},{2,10},{6,14},... | collective-permute-start | bytes 221192 | tf_op jit(solution)/shard_map/ppermute | solution.py:326
  10.6 6.3 %collective-permute-start = (bf16[288,128]{1,0:T(8,128)(2,1)S(1)}, bf16[288,128]{1,0:T(8,128)(2,1)S(1)}, u32[]{:S(2)}, u32[]{:S(2)}) collective-permute-start(bf16[288,128]{1,0:T(8,128)(2,1)S(1)} %factors.1.after.refs_3_), channel_id=1, source_target_pairs={{0,12},{4,8},{8,4},{12,0},{1,13},{5,9},{9,5},{13,1},{2,14},{6,10},... | collective-permute-start | bytes 221192 | tf_op jit(solution)/shard_map/ppermute | solution.py:326
  18.2 1.4 %collective-permute-start.4 = (bf16[144,240]{1,0:T(8,128)(2,1)S(1)}, bf16[144,240]{1,0:T(8,128)(2,1)S(1)}, u32[]{:S(2)}, u32[]{:S(2)}) collective-permute-start(bf16[144,240]{1,0:T(8,128)(2,1)S(1)} %get-tuple-element.8), channel_id=1, source_target_pairs={{0,1},{1,0},{2,3},{3,2},{4,5},{5,4},{6,7},{7,6},{8,9},{9,8},{10,11... | collective-permute-start | bytes 207368 | tf_op jit(solution)/shard_map/ppermute | solution.py:326
  19.0 3.6 %collective-permute-start.3 = (bf16[144,240]{1,0:T(8,128)(2,1)S(1)}, bf16[144,240]{1,0:T(8,128)(2,1)S(1)}, u32[]{:S(2)}, u32[]{:S(2)}) collective-permute-start(bf16[144,240]{1,0:T(8,128)(2,1)S(1)} %scores.4), channel_id=1, source_target_pairs={{0,1},{1,0},{2,3},{3,2},{4,5},{5,4},{6,7},{7,6},{8,9},{9,8},{10,11... | collective-permute-start | bytes 207368 | tf_op jit(solution)/shard_map/ppermute | solution.py:326
  20.3 4.4 %collective-permute-start.5 = (bf16[144,240]{1,0:T(8,128)(2,1)S(1)}, bf16[144,240]{1,0:T(8,128)(2,1)S(1)}, u32[]{:S(2)}, u32[]{:S(2)}) collective-permute-start(bf16[144,240]{1,0:T(8,128)(2,1)S(1)} %scores.5), channel_id=1, source_target_pairs={{0,2},{1,3},{2,0},{3,1},{4,6},{5,7},{6,4},{7,5},{8,10},{9,11},{10,... | collective-permute-start | bytes 207368 | tf_op jit(solution)/shard_map/ppermute | solution.py:326

commit v13 on v12

--- a/solution.py
+++ b/solution.py
@@ -290,12 +290,16 @@
             ).astype(bf16)
 
 
+def store_order(n):
+    return [1, 3, 2] if n == 4 else list(range(1, n))
+
+
 def grads_kernel(n_store, full_groups, k, *refs):
     gathered = refs[:n_store]
     slab, grads, out, shards = refs[n_store:]
     me_store = lax.axis_index("store")
-    for at in range(n_store):
-        shards[partner(me_store, n_store - 1 - at, n_store)] = gathered[at][...]
+    for block, away in zip(gathered, [0] + store_order(n_store)):
+        shards[partner(me_store, away, n_store)] = block[...]
     four = 4 * (full_groups * G + H)
     if n_store == 4:
         build_grads(shards, 0, 0, full_groups, grads)
@@ -374,7 +378,7 @@
         in_proj[0],
         out_proj[0],
     )
-    gathered = [swap(packed, "store", n_store, k) for k in reversed(range(1, n_store))] + [packed]
+    gathered = [packed] + [swap(packed, "store", n_store, k) for k in store_order(n_store)]
     slab = fetch(packed, store[0], n_layer)
     grads, partial = grads_and_scores(gathered, slab, n_store, n_layer, n_layer - 1)
     other = swap(partial, "layer", n_layer, 1)

time: 25.6 us -> 24.4 us (0.953)
  waiting for transfers between devices: 5.01 us -> 3.61 us
    ppermute x6, waiting for transfers between devices: 5.01 us -> 3.61 us  [swap(): return lax.ppermute(x, axis, pairs)]
  transfers between devices with their start and end apart: 6 -> 6, of which waited for: 3 -> 3; matrix products, arithmetic and copies ran while one was open for 0% -> 0% of each run, Pallas kernels for 22% -> 23%
where the time goes in v13:
time: 24.4 us; the launch traced here: 24.3 us
  Pallas kernels  11.8 us (48%)
  starting transfers between devices  8.08 us (33%)
  waiting for transfers between devices  3.61 us (15%)
  other arithmetic  0.69 us (3%)
    ppermute x6, starting transfers between devices, swap(): return lax.ppermute(x, axis, pairs)  8.08 us
    pallas_call x1, Pallas kernels, factors(): pl.pallas_call(functools.partial(factors_kernel, 2), out_shape=jax.ShapeD...  4.96 us
    ppermute x6, waiting for transfers between devices, swap(): return lax.ppermute(x, axis, pairs)  3.61 us
    pallas_call x1, Pallas kernels, fetch(): pl.pallas_call(functools.partial(fetch_kernel, n_layer), out_shape=jax.Sh...  3.34 us
    pallas_call x3, Pallas kernels, scores(): pl.pallas_call(functools.partial(scores_kernel, k), out_shape=jax.ShapeDt...  2.24 us
    pallas_call x1, Pallas kernels, grads_and_scores(): pl.pallas_call(functools.partial(grads_kernel, n_store, queries // n_stor...  1.28 us
    transpose x1, other arithmetic, on_device(): return total.T  0.69 us
  transfers between devices with their start and end apart: 6, of which 3 were waited for; matrix products, arithmetic and copies ran while one was open for 0% of the time, Pallas kernels for 23%

profile of v13, /device:TPU:0, one launch (start us, length us, event | category | flops | bytes accessed | tf_op | source)
XLA Modules:
  0.0 24.3 jit_solution(7985702439297833845)
XLA Ops:
  0.0 5.0 %factors.1.after.refs_0_ = bf16[288,128]{1,0:T(8,128)(2,1)S(1)} custom-call(s32[36]{0:T(128)} %hbm_lengths.1, bf16[288,8192]{1,0:T(8,128)(2,1)} %bitcast.8, bf16[288,1024]{1,0:T(8,128)(2,1)} %bitcast.10, bf16[1,8192]{1,0:T(2,128)(2,1)} %hbm_gain.1, bf16[64,8192]{1,0:T(8,128)(2,1)} %bitcast.9, bf16[64,1024]{1,0:T(8,128)(2,1)} %bitcast.11), custom_call_target="tpu_custom_call" | custom-call | tf_op jit(solution)/shard_map/factors/pallas_call | solution.py:153
  5.0 4.1 %collective-permute-start.2 = (bf16[288,128]{1,0:T(8,128)(2,1)S(1)}, bf16[288,128]{1,0:T(8,128)(2,1)S(1)}, u32[]{:S(2)}, u32[]{:S(2)}) collective-permute-start(bf16[288,128]{1,0:T(8,128)(2,1)S(1)} %factors.1.after.refs_0_), channel_id=1, source_target_pairs={{0,8},{4,12},{8,0},{12,4},{1,9},{5,13},{9,1},{13,5},{2,10},{6,14},... | collective-permute-start | bytes 221192 | tf_op jit(solution)/shard_map/ppermute | solution.py:330
  9.1 1.3 %collective-permute-start.1 = (bf16[288,128]{1,0:T(8,128)(2,1)S(1)}, bf16[288,128]{1,0:T(8,128)(2,1)S(1)}, u32[]{:S(2)}, u32[]{:S(2)}) collective-permute-start(bf16[288,128]{1,0:T(8,128)(2,1)S(1)} %factors.1.after.refs_0_), channel_id=1, source_target_pairs={{0,12},{4,8},{8,4},{12,0},{1,13},{5,9},{9,5},{13,1},{2,14},{6,10},... | collective-permute-start | bytes 221192 | tf_op jit(solution)/shard_map/ppermute | solution.py:330
  10.4 0.2 collective-permute-start
  10.7 3.3 %fetch.1.refs_4_.slab = bf16[960,4096]{1,0:T(8,128)(2,1)S(1)} custom-call(bf16[288,128]{1,0:T(8,128)(2,1)S(1)} %factors.1.after.refs_0_, bf16[960,4096]{1,0:T(8,128)(2,1)} %bitcast.7), custom_call_target="tpu_custom_call" | custom-call | bytes 7864320 | tf_op jit(solution)/shard_map/fetch/pallas_call | solution.py:191
  14.0 0.0 collective-permute-done.2.refs_3_
  14.0 1.5 %collective-permute-done.1.refs_2_ = bf16[288,128]{1,0:T(8,128)(2,1)S(1)} collective-permute-done((bf16[288,128]{1,0:T(8,128)(2,1)S(1)}, bf16[288,128]{1,0:T(8,128)(2,1)S(1)}, u32[]{:S(2)}, u32[]{:S(2)}) %collective-permute-start.1) | collective-permute-done | bytes 73760 | tf_op jit(solution)/shard_map/ppermute | solution.py:330
  15.5 0.2 collective-permute-done.refs_1_
  15.7 1.3 %grads.1 = (bf16[144,4096]{1,0:T(8,128)(2,1)S(1)}, bf16[144,240]{1,0:T(8,128)(2,1)S(1)}) custom-call(bf16[288,128]{1,0:T(8,128)(2,1)S(1)} %factors.1.after.refs_0_, bf16[288,128]{1,0:T(8,128)(2,1)S(1)} %collective-permute-done.refs_1_, bf16[288,128]{1,0:T(8,128)(2,1)S(1)} %collective-permute-done.1.refs_2_, ...), custom_call_target="tpu_custom_call" | custom-call | tf_op jit(solution)/shard_map/grads/pallas_call | solution.py:337
  17.0 0.1 collective-permute-start.4
  17.1 0.7 %scores.4 = bf16[144,240]{1,0:T(8,128)(2,1)S(1)} custom-call(bf16[144,4096]{1,0:T(8,128)(2,1)S(1)} %get-tuple-element.7.grads, bf16[960,4096]{1,0:T(8,128)(2,1)S(1)} %fetch.1.refs_4_.slab), custom_call_target="tpu_custom_call" | custom-call | flops 283115520 | bytes 3145728 | tf_op jit(solution)/shard_map/scores/pallas_call | solution.py:356
  17.8 0.6 %collective-permute-start.3 = (bf16[144,240]{1,0:T(8,128)(2,1)S(1)}, bf16[144,240]{1,0:T(8,128)(2,1)S(1)}, u32[]{:S(2)}, u32[]{:S(2)}) collective-permute-start(bf16[144,240]{1,0:T(8,128)(2,1)S(1)} %scores.4), channel_id=1, source_target_pairs={{0,1},{1,0},{2,3},{3,2},{4,5},{5,4},{6,7},{7,6},{8,9},{9,8},{10,11... | collective-permute-start | bytes 207368 | tf_op jit(solution)/shard_map/ppermute | solution.py:330
  18.4 0.0 collective-permute-done.4.refs_0_
  18.4 0.7 %scores.5 = bf16[144,240]{1,0:T(8,128)(2,1)S(1)} custom-call(bf16[144,4096]{1,0:T(8,128)(2,1)S(1)} %get-tuple-element.7.grads, bf16[960,4096]{1,0:T(8,128)(2,1)S(1)} %fetch.1.refs_4_.slab, bf16[144,240]{1,0:T(8,128)(2,1)S(1)} %collective-permute-done.4.refs_0_), custom_call_target="tpu_custom_call" | custom-call | flops 283115520 | bytes 3145728 | tf_op jit(solution)/shard_map/scores/pallas_call | solution.py:356
  19.1 1.8 %collective-permute-start.5 = (bf16[144,240]{1,0:T(8,128)(2,1)S(1)}, bf16[144,240]{1,0:T(8,128)(2,1)S(1)}, u32[]{:S(2)}, u32[]{:S(2)}) collective-permute-start(bf16[144,240]{1,0:T(8,128)(2,1)S(1)} %scores.5), channel_id=1, source_target_pairs={{0,2},{1,3},{2,0},{3,1},{4,6},{5,7},{6,4},{7,5},{8,10},{9,11},{10,... | collective-permute-start | bytes 207368 | tf_op jit(solution)/shard_map/ppermute | solution.py:330
  20.9 0.7 %scores.3 = f32[144,240]{1,0:T(8,128)S(1)} custom-call(bf16[144,4096]{1,0:T(8,128)(2,1)S(1)} %get-tuple-element.7.grads, bf16[960,4096]{1,0:T(8,128)(2,1)S(1)} %fetch.1.refs_4_.slab), custom_call_target="tpu_custom_call" | custom-call | flops 283115520 | bytes 3145728 | tf_op jit(solution)/shard_map/scores/pallas_call | solution.py:356
  21.6 0.0 collective-permute-done.3
  21.7 1.9 %collective-permute-done.5 = bf16[144,240]{1,0:T(8,128)(2,1)S(1)} collective-permute-done((bf16[144,240]{1,0:T(8,128)(2,1)S(1)}, bf16[144,240]{1,0:T(8,128)(2,1)S(1)}, u32[]{:S(2)}, u32[]{:S(2)}) %collective-permute-start.5) | collective-permute-done | bytes 69152 | tf_op jit(solution)/shard_map/ppermute | solution.py:330
  23.6 0.7 %add_bitcast_fusion = f32[240,144]{0,1:T(8,128)} fusion(bf16[144,240]{1,0:T(8,128)(2,1)S(1)} %collective-permute-done.5, f32[144,240]{1,0:T(8,128)S(1)} %scores.3, bf16[144,240]{1,0:T(8,128)(2,1)S(1)} %collective-permute-done.3), kind=kLoop, calls=%fused_computation | loop fusion | flops 138240 | bytes 414720 | tf_op jit(solution)/shard_map/transpose | solution.py:394
Async XLA Ops:
  5.0 9.0 %collective-permute-start.2 = (bf16[288,128]{1,0:T(8,128)(2,1)S(1)}, bf16[288,128]{1,0:T(8,128)(2,1)S(1)}, u32[]{:S(2)}, u32[]{:S(2)}) collective-permute-start(bf16[288,128]{1,0:T(8,128)(2,1)S(1)} %factors.1.after.refs_0_), channel_id=1, source_target_pairs={{0,8},{4,12},{8,0},{12,4},{1,9},{5,13},{9,1},{13,5},{2,10},{6,14},... | collective-permute-start | bytes 221192 | tf_op jit(solution)/shard_map/ppermute | solution.py:330
  9.1 6.5 %collective-permute-start.1 = (bf16[288,128]{1,0:T(8,128)(2,1)S(1)}, bf16[288,128]{1,0:T(8,128)(2,1)S(1)}, u32[]{:S(2)}, u32[]{:S(2)}) collective-permute-start(bf16[288,128]{1,0:T(8,128)(2,1)S(1)} %factors.1.after.refs_0_), channel_id=1, source_target_pairs={{0,12},{4,8},{8,4},{12,0},{1,13},{5,9},{9,5},{13,1},{2,14},{6,10},... | collective-permute-start | bytes 221192 | tf_op jit(solution)/shard_map/ppermute | solution.py:330
  10.4 5.3 %collective-permute-start = (bf16[288,128]{1,0:T(8,128)(2,1)S(1)}, bf16[288,128]{1,0:T(8,128)(2,1)S(1)}, u32[]{:S(2)}, u32[]{:S(2)}) collective-permute-start(bf16[288,128]{1,0:T(8,128)(2,1)S(1)} %factors.1.after.refs_0_), channel_id=1, source_target_pairs={{0,4},{4,0},{8,12},{12,8},{1,5},{5,1},{9,13},{13,9},{2,6},{6,2},{1... | collective-permute-start | bytes 221192 | tf_op jit(solution)/shard_map/ppermute | solution.py:330
  17.0 1.4 %collective-permute-start.4 = (bf16[144,240]{1,0:T(8,128)(2,1)S(1)}, bf16[144,240]{1,0:T(8,128)(2,1)S(1)}, u32[]{:S(2)}, u32[]{:S(2)}) collective-permute-start(bf16[144,240]{1,0:T(8,128)(2,1)S(1)} %get-tuple-element.8), channel_id=1, source_target_pairs={{0,1},{1,0},{2,3},{3,2},{4,5},{5,4},{6,7},{7,6},{8,9},{9,8},{10,11... | collective-permute-start | bytes 207368 | tf_op jit(solution)/shard_map/ppermute | solution.py:330
  17.8 3.8 %collective-permute-start.3 = (bf16[144,240]{1,0:T(8,128)(2,1)S(1)}, bf16[144,240]{1,0:T(8,128)(2,1)S(1)}, u32[]{:S(2)}, u32[]{:S(2)}) collective-permute-start(bf16[144,240]{1,0:T(8,128)(2,1)S(1)} %scores.4), channel_id=1, source_target_pairs={{0,1},{1,0},{2,3},{3,2},{4,5},{5,4},{6,7},{7,6},{8,9},{9,8},{10,11... | collective-permute-start | bytes 207368 | tf_op jit(solution)/shard_map/ppermute | solution.py:330
  19.1 4.4 %collective-permute-start.5 = (bf16[144,240]{1,0:T(8,128)(2,1)S(1)}, bf16[144,240]{1,0:T(8,128)(2,1)S(1)}, u32[]{:S(2)}, u32[]{:S(2)}) collective-permute-start(bf16[144,240]{1,0:T(8,128)(2,1)S(1)} %scores.5), channel_id=1, source_target_pairs={{0,2},{1,3},{2,0},{3,1},{4,6},{5,7},{6,4},{7,5},{8,10},{9,11},{10,... | collective-permute-start | bytes 207368 | tf_op jit(solution)/shard_map/ppermute | solution.py:330

commit v14 on v13

--- a/solution.py
+++ b/solution.py
@@ -28,7 +28,7 @@
 
 
 def factors_kernel(
-    window,
+    cuts,
     hbm_lengths,
     hbm_hidden,
     hbm_cot,
@@ -47,55 +47,57 @@
     out_t,
     sems,
 ):
-    chunks, rows, columns = hidden.shape
+    rows, width = hidden.shape
     queries = lengths.shape[0]
     full = queries // G * G * S
     half = rows - full
     mid, low = full // 2, half // 2
+    chunks = len(cuts) - 1
 
     def copy(source, target, at):
         return pltpu.make_async_copy(source, target, sems.at[at])
 
-    def chunk(c):
-        cut = pl.ds(pl.multiple_of(c * columns, columns), columns)
-        return [
-            copy(hbm_gain.at[:, cut], gain.at[c], 3 + c),
-            copy(hbm_inp.at[:, cut], inp.at[c], 3 + chunks + c),
-            copy(hbm_hidden.at[:, cut], hidden.at[c], 3 + 2 * chunks + c),
-        ]
-
-    def start_chunk(c):
-        for piece in chunk(c):
+    copy_gain = copy(hbm_gain, gain, 0)
+    early = [copy(hbm_outp, outp, 1), copy(hbm_cot, cot, 2), copy(hbm_lengths, lengths, 3)]
+    pieces = []
+    for c in range(chunks):
+        cut = pl.ds(cuts[c], cuts[c + 1] - cuts[c])
+        pieces.append(
+            [
+                copy(hbm_inp.at[:, cut], inp.at[:, cut], 4 + 2 * c),
+                copy(hbm_hidden.at[:, cut], hidden.at[:, cut], 5 + 2 * c),
+            ]
+        )
+
+    def start(group):
+        for piece in group:
             piece.start()
 
-    early = [copy(hbm_outp, outp, 0), copy(hbm_cot, cot, 1), copy(hbm_lengths, lengths, 2)]
-    for c in range(window):
-        start_chunk(c)
-    for piece in early:
-        piece.start()
-    in_acc[...] = jnp.zeros_like(in_acc)
-    sq_acc[...] = jnp.zeros_like(sq_acc)
-
-    @pl.loop(0, chunks)
-    def _(c):
-        for piece in chunk(c):
+    copy_gain.start()
+    for c in range(3):
+        start(pieces[c])
+    copy_gain.wait()
+    start(pieces[3])
+    for c in range(chunks):
+        for piece in pieces[c]:
             piece.wait()
-
-        @pl.when(c + window < chunks)
-        def _():
-            start_chunk(c + window)
-
-        scaled = inp[c].astype(f32) * gain[c].astype(f32)
+        if c + 4 < chunks:
+            start(pieces[c + 4])
+        if c + 4 == chunks:
+            start(early)
+        cut = slice(cuts[c], cuts[c + 1])
+        scaled = inp[:, cut].astype(f32) * gain[:, cut].astype(f32)
         high = scaled.astype(bf16)
         rest = (scaled - high.astype(f32)).astype(bf16)
-        in_acc[...] += dot_nt(hidden[c], jnp.concatenate([high, high, rest, rest], axis=0))
+        product = dot_nt(hidden[:, cut], jnp.concatenate([high, rest], axis=0))
+        in_acc[...] = product if c == 0 else in_acc[...] + product
         for r in range(0, rows, 48):
-            wide = hidden[c, r : r + 48, :].astype(f32)
+            wide = hidden[r : r + 48, cut].astype(f32)
             square = wide * wide
             total = square[:, :LANES]
-            for at in range(LANES, columns, LANES):
+            for at in range(LANES, cuts[c + 1] - cuts[c], LANES):
                 total += square[:, at : at + LANES]
-            sq_acc[r : r + 48, :] += total
+            sq_acc[r : r + 48, :] = total if c == 0 else sq_acc[r : r + 48, :] + total
 
     for piece in early:
         piece.wait()
@@ -108,8 +110,8 @@
     def in_rows(at, count):
         sums = in_acc[pl.ds(at, count), :]
         square = jnp.sum(sq_acc[pl.ds(at, count), :], axis=1, keepdims=True)
-        scale = lax.rsqrt(square * (1.0 / (chunks * columns)) + norm_epsilon)
-        factor = (sums[:, :LANES] + sums[:, LANES:]) * scale
+        scale = lax.rsqrt(square * (1.0 / width) + norm_epsilon)
+        factor = (sums + pltpu.roll(sums, R, 1)) * scale
         return [
             jnp.where(position < lengths[at // S + q], factor[q * S : (q + 1) * S], 0.0)
             for q in range(count // S)
@@ -148,24 +150,23 @@
 
 def factors(lengths, hidden, cotangent, gain, in_projection, out_projection):
     rows, width = hidden.shape
-    columns = 2048
-    chunks = width // columns
+    cuts = [width * part // 16 for part in (0, 1, 2, 4, 8, 12, 16)]
     return pl.pallas_call(
-        functools.partial(factors_kernel, 2),
+        functools.partial(factors_kernel, cuts),
         out_shape=jax.ShapeDtypeStruct((rows, 2 * R), bf16),
         in_specs=[pl.BlockSpec(memory_space=pl.ANY)] * 6,
         out_specs=pl.BlockSpec(memory_space=pltpu.VMEM),
         scratch_shapes=[
             pltpu.SMEM(lengths.shape, jnp.int32),
-            pltpu.VMEM((chunks, rows, columns), bf16),
+            pltpu.VMEM(hidden.shape, bf16),
             pltpu.VMEM(cotangent.shape, bf16),
-            pltpu.VMEM((chunks, 1, columns), bf16),
-            pltpu.VMEM((chunks, R, columns), bf16),
+            pltpu.VMEM(gain.shape, bf16),
+            pltpu.VMEM(in_projection.shape, bf16),
             pltpu.VMEM(out_projection.shape, bf16),
-            pltpu.VMEM((rows, 4 * R), f32),
+            pltpu.VMEM((rows, 2 * R), f32),
             pltpu.VMEM((rows, LANES), f32),
             pltpu.VMEM((-(-rows // LANES) * R, LANES), f32),
-            pltpu.SemaphoreType.DMA((3 + 3 * chunks,)),
+            pltpu.SemaphoreType.DMA((2 + 2 * len(cuts),)),
         ],
         compiler_params=pltpu.CompilerParams(vmem_limit_bytes=24 * 2**20),
         name="factors",

time: 24.4 us -> 25.2 us (1.033)
  Pallas kernels: 11.8 us -> 12.6 us
    pallas_call x1, Pallas kernels: 4.96 us -> 5.75 us  [factors(): pl.pallas_call(functools.partial(factors_kernel, cuts), out_shape=jax.Sha...]
  transfers between devices with their start and end apart: 6 -> 6, of which waited for: 3 -> 3; matrix products, arithmetic and copies ran while one was open for 0% -> 0% of each run, Pallas kernels for 23% -> 22%
where the time goes in v14:
time: 25.2 us; the launch traced here: 25 us
  Pallas kernels  12.6 us (50%)
  starting transfers between devices  8.08 us (32%)
  waiting for transfers between devices  3.6 us (14%)
  other arithmetic  0.69 us (3%)
    ppermute x6, starting transfers between devices, swap(): return lax.ppermute(x, axis, pairs)  8.08 us
    pallas_call x1, Pallas kernels, factors(): pl.pallas_call(functools.partial(factors_kernel, cuts), out_shape=jax.Sha...  5.75 us
    ppermute x6, waiting for transfers between devices, swap(): return lax.ppermute(x, axis, pairs)  3.6 us
    pallas_call x1, Pallas kernels, fetch(): pl.pallas_call(functools.partial(fetch_kernel, n_layer), out_shape=jax.Sh...  3.34 us
    pallas_call x3, Pallas kernels, scores(): pl.pallas_call(functools.partial(scores_kernel, k), out_shape=jax.ShapeDt...  2.24 us
    pallas_call x1, Pallas kernels, grads_and_scores(): pl.pallas_call(functools.partial(grads_kernel, n_store, queries // n_stor...  1.28 us
    transpose x1, other arithmetic, on_device(): return total.T  0.69 us
  transfers between devices with their start and end apart: 6, of which 3 were waited for; matrix products, arithmetic and copies ran while one was open for 0% of the time, Pallas kernels for 22%

profile of v14, /device:TPU:0, one launch (start us, length us, event | category | flops | bytes accessed | tf_op | source)
XLA Modules:
  0.0 25.0 jit_solution(6330861774193180392)
XLA Ops:
  0.0 5.8 %factors.1.after.refs_0_ = bf16[288,128]{1,0:T(8,128)(2,1)S(1)} custom-call(s32[36]{0:T(128)} %hbm_lengths.1, bf16[288,8192]{1,0:T(8,128)(2,1)} %bitcast.8, bf16[288,1024]{1,0:T(8,128)(2,1)} %bitcast.10, bf16[1,8192]{1,0:T(2,128)(2,1)} %hbm_gain.1, bf16[64,8192]{1,0:T(8,128)(2,1)} %bitcast.9, bf16[64,1024]{1,0:T(8,128)(2,1)} %bitcast.11), custom_call_target="tpu_custom_call" | custom-call | tf_op jit(solution)/shard_map/factors/pallas_call | solution.py:154
  5.8 4.1 %collective-permute-start.2 = (bf16[288,128]{1,0:T(8,128)(2,1)S(1)}, bf16[288,128]{1,0:T(8,128)(2,1)S(1)}, u32[]{:S(2)}, u32[]{:S(2)}) collective-permute-start(bf16[288,128]{1,0:T(8,128)(2,1)S(1)} %factors.1.after.refs_0_), channel_id=1, source_target_pairs={{0,8},{4,12},{8,0},{12,4},{1,9},{5,13},{9,1},{13,5},{2,10},{6,14},... | collective-permute-start | bytes 221192 | tf_op jit(solution)/shard_map/ppermute | solution.py:331
  9.9 1.3 %collective-permute-start.1 = (bf16[288,128]{1,0:T(8,128)(2,1)S(1)}, bf16[288,128]{1,0:T(8,128)(2,1)S(1)}, u32[]{:S(2)}, u32[]{:S(2)}) collective-permute-start(bf16[288,128]{1,0:T(8,128)(2,1)S(1)} %factors.1.after.refs_0_), channel_id=1, source_target_pairs={{0,12},{4,8},{8,4},{12,0},{1,13},{5,9},{9,5},{13,1},{2,14},{6,10},... | collective-permute-start | bytes 221192 | tf_op jit(solution)/shard_map/ppermute | solution.py:331
  11.2 0.2 collective-permute-start
  11.4 3.3 %fetch.1.refs_4_.slab = bf16[960,4096]{1,0:T(8,128)(2,1)S(1)} custom-call(bf16[288,128]{1,0:T(8,128)(2,1)S(1)} %factors.1.after.refs_0_, bf16[960,4096]{1,0:T(8,128)(2,1)} %bitcast.7), custom_call_target="tpu_custom_call" | custom-call | bytes 7864320 | tf_op jit(solution)/shard_map/fetch/pallas_call | solution.py:192
  14.8 0.0 collective-permute-done.2.refs_3_
  14.8 1.5 %collective-permute-done.1.refs_2_ = bf16[288,128]{1,0:T(8,128)(2,1)S(1)} collective-permute-done((bf16[288,128]{1,0:T(8,128)(2,1)S(1)}, bf16[288,128]{1,0:T(8,128)(2,1)S(1)}, u32[]{:S(2)}, u32[]{:S(2)}) %collective-permute-start.1) | collective-permute-done | bytes 73760 | tf_op jit(solution)/shard_map/ppermute | solution.py:331
  16.3 0.2 collective-permute-done.refs_1_
  16.5 1.3 %grads.1 = (bf16[144,4096]{1,0:T(8,128)(2,1)S(1)}, bf16[144,240]{1,0:T(8,128)(2,1)S(1)}) custom-call(bf16[288,128]{1,0:T(8,128)(2,1)S(1)} %factors.1.after.refs_0_, bf16[288,128]{1,0:T(8,128)(2,1)S(1)} %collective-permute-done.refs_1_, bf16[288,128]{1,0:T(8,128)(2,1)S(1)} %collective-permute-done.1.refs_2_, ...), custom_call_target="tpu_custom_call" | custom-call | tf_op jit(solution)/shard_map/grads/pallas_call | solution.py:338
  17.8 0.1 collective-permute-start.4
  17.9 0.7 %scores.4 = bf16[144,240]{1,0:T(8,128)(2,1)S(1)} custom-call(bf16[144,4096]{1,0:T(8,128)(2,1)S(1)} %get-tuple-element.7.grads, bf16[960,4096]{1,0:T(8,128)(2,1)S(1)} %fetch.1.refs_4_.slab), custom_call_target="tpu_custom_call" | custom-call | flops 283115520 | bytes 3145728 | tf_op jit(solution)/shard_map/scores/pallas_call | solution.py:357
  18.6 0.6 %collective-permute-start.3 = (bf16[144,240]{1,0:T(8,128)(2,1)S(1)}, bf16[144,240]{1,0:T(8,128)(2,1)S(1)}, u32[]{:S(2)}, u32[]{:S(2)}) collective-permute-start(bf16[144,240]{1,0:T(8,128)(2,1)S(1)} %scores.4), channel_id=1, source_target_pairs={{0,1},{1,0},{2,3},{3,2},{4,5},{5,4},{6,7},{7,6},{8,9},{9,8},{10,11... | collective-permute-start | bytes 207368 | tf_op jit(solution)/shard_map/ppermute | solution.py:331
  19.2 0.0 collective-permute-done.4.refs_0_
  19.2 0.7 %scores.5 = bf16[144,240]{1,0:T(8,128)(2,1)S(1)} custom-call(bf16[144,4096]{1,0:T(8,128)(2,1)S(1)} %get-tuple-element.7.grads, bf16[960,4096]{1,0:T(8,128)(2,1)S(1)} %fetch.1.refs_4_.slab, bf16[144,240]{1,0:T(8,128)(2,1)S(1)} %collective-permute-done.4.refs_0_), custom_call_target="tpu_custom_call" | custom-call | flops 283115520 | bytes 3145728 | tf_op jit(solution)/shard_map/scores/pallas_call | solution.py:357
  19.9 1.8 %collective-permute-start.5 = (bf16[144,240]{1,0:T(8,128)(2,1)S(1)}, bf16[144,240]{1,0:T(8,128)(2,1)S(1)}, u32[]{:S(2)}, u32[]{:S(2)}) collective-permute-start(bf16[144,240]{1,0:T(8,128)(2,1)S(1)} %scores.5), channel_id=1, source_target_pairs={{0,2},{1,3},{2,0},{3,1},{4,6},{5,7},{6,4},{7,5},{8,10},{9,11},{10,... | collective-permute-start | bytes 207368 | tf_op jit(solution)/shard_map/ppermute | solution.py:331
  21.7 0.7 %scores.3 = f32[144,240]{1,0:T(8,128)S(1)} custom-call(bf16[144,4096]{1,0:T(8,128)(2,1)S(1)} %get-tuple-element.7.grads, bf16[960,4096]{1,0:T(8,128)(2,1)S(1)} %fetch.1.refs_4_.slab), custom_call_target="tpu_custom_call" | custom-call | flops 283115520 | bytes 3145728 | tf_op jit(solution)/shard_map/scores/pallas_call | solution.py:357
  22.4 0.0 collective-permute-done.3
  22.5 1.9 %collective-permute-done.5 = bf16[144,240]{1,0:T(8,128)(2,1)S(1)} collective-permute-done((bf16[144,240]{1,0:T(8,128)(2,1)S(1)}, bf16[144,240]{1,0:T(8,128)(2,1)S(1)}, u32[]{:S(2)}, u32[]{:S(2)}) %collective-permute-start.5) | collective-permute-done | bytes 69152 | tf_op jit(solution)/shard_map/ppermute | solution.py:331
  24.4 0.7 %add_bitcast_fusion = f32[240,144]{0,1:T(8,128)} fusion(bf16[144,240]{1,0:T(8,128)(2,1)S(1)} %collective-permute-done.5, f32[144,240]{1,0:T(8,128)S(1)} %scores.3, bf16[144,240]{1,0:T(8,128)(2,1)S(1)} %collective-permute-done.3), kind=kLoop, calls=%fused_computation | loop fusion | flops 138240 | bytes 414720 | tf_op jit(solution)/shard_map/transpose | solution.py:395
Async XLA Ops:
  5.8 9.0 %collective-permute-start.2 = (bf16[288,128]{1,0:T(8,128)(2,1)S(1)}, bf16[288,128]{1,0:T(8,128)(2,1)S(1)}, u32[]{:S(2)}, u32[]{:S(2)}) collective-permute-start(bf16[288,128]{1,0:T(8,128)(2,1)S(1)} %factors.1.after.refs_0_), channel_id=1, source_target_pairs={{0,8},{4,12},{8,0},{12,4},{1,9},{5,13},{9,1},{13,5},{2,10},{6,14},... | collective-permute-start | bytes 221192 | tf_op jit(solution)/shard_map/ppermute | solution.py:331
  9.9 6.5 %collective-permute-start.1 = (bf16[288,128]{1,0:T(8,128)(2,1)S(1)}, bf16[288,128]{1,0:T(8,128)(2,1)S(1)}, u32[]{:S(2)}, u32[]{:S(2)}) collective-permute-start(bf16[288,128]{1,0:T(8,128)(2,1)S(1)} %factors.1.after.refs_0_), channel_id=1, source_target_pairs={{0,12},{4,8},{8,4},{12,0},{1,13},{5,9},{9,5},{13,1},{2,14},{6,10},... | collective-permute-start | bytes 221192 | tf_op jit(solution)/shard_map/ppermute | solution.py:331
  11.2 5.3 %collective-permute-start = (bf16[288,128]{1,0:T(8,128)(2,1)S(1)}, bf16[288,128]{1,0:T(8,128)(2,1)S(1)}, u32[]{:S(2)}, u32[]{:S(2)}) collective-permute-start(bf16[288,128]{1,0:T(8,128)(2,1)S(1)} %factors.1.after.refs_0_), channel_id=1, source_target_pairs={{0,4},{4,0},{8,12},{12,8},{1,5},{5,1},{9,13},{13,9},{2,6},{6,2},{1... | collective-permute-start | bytes 221192 | tf_op jit(solution)/shard_map/ppermute | solution.py:331
  17.8 1.4 %collective-permute-start.4 = (bf16[144,240]{1,0:T(8,128)(2,1)S(1)}, bf16[144,240]{1,0:T(8,128)(2,1)S(1)}, u32[]{:S(2)}, u32[]{:S(2)}) collective-permute-start(bf16[144,240]{1,0:T(8,128)(2,1)S(1)} %get-tuple-element.8), channel_id=1, source_target_pairs={{0,1},{1,0},{2,3},{3,2},{4,5},{5,4},{6,7},{7,6},{8,9},{9,8},{10,11... | collective-permute-start | bytes 207368 | tf_op jit(solution)/shard_map/ppermute | solution.py:331
  18.6 3.8 %collective-permute-start.3 = (bf16[144,240]{1,0:T(8,128)(2,1)S(1)}, bf16[144,240]{1,0:T(8,128)(2,1)S(1)}, u32[]{:S(2)}, u32[]{:S(2)}) collective-permute-start(bf16[144,240]{1,0:T(8,128)(2,1)S(1)} %scores.4), channel_id=1, source_target_pairs={{0,1},{1,0},{2,3},{3,2},{4,5},{5,4},{6,7},{7,6},{8,9},{9,8},{10,11... | collective-permute-start | bytes 207368 | tf_op jit(solution)/shard_map/ppermute | solution.py:331
  19.9 4.4 %collective-permute-start.5 = (bf16[144,240]{1,0:T(8,128)(2,1)S(1)}, bf16[144,240]{1,0:T(8,128)(2,1)S(1)}, u32[]{:S(2)}, u32[]{:S(2)}) collective-permute-start(bf16[144,240]{1,0:T(8,128)(2,1)S(1)} %scores.5), channel_id=1, source_target_pairs={{0,2},{1,3},{2,0},{3,1},{4,6},{5,7},{6,4},{7,5},{8,10},{9,11},{10,... | collective-permute-start | bytes 207368 | tf_op jit(solution)/shard_map/ppermute | solution.py:331

commit v15 on v13

--- a/solution.py
+++ b/solution.py
@@ -28,7 +28,6 @@
 
 
 def factors_kernel(
-    window,
     hbm_lengths,
     hbm_hidden,
     hbm_cot,
@@ -48,6 +47,7 @@
     sems,
 ):
     chunks, rows, columns = hidden.shape
+    width = chunks * columns
     queries = lengths.shape[0]
     full = queries // G * G * S
     half = rows - full
@@ -56,39 +56,45 @@
     def copy(source, target, at):
         return pltpu.make_async_copy(source, target, sems.at[at])
 
-    def chunk(c):
+    def pieces(c):
         cut = pl.ds(pl.multiple_of(c * columns, columns), columns)
         return [
-            copy(hbm_gain.at[:, cut], gain.at[c], 3 + c),
-            copy(hbm_inp.at[:, cut], inp.at[c], 3 + chunks + c),
-            copy(hbm_hidden.at[:, cut], hidden.at[c], 3 + 2 * chunks + c),
+            copy(hbm_inp.at[:, cut], inp.at[c], 4 + c),
+            copy(hbm_hidden.at[:, cut], hidden.at[c], 4 + chunks + c),
         ]
 
-    def start_chunk(c):
-        for piece in chunk(c):
+    def start(group):
+        for piece in group:
             piece.start()
 
-    early = [copy(hbm_outp, outp, 0), copy(hbm_cot, cot, 1), copy(hbm_lengths, lengths, 2)]
-    for c in range(window):
-        start_chunk(c)
-    for piece in early:
-        piece.start()
+    copy_gain = copy(hbm_gain, gain, 0)
+    early = [copy(hbm_outp, outp, 1), copy(hbm_cot, cot, 2), copy(hbm_lengths, lengths, 3)]
+    copy_gain.start()
+    start(pieces(0))
+    start(pieces(1))
     in_acc[...] = jnp.zeros_like(in_acc)
     sq_acc[...] = jnp.zeros_like(sq_acc)
+    copy_gain.wait()
+    start(pieces(2))
 
     @pl.loop(0, chunks)
     def _(c):
-        for piece in chunk(c):
+        for piece in pieces(c):
             piece.wait()
 
-        @pl.when(c + window < chunks)
+        @pl.when(c + 3 < chunks)
         def _():
-            start_chunk(c + window)
-
-        scaled = inp[c].astype(f32) * gain[c].astype(f32)
+            start(pieces(c + 3))
+
+        @pl.when(c + 3 == chunks)
+        def _():
+            start(early)
+
+        cut = pl.ds(pl.multiple_of(c * columns, columns), columns)
+        scaled = inp[c].astype(f32) * gain[:, cut].astype(f32)
         high = scaled.astype(bf16)
         rest = (scaled - high.astype(f32)).astype(bf16)
-        in_acc[...] += dot_nt(hidden[c], jnp.concatenate([high, high, rest, rest], axis=0))
+        in_acc[...] += dot_nt(hidden[c], jnp.concatenate([high, rest], axis=0))
         for r in range(0, rows, 48):
             wide = hidden[c, r : r + 48, :].astype(f32)
             square = wide * wide
@@ -108,8 +114,8 @@
     def in_rows(at, count):
         sums = in_acc[pl.ds(at, count), :]
         square = jnp.sum(sq_acc[pl.ds(at, count), :], axis=1, keepdims=True)
-        scale = lax.rsqrt(square * (1.0 / (chunks * columns)) + norm_epsilon)
-        factor = (sums[:, :LANES] + sums[:, LANES:]) * scale
+        scale = lax.rsqrt(square * (1.0 / width) + norm_epsilon)
+        factor = (sums + pltpu.roll(sums, R, 1)) * scale
         return [
             jnp.where(position < lengths[at // S + q], factor[q * S : (q + 1) * S], 0.0)
             for q in range(count // S)
@@ -148,10 +154,10 @@
 
 def factors(lengths, hidden, cotangent, gain, in_projection, out_projection):
     rows, width = hidden.shape
-    columns = 2048
+    columns = 1024
     chunks = width // columns
     return pl.pallas_call(
-        functools.partial(factors_kernel, 2),
+        factors_kernel,
         out_shape=jax.ShapeDtypeStruct((rows, 2 * R), bf16),
         in_specs=[pl.BlockSpec(memory_space=pl.ANY)] * 6,
         out_specs=pl.BlockSpec(memory_space=pltpu.VMEM),
@@ -159,13 +165,13 @@
             pltpu.SMEM(lengths.shape, jnp.int32),
             pltpu.VMEM((chunks, rows, columns), bf16),
             pltpu.VMEM(cotangent.shape, bf16),
-            pltpu.VMEM((chunks, 1, columns), bf16),
+            pltpu.VMEM(gain.shape, bf16),
             pltpu.VMEM((chunks, R, columns), bf16),
             pltpu.VMEM(out_projection.shape, bf16),
-            pltpu.VMEM((rows, 4 * R), f32),
+            pltpu.VMEM((rows, 2 * R), f32),
             pltpu.VMEM((rows, LANES), f32),
             pltpu.VMEM((-(-rows // LANES) * R, LANES), f32),
-            pltpu.SemaphoreType.DMA((3 + 3 * chunks,)),
+            pltpu.SemaphoreType.DMA((4 + 2 * chunks,)),
         ],
         compiler_params=pltpu.CompilerParams(vmem_limit_bytes=24 * 2**20),
         name="factors",

time: 24.4 us -> 24.8 us (1.016)
  Pallas kernels: 11.8 us -> 12.2 us
    pallas_call x1, Pallas kernels: 4.96 us -> 5.32 us  [factors(): pl.pallas_call(factors_kernel, out_shape=jax.ShapeDtypeStruct((rows, 2 *...]
where the time goes in v15:
time: 24.8 us; the launch traced here: 24.6 us
  Pallas kernels  12.2 us (49%)
  starting transfers between devices  8.06 us (32%)
  waiting for transfers between devices  3.62 us (15%)
  other arithmetic  0.69 us (3%)
    ppermute x6, starting transfers between devices, swap(): return lax.ppermute(x, axis, pairs)  8.06 us
    pallas_call x1, Pallas kernels, factors(): pl.pallas_call(factors_kernel, out_shape=jax.ShapeDtypeStruct((rows, 2 *...  5.32 us
    ppermute x6, waiting for transfers between devices, swap(): return lax.ppermute(x, axis, pairs)  3.62 us
    pallas_call x1, Pallas kernels, fetch(): pl.pallas_call(functools.partial(fetch_kernel, n_layer), out_shape=jax.Sh...  3.34 us
    pallas_call x3, Pallas kernels, scores(): pl.pallas_call(functools.partial(scores_kernel, k), out_shape=jax.ShapeDt...  2.24 us
    pallas_call x1, Pallas kernels, grads_and_scores(): pl.pallas_call(functools.partial(grads_kernel, n_store, queries // n_stor...  1.28 us
    transpose x1, other arithmetic, on_device(): return total.T  0.69 us
  transfers between devices with their start and end apart: 6, of which 3 were waited for; matrix products, arithmetic and copies ran while one was open for 0% of the time, Pallas kernels for 23%

profile of v15, /device:TPU:0, one launch (start us, length us, event | category | flops | bytes accessed | tf_op | source)
XLA Modules:
  0.0 24.6 jit_solution(14370412803893714283)
XLA Ops:
  0.0 5.3 %factors.1.after.refs_0_ = bf16[288,128]{1,0:T(8,128)(2,1)S(1)} custom-call(s32[36]{0:T(128)} %hbm_lengths.1, bf16[288,8192]{1,0:T(8,128)(2,1)} %bitcast.8, bf16[288,1024]{1,0:T(8,128)(2,1)} %bitcast.10, bf16[1,8192]{1,0:T(2,128)(2,1)} %hbm_gain.1, bf16[64,8192]{1,0:T(8,128)(2,1)} %bitcast.9, bf16[64,1024]{1,0:T(8,128)(2,1)} %bitcast.11), custom_call_target="tpu_custom_call" | custom-call | tf_op jit(solution)/shard_map/factors/pallas_call | solution.py:159
  5.3 4.1 %collective-permute-start.2 = (bf16[288,128]{1,0:T(8,128)(2,1)S(1)}, bf16[288,128]{1,0:T(8,128)(2,1)S(1)}, u32[]{:S(2)}, u32[]{:S(2)}) collective-permute-start(bf16[288,128]{1,0:T(8,128)(2,1)S(1)} %factors.1.after.refs_0_), channel_id=1, source_target_pairs={{0,8},{4,12},{8,0},{12,4},{1,9},{5,13},{9,1},{13,5},{2,10},{6,14},... | collective-permute-start | bytes 221192 | tf_op jit(solution)/shard_map/ppermute | solution.py:336
  9.4 1.3 %collective-permute-start.1 = (bf16[288,128]{1,0:T(8,128)(2,1)S(1)}, bf16[288,128]{1,0:T(8,128)(2,1)S(1)}, u32[]{:S(2)}, u32[]{:S(2)}) collective-permute-start(bf16[288,128]{1,0:T(8,128)(2,1)S(1)} %factors.1.after.refs_0_), channel_id=1, source_target_pairs={{0,12},{4,8},{8,4},{12,0},{1,13},{5,9},{9,5},{13,1},{2,14},{6,10},... | collective-permute-start | bytes 221192 | tf_op jit(solution)/shard_map/ppermute | solution.py:336
  10.8 0.2 collective-permute-start
  11.0 3.3 %fetch.1.refs_4_.slab = bf16[960,4096]{1,0:T(8,128)(2,1)S(1)} custom-call(bf16[288,128]{1,0:T(8,128)(2,1)S(1)} %factors.1.after.refs_0_, bf16[960,4096]{1,0:T(8,128)(2,1)} %bitcast.7), custom_call_target="tpu_custom_call" | custom-call | bytes 7864320 | tf_op jit(solution)/shard_map/fetch/pallas_call | solution.py:197
  14.4 0.0 collective-permute-done.2.refs_3_
  14.4 1.5 %collective-permute-done.1.refs_2_ = bf16[288,128]{1,0:T(8,128)(2,1)S(1)} collective-permute-done((bf16[288,128]{1,0:T(8,128)(2,1)S(1)}, bf16[288,128]{1,0:T(8,128)(2,1)S(1)}, u32[]{:S(2)}, u32[]{:S(2)}) %collective-permute-start.1) | collective-permute-done | bytes 73760 | tf_op jit(solution)/shard_map/ppermute | solution.py:336
  15.9 0.2 collective-permute-done.refs_1_
  16.1 1.3 %grads.1 = (bf16[144,4096]{1,0:T(8,128)(2,1)S(1)}, bf16[144,240]{1,0:T(8,128)(2,1)S(1)}) custom-call(bf16[288,128]{1,0:T(8,128)(2,1)S(1)} %factors.1.after.refs_0_, bf16[288,128]{1,0:T(8,128)(2,1)S(1)} %collective-permute-done.refs_1_, bf16[288,128]{1,0:T(8,128)(2,1)S(1)} %collective-permute-done.1.refs_2_, ...), custom_call_target="tpu_custom_call" | custom-call | tf_op jit(solution)/shard_map/grads/pallas_call | solution.py:343
  17.4 0.1 collective-permute-start.4
  17.4 0.7 %scores.4 = bf16[144,240]{1,0:T(8,128)(2,1)S(1)} custom-call(bf16[144,4096]{1,0:T(8,128)(2,1)S(1)} %get-tuple-element.7.grads, bf16[960,4096]{1,0:T(8,128)(2,1)S(1)} %fetch.1.refs_4_.slab), custom_call_target="tpu_custom_call" | custom-call | flops 283115520 | bytes 3145728 | tf_op jit(solution)/shard_map/scores/pallas_call | solution.py:362
  18.2 0.6 %collective-permute-start.3 = (bf16[144,240]{1,0:T(8,128)(2,1)S(1)}, bf16[144,240]{1,0:T(8,128)(2,1)S(1)}, u32[]{:S(2)}, u32[]{:S(2)}) collective-permute-start(bf16[144,240]{1,0:T(8,128)(2,1)S(1)} %scores.4), channel_id=1, source_target_pairs={{0,1},{1,0},{2,3},{3,2},{4,5},{5,4},{6,7},{7,6},{8,9},{9,8},{10,11... | collective-permute-start | bytes 207368 | tf_op jit(solution)/shard_map/ppermute | solution.py:336
  18.8 0.0 collective-permute-done.4.refs_0_
  18.8 0.7 %scores.5 = bf16[144,240]{1,0:T(8,128)(2,1)S(1)} custom-call(bf16[144,4096]{1,0:T(8,128)(2,1)S(1)} %get-tuple-element.7.grads, bf16[960,4096]{1,0:T(8,128)(2,1)S(1)} %fetch.1.refs_4_.slab, bf16[144,240]{1,0:T(8,128)(2,1)S(1)} %collective-permute-done.4.refs_0_), custom_call_target="tpu_custom_call" | custom-call | flops 283115520 | bytes 3145728 | tf_op jit(solution)/shard_map/scores/pallas_call | solution.py:362
  19.5 1.7 %collective-permute-start.5 = (bf16[144,240]{1,0:T(8,128)(2,1)S(1)}, bf16[144,240]{1,0:T(8,128)(2,1)S(1)}, u32[]{:S(2)}, u32[]{:S(2)}) collective-permute-start(bf16[144,240]{1,0:T(8,128)(2,1)S(1)} %scores.5), channel_id=1, source_target_pairs={{0,2},{1,3},{2,0},{3,1},{4,6},{5,7},{6,4},{7,5},{8,10},{9,11},{10,... | collective-permute-start | bytes 207368 | tf_op jit(solution)/shard_map/ppermute | solution.py:336
  21.3 0.7 %scores.3 = f32[144,240]{1,0:T(8,128)S(1)} custom-call(bf16[144,4096]{1,0:T(8,128)(2,1)S(1)} %get-tuple-element.7.grads, bf16[960,4096]{1,0:T(8,128)(2,1)S(1)} %fetch.1.refs_4_.slab), custom_call_target="tpu_custom_call" | custom-call | flops 283115520 | bytes 3145728 | tf_op jit(solution)/shard_map/scores/pallas_call | solution.py:362
  22.0 0.0 collective-permute-done.3
  22.0 1.9 %collective-permute-done.5 = bf16[144,240]{1,0:T(8,128)(2,1)S(1)} collective-permute-done((bf16[144,240]{1,0:T(8,128)(2,1)S(1)}, bf16[144,240]{1,0:T(8,128)(2,1)S(1)}, u32[]{:S(2)}, u32[]{:S(2)}) %collective-permute-start.5) | collective-permute-done | bytes 69152 | tf_op jit(solution)/shard_map/ppermute | solution.py:336
  23.9 0.7 %add_bitcast_fusion = f32[240,144]{0,1:T(8,128)} fusion(bf16[144,240]{1,0:T(8,128)(2,1)S(1)} %collective-permute-done.5, f32[144,240]{1,0:T(8,128)S(1)} %scores.3, bf16[144,240]{1,0:T(8,128)(2,1)S(1)} %collective-permute-done.3), kind=kLoop, calls=%fused_computation | loop fusion | flops 138240 | bytes 414720 | tf_op jit(solution)/shard_map/transpose | solution.py:400
Async XLA Ops:
  5.3 9.0 %collective-permute-start.2 = (bf16[288,128]{1,0:T(8,128)(2,1)S(1)}, bf16[288,128]{1,0:T(8,128)(2,1)S(1)}, u32[]{:S(2)}, u32[]{:S(2)}) collective-permute-start(bf16[288,128]{1,0:T(8,128)(2,1)S(1)} %factors.1.after.refs_0_), channel_id=1, source_target_pairs={{0,8},{4,12},{8,0},{12,4},{1,9},{5,13},{9,1},{13,5},{2,10},{6,14},... | collective-permute-start | bytes 221192 | tf_op jit(solution)/shard_map/ppermute | solution.py:336
  9.4 6.5 %collective-permute-start.1 = (bf16[288,128]{1,0:T(8,128)(2,1)S(1)}, bf16[288,128]{1,0:T(8,128)(2,1)S(1)}, u32[]{:S(2)}, u32[]{:S(2)}) collective-permute-start(bf16[288,128]{1,0:T(8,128)(2,1)S(1)} %factors.1.after.refs_0_), channel_id=1, source_target_pairs={{0,12},{4,8},{8,4},{12,0},{1,13},{5,9},{9,5},{13,1},{2,14},{6,10},... | collective-permute-start | bytes 221192 | tf_op jit(solution)/shard_map/ppermute | solution.py:336
  10.8 5.3 %collective-permute-start = (bf16[288,128]{1,0:T(8,128)(2,1)S(1)}, bf16[288,128]{1,0:T(8,128)(2,1)S(1)}, u32[]{:S(2)}, u32[]{:S(2)}) collective-permute-start(bf16[288,128]{1,0:T(8,128)(2,1)S(1)} %factors.1.after.refs_0_), channel_id=1, source_target_pairs={{0,4},{4,0},{8,12},{12,8},{1,5},{5,1},{9,13},{13,9},{2,6},{6,2},{1... | collective-permute-start | bytes 221192 | tf_op jit(solution)/shard_map/ppermute | solution.py:336
  17.4 1.4 %collective-permute-start.4 = (bf16[144,240]{1,0:T(8,128)(2,1)S(1)}, bf16[144,240]{1,0:T(8,128)(2,1)S(1)}, u32[]{:S(2)}, u32[]{:S(2)}) collective-permute-start(bf16[144,240]{1,0:T(8,128)(2,1)S(1)} %get-tuple-element.8), channel_id=1, source_target_pairs={{0,1},{1,0},{2,3},{3,2},{4,5},{5,4},{6,7},{7,6},{8,9},{9,8},{10,11... | collective-permute-start | bytes 207368 | tf_op jit(solution)/shard_map/ppermute | solution.py:336
  18.2 3.8 %collective-permute-start.3 = (bf16[144,240]{1,0:T(8,128)(2,1)S(1)}, bf16[144,240]{1,0:T(8,128)(2,1)S(1)}, u32[]{:S(2)}, u32[]{:S(2)}) collective-permute-start(bf16[144,240]{1,0:T(8,128)(2,1)S(1)} %scores.4), channel_id=1, source_target_pairs={{0,1},{1,0},{2,3},{3,2},{4,5},{5,4},{6,7},{7,6},{8,9},{9,8},{10,11... | collective-permute-start | bytes 207368 | tf_op jit(solution)/shard_map/ppermute | solution.py:336
  19.5 4.4 %collective-permute-start.5 = (bf16[144,240]{1,0:T(8,128)(2,1)S(1)}, bf16[144,240]{1,0:T(8,128)(2,1)S(1)}, u32[]{:S(2)}, u32[]{:S(2)}) collective-permute-start(bf16[144,240]{1,0:T(8,128)(2,1)S(1)} %scores.5), channel_id=1, source_target_pairs={{0,2},{1,3},{2,0},{3,1},{4,6},{5,7},{6,4},{7,5},{8,10},{9,11},{10,... | collective-permute-start | bytes 207368 | tf_op jit(solution)/shard_map/ppermute | solution.py:336

commit v16 on v15

--- a/solution.py
+++ b/solution.py
@@ -86,7 +86,7 @@
         def _():
             start(pieces(c + 3))
 
-        @pl.when(c + 3 == chunks)
+        @pl.when(c == 1)
         def _():
             start(early)
 
@@ -154,7 +154,7 @@
 
 def factors(lengths, hidden, cotangent, gain, in_projection, out_projection):
     rows, width = hidden.shape
-    columns = 1024
+    columns = 2048
     chunks = width // columns
     return pl.pallas_call(
         factors_kernel,

time: 24.8 us -> 24.3 us (0.980)
  Pallas kernels: 12.2 us -> 11.8 us
    pallas_call x1, Pallas kernels: 5.32 us -> 4.92 us  [factors(): pl.pallas_call(factors_kernel, out_shape=jax.ShapeDtypeStruct((rows, 2 *...]
where the time goes in v16:
time: 24.3 us; the launch traced here: 24.2 us
  Pallas kernels  11.8 us (49%)
  starting transfers between devices  8.09 us (33%)
  waiting for transfers between devices  3.57 us (15%)
  other arithmetic  0.69 us (3%)
    ppermute x6, starting transfers between devices, swap(): return lax.ppermute(x, axis, pairs)  8.09 us
    pallas_call x1, Pallas kernels, factors(): pl.pallas_call(factors_kernel, out_shape=jax.ShapeDtypeStruct((rows, 2 *...  4.92 us
    ppermute x6, waiting for transfers between devices, swap(): return lax.ppermute(x, axis, pairs)  3.57 us
    pallas_call x1, Pallas kernels, fetch(): pl.pallas_call(functools.partial(fetch_kernel, n_layer), out_shape=jax.Sh...  3.34 us
    pallas_call x3, Pallas kernels, scores(): pl.pallas_call(functools.partial(scores_kernel, k), out_shape=jax.ShapeDt...  2.25 us
    pallas_call x1, Pallas kernels, grads_and_scores(): pl.pallas_call(functools.partial(grads_kernel, n_store, queries // n_stor...  1.28 us
    transpose x1, other arithmetic, on_device(): return total.T  0.69 us
  transfers between devices with their start and end apart: 6, of which 3 were waited for; matrix products, arithmetic and copies ran while one was open for 0% of the time, Pallas kernels for 23%

profile of v16, /device:TPU:0, one launch (start us, length us, event | category | flops | bytes accessed | tf_op | source)
XLA Modules:
  0.0 24.2 jit_solution(5633450746132250113)
XLA Ops:
  0.0 4.9 %factors.1.after.refs_0_ = bf16[288,128]{1,0:T(8,128)(2,1)S(1)} custom-call(s32[36]{0:T(128)} %hbm_lengths.1, bf16[288,8192]{1,0:T(8,128)(2,1)} %bitcast.8, bf16[288,1024]{1,0:T(8,128)(2,1)} %bitcast.10, bf16[1,8192]{1,0:T(2,128)(2,1)} %hbm_gain.1, bf16[64,8192]{1,0:T(8,128)(2,1)} %bitcast.9, bf16[64,1024]{1,0:T(8,128)(2,1)} %bitcast.11), custom_call_target="tpu_custom_call" | custom-call | tf_op jit(solution)/shard_map/factors/pallas_call | solution.py:159
  4.9 4.1 %collective-permute-start.2 = (bf16[288,128]{1,0:T(8,128)(2,1)S(1)}, bf16[288,128]{1,0:T(8,128)(2,1)S(1)}, u32[]{:S(2)}, u32[]{:S(2)}) collective-permute-start(bf16[288,128]{1,0:T(8,128)(2,1)S(1)} %factors.1.after.refs_0_), channel_id=1, source_target_pairs={{0,8},{4,12},{8,0},{12,4},{1,9},{5,13},{9,1},{13,5},{2,10},{6,14},... | collective-permute-start | bytes 221192 | tf_op jit(solution)/shard_map/ppermute | solution.py:336
  9.0 1.4 %collective-permute-start.1 = (bf16[288,128]{1,0:T(8,128)(2,1)S(1)}, bf16[288,128]{1,0:T(8,128)(2,1)S(1)}, u32[]{:S(2)}, u32[]{:S(2)}) collective-permute-start(bf16[288,128]{1,0:T(8,128)(2,1)S(1)} %factors.1.after.refs_0_), channel_id=1, source_target_pairs={{0,12},{4,8},{8,4},{12,0},{1,13},{5,9},{9,5},{13,1},{2,14},{6,10},... | collective-permute-start | bytes 221192 | tf_op jit(solution)/shard_map/ppermute | solution.py:336
  10.4 0.2 collective-permute-start
  10.6 3.3 %fetch.1.refs_4_.slab = bf16[960,4096]{1,0:T(8,128)(2,1)S(1)} custom-call(bf16[288,128]{1,0:T(8,128)(2,1)S(1)} %factors.1.after.refs_0_, bf16[960,4096]{1,0:T(8,128)(2,1)} %bitcast.7), custom_call_target="tpu_custom_call" | custom-call | bytes 7864320 | tf_op jit(solution)/shard_map/fetch/pallas_call | solution.py:197
  14.0 0.0 collective-permute-done.2.refs_3_
  14.0 1.5 %collective-permute-done.1.refs_2_ = bf16[288,128]{1,0:T(8,128)(2,1)S(1)} collective-permute-done((bf16[288,128]{1,0:T(8,128)(2,1)S(1)}, bf16[288,128]{1,0:T(8,128)(2,1)S(1)}, u32[]{:S(2)}, u32[]{:S(2)}) %collective-permute-start.1) | collective-permute-done | bytes 73760 | tf_op jit(solution)/shard_map/ppermute | solution.py:336
  15.5 0.2 collective-permute-done.refs_1_
  15.7 1.3 %grads.1 = (bf16[144,4096]{1,0:T(8,128)(2,1)S(1)}, bf16[144,240]{1,0:T(8,128)(2,1)S(1)}) custom-call(bf16[288,128]{1,0:T(8,128)(2,1)S(1)} %factors.1.after.refs_0_, bf16[288,128]{1,0:T(8,128)(2,1)S(1)} %collective-permute-done.refs_1_, bf16[288,128]{1,0:T(8,128)(2,1)S(1)} %collective-permute-done.1.refs_2_, ...), custom_call_target="tpu_custom_call" | custom-call | tf_op jit(solution)/shard_map/grads/pallas_call | solution.py:343
  16.9 0.1 collective-permute-start.4
  17.0 0.8 %scores.4 = bf16[144,240]{1,0:T(8,128)(2,1)S(1)} custom-call(bf16[144,4096]{1,0:T(8,128)(2,1)S(1)} %get-tuple-element.7.grads, bf16[960,4096]{1,0:T(8,128)(2,1)S(1)} %fetch.1.refs_4_.slab), custom_call_target="tpu_custom_call" | custom-call | flops 283115520 | bytes 3145728 | tf_op jit(solution)/shard_map/scores/pallas_call | solution.py:362
  17.8 0.6 %collective-permute-start.3 = (bf16[144,240]{1,0:T(8,128)(2,1)S(1)}, bf16[144,240]{1,0:T(8,128)(2,1)S(1)}, u32[]{:S(2)}, u32[]{:S(2)}) collective-permute-start(bf16[144,240]{1,0:T(8,128)(2,1)S(1)} %scores.4), channel_id=1, source_target_pairs={{0,1},{1,0},{2,3},{3,2},{4,5},{5,4},{6,7},{7,6},{8,9},{9,8},{10,11... | collective-permute-start | bytes 207368 | tf_op jit(solution)/shard_map/ppermute | solution.py:336
  18.3 0.0 collective-permute-done.4.refs_0_
  18.3 0.7 %scores.5 = bf16[144,240]{1,0:T(8,128)(2,1)S(1)} custom-call(bf16[144,4096]{1,0:T(8,128)(2,1)S(1)} %get-tuple-element.7.grads, bf16[960,4096]{1,0:T(8,128)(2,1)S(1)} %fetch.1.refs_4_.slab, bf16[144,240]{1,0:T(8,128)(2,1)S(1)} %collective-permute-done.4.refs_0_), custom_call_target="tpu_custom_call" | custom-call | flops 283115520 | bytes 3145728 | tf_op jit(solution)/shard_map/scores/pallas_call | solution.py:362
  19.1 1.8 %collective-permute-start.5 = (bf16[144,240]{1,0:T(8,128)(2,1)S(1)}, bf16[144,240]{1,0:T(8,128)(2,1)S(1)}, u32[]{:S(2)}, u32[]{:S(2)}) collective-permute-start(bf16[144,240]{1,0:T(8,128)(2,1)S(1)} %scores.5), channel_id=1, source_target_pairs={{0,2},{1,3},{2,0},{3,1},{4,6},{5,7},{6,4},{7,5},{8,10},{9,11},{10,... | collective-permute-start | bytes 207368 | tf_op jit(solution)/shard_map/ppermute | solution.py:336
  20.9 0.7 %scores.3 = f32[144,240]{1,0:T(8,128)S(1)} custom-call(bf16[144,4096]{1,0:T(8,128)(2,1)S(1)} %get-tuple-element.7.grads, bf16[960,4096]{1,0:T(8,128)(2,1)S(1)} %fetch.1.refs_4_.slab), custom_call_target="tpu_custom_call" | custom-call | flops 283115520 | bytes 3145728 | tf_op jit(solution)/shard_map/scores/pallas_call | solution.py:362
  21.6 0.0 collective-permute-done.3
  21.6 1.9 %collective-permute-done.5 = bf16[144,240]{1,0:T(8,128)(2,1)S(1)} collective-permute-done((bf16[144,240]{1,0:T(8,128)(2,1)S(1)}, bf16[144,240]{1,0:T(8,128)(2,1)S(1)}, u32[]{:S(2)}, u32[]{:S(2)}) %collective-permute-start.5) | collective-permute-done | bytes 69152 | tf_op jit(solution)/shard_map/ppermute | solution.py:336
  23.5 0.7 %add_bitcast_fusion = f32[240,144]{0,1:T(8,128)} fusion(bf16[144,240]{1,0:T(8,128)(2,1)S(1)} %collective-permute-done.5, f32[144,240]{1,0:T(8,128)S(1)} %scores.3, bf16[144,240]{1,0:T(8,128)(2,1)S(1)} %collective-permute-done.3), kind=kLoop, calls=%fused_computation | loop fusion | flops 138240 | bytes 414720 | tf_op jit(solution)/shard_map/transpose | solution.py:400
Async XLA Ops:
  4.9 9.0 %collective-permute-start.2 = (bf16[288,128]{1,0:T(8,128)(2,1)S(1)}, bf16[288,128]{1,0:T(8,128)(2,1)S(1)}, u32[]{:S(2)}, u32[]{:S(2)}) collective-permute-start(bf16[288,128]{1,0:T(8,128)(2,1)S(1)} %factors.1.after.refs_0_), channel_id=1, source_target_pairs={{0,8},{4,12},{8,0},{12,4},{1,9},{5,13},{9,1},{13,5},{2,10},{6,14},... | collective-permute-start | bytes 221192 | tf_op jit(solution)/shard_map/ppermute | solution.py:336
  9.0 6.5 %collective-permute-start.1 = (bf16[288,128]{1,0:T(8,128)(2,1)S(1)}, bf16[288,128]{1,0:T(8,128)(2,1)S(1)}, u32[]{:S(2)}, u32[]{:S(2)}) collective-permute-start(bf16[288,128]{1,0:T(8,128)(2,1)S(1)} %factors.1.after.refs_0_), channel_id=1, source_target_pairs={{0,12},{4,8},{8,4},{12,0},{1,13},{5,9},{9,5},{13,1},{2,14},{6,10},... | collective-permute-start | bytes 221192 | tf_op jit(solution)/shard_map/ppermute | solution.py:336
  10.4 5.3 %collective-permute-start = (bf16[288,128]{1,0:T(8,128)(2,1)S(1)}, bf16[288,128]{1,0:T(8,128)(2,1)S(1)}, u32[]{:S(2)}, u32[]{:S(2)}) collective-permute-start(bf16[288,128]{1,0:T(8,128)(2,1)S(1)} %factors.1.after.refs_0_), channel_id=1, source_target_pairs={{0,4},{4,0},{8,12},{12,8},{1,5},{5,1},{9,13},{13,9},{2,6},{6,2},{1... | collective-permute-start | bytes 221192 | tf_op jit(solution)/shard_map/ppermute | solution.py:336
  16.9 1.4 %collective-permute-start.4 = (bf16[144,240]{1,0:T(8,128)(2,1)S(1)}, bf16[144,240]{1,0:T(8,128)(2,1)S(1)}, u32[]{:S(2)}, u32[]{:S(2)}) collective-permute-start(bf16[144,240]{1,0:T(8,128)(2,1)S(1)} %get-tuple-element.8), channel_id=1, source_target_pairs={{0,1},{1,0},{2,3},{3,2},{4,5},{5,4},{6,7},{7,6},{8,9},{9,8},{10,11... | collective-permute-start | bytes 207368 | tf_op jit(solution)/shard_map/ppermute | solution.py:336
  17.8 3.8 %collective-permute-start.3 = (bf16[144,240]{1,0:T(8,128)(2,1)S(1)}, bf16[144,240]{1,0:T(8,128)(2,1)S(1)}, u32[]{:S(2)}, u32[]{:S(2)}) collective-permute-start(bf16[144,240]{1,0:T(8,128)(2,1)S(1)} %scores.4), channel_id=1, source_target_pairs={{0,1},{1,0},{2,3},{3,2},{4,5},{5,4},{6,7},{7,6},{8,9},{9,8},{10,11... | collective-permute-start | bytes 207368 | tf_op jit(solution)/shard_map/ppermute | solution.py:336
  19.1 4.4 %collective-permute-start.5 = (bf16[144,240]{1,0:T(8,128)(2,1)S(1)}, bf16[144,240]{1,0:T(8,128)(2,1)S(1)}, u32[]{:S(2)}, u32[]{:S(2)}) collective-permute-start(bf16[144,240]{1,0:T(8,128)(2,1)S(1)} %scores.5), channel_id=1, source_target_pairs={{0,2},{1,3},{2,0},{3,1},{4,6},{5,7},{6,4},{7,5},{8,10},{9,11},{10,... | collective-permute-start | bytes 207368 | tf_op jit(solution)/shard_map/ppermute | solution.py:336

commit v17 on v16

--- a/solution.py
+++ b/solution.py
@@ -70,23 +70,18 @@
     copy_gain = copy(hbm_gain, gain, 0)
     early = [copy(hbm_outp, outp, 1), copy(hbm_cot, cot, 2), copy(hbm_lengths, lengths, 3)]
     copy_gain.start()
-    start(pieces(0))
-    start(pieces(1))
+    for c in range(chunks):
+        start(pieces(c))
     in_acc[...] = jnp.zeros_like(in_acc)
     sq_acc[...] = jnp.zeros_like(sq_acc)
     copy_gain.wait()
-    start(pieces(2))
 
     @pl.loop(0, chunks)
     def _(c):
         for piece in pieces(c):
             piece.wait()
 
-        @pl.when(c + 3 < chunks)
-        def _():
-            start(pieces(c + 3))
-
-        @pl.when(c == 1)
+        @pl.when(c == 0)
         def _():
             start(early)
 
@@ -318,13 +313,14 @@
     scores_kernel(k, grads, slab, out)
 
 
-def scores_kernel(k, grads, slab, *refs):
-    *terms, out = refs
-    block = out.shape[1]
+def scores_kernel(k, grads, slab, *refs, skip=0):
+    outs = refs[skip:]
+    block = outs[0].shape[1]
     total = dot_nt(slab[k * block : (k + 1) * block, :], grads[...]).T
-    for term in terms:
-        total += term[...].astype(f32)
-    out[...] = total.astype(out.dtype)
+    at = 0
+    for out in outs:
+        out[...] = total[at : at + out.shape[0]].astype(out.dtype)
+        at += out.shape[0]
 
 
 def partner(me, k, n):
@@ -354,16 +350,16 @@
     )(*gathered, slab)
 
 
-def scores(grads, slab, n_layer, k, terms=()):
+def scores(grads, slab, n_layer, k, pieces=1, after=()):
     rows, features = slab.shape
     block = rows // n_layer
     queries = grads.shape[0]
     vmem = pl.BlockSpec(memory_space=pltpu.VMEM)
     return pl.pallas_call(
-        functools.partial(scores_kernel, k),
-        out_shape=jax.ShapeDtypeStruct((queries, block), bf16 if k else f32),
-        in_specs=[vmem] * (2 + len(terms)),
-        out_specs=vmem,
+        functools.partial(scores_kernel, k, skip=len(after)),
+        out_shape=[jax.ShapeDtypeStruct((queries // pieces, block), bf16 if k % 2 else f32)] * pieces,
+        in_specs=[vmem] * 2 + [pl.BlockSpec(memory_space=pl.ANY)] * len(after),
+        out_specs=[vmem] * pieces,
         compiler_params=pltpu.CompilerParams(vmem_limit_bytes=24 * 2**20),
         cost_estimate=pl.CostEstimate(
             flops=2 * queries * block * features,
@@ -371,7 +367,7 @@
             transcendentals=0,
         ),
         name="scores",
-    )(grads, slab, *terms)
+    )(grads, slab, *after)
 
 
 def on_device(n_store, n_layer, hidden, cotangent, lengths, norm_gain, in_proj, out_proj, store):
@@ -387,14 +383,17 @@
     gathered = [packed] + [swap(packed, "store", n_store, k) for k in store_order(n_store)]
     slab = fetch(packed, store[0], n_layer)
     grads, partial = grads_and_scores(gathered, slab, n_store, n_layer, n_layer - 1)
-    other = swap(partial, "layer", n_layer, 1)
-    near = swap(scores(grads, slab, n_layer, 1), "layer", n_layer, 1)
-    crossed = [near]
+    crossed = []
     for k in reversed(range(2, n_layer, 2)):
         if k < n_layer - 2:
-            other = swap(scores(grads, slab, n_layer, k + 1), "layer", n_layer, 1)
-        crossed.append(swap(scores(grads, slab, n_layer, k, [other]), "layer", n_layer, k))
-    total = scores(grads, slab, n_layer, 0)
+            (partial,) = scores(grads, slab, n_layer, k + 1)
+        other = swap(partial, "layer", n_layer, 1)
+        (mine,) = scores(grads, slab, n_layer, k)
+        joined = (mine + other.astype(f32)).astype(bf16)
+        crossed.append(swap(joined, "layer", n_layer, k))
+    near = [swap(x, "layer", n_layer, 1) for x in scores(grads, slab, n_layer, 1, 2, [joined])]
+    (total,) = scores(grads, slab, n_layer, 0)
+    total = total + jnp.concatenate(near, axis=0).astype(f32)
     for x in crossed:
         total = total + x.astype(f32)
     return total.T

time: 24.3 us -> 23.6 us (0.971)
  waiting for transfers between devices: 3.57 us -> 2.77 us
    ppermute x6 -> x7, waiting for transfers between devices: 3.57 us -> 2.77 us  [swap(): return lax.ppermute(x, axis, pairs)]
    ppermute x6 -> x7, starting transfers between devices: 8.09 us -> 8.09 us  [swap(): return lax.ppermute(x, axis, pairs)]
  transfers between devices with their start and end apart: 6 -> 7, of which waited for: 3 -> 5; matrix products, arithmetic and copies ran while one was open for 0% -> 0% of each run, Pallas kernels for 23% -> 24%
where the time goes in v17:
time: 23.6 us; the launch traced here: 23.5 us
  Pallas kernels  11.8 us (50%)
  starting transfers between devices  8.09 us (34%)
  waiting for transfers between devices  2.77 us (12%)
  other arithmetic  0.71 us (3%)
    ppermute x7, starting transfers between devices, swap(): return lax.ppermute(x, axis, pairs)  8.09 us
    pallas_call x1, Pallas kernels, factors(): pl.pallas_call(factors_kernel, out_shape=jax.ShapeDtypeStruct((rows, 2 *...  4.98 us
    pallas_call x1, Pallas kernels, fetch(): pl.pallas_call(functools.partial(fetch_kernel, n_layer), out_shape=jax.Sh...  3.34 us
    ppermute x7, waiting for transfers between devices, swap(): return lax.ppermute(x, axis, pairs)  2.77 us
    pallas_call x3, Pallas kernels, scores(): pl.pallas_call(functools.partial(scores_kernel, k, skip=len(after)), out_...  2.23 us
    pallas_call x1, Pallas kernels, grads_and_scores(): pl.pallas_call(functools.partial(grads_kernel, n_store, queries // n_stor...  1.27 us
    transpose x1, other arithmetic, on_device(): return total.T  0.69 us
  transfers between devices with their start and end apart: 7, of which 5 were waited for; matrix products, arithmetic and copies ran while one was open for 0% of the time, Pallas kernels for 24%

profile of v17, /device:TPU:0, one launch (start us, length us, event | category | flops | bytes accessed | tf_op | source)
XLA Modules:
  0.0 23.5 jit_solution(6839679126395675622)
XLA Ops:
  0.0 5.0 %factors.1.after.refs_0_ = bf16[288,128]{1,0:T(8,128)(2,1)S(1)} custom-call(s32[36]{0:T(128)} %hbm_lengths.1, bf16[288,8192]{1,0:T(8,128)(2,1)} %bitcast.8, bf16[288,1024]{1,0:T(8,128)(2,1)} %bitcast.10, bf16[1,8192]{1,0:T(2,128)(2,1)} %hbm_gain.1, bf16[64,8192]{1,0:T(8,128)(2,1)} %bitcast.9, bf16[64,1024]{1,0:T(8,128)(2,1)} %bitcast.11), custom_call_target="tpu_custom_call" | custom-call | tf_op jit(solution)/shard_map/factors/pallas_call | solution.py:154
  5.0 4.1 %collective-permute-start.2 = (bf16[288,128]{1,0:T(8,128)(2,1)S(1)}, bf16[288,128]{1,0:T(8,128)(2,1)S(1)}, u32[]{:S(2)}, u32[]{:S(2)}) collective-permute-start(bf16[288,128]{1,0:T(8,128)(2,1)S(1)} %factors.1.after.refs_0_), channel_id=1, source_target_pairs={{0,8},{4,12},{8,0},{12,4},{1,9},{5,13},{9,1},{13,5},{2,10},{6,14},... | collective-permute-start | bytes 221192 | tf_op jit(solution)/shard_map/ppermute | solution.py:332
  9.1 1.3 %collective-permute-start.1 = (bf16[288,128]{1,0:T(8,128)(2,1)S(1)}, bf16[288,128]{1,0:T(8,128)(2,1)S(1)}, u32[]{:S(2)}, u32[]{:S(2)}) collective-permute-start(bf16[288,128]{1,0:T(8,128)(2,1)S(1)} %factors.1.after.refs_0_), channel_id=1, source_target_pairs={{0,12},{4,8},{8,4},{12,0},{1,13},{5,9},{9,5},{13,1},{2,14},{6,10},... | collective-permute-start | bytes 221192 | tf_op jit(solution)/shard_map/ppermute | solution.py:332
  10.4 0.2 collective-permute-start
  10.7 3.3 %fetch.1.refs_4_.slab = bf16[960,4096]{1,0:T(8,128)(2,1)S(1)} custom-call(bf16[288,128]{1,0:T(8,128)(2,1)S(1)} %factors.1.after.refs_0_, bf16[960,4096]{1,0:T(8,128)(2,1)} %bitcast.7), custom_call_target="tpu_custom_call" | custom-call | bytes 7864320 | tf_op jit(solution)/shard_map/fetch/pallas_call | solution.py:192
  14.0 0.0 collective-permute-done.2.refs_3_
  14.0 1.5 %collective-permute-done.1.refs_2_ = bf16[288,128]{1,0:T(8,128)(2,1)S(1)} collective-permute-done((bf16[288,128]{1,0:T(8,128)(2,1)S(1)}, bf16[288,128]{1,0:T(8,128)(2,1)S(1)}, u32[]{:S(2)}, u32[]{:S(2)}) %collective-permute-start.1) | collective-permute-done | bytes 73760 | tf_op jit(solution)/shard_map/ppermute | solution.py:332
  15.6 0.2 collective-permute-done.refs_1_
  15.7 1.3 %grads.1 = (bf16[144,4096]{1,0:T(8,128)(2,1)S(1)}, bf16[144,240]{1,0:T(8,128)(2,1)S(1)}) custom-call(bf16[288,128]{1,0:T(8,128)(2,1)S(1)} %factors.1.after.refs_0_, bf16[288,128]{1,0:T(8,128)(2,1)S(1)} %collective-permute-done.refs_1_, bf16[288,128]{1,0:T(8,128)(2,1)S(1)} %collective-permute-done.1.refs_2_, ...), custom_call_target="tpu_custom_call" | custom-call | tf_op jit(solution)/shard_map/grads/pallas_call | solution.py:339
  17.0 0.1 collective-permute-start.3
  17.1 0.7 %scores.4 = f32[144,240]{1,0:T(8,128)S(1)} custom-call(bf16[144,4096]{1,0:T(8,128)(2,1)S(1)} %get-tuple-element.9.grads, bf16[960,4096]{1,0:T(8,128)(2,1)S(1)} %fetch.1.refs_4_.slab), custom_call_target="tpu_custom_call" | custom-call | flops 283115520 | bytes 3145728 | tf_op jit(solution)/shard_map/scores/pallas_call | solution.py:358
  17.8 0.5 %collective-permute-done.3 = bf16[144,240]{1,0:T(8,128)(2,1)S(1)} collective-permute-done((bf16[144,240]{1,0:T(8,128)(2,1)S(1)}, bf16[144,240]{1,0:T(8,128)(2,1)S(1)}, u32[]{:S(2)}, u32[]{:S(2)}) %collective-permute-start.3) | collective-permute-done | bytes 69152 | tf_op jit(solution)/shard_map/ppermute | solution.py:332
  18.4 1.8 %collective-permute-start.6 = (bf16[144,240]{1,0:T(8,128)(2,1)S(1)}, bf16[144,240]{1,0:T(8,128)(2,1)S(1)}, u32[]{:S(2)}, u32[]{:S(2)}) collective-permute-start(bf16[144,240]{1,0:T(8,128)(2,1)S(1)} %add_convert_fusion.refs_0_), channel_id=1, source_target_pairs={{0,2},{1,3},{2,0},{3,1},{4,6},{5,7},{6,4},{7,5},{8,10},{9,11},{10,... | collective-permute-start | bytes 207368 | tf_op jit(solution)/shard_map/ppermute | solution.py:332
  20.1 0.7 %scores.5 = (bf16[72,240]{1,0:T(8,128)(2,1)S(1)}, bf16[72,240]{1,0:T(8,128)(2,1)S(1)}) custom-call(bf16[144,4096]{1,0:T(8,128)(2,1)S(1)} %get-tuple-element.9.grads, bf16[960,4096]{1,0:T(8,128)(2,1)S(1)} %fetch.1.refs_4_.slab, bf16[144,240]{1,0:T(8,128)(2,1)S(1)} %add_convert_fusion.refs_0_), custom_call_target="tpu_custom_call" | custom-call | flops 283115520 | bytes 3145728 | tf_op jit(solution)/shard_map/scores/pallas_call | solution.py:358
  20.9 0.1 collective-permute-start.4
  21.0 0.5 %collective-permute-start.5 = (bf16[72,240]{1,0:T(8,128)(2,1)S(1)}, bf16[72,240]{1,0:T(8,128)(2,1)S(1)}, u32[]{:S(2)}, u32[]{:S(2)}) collective-permute-start(bf16[72,240]{1,0:T(8,128)(2,1)S(1)} %get-tuple-element.12), channel_id=1, source_target_pairs={{0,1},{1,0},{2,3},{3,2},{4,5},{5,4},{6,7},{7,6},{8,9},{9,8},{10,11... | collective-permute-start | bytes 103688 | tf_op jit(solution)/shard_map/ppermute | solution.py:332
  21.5 0.7 %scores.3 = f32[144,240]{1,0:T(8,128)S(1)} custom-call(bf16[144,4096]{1,0:T(8,128)(2,1)S(1)} %get-tuple-element.9.grads, bf16[960,4096]{1,0:T(8,128)(2,1)S(1)} %fetch.1.refs_4_.slab), custom_call_target="tpu_custom_call" | custom-call | flops 283115520 | bytes 3145728 | tf_op jit(solution)/shard_map/scores/pallas_call | solution.py:358
  22.2 0.0 collective-permute-done.4
  22.2 0.1 collective-permute-done.5
  22.3 0.5 %collective-permute-done.6 = bf16[144,240]{1,0:T(8,128)(2,1)S(1)} collective-permute-done((bf16[144,240]{1,0:T(8,128)(2,1)S(1)}, bf16[144,240]{1,0:T(8,128)(2,1)S(1)}, u32[]{:S(2)}, u32[]{:S(2)}) %collective-permute-start.6) | collective-permute-done | bytes 69152 | tf_op jit(solution)/shard_map/ppermute | solution.py:332
  22.8 0.7 %add_bitcast_fusion = f32[240,144]{0,1:T(8,128)} fusion(bf16[144,240]{1,0:T(8,128)(2,1)S(1)} %collective-permute-done.6, f32[144,240]{1,0:T(8,128)S(1)} %scores.3, bf16[72,240]{1,0:T(8,128)(2,1)S(1)} %collective-permute-done.5, bf16[72,240]{1,0:T(8,128)(2,1)S(1)} %collective-permute-done.4), kind=kLoop, calls=%fused_computation | loop fusion | flops 241920 | bytes 414720 | tf_op jit(solution)/shard_map/transpose | solution.py:399
  (1 shorter events, 0.0 us)
Async XLA Ops:
  5.0 9.0 %collective-permute-start.2 = (bf16[288,128]{1,0:T(8,128)(2,1)S(1)}, bf16[288,128]{1,0:T(8,128)(2,1)S(1)}, u32[]{:S(2)}, u32[]{:S(2)}) collective-permute-start(bf16[288,128]{1,0:T(8,128)(2,1)S(1)} %factors.1.after.refs_0_), channel_id=1, source_target_pairs={{0,8},{4,12},{8,0},{12,4},{1,9},{5,13},{9,1},{13,5},{2,10},{6,14},... | collective-permute-start | bytes 221192 | tf_op jit(solution)/shard_map/ppermute | solution.py:332
  9.1 6.5 %collective-permute-start.1 = (bf16[288,128]{1,0:T(8,128)(2,1)S(1)}, bf16[288,128]{1,0:T(8,128)(2,1)S(1)}, u32[]{:S(2)}, u32[]{:S(2)}) collective-permute-start(bf16[288,128]{1,0:T(8,128)(2,1)S(1)} %factors.1.after.refs_0_), channel_id=1, source_target_pairs={{0,12},{4,8},{8,4},{12,0},{1,13},{5,9},{9,5},{13,1},{2,14},{6,10},... | collective-permute-start | bytes 221192 | tf_op jit(solution)/shard_map/ppermute | solution.py:332
  10.4 5.3 %collective-permute-start = (bf16[288,128]{1,0:T(8,128)(2,1)S(1)}, bf16[288,128]{1,0:T(8,128)(2,1)S(1)}, u32[]{:S(2)}, u32[]{:S(2)}) collective-permute-start(bf16[288,128]{1,0:T(8,128)(2,1)S(1)} %factors.1.after.refs_0_), channel_id=1, source_target_pairs={{0,4},{4,0},{8,12},{12,8},{1,5},{5,1},{9,13},{13,9},{2,6},{6,2},{1... | collective-permute-start | bytes 221192 | tf_op jit(solution)/shard_map/ppermute | solution.py:332
  17.0 1.3 %collective-permute-start.3 = (bf16[144,240]{1,0:T(8,128)(2,1)S(1)}, bf16[144,240]{1,0:T(8,128)(2,1)S(1)}, u32[]{:S(2)}, u32[]{:S(2)}) collective-permute-start(bf16[144,240]{1,0:T(8,128)(2,1)S(1)} %get-tuple-element.10), channel_id=1, source_target_pairs={{0,1},{1,0},{2,3},{3,2},{4,5},{5,4},{6,7},{7,6},{8,9},{9,8},{10,11... | collective-permute-start | bytes 207368 | tf_op jit(solution)/shard_map/ppermute | solution.py:332
  18.4 4.4 %collective-permute-start.6 = (bf16[144,240]{1,0:T(8,128)(2,1)S(1)}, bf16[144,240]{1,0:T(8,128)(2,1)S(1)}, u32[]{:S(2)}, u32[]{:S(2)}) collective-permute-start(bf16[144,240]{1,0:T(8,128)(2,1)S(1)} %add_convert_fusion.refs_0_), channel_id=1, source_target_pairs={{0,2},{1,3},{2,0},{3,1},{4,6},{5,7},{6,4},{7,5},{8,10},{9,11},{10,... | collective-permute-start | bytes 207368 | tf_op jit(solution)/shard_map/ppermute | solution.py:332
  20.9 1.3 %collective-permute-start.4 = (bf16[72,240]{1,0:T(8,128)(2,1)S(1)}, bf16[72,240]{1,0:T(8,128)(2,1)S(1)}, u32[]{:S(2)}, u32[]{:S(2)}) collective-permute-start(bf16[72,240]{1,0:T(8,128)(2,1)S(1)} %get-tuple-element.11), channel_id=1, source_target_pairs={{0,1},{1,0},{2,3},{3,2},{4,5},{5,4},{6,7},{7,6},{8,9},{9,8},{10,11... | collective-permute-start | bytes 103688 | tf_op jit(solution)/shard_map/ppermute | solution.py:332
  21.0 1.4 %collective-permute-start.5 = (bf16[72,240]{1,0:T(8,128)(2,1)S(1)}, bf16[72,240]{1,0:T(8,128)(2,1)S(1)}, u32[]{:S(2)}, u32[]{:S(2)}) collective-permute-start(bf16[72,240]{1,0:T(8,128)(2,1)S(1)} %get-tuple-element.12), channel_id=1, source_target_pairs={{0,1},{1,0},{2,3},{3,2},{4,5},{5,4},{6,7},{7,6},{8,9},{9,8},{10,11... | collective-permute-start | bytes 103688 | tf_op jit(solution)/shard_map/ppermute | solution.py:332

commit v18 on v17

--- a/solution.py
+++ b/solution.py
@@ -70,18 +70,23 @@
     copy_gain = copy(hbm_gain, gain, 0)
     early = [copy(hbm_outp, outp, 1), copy(hbm_cot, cot, 2), copy(hbm_lengths, lengths, 3)]
     copy_gain.start()
-    for c in range(chunks):
-        start(pieces(c))
+    start(pieces(0))
+    start(pieces(1))
     in_acc[...] = jnp.zeros_like(in_acc)
     sq_acc[...] = jnp.zeros_like(sq_acc)
     copy_gain.wait()
+    start(pieces(2))
 
     @pl.loop(0, chunks)
     def _(c):
         for piece in pieces(c):
             piece.wait()
 
-        @pl.when(c == 0)
+        @pl.when(c + 3 < chunks)
+        def _():
+            start(pieces(c + 3))
+
+        @pl.when(c == 1)
         def _():
             start(early)
 
@@ -173,31 +178,30 @@
     )(*[in_hbm(x) for x in (lengths, hidden, cotangent, gain, in_projection, out_projection)])
 
 
-def fetch_kernel(n_layer, after, store, slab, sems):
-    block = slab.shape[0] // n_layer
+def block_copy(store, k, slab, sem, n_layer):
+    block = slab.shape[0]
     rows = 16 if block % 16 == 0 else 8
-    me = lax.axis_index("layer")
-    copies = []
-    for k in range(n_layer):
-        at = pl.multiple_of(partner(me, k, n_layer) * block, rows)
-        to = slab.at[pl.ds(k * block, block)]
-        copies.append(pltpu.make_async_copy(store.at[pl.ds(at, block)], to, sems.at[k]))
-        copies[-1].start()
-    for copy in copies:
-        copy.wait()
-
-
-def fetch(after, store, n_layer):
+    at = pl.multiple_of(partner(lax.axis_index("layer"), k, n_layer) * block, rows)
+    return pltpu.make_async_copy(store.at[pl.ds(at, block)], slab, sem)
+
+
+def fetch_kernel(n_layer, k, after, store, slab, sem):
+    copy = block_copy(store, k, slab, sem, n_layer)
+    copy.start()
+    copy.wait()
+
+
+def fetch(after, store, n_layer, k):
     rows, features = store.shape
     return pl.pallas_call(
-        functools.partial(fetch_kernel, n_layer),
-        out_shape=jax.ShapeDtypeStruct((rows, features), bf16),
+        functools.partial(fetch_kernel, n_layer, k),
+        out_shape=jax.ShapeDtypeStruct((rows // n_layer, features), bf16),
         in_specs=[pl.BlockSpec(memory_space=pl.ANY)] * 2,
         out_specs=pl.BlockSpec(memory_space=pltpu.VMEM),
-        scratch_shapes=[pltpu.SemaphoreType.DMA((n_layer,))],
+        scratch_shapes=[pltpu.SemaphoreType.DMA],
         compiler_params=pltpu.CompilerParams(vmem_limit_bytes=12 * 2**20),
         cost_estimate=pl.CostEstimate(
-            flops=0, bytes_accessed=2 * rows * features, transcendentals=0
+            flops=0, bytes_accessed=2 * rows * features // n_layer, transcendentals=0
         ),
         name="fetch",
     )(after, in_hbm(store))
@@ -291,16 +295,14 @@
             ).astype(bf16)
 
 
-def store_order(n):
-    return [1, 3, 2] if n == 4 else list(range(1, n))
-
-
-def grads_kernel(n_store, full_groups, k, *refs):
+def grads_kernel(n_store, n_layer, full_groups, k, *refs):
     gathered = refs[:n_store]
-    slab, grads, out, shards = refs[n_store:]
+    slab, store, grads, out, following, shards, sem = refs[n_store:]
+    copy = block_copy(store, k - 1, following, sem, n_layer)
+    copy.start()
     me_store = lax.axis_index("store")
-    for block, away in zip(gathered, [0] + store_order(n_store)):
-        shards[partner(me_store, away, n_store)] = block[...]
+    for away in range(n_store):
+        shards[lax.rem(me_store + away, n_store)] = gathered[away][...]
     four = 4 * (full_groups * G + H)
     if n_store == 4:
         build_grads(shards, 0, 0, full_groups, grads)
@@ -310,19 +312,29 @@
         def _(at):
             build_grads(shards, at * 4, pl.multiple_of(at * four, 16), full_groups, grads)
 
-    scores_kernel(k, grads, slab, out)
-
-
-def scores_kernel(k, grads, slab, *refs, skip=0):
-    outs = refs[skip:]
-    block = outs[0].shape[1]
-    total = dot_nt(slab[k * block : (k + 1) * block, :], grads[...]).T
+    score(grads, slab, [out])
+    copy.wait()
+
+
+def score(grads, slab, outs):
+    total = dot_nt(slab[...], grads[...]).T
     at = 0
     for out in outs:
         out[...] = total[at : at + out.shape[0]].astype(out.dtype)
         at += out.shape[0]
 
 
+def scores_kernel(n_layer, k, pieces, grads, slab, store, *refs):
+    if k == 0:
+        score(grads, slab, refs[-pieces:])
+        return
+    following, sem = refs[-2:]
+    copy = block_copy(store, k - 1, following, sem, n_layer)
+    copy.start()
+    score(grads, slab, refs[-2 - pieces : -2])
+    copy.wait()
+
+
 def partner(me, k, n):
     return jnp.bitwise_xor(me, k) if n & (n - 1) == 0 else lax.rem(n + k - me, n)
 
@@ -332,42 +344,49 @@
     return lax.ppermute(x, axis, pairs)
 
 
-def grads_and_scores(gathered, slab, n_store, n_layer, k):
-    rows, features = slab.shape
-    queries = n_store * gathered[0].shape[0] // S
+def grads_and_scores(packed, slab, store, n_store, n_layer, k):
+    block, features = slab.shape
+    queries = packed.shape[0] // S
+    gathered = [packed]
+    for away in range(1, n_store):
+        pairs = [((to + away) % n_store, to) for to in range(n_store)]
+        gathered.append(lax.ppermute(packed, "store", pairs))
     vmem = pl.BlockSpec(memory_space=pltpu.VMEM)
     return pl.pallas_call(
-        functools.partial(grads_kernel, n_store, queries // n_store // G, k),
+        functools.partial(grads_kernel, n_store, n_layer, queries // G, k),
         out_shape=[
-            jax.ShapeDtypeStruct((queries, features), bf16),
-            jax.ShapeDtypeStruct((queries, rows // n_layer), bf16),
+            jax.ShapeDtypeStruct((n_store * queries, features), bf16),
+            jax.ShapeDtypeStruct((n_store * queries, block), bf16),
+            jax.ShapeDtypeStruct(slab.shape, bf16),
         ],
-        in_specs=[vmem] * (n_store + 1),
-        out_specs=[vmem] * 2,
-        scratch_shapes=[pltpu.VMEM((n_store,) + gathered[0].shape, bf16)],
+        in_specs=[vmem] * (n_store + 1) + [pl.BlockSpec(memory_space=pl.ANY)],
+        out_specs=[vmem] * 3,
+        scratch_shapes=[pltpu.VMEM((n_store,) + packed.shape, bf16), pltpu.SemaphoreType.DMA],
         compiler_params=pltpu.CompilerParams(vmem_limit_bytes=24 * 2**20),
         name="grads",
-    )(*gathered, slab)
-
-
-def scores(grads, slab, n_layer, k, pieces=1, after=()):
-    rows, features = slab.shape
-    block = rows // n_layer
+    )(*gathered, slab, in_hbm(store))
+
+
+def scores(grads, slab, store, n_layer, k, pieces=1, after=()):
+    block, features = slab.shape
     queries = grads.shape[0]
     vmem = pl.BlockSpec(memory_space=pltpu.VMEM)
+    piece = jax.ShapeDtypeStruct((queries // pieces, block), bf16 if k % 2 else f32)
+    following = [jax.ShapeDtypeStruct(slab.shape, bf16)] if k else []
     return pl.pallas_call(
-        functools.partial(scores_kernel, k, skip=len(after)),
-        out_shape=[jax.ShapeDtypeStruct((queries // pieces, block), bf16 if k % 2 else f32)] * pieces,
-        in_specs=[vmem] * 2 + [pl.BlockSpec(memory_space=pl.ANY)] * len(after),
-        out_specs=[vmem] * pieces,
+        functools.partial(scores_kernel, n_layer, k, pieces),
+        out_shape=[piece] * pieces + following,
+        in_specs=[vmem] * 2 + [pl.BlockSpec(memory_space=pl.ANY)] * (1 + len(after)),
+        out_specs=[vmem] * (pieces + len(following)),
+        scratch_shapes=[pltpu.SemaphoreType.DMA] * len(following),
         compiler_params=pltpu.CompilerParams(vmem_limit_bytes=24 * 2**20),
         cost_estimate=pl.CostEstimate(
             flops=2 * queries * block * features,
-            bytes_accessed=2 * (queries + block) * features,
+            bytes_accessed=2 * (queries + 2 * block) * features,
             transcendentals=0,
         ),
         name="scores",
-    )(grads, slab, *after)
+    )(grads, slab, in_hbm(store), *after)
 
 
 def on_device(n_store, n_layer, hidden, cotangent, lengths, norm_gain, in_proj, out_proj, store):
@@ -380,19 +399,20 @@
         in_proj[0],
         out_proj[0],
     )
-    gathered = [packed] + [swap(packed, "store", n_store, k) for k in store_order(n_store)]
-    slab = fetch(packed, store[0], n_layer)
-    grads, partial = grads_and_scores(gathered, slab, n_store, n_layer, n_layer - 1)
+    rows = store[0]
+    slab = fetch(packed, rows, n_layer, n_layer - 1)
+    grads, partial, slab = grads_and_scores(packed, slab, rows, n_store, n_layer, n_layer - 1)
     crossed = []
     for k in reversed(range(2, n_layer, 2)):
         if k < n_layer - 2:
-            (partial,) = scores(grads, slab, n_layer, k + 1)
+            partial, slab = scores(grads, slab, rows, n_layer, k + 1)
         other = swap(partial, "layer", n_layer, 1)
-        (mine,) = scores(grads, slab, n_layer, k)
+        mine, slab = scores(grads, slab, rows, n_layer, k)
         joined = (mine + other.astype(f32)).astype(bf16)
         crossed.append(swap(joined, "layer", n_layer, k))
-    near = [swap(x, "layer", n_layer, 1) for x in scores(grads, slab, n_layer, 1, 2, [joined])]
-    (total,) = scores(grads, slab, n_layer, 0)
+    *near, slab = scores(grads, slab, rows, n_layer, 1, 2, [joined])
+    (total,) = scores(grads, slab, rows, n_layer, 0)
+    near = [swap(x, "layer", n_layer, 1) for x in near]
     total = total + jnp.concatenate(near, axis=0).astype(f32)
     for x in crossed:
         total = total + x.astype(f32)

time: 23.6 us -> 26.6 us (1.13)
  Pallas kernels: 11.8 us -> 13.9 us
  starting transfers between devices: 8.09 us -> 9.22 us
  waiting for transfers between devices: 2.77 us -> 2.43 us
    ppermute x0 -> x3, starting transfers between devices: none -> 7.01 us  [grads_and_scores(): gathered.append(lax.ppermute(packed, 'store', pairs))]
    ppermute x7 -> x4, starting transfers between devices: 8.09 us -> 2.2 us  [swap(): return lax.ppermute(x, axis, pairs)]
    ppermute x7 -> x4, waiting for transfers between devices: 2.77 us -> 0.17 us  [swap(): return lax.ppermute(x, axis, pairs)]
    ppermute x0 -> x3, waiting for transfers between devices: none -> 2.26 us  [grads_and_scores(): gathered.append(lax.ppermute(packed, 'store', pairs))]
    pallas_call x5, Pallas kernels: 6.85 us -> 9.01 us  [the longest x3 4.87 us: scores(): pl.pallas_call(functools.partial(scores_kernel, n_layer, k, pieces), out_...]
  transfers between devices with their start and end apart: 7 -> 7, of which waited for: 5 -> 3; matrix products, arithmetic and copies ran while one was open for 0% -> 0% of each run, Pallas kernels for 24% -> 24%
where the time goes in v18:
time: 26.6 us; the launch traced here: 26.4 us
  Pallas kernels  13.9 us (52%)
  starting transfers between devices  9.22 us (35%)
  waiting for transfers between devices  2.43 us (9%)
  other arithmetic  0.71 us (3%)
    ppermute x3, starting transfers between devices, grads_and_scores(): gathered.append(lax.ppermute(packed, 'store', pairs))  7.01 us
    pallas_call x1, Pallas kernels, factors(): pl.pallas_call(factors_kernel, out_shape=jax.ShapeDtypeStruct((rows, 2 *...  4.92 us
    pallas_call x3, Pallas kernels, scores(): pl.pallas_call(functools.partial(scores_kernel, n_layer, k, pieces), out_...  4.87 us
    pallas_call x1, Pallas kernels, grads_and_scores(): pl.pallas_call(functools.partial(grads_kernel, n_store, n_layer, queries...  2.59 us
    ppermute x3, waiting for transfers between devices, grads_and_scores(): gathered.append(lax.ppermute(packed, 'store', pairs))  2.26 us
    ppermute x4, starting transfers between devices, swap(): return lax.ppermute(x, axis, pairs)  2.2 us
    pallas_call x1, Pallas kernels, fetch(): pl.pallas_call(functools.partial(fetch_kernel, n_layer, k), out_shape=jax...  1.55 us
    transpose x1, other arithmetic, on_device(): return total.T  0.69 us
  transfers between devices with their start and end apart: 7, of which 3 were waited for; matrix products, arithmetic and copies ran while one was open for 0% of the time, Pallas kernels for 24%

profile of v18, /device:TPU:0, one launch (start us, length us, event | category | flops | bytes accessed | tf_op | source)
XLA Modules:
  0.0 26.4 jit_solution(10809821961651836828)
XLA Ops:
  0.0 4.9 %factors.1.after.refs_0_ = bf16[288,128]{1,0:T(8,128)(2,1)S(1)} custom-call(s32[36]{0:T(128)} %hbm_lengths.1, bf16[288,8192]{1,0:T(8,128)(2,1)} %bitcast.12, bf16[288,1024]{1,0:T(8,128)(2,1)} %bitcast.14, bf16[1,8192]{1,0:T(2,128)(2,1)} %hbm_gain.1, bf16[64,8192]{1,0:T(8,128)(2,1)} %bitcast.13, bf16[64,1024]{1,0:T(8,128)(2,1)} %bitcast.15), custom_call_target="tpu_custom_call" | custom-call | tf_op jit(solution)/shard_map/factors/pallas_call | solution.py:159
  4.9 3.1 %collective-permute-start.2 = (bf16[288,128]{1,0:T(8,128)(2,1)S(1)}, bf16[288,128]{1,0:T(8,128)(2,1)S(1)}, u32[]{:S(2)}, u32[]{:S(2)}) collective-permute-start(bf16[288,128]{1,0:T(8,128)(2,1)S(1)} %factors.1.after.refs_0_), channel_id=1, source_target_pairs={{12,0},{0,4},{4,8},{8,12},{13,1},{1,5},{5,9},{9,13},{14,2},{2,6},{... | collective-permute-start | bytes 221192 | tf_op jit(solution)/shard_map/ppermute | solution.py:353
  8.0 2.6 %collective-permute-start.1 = (bf16[288,128]{1,0:T(8,128)(2,1)S(1)}, bf16[288,128]{1,0:T(8,128)(2,1)S(1)}, u32[]{:S(2)}, u32[]{:S(2)}) collective-permute-start(bf16[288,128]{1,0:T(8,128)(2,1)S(1)} %factors.1.after.refs_0_), channel_id=1, source_target_pairs={{8,0},{12,4},{0,8},{4,12},{9,1},{13,5},{1,9},{5,13},{10,2},{14,6},... | collective-permute-start | bytes 221192 | tf_op jit(solution)/shard_map/ppermute | solution.py:353
  10.6 1.3 %collective-permute-start = (bf16[288,128]{1,0:T(8,128)(2,1)S(1)}, bf16[288,128]{1,0:T(8,128)(2,1)S(1)}, u32[]{:S(2)}, u32[]{:S(2)}) collective-permute-start(bf16[288,128]{1,0:T(8,128)(2,1)S(1)} %factors.1.after.refs_0_), channel_id=1, source_target_pairs={{4,0},{8,4},{12,8},{0,12},{5,1},{9,5},{13,9},{1,13},{6,2},{10,6},{... | collective-permute-start | bytes 221192 | tf_op jit(solution)/shard_map/ppermute | solution.py:353
  11.9 1.6 %fetch.1.refs_4_ = bf16[240,4096]{1,0:T(8,128)(2,1)S(1)} custom-call(bf16[288,128]{1,0:T(8,128)(2,1)S(1)} %factors.1.after.refs_0_, bf16[960,4096]{1,0:T(8,128)(2,1)} %bitcast.7), custom_call_target="tpu_custom_call" | custom-call | bytes 1966080 | tf_op jit(solution)/shard_map/fetch/pallas_call | solution.py:196
  13.5 0.0 collective-permute-done.2.refs_3_
  13.5 2.0 %collective-permute-done.1.refs_2_ = bf16[288,128]{1,0:T(8,128)(2,1)S(1)} collective-permute-done((bf16[288,128]{1,0:T(8,128)(2,1)S(1)}, bf16[288,128]{1,0:T(8,128)(2,1)S(1)}, u32[]{:S(2)}, u32[]{:S(2)}) %collective-permute-start.1) | collective-permute-done | bytes 73760 | tf_op jit(solution)/shard_map/ppermute | solution.py:353
  15.6 0.2 collective-permute-done.refs_1_
  15.8 2.6 %grads.1 = (bf16[144,4096]{1,0:T(8,128)(2,1)S(1)}, bf16[144,240]{1,0:T(8,128)(2,1)S(1)}, bf16[240,4096]{1,0:T(8,128)(2,1)S(1)}) custom-call(bf16[288,128]{1,0:T(8,128)(2,1)S(1)} %factors.1.after.refs_0_, bf16[288,128]{1,0:T(8,128)(2,1)S(1)} %collective-permute-done.refs_1_, bf16[288,128]{1,0:T(8,128)(2,1)S(1)} %collective-permute-done.1.refs_2_, ...), custom_call_target="tpu_custom_call" | custom-call | tf_op jit(solution)/shard_map/grads/pallas_call | solution.py:355
  18.4 0.1 collective-permute-start.3
  18.5 2.1 %scores.3 = (f32[144,240]{1,0:T(8,128)S(1)}, bf16[240,4096]{1,0:T(8,128)(2,1)S(1)}) custom-call(bf16[144,4096]{1,0:T(8,128)(2,1)S(1)} %get-tuple-element.13.grads, bf16[240,4096]{1,0:T(8,128)(2,1)S(1)} %get-tuple-element.14.slab, bf16[960,4096]{1,0:T(8,128)(2,1)} %bitcast.9), custom_call_target="tpu_custom_call" | custom-call | flops 283115520 | bytes 5111808 | tf_op jit(solution)/shard_map/scores/pallas_call | solution.py:376
  20.5 0.0 collective-permute-done.3
  20.6 1.6 %collective-permute-start.6 = (bf16[144,240]{1,0:T(8,128)(2,1)S(1)}, bf16[144,240]{1,0:T(8,128)(2,1)S(1)}, u32[]{:S(2)}, u32[]{:S(2)}) collective-permute-start(bf16[144,240]{1,0:T(8,128)(2,1)S(1)} %add_convert_fusion.refs_0_), channel_id=1, source_target_pairs={{0,2},{1,3},{2,0},{3,1},{4,6},{5,7},{6,4},{7,5},{8,10},{9,11},{10,... | collective-permute-start | bytes 207368 | tf_op jit(solution)/shard_map/ppermute | solution.py:344
  22.1 2.1 %scores.4 = (bf16[72,240]{1,0:T(8,128)(2,1)S(1)}, bf16[72,240]{1,0:T(8,128)(2,1)S(1)}, bf16[240,4096]{1,0:T(8,128)(2,1)S(1)}) custom-call(bf16[144,4096]{1,0:T(8,128)(2,1)S(1)} %get-tuple-element.13.grads, bf16[240,4096]{1,0:T(8,128)(2,1)S(1)} %get-tuple-element.15.slab, bf16[960,4096]{1,0:T(8,128)(2,1)} %bitcast.10, ...), custom_call_target="tpu_custom_call" | custom-call | flops 283115520 | bytes 5111808 | tf_op jit(solution)/shard_map/scores/pallas_call | solution.py:376
  24.2 0.3 %collective-permute-start.4 = (bf16[72,240]{1,0:T(8,128)(2,1)S(1)}, bf16[72,240]{1,0:T(8,128)(2,1)S(1)}, u32[]{:S(2)}, u32[]{:S(2)}) collective-permute-start(bf16[72,240]{1,0:T(8,128)(2,1)S(1)} %get-tuple-element.19), channel_id=1, source_target_pairs={{0,1},{1,0},{2,3},{3,2},{4,5},{5,4},{6,7},{7,6},{8,9},{9,8},{10,11... | collective-permute-start | bytes 103688 | tf_op jit(solution)/shard_map/ppermute | solution.py:344
  24.5 0.3 %collective-permute-start.5 = (bf16[72,240]{1,0:T(8,128)(2,1)S(1)}, bf16[72,240]{1,0:T(8,128)(2,1)S(1)}, u32[]{:S(2)}, u32[]{:S(2)}) collective-permute-start(bf16[72,240]{1,0:T(8,128)(2,1)S(1)} %get-tuple-element.20), channel_id=1, source_target_pairs={{0,1},{1,0},{2,3},{3,2},{4,5},{5,4},{6,7},{7,6},{8,9},{9,8},{10,11... | collective-permute-start | bytes 103688 | tf_op jit(solution)/shard_map/ppermute | solution.py:344
  24.8 0.7 %scores.5 = f32[144,240]{1,0:T(8,128)S(1)} custom-call(bf16[144,4096]{1,0:T(8,128)(2,1)S(1)} %get-tuple-element.13.grads, bf16[240,4096]{1,0:T(8,128)(2,1)S(1)} %get-tuple-element.18.slab, bf16[960,4096]{1,0:T(8,128)(2,1)} %bitcast.11), custom_call_target="tpu_custom_call" | custom-call | flops 283115520 | bytes 5111808 | tf_op jit(solution)/shard_map/scores/pallas_call | solution.py:376
  25.5 0.0 collective-permute-done.4
  25.5 0.2 collective-permute-done.5
  25.7 0.0 collective-permute-done.6
  25.7 0.7 %add_bitcast_fusion = f32[240,144]{0,1:T(8,128)} fusion(bf16[144,240]{1,0:T(8,128)(2,1)S(1)} %collective-permute-done.6, f32[144,240]{1,0:T(8,128)S(1)} %scores.5, bf16[72,240]{1,0:T(8,128)(2,1)S(1)} %collective-permute-done.5, bf16[72,240]{1,0:T(8,128)(2,1)S(1)} %collective-permute-done.4), kind=kLoop, calls=%fused_computation | loop fusion | flops 241920 | bytes 414720 | tf_op jit(solution)/shard_map/transpose | solution.py:419
  (1 shorter events, 0.0 us)
Async XLA Ops:
  4.9 8.6 %collective-permute-start.2 = (bf16[288,128]{1,0:T(8,128)(2,1)S(1)}, bf16[288,128]{1,0:T(8,128)(2,1)S(1)}, u32[]{:S(2)}, u32[]{:S(2)}) collective-permute-start(bf16[288,128]{1,0:T(8,128)(2,1)S(1)} %factors.1.after.refs_0_), channel_id=1, source_target_pairs={{12,0},{0,4},{4,8},{8,12},{13,1},{1,5},{5,9},{9,13},{14,2},{2,6},{... | collective-permute-start | bytes 221192 | tf_op jit(solution)/shard_map/ppermute | solution.py:353
  8.0 7.5 %collective-permute-start.1 = (bf16[288,128]{1,0:T(8,128)(2,1)S(1)}, bf16[288,128]{1,0:T(8,128)(2,1)S(1)}, u32[]{:S(2)}, u32[]{:S(2)}) collective-permute-start(bf16[288,128]{1,0:T(8,128)(2,1)S(1)} %factors.1.after.refs_0_), channel_id=1, source_target_pairs={{8,0},{12,4},{0,8},{4,12},{9,1},{13,5},{1,9},{5,13},{10,2},{14,6},... | collective-permute-start | bytes 221192 | tf_op jit(solution)/shard_map/ppermute | solution.py:353
  10.6 5.2 %collective-permute-start = (bf16[288,128]{1,0:T(8,128)(2,1)S(1)}, bf16[288,128]{1,0:T(8,128)(2,1)S(1)}, u32[]{:S(2)}, u32[]{:S(2)}) collective-permute-start(bf16[288,128]{1,0:T(8,128)(2,1)S(1)} %factors.1.after.refs_0_), channel_id=1, source_target_pairs={{4,0},{8,4},{12,8},{0,12},{5,1},{9,5},{13,9},{1,13},{6,2},{10,6},{... | collective-permute-start | bytes 221192 | tf_op jit(solution)/shard_map/ppermute | solution.py:353
  18.4 2.2 %collective-permute-start.3 = (bf16[144,240]{1,0:T(8,128)(2,1)S(1)}, bf16[144,240]{1,0:T(8,128)(2,1)S(1)}, u32[]{:S(2)}, u32[]{:S(2)}) collective-permute-start(bf16[144,240]{1,0:T(8,128)(2,1)S(1)} %get-tuple-element.17), channel_id=1, source_target_pairs={{0,1},{1,0},{2,3},{3,2},{4,5},{5,4},{6,7},{7,6},{8,9},{9,8},{10,11... | collective-permute-start | bytes 207368 | tf_op jit(solution)/shard_map/ppermute | solution.py:344
  20.6 5.1 %collective-permute-start.6 = (bf16[144,240]{1,0:T(8,128)(2,1)S(1)}, bf16[144,240]{1,0:T(8,128)(2,1)S(1)}, u32[]{:S(2)}, u32[]{:S(2)}) collective-permute-start(bf16[144,240]{1,0:T(8,128)(2,1)S(1)} %add_convert_fusion.refs_0_), channel_id=1, source_target_pairs={{0,2},{1,3},{2,0},{3,1},{4,6},{5,7},{6,4},{7,5},{8,10},{9,11},{10,... | collective-permute-start | bytes 207368 | tf_op jit(solution)/shard_map/ppermute | solution.py:344
  24.2 1.3 %collective-permute-start.4 = (bf16[72,240]{1,0:T(8,128)(2,1)S(1)}, bf16[72,240]{1,0:T(8,128)(2,1)S(1)}, u32[]{:S(2)}, u32[]{:S(2)}) collective-permute-start(bf16[72,240]{1,0:T(8,128)(2,1)S(1)} %get-tuple-element.19), channel_id=1, source_target_pairs={{0,1},{1,0},{2,3},{3,2},{4,5},{5,4},{6,7},{7,6},{8,9},{9,8},{10,11... | collective-permute-start | bytes 103688 | tf_op jit(solution)/shard_map/ppermute | solution.py:344
  24.5 1.2 %collective-permute-start.5 = (bf16[72,240]{1,0:T(8,128)(2,1)S(1)}, bf16[72,240]{1,0:T(8,128)(2,1)S(1)}, u32[]{:S(2)}, u32[]{:S(2)}) collective-permute-start(bf16[72,240]{1,0:T(8,128)(2,1)S(1)} %get-tuple-element.20), channel_id=1, source_target_pairs={{0,1},{1,0},{2,3},{3,2},{4,5},{5,4},{6,7},{7,6},{8,9},{9,8},{10,11... | collective-permute-start | bytes 103688 | tf_op jit(solution)/shard_map/ppermute | solution.py:344

commit v19 on v17

--- a/solution.py
+++ b/solution.py
@@ -41,13 +41,13 @@
     gain,
     inp,
     outp,
+    weights,
     in_acc,
-    sq_acc,
     out_t,
     sems,
 ):
-    chunks, rows, columns = hidden.shape
-    width = chunks * columns
+    blocks, step, width = hidden.shape
+    rows = blocks * step
     queries = lengths.shape[0]
     full = queries // G * G * S
     half = rows - full
@@ -56,72 +56,19 @@
     def copy(source, target, at):
         return pltpu.make_async_copy(source, target, sems.at[at])
 
-    def pieces(c):
-        cut = pl.ds(pl.multiple_of(c * columns, columns), columns)
-        return [
-            copy(hbm_inp.at[:, cut], inp.at[c], 4 + c),
-            copy(hbm_hidden.at[:, cut], hidden.at[c], 4 + chunks + c),
-        ]
-
-    def start(group):
-        for piece in group:
-            piece.start()
-
-    copy_gain = copy(hbm_gain, gain, 0)
-    early = [copy(hbm_outp, outp, 1), copy(hbm_cot, cot, 2), copy(hbm_lengths, lengths, 3)]
-    copy_gain.start()
-    for c in range(chunks):
-        start(pieces(c))
-    in_acc[...] = jnp.zeros_like(in_acc)
-    sq_acc[...] = jnp.zeros_like(sq_acc)
-    copy_gain.wait()
-
-    @pl.loop(0, chunks)
-    def _(c):
-        for piece in pieces(c):
-            piece.wait()
-
-        @pl.when(c == 0)
-        def _():
-            start(early)
-
-        cut = pl.ds(pl.multiple_of(c * columns, columns), columns)
-        scaled = inp[c].astype(f32) * gain[:, cut].astype(f32)
-        high = scaled.astype(bf16)
-        rest = (scaled - high.astype(f32)).astype(bf16)
-        in_acc[...] += dot_nt(hidden[c], jnp.concatenate([high, rest], axis=0))
-        for r in range(0, rows, 48):
-            wide = hidden[c, r : r + 48, :].astype(f32)
-            square = wide * wide
-            total = square[:, :LANES]
-            for at in range(LANES, columns, LANES):
-                total += square[:, at : at + LANES]
-            sq_acc[r : r + 48, :] += total
-
-    for piece in early:
-        piece.wait()
+    def block_rows(r):
+        at = pl.ds(pl.multiple_of(r * step, step), step)
+        return copy(hbm_hidden.at[at, :], hidden.at[r], 5 + r)
+
+    first = [copy(hbm_outp, outp, 0), copy(hbm_cot, cot, 1)]
+    then = [copy(hbm_gain, gain, 2), copy(hbm_inp, inp, 3), copy(hbm_lengths, lengths, 4)]
+    for piece in first + then + [block_rows(r) for r in range(blocks)]:
+        piece.start()
     odd = lax.rem(lax.axis_index("store"), 2)
     at_full = pl.multiple_of(odd * half, half)
     at_half = pl.multiple_of((1 - odd) * full, half)
-    low_lanes = iota((S, LANES), 1) < R
-    position = iota((S, LANES), 0)
-
-    def in_rows(at, count):
-        sums = in_acc[pl.ds(at, count), :]
-        square = jnp.sum(sq_acc[pl.ds(at, count), :], axis=1, keepdims=True)
-        scale = lax.rsqrt(square * (1.0 / width) + norm_epsilon)
-        factor = (sums + pltpu.roll(sums, R, 1)) * scale
-        return [
-            jnp.where(position < lengths[at // S + q], factor[q * S : (q + 1) * S], 0.0)
-            for q in range(count // S)
-        ]
-
-    def side_by_side(tiles):
-        both = zip(tiles[: len(tiles) // 2], tiles[len(tiles) // 2 :])
-        return jnp.concatenate([jnp.where(low_lanes, x, y) for x, y in both], axis=0)
-
-    packed[:mid, :] = side_by_side(in_rows(at_full, full)).astype(bf16)
-    packed[mid : mid + low, :] = side_by_side(in_rows(at_half, half)).astype(bf16)
+    for piece in first:
+        piece.wait()
 
     whole = dot_nt(outp[...], cot[pl.ds(at_full, full), :])
     for t in range(full // LANES):
@@ -142,6 +89,40 @@
         [part(full // LANES, b)[:, :half] for b in range(B)], axis=1
     ).astype(bf16)
 
+    for piece in then:
+        piece.wait()
+    weights[...] = inp[...] * gain[...]
+
+    @pl.loop(0, blocks)
+    def _(r):
+        block_rows(r).wait()
+        product = dot_nt(hidden[r], weights[...])
+        total = jnp.zeros((step, LANES), f32)
+        for at in range(0, width, LANES):
+            wide = hidden[r, :, at : at + LANES].astype(f32)
+            total += wide * wide
+        mean_square = jnp.sum(total, axis=1, keepdims=True) * (1.0 / width)
+        factor = product * lax.rsqrt(mean_square + norm_epsilon)
+        at = pl.ds(pl.multiple_of(r * step, step), step)
+        in_acc[at, :] = jnp.concatenate([factor, factor], axis=1)
+
+    low_lanes = iota((S, LANES), 1) < R
+    position = iota((S, LANES), 0)
+
+    def in_rows(at, count):
+        factor = in_acc[pl.ds(at, count), :]
+        return [
+            jnp.where(position < lengths[at // S + q], factor[q * S : (q + 1) * S], 0.0)
+            for q in range(count // S)
+        ]
+
+    def side_by_side(tiles):
+        both = zip(tiles[: len(tiles) // 2], tiles[len(tiles) // 2 :])
+        return jnp.concatenate([jnp.where(low_lanes, x, y) for x, y in both], axis=0)
+
+    packed[:mid, :] = side_by_side(in_rows(at_full, full)).astype(bf16)
+    packed[mid : mid + low, :] = side_by_side(in_rows(at_half, half)).astype(bf16)
+
 
 def in_hbm(x):
     return pltpu.with_memory_space_constraint(x, pltpu.HBM)
@@ -149,8 +130,7 @@
 
 def factors(lengths, hidden, cotangent, gain, in_projection, out_projection):
     rows, width = hidden.shape
-    columns = 2048
-    chunks = width // columns
+    blocks = 3
     return pl.pallas_call(
         factors_kernel,
         out_shape=jax.ShapeDtypeStruct((rows, 2 * R), bf16),
@@ -158,15 +138,15 @@
         out_specs=pl.BlockSpec(memory_space=pltpu.VMEM),
         scratch_shapes=[
             pltpu.SMEM(lengths.shape, jnp.int32),
-            pltpu.VMEM((chunks, rows, columns), bf16),
+            pltpu.VMEM((blocks, rows // blocks, width), bf16),
             pltpu.VMEM(cotangent.shape, bf16),
             pltpu.VMEM(gain.shape, bf16),
-            pltpu.VMEM((chunks, R, columns), bf16),
+            pltpu.VMEM(in_projection.shape, bf16),
             pltpu.VMEM(out_projection.shape, bf16),
+            pltpu.VMEM(in_projection.shape, bf16),
             pltpu.VMEM((rows, 2 * R), f32),
-            pltpu.VMEM((rows, LANES), f32),
             pltpu.VMEM((-(-rows // LANES) * R, LANES), f32),
-            pltpu.SemaphoreType.DMA((4 + 2 * chunks,)),
+            pltpu.SemaphoreType.DMA((5 + blocks,)),
         ],
         compiler_params=pltpu.CompilerParams(vmem_limit_bytes=24 * 2**20),
         name="factors",

time: 23.6 us -> 23.1 us (0.979)
  Pallas kernels: 11.8 us -> 11.4 us
    pallas_call x1, Pallas kernels: 4.98 us -> 4.52 us  [factors(): pl.pallas_call(factors_kernel, out_shape=jax.ShapeDtypeStruct((rows, 2 *...]
where the time goes in v19:
time: 23.1 us; the launch traced here: 23 us
  Pallas kernels  11.4 us (49%)
  starting transfers between devices  8.09 us (35%)
  waiting for transfers between devices  2.76 us (12%)
  other arithmetic  0.71 us (3%)
    ppermute x7, starting transfers between devices, swap(): return lax.ppermute(x, axis, pairs)  8.09 us
    pallas_call x1, Pallas kernels, factors(): pl.pallas_call(factors_kernel, out_shape=jax.ShapeDtypeStruct((rows, 2 *...  4.52 us
    pallas_call x1, Pallas kernels, fetch(): pl.pallas_call(functools.partial(fetch_kernel, n_layer), out_shape=jax.Sh...  3.34 us
    ppermute x7, waiting for transfers between devices, swap(): return lax.ppermute(x, axis, pairs)  2.76 us
    pallas_call x3, Pallas kernels, scores(): pl.pallas_call(functools.partial(scores_kernel, k, skip=len(after)), out_...  2.24 us
    pallas_call x1, Pallas kernels, grads_and_scores(): pl.pallas_call(functools.partial(grads_kernel, n_store, queries // n_stor...  1.28 us
    transpose x1, other arithmetic, on_device(): return total.T  0.69 us
  transfers between devices with their start and end apart: 7, of which 5 were waited for; matrix products, arithmetic and copies ran while one was open for 0% of the time, Pallas kernels for 24%

profile of v19, /device:TPU:0, one launch (start us, length us, event | category | flops | bytes accessed | tf_op | source)
XLA Modules:
  0.0 23.0 jit_solution(8729887466952414771)
XLA Ops:
  0.0 4.5 %factors.1.after.refs_0_ = bf16[288,128]{1,0:T(8,128)(2,1)S(1)} custom-call(s32[36]{0:T(128)} %hbm_lengths.1, bf16[288,8192]{1,0:T(8,128)(2,1)} %bitcast.8, bf16[288,1024]{1,0:T(8,128)(2,1)} %bitcast.10, bf16[1,8192]{1,0:T(2,128)(2,1)} %hbm_gain.1, bf16[64,8192]{1,0:T(8,128)(2,1)} %bitcast.9, bf16[64,1024]{1,0:T(8,128)(2,1)} %bitcast.11), custom_call_target="tpu_custom_call" | custom-call | tf_op jit(solution)/shard_map/factors/pallas_call | solution.py:134
  4.5 4.1 %collective-permute-start.2 = (bf16[288,128]{1,0:T(8,128)(2,1)S(1)}, bf16[288,128]{1,0:T(8,128)(2,1)S(1)}, u32[]{:S(2)}, u32[]{:S(2)}) collective-permute-start(bf16[288,128]{1,0:T(8,128)(2,1)S(1)} %factors.1.after.refs_0_), channel_id=1, source_target_pairs={{0,8},{4,12},{8,0},{12,4},{1,9},{5,13},{9,1},{13,5},{2,10},{6,14},... | collective-permute-start | bytes 221192 | tf_op jit(solution)/shard_map/ppermute | solution.py:312
  8.6 1.4 %collective-permute-start.1 = (bf16[288,128]{1,0:T(8,128)(2,1)S(1)}, bf16[288,128]{1,0:T(8,128)(2,1)S(1)}, u32[]{:S(2)}, u32[]{:S(2)}) collective-permute-start(bf16[288,128]{1,0:T(8,128)(2,1)S(1)} %factors.1.after.refs_0_), channel_id=1, source_target_pairs={{0,12},{4,8},{8,4},{12,0},{1,13},{5,9},{9,5},{13,1},{2,14},{6,10},... | collective-permute-start | bytes 221192 | tf_op jit(solution)/shard_map/ppermute | solution.py:312
  10.0 0.2 collective-permute-start
  10.2 3.3 %fetch.1.refs_4_.slab = bf16[960,4096]{1,0:T(8,128)(2,1)S(1)} custom-call(bf16[288,128]{1,0:T(8,128)(2,1)S(1)} %factors.1.after.refs_0_, bf16[960,4096]{1,0:T(8,128)(2,1)} %bitcast.7), custom_call_target="tpu_custom_call" | custom-call | bytes 7864320 | tf_op jit(solution)/shard_map/fetch/pallas_call | solution.py:172
  13.6 0.0 collective-permute-done.2.refs_3_
  13.6 1.5 %collective-permute-done.1.refs_2_ = bf16[288,128]{1,0:T(8,128)(2,1)S(1)} collective-permute-done((bf16[288,128]{1,0:T(8,128)(2,1)S(1)}, bf16[288,128]{1,0:T(8,128)(2,1)S(1)}, u32[]{:S(2)}, u32[]{:S(2)}) %collective-permute-start.1) | collective-permute-done | bytes 73760 | tf_op jit(solution)/shard_map/ppermute | solution.py:312
  15.1 0.2 collective-permute-done.refs_1_
  15.3 1.3 %grads.1 = (bf16[144,4096]{1,0:T(8,128)(2,1)S(1)}, bf16[144,240]{1,0:T(8,128)(2,1)S(1)}) custom-call(bf16[288,128]{1,0:T(8,128)(2,1)S(1)} %factors.1.after.refs_0_, bf16[288,128]{1,0:T(8,128)(2,1)S(1)} %collective-permute-done.refs_1_, bf16[288,128]{1,0:T(8,128)(2,1)S(1)} %collective-permute-done.1.refs_2_, ...), custom_call_target="tpu_custom_call" | custom-call | tf_op jit(solution)/shard_map/grads/pallas_call | solution.py:319
  16.5 0.1 collective-permute-start.3
  16.6 0.7 %scores.4 = f32[144,240]{1,0:T(8,128)S(1)} custom-call(bf16[144,4096]{1,0:T(8,128)(2,1)S(1)} %get-tuple-element.9.grads, bf16[960,4096]{1,0:T(8,128)(2,1)S(1)} %fetch.1.refs_4_.slab), custom_call_target="tpu_custom_call" | custom-call | flops 283115520 | bytes 3145728 | tf_op jit(solution)/shard_map/scores/pallas_call | solution.py:338
  17.4 0.5 %collective-permute-done.3 = bf16[144,240]{1,0:T(8,128)(2,1)S(1)} collective-permute-done((bf16[144,240]{1,0:T(8,128)(2,1)S(1)}, bf16[144,240]{1,0:T(8,128)(2,1)S(1)}, u32[]{:S(2)}, u32[]{:S(2)}) %collective-permute-start.3) | collective-permute-done | bytes 69152 | tf_op jit(solution)/shard_map/ppermute | solution.py:312
  17.9 1.8 %collective-permute-start.6 = (bf16[144,240]{1,0:T(8,128)(2,1)S(1)}, bf16[144,240]{1,0:T(8,128)(2,1)S(1)}, u32[]{:S(2)}, u32[]{:S(2)}) collective-permute-start(bf16[144,240]{1,0:T(8,128)(2,1)S(1)} %add_convert_fusion.refs_0_), channel_id=1, source_target_pairs={{0,2},{1,3},{2,0},{3,1},{4,6},{5,7},{6,4},{7,5},{8,10},{9,11},{10,... | collective-permute-start | bytes 207368 | tf_op jit(solution)/shard_map/ppermute | solution.py:312
  19.7 0.7 %scores.5 = (bf16[72,240]{1,0:T(8,128)(2,1)S(1)}, bf16[72,240]{1,0:T(8,128)(2,1)S(1)}) custom-call(bf16[144,4096]{1,0:T(8,128)(2,1)S(1)} %get-tuple-element.9.grads, bf16[960,4096]{1,0:T(8,128)(2,1)S(1)} %fetch.1.refs_4_.slab, bf16[144,240]{1,0:T(8,128)(2,1)S(1)} %add_convert_fusion.refs_0_), custom_call_target="tpu_custom_call" | custom-call | flops 283115520 | bytes 3145728 | tf_op jit(solution)/shard_map/scores/pallas_call | solution.py:338
  20.4 0.1 collective-permute-start.4
  20.5 0.5 %collective-permute-start.5 = (bf16[72,240]{1,0:T(8,128)(2,1)S(1)}, bf16[72,240]{1,0:T(8,128)(2,1)S(1)}, u32[]{:S(2)}, u32[]{:S(2)}) collective-permute-start(bf16[72,240]{1,0:T(8,128)(2,1)S(1)} %get-tuple-element.12), channel_id=1, source_target_pairs={{0,1},{1,0},{2,3},{3,2},{4,5},{5,4},{6,7},{7,6},{8,9},{9,8},{10,11... | collective-permute-start | bytes 103688 | tf_op jit(solution)/shard_map/ppermute | solution.py:312
  21.0 0.7 %scores.3 = f32[144,240]{1,0:T(8,128)S(1)} custom-call(bf16[144,4096]{1,0:T(8,128)(2,1)S(1)} %get-tuple-element.9.grads, bf16[960,4096]{1,0:T(8,128)(2,1)S(1)} %fetch.1.refs_4_.slab), custom_call_target="tpu_custom_call" | custom-call | flops 283115520 | bytes 3145728 | tf_op jit(solution)/shard_map/scores/pallas_call | solution.py:338
  21.7 0.0 collective-permute-done.4
  21.8 0.1 collective-permute-done.5
  21.9 0.5 %collective-permute-done.6 = bf16[144,240]{1,0:T(8,128)(2,1)S(1)} collective-permute-done((bf16[144,240]{1,0:T(8,128)(2,1)S(1)}, bf16[144,240]{1,0:T(8,128)(2,1)S(1)}, u32[]{:S(2)}, u32[]{:S(2)}) %collective-permute-start.6) | collective-permute-done | bytes 69152 | tf_op jit(solution)/shard_map/ppermute | solution.py:312
  22.3 0.7 %add_bitcast_fusion = f32[240,144]{0,1:T(8,128)} fusion(bf16[144,240]{1,0:T(8,128)(2,1)S(1)} %collective-permute-done.6, f32[144,240]{1,0:T(8,128)S(1)} %scores.3, bf16[72,240]{1,0:T(8,128)(2,1)S(1)} %collective-permute-done.5, bf16[72,240]{1,0:T(8,128)(2,1)S(1)} %collective-permute-done.4), kind=kLoop, calls=%fused_computation | loop fusion | flops 241920 | bytes 414720 | tf_op jit(solution)/shard_map/transpose | solution.py:379
  (1 shorter events, 0.0 us)
Async XLA Ops:
  4.5 9.0 %collective-permute-start.2 = (bf16[288,128]{1,0:T(8,128)(2,1)S(1)}, bf16[288,128]{1,0:T(8,128)(2,1)S(1)}, u32[]{:S(2)}, u32[]{:S(2)}) collective-permute-start(bf16[288,128]{1,0:T(8,128)(2,1)S(1)} %factors.1.after.refs_0_), channel_id=1, source_target_pairs={{0,8},{4,12},{8,0},{12,4},{1,9},{5,13},{9,1},{13,5},{2,10},{6,14},... | collective-permute-start | bytes 221192 | tf_op jit(solution)/shard_map/ppermute | solution.py:312
  8.6 6.5 %collective-permute-start.1 = (bf16[288,128]{1,0:T(8,128)(2,1)S(1)}, bf16[288,128]{1,0:T(8,128)(2,1)S(1)}, u32[]{:S(2)}, u32[]{:S(2)}) collective-permute-start(bf16[288,128]{1,0:T(8,128)(2,1)S(1)} %factors.1.after.refs_0_), channel_id=1, source_target_pairs={{0,12},{4,8},{8,4},{12,0},{1,13},{5,9},{9,5},{13,1},{2,14},{6,10},... | collective-permute-start | bytes 221192 | tf_op jit(solution)/shard_map/ppermute | solution.py:312
  10.0 5.3 %collective-permute-start = (bf16[288,128]{1,0:T(8,128)(2,1)S(1)}, bf16[288,128]{1,0:T(8,128)(2,1)S(1)}, u32[]{:S(2)}, u32[]{:S(2)}) collective-permute-start(bf16[288,128]{1,0:T(8,128)(2,1)S(1)} %factors.1.after.refs_0_), channel_id=1, source_target_pairs={{0,4},{4,0},{8,12},{12,8},{1,5},{5,1},{9,13},{13,9},{2,6},{6,2},{1... | collective-permute-start | bytes 221192 | tf_op jit(solution)/shard_map/ppermute | solution.py:312
  16.5 1.3 %collective-permute-start.3 = (bf16[144,240]{1,0:T(8,128)(2,1)S(1)}, bf16[144,240]{1,0:T(8,128)(2,1)S(1)}, u32[]{:S(2)}, u32[]{:S(2)}) collective-permute-start(bf16[144,240]{1,0:T(8,128)(2,1)S(1)} %get-tuple-element.10), channel_id=1, source_target_pairs={{0,1},{1,0},{2,3},{3,2},{4,5},{5,4},{6,7},{7,6},{8,9},{9,8},{10,11... | collective-permute-start | bytes 207368 | tf_op jit(solution)/shard_map/ppermute | solution.py:312
  17.9 4.4 %collective-permute-start.6 = (bf16[144,240]{1,0:T(8,128)(2,1)S(1)}, bf16[144,240]{1,0:T(8,128)(2,1)S(1)}, u32[]{:S(2)}, u32[]{:S(2)}) collective-permute-start(bf16[144,240]{1,0:T(8,128)(2,1)S(1)} %add_convert_fusion.refs_0_), channel_id=1, source_target_pairs={{0,2},{1,3},{2,0},{3,1},{4,6},{5,7},{6,4},{7,5},{8,10},{9,11},{10,... | collective-permute-start | bytes 207368 | tf_op jit(solution)/shard_map/ppermute | solution.py:312
  20.4 1.3 %collective-permute-start.4 = (bf16[72,240]{1,0:T(8,128)(2,1)S(1)}, bf16[72,240]{1,0:T(8,128)(2,1)S(1)}, u32[]{:S(2)}, u32[]{:S(2)}) collective-permute-start(bf16[72,240]{1,0:T(8,128)(2,1)S(1)} %get-tuple-element.11), channel_id=1, source_target_pairs={{0,1},{1,0},{2,3},{3,2},{4,5},{5,4},{6,7},{7,6},{8,9},{9,8},{10,11... | collective-permute-start | bytes 103688 | tf_op jit(solution)/shard_map/ppermute | solution.py:312
  20.5 1.4 %collective-permute-start.5 = (bf16[72,240]{1,0:T(8,128)(2,1)S(1)}, bf16[72,240]{1,0:T(8,128)(2,1)S(1)}, u32[]{:S(2)}, u32[]{:S(2)}) collective-permute-start(bf16[72,240]{1,0:T(8,128)(2,1)S(1)} %get-tuple-element.12), channel_id=1, source_target_pairs={{0,1},{1,0},{2,3},{3,2},{4,5},{5,4},{6,7},{7,6},{8,9},{9,8},{10,11... | collective-permute-start | bytes 103688 | tf_op jit(solution)/shard_map/ppermute | solution.py:312

commit v20 on v19

--- a/solution.py
+++ b/solution.py
@@ -62,13 +62,18 @@
 
     first = [copy(hbm_outp, outp, 0), copy(hbm_cot, cot, 1)]
     then = [copy(hbm_gain, gain, 2), copy(hbm_inp, inp, 3), copy(hbm_lengths, lengths, 4)]
-    for piece in first + then + [block_rows(r) for r in range(blocks)]:
+    for piece in first + then + [block_rows(0)]:
         piece.start()
     odd = lax.rem(lax.axis_index("store"), 2)
     at_full = pl.multiple_of(odd * half, half)
     at_half = pl.multiple_of((1 - odd) * full, half)
     for piece in first:
         piece.wait()
+
+    @pl.when(odd >= 0)
+    def _():
+        for r in range(1, blocks):
+            block_rows(r).start()
 
     whole = dot_nt(outp[...], cot[pl.ds(at_full, full), :])
     for t in range(full // LANES):
@@ -271,16 +276,19 @@
             ).astype(bf16)
 
 
-def store_order(n):
-    return [1, 3, 2] if n == 4 else list(range(1, n))
+def source(to, away, n):
+    if n != 4:
+        return (to + away) % n
+    place = ((to ^ to // 2) + away) % n
+    return place ^ place // 2
 
 
 def grads_kernel(n_store, full_groups, k, *refs):
     gathered = refs[:n_store]
     slab, grads, out, shards = refs[n_store:]
     me_store = lax.axis_index("store")
-    for block, away in zip(gathered, [0] + store_order(n_store)):
-        shards[partner(me_store, away, n_store)] = block[...]
+    for away, block in enumerate(gathered):
+        shards[source(me_store, away, n_store)] = block[...]
     four = 4 * (full_groups * G + H)
     if n_store == 4:
         build_grads(shards, 0, 0, full_groups, grads)
@@ -360,7 +368,10 @@
         in_proj[0],
         out_proj[0],
     )
-    gathered = [packed] + [swap(packed, "store", n_store, k) for k in store_order(n_store)]
+    gathered = [packed]
+    for away in range(1, n_store):
+        pairs = [(source(to, away, n_store), to) for to in range(n_store)]
+        gathered.append(lax.ppermute(packed, "store", pairs))
     slab = fetch(packed, store[0], n_layer)
     grads, partial = grads_and_scores(gathered, slab, n_store, n_layer, n_layer - 1)
     crossed = []

time: 23.1 us -> 23 us (level)
  waiting for transfers between devices: 2.76 us -> 1.3 us
  starting transfers between devices: 8.09 us -> 9.33 us
    ppermute x0 -> x3, starting transfers between devices: none -> 7.12 us  [on_device(): gathered.append(lax.ppermute(packed, 'store', pairs))]
    ppermute x7 -> x4, starting transfers between devices: 8.09 us -> 2.2 us  [swap(): return lax.ppermute(x, axis, pairs)]
    ppermute x7 -> x4, waiting for transfers between devices: 2.76 us -> 1.27 us  [swap(): return lax.ppermute(x, axis, pairs)]
  transfers between devices with their start and end apart: 7 -> 7, of which waited for: 5 -> 3; matrix products, arithmetic and copies ran while one was open for 0% -> 0% of each run, Pallas kernels for 24% -> 24%
where the time goes in v20:
time: 23 us; the launch traced here: 22.8 us
  Pallas kernels  11.4 us (50%)
  starting transfers between devices  9.33 us (41%)
  waiting for transfers between devices  1.3 us (6%)
  other arithmetic  0.71 us (3%)
    ppermute x3, starting transfers between devices, on_device(): gathered.append(lax.ppermute(packed, 'store', pairs))  7.12 us
    pallas_call x1, Pallas kernels, factors(): pl.pallas_call(factors_kernel, out_shape=jax.ShapeDtypeStruct((rows, 2 *...  4.52 us
    pallas_call x1, Pallas kernels, fetch(): pl.pallas_call(functools.partial(fetch_kernel, n_layer), out_shape=jax.Sh...  3.34 us
    pallas_call x3, Pallas kernels, scores(): pl.pallas_call(functools.partial(scores_kernel, k, skip=len(after)), out_...  2.24 us
    ppermute x4, starting transfers between devices, swap(): return lax.ppermute(x, axis, pairs)  2.2 us
    pallas_call x1, Pallas kernels, grads_and_scores(): pl.pallas_call(functools.partial(grads_kernel, n_store, queries // n_stor...  1.29 us
    ppermute x4, waiting for transfers between devices, swap(): return lax.ppermute(x, axis, pairs)  1.27 us
    transpose x1, other arithmetic, on_device(): return total.T  0.69 us
  transfers between devices with their start and end apart: 7, of which 3 were waited for; matrix products, arithmetic and copies ran while one was open for 0% of the time, Pallas kernels for 24%

profile of v20, /device:TPU:0, one launch (start us, length us, event | category | flops | bytes accessed | tf_op | source)
XLA Modules:
  0.0 22.8 jit_solution(13928381493295450617)
XLA Ops:
  0.0 4.5 %factors.1.after.refs_0_ = bf16[288,128]{1,0:T(8,128)(2,1)S(1)} custom-call(s32[36]{0:T(128)} %hbm_lengths.1, bf16[288,8192]{1,0:T(8,128)(2,1)} %bitcast.8, bf16[288,1024]{1,0:T(8,128)(2,1)} %bitcast.10, bf16[1,8192]{1,0:T(2,128)(2,1)} %hbm_gain.1, bf16[64,8192]{1,0:T(8,128)(2,1)} %bitcast.9, bf16[64,1024]{1,0:T(8,128)(2,1)} %bitcast.11), custom_call_target="tpu_custom_call" | custom-call | tf_op jit(solution)/shard_map/factors/pallas_call | solution.py:139
  4.5 3.1 %collective-permute-start.2 = (bf16[288,128]{1,0:T(8,128)(2,1)S(1)}, bf16[288,128]{1,0:T(8,128)(2,1)S(1)}, u32[]{:S(2)}, u32[]{:S(2)}) collective-permute-start(bf16[288,128]{1,0:T(8,128)(2,1)S(1)} %factors.1.after.refs_0_), channel_id=1, source_target_pairs={{8,0},{0,4},{12,8},{4,12},{9,1},{1,5},{13,9},{5,13},{10,2},{2,6},{... | collective-permute-start | bytes 221192 | tf_op jit(solution)/shard_map/ppermute | solution.py:374
  7.6 2.5 %collective-permute-start.1 = (bf16[288,128]{1,0:T(8,128)(2,1)S(1)}, bf16[288,128]{1,0:T(8,128)(2,1)S(1)}, u32[]{:S(2)}, u32[]{:S(2)}) collective-permute-start(bf16[288,128]{1,0:T(8,128)(2,1)S(1)} %factors.1.after.refs_0_), channel_id=1, source_target_pairs={{12,0},{8,4},{4,8},{0,12},{13,1},{9,5},{5,9},{1,13},{14,2},{10,6},... | collective-permute-start | bytes 221192 | tf_op jit(solution)/shard_map/ppermute | solution.py:374
  10.1 1.6 %collective-permute-start = (bf16[288,128]{1,0:T(8,128)(2,1)S(1)}, bf16[288,128]{1,0:T(8,128)(2,1)S(1)}, u32[]{:S(2)}, u32[]{:S(2)}) collective-permute-start(bf16[288,128]{1,0:T(8,128)(2,1)S(1)} %factors.1.after.refs_0_), channel_id=1, source_target_pairs={{4,0},{12,4},{0,8},{8,12},{5,1},{13,5},{1,9},{9,13},{6,2},{14,6},{... | collective-permute-start | bytes 221192 | tf_op jit(solution)/shard_map/ppermute | solution.py:374
  11.7 3.3 %fetch.1.refs_4_.slab = bf16[960,4096]{1,0:T(8,128)(2,1)S(1)} custom-call(bf16[288,128]{1,0:T(8,128)(2,1)S(1)} %factors.1.after.refs_0_, bf16[960,4096]{1,0:T(8,128)(2,1)} %bitcast.7), custom_call_target="tpu_custom_call" | custom-call | bytes 7864320 | tf_op jit(solution)/shard_map/fetch/pallas_call | solution.py:177
  15.0 0.0 collective-permute-done.2.refs_3_
  15.0 0.0 collective-permute-done.1.refs_2_
  15.0 0.0 collective-permute-done.refs_1_
  15.0 1.3 %grads.1 = (bf16[144,4096]{1,0:T(8,128)(2,1)S(1)}, bf16[144,240]{1,0:T(8,128)(2,1)S(1)}) custom-call(bf16[288,128]{1,0:T(8,128)(2,1)S(1)} %factors.1.after.refs_0_, bf16[288,128]{1,0:T(8,128)(2,1)S(1)} %collective-permute-done.refs_1_, bf16[288,128]{1,0:T(8,128)(2,1)S(1)} %collective-permute-done.1.refs_2_, ...), custom_call_target="tpu_custom_call" | custom-call | tf_op jit(solution)/shard_map/grads/pallas_call | solution.py:327
  16.3 0.1 collective-permute-start.3
  16.4 0.7 %scores.4 = f32[144,240]{1,0:T(8,128)S(1)} custom-call(bf16[144,4096]{1,0:T(8,128)(2,1)S(1)} %get-tuple-element.9.grads, bf16[960,4096]{1,0:T(8,128)(2,1)S(1)} %fetch.1.refs_4_.slab), custom_call_target="tpu_custom_call" | custom-call | flops 283115520 | bytes 3145728 | tf_op jit(solution)/shard_map/scores/pallas_call | solution.py:346
  17.2 0.5 %collective-permute-done.3 = bf16[144,240]{1,0:T(8,128)(2,1)S(1)} collective-permute-done((bf16[144,240]{1,0:T(8,128)(2,1)S(1)}, bf16[144,240]{1,0:T(8,128)(2,1)S(1)}, u32[]{:S(2)}, u32[]{:S(2)}) %collective-permute-start.3) | collective-permute-done | bytes 69152 | tf_op jit(solution)/shard_map/ppermute | solution.py:320
  17.7 1.6 %collective-permute-start.6 = (bf16[144,240]{1,0:T(8,128)(2,1)S(1)}, bf16[144,240]{1,0:T(8,128)(2,1)S(1)}, u32[]{:S(2)}, u32[]{:S(2)}) collective-permute-start(bf16[144,240]{1,0:T(8,128)(2,1)S(1)} %add_convert_fusion.refs_0_), channel_id=1, source_target_pairs={{0,2},{1,3},{2,0},{3,1},{4,6},{5,7},{6,4},{7,5},{8,10},{9,11},{10,... | collective-permute-start | bytes 207368 | tf_op jit(solution)/shard_map/ppermute | solution.py:320
  19.3 0.7 %scores.5 = (bf16[72,240]{1,0:T(8,128)(2,1)S(1)}, bf16[72,240]{1,0:T(8,128)(2,1)S(1)}) custom-call(bf16[144,4096]{1,0:T(8,128)(2,1)S(1)} %get-tuple-element.9.grads, bf16[960,4096]{1,0:T(8,128)(2,1)S(1)} %fetch.1.refs_4_.slab, bf16[144,240]{1,0:T(8,128)(2,1)S(1)} %add_convert_fusion.refs_0_), custom_call_target="tpu_custom_call" | custom-call | flops 283115520 | bytes 3145728 | tf_op jit(solution)/shard_map/scores/pallas_call | solution.py:346
  20.0 0.1 collective-permute-start.4
  20.1 0.5 %collective-permute-start.5 = (bf16[72,240]{1,0:T(8,128)(2,1)S(1)}, bf16[72,240]{1,0:T(8,128)(2,1)S(1)}, u32[]{:S(2)}, u32[]{:S(2)}) collective-permute-start(bf16[72,240]{1,0:T(8,128)(2,1)S(1)} %get-tuple-element.12), channel_id=1, source_target_pairs={{0,1},{1,0},{2,3},{3,2},{4,5},{5,4},{6,7},{7,6},{8,9},{9,8},{10,11... | collective-permute-start | bytes 103688 | tf_op jit(solution)/shard_map/ppermute | solution.py:320
  20.6 0.7 %scores.3 = f32[144,240]{1,0:T(8,128)S(1)} custom-call(bf16[144,4096]{1,0:T(8,128)(2,1)S(1)} %get-tuple-element.9.grads, bf16[960,4096]{1,0:T(8,128)(2,1)S(1)} %fetch.1.refs_4_.slab), custom_call_target="tpu_custom_call" | custom-call | flops 283115520 | bytes 3145728 | tf_op jit(solution)/shard_map/scores/pallas_call | solution.py:346
  21.3 0.0 collective-permute-done.4
  21.3 0.1 collective-permute-done.5
  21.5 0.7 %collective-permute-done.6 = bf16[144,240]{1,0:T(8,128)(2,1)S(1)} collective-permute-done((bf16[144,240]{1,0:T(8,128)(2,1)S(1)}, bf16[144,240]{1,0:T(8,128)(2,1)S(1)}, u32[]{:S(2)}, u32[]{:S(2)}) %collective-permute-start.6) | collective-permute-done | bytes 69152 | tf_op jit(solution)/shard_map/ppermute | solution.py:320
  22.1 0.7 %add_bitcast_fusion = f32[240,144]{0,1:T(8,128)} fusion(bf16[144,240]{1,0:T(8,128)(2,1)S(1)} %collective-permute-done.6, f32[144,240]{1,0:T(8,128)S(1)} %scores.3, bf16[72,240]{1,0:T(8,128)(2,1)S(1)} %collective-permute-done.5, bf16[72,240]{1,0:T(8,128)(2,1)S(1)} %collective-permute-done.4), kind=kLoop, calls=%fused_computation | loop fusion | flops 241920 | bytes 414720 | tf_op jit(solution)/shard_map/transpose | solution.py:390
  (1 shorter events, 0.0 us)
Async XLA Ops:
  4.5 10.5 %collective-permute-start.2 = (bf16[288,128]{1,0:T(8,128)(2,1)S(1)}, bf16[288,128]{1,0:T(8,128)(2,1)S(1)}, u32[]{:S(2)}, u32[]{:S(2)}) collective-permute-start(bf16[288,128]{1,0:T(8,128)(2,1)S(1)} %factors.1.after.refs_0_), channel_id=1, source_target_pairs={{8,0},{0,4},{12,8},{4,12},{9,1},{1,5},{13,9},{5,13},{10,2},{2,6},{... | collective-permute-start | bytes 221192 | tf_op jit(solution)/shard_map/ppermute | solution.py:374
  7.6 7.4 %collective-permute-start.1 = (bf16[288,128]{1,0:T(8,128)(2,1)S(1)}, bf16[288,128]{1,0:T(8,128)(2,1)S(1)}, u32[]{:S(2)}, u32[]{:S(2)}) collective-permute-start(bf16[288,128]{1,0:T(8,128)(2,1)S(1)} %factors.1.after.refs_0_), channel_id=1, source_target_pairs={{12,0},{8,4},{4,8},{0,12},{13,1},{9,5},{5,9},{1,13},{14,2},{10,6},... | collective-permute-start | bytes 221192 | tf_op jit(solution)/shard_map/ppermute | solution.py:374
  10.1 5.0 %collective-permute-start = (bf16[288,128]{1,0:T(8,128)(2,1)S(1)}, bf16[288,128]{1,0:T(8,128)(2,1)S(1)}, u32[]{:S(2)}, u32[]{:S(2)}) collective-permute-start(bf16[288,128]{1,0:T(8,128)(2,1)S(1)} %factors.1.after.refs_0_), channel_id=1, source_target_pairs={{4,0},{12,4},{0,8},{8,12},{5,1},{13,5},{1,9},{9,13},{6,2},{14,6},{... | collective-permute-start | bytes 221192 | tf_op jit(solution)/shard_map/ppermute | solution.py:374
  16.3 1.3 %collective-permute-start.3 = (bf16[144,240]{1,0:T(8,128)(2,1)S(1)}, bf16[144,240]{1,0:T(8,128)(2,1)S(1)}, u32[]{:S(2)}, u32[]{:S(2)}) collective-permute-start(bf16[144,240]{1,0:T(8,128)(2,1)S(1)} %get-tuple-element.10), channel_id=1, source_target_pairs={{0,1},{1,0},{2,3},{3,2},{4,5},{5,4},{6,7},{7,6},{8,9},{9,8},{10,11... | collective-permute-start | bytes 207368 | tf_op jit(solution)/shard_map/ppermute | solution.py:320
  17.7 4.4 %collective-permute-start.6 = (bf16[144,240]{1,0:T(8,128)(2,1)S(1)}, bf16[144,240]{1,0:T(8,128)(2,1)S(1)}, u32[]{:S(2)}, u32[]{:S(2)}) collective-permute-start(bf16[144,240]{1,0:T(8,128)(2,1)S(1)} %add_convert_fusion.refs_0_), channel_id=1, source_target_pairs={{0,2},{1,3},{2,0},{3,1},{4,6},{5,7},{6,4},{7,5},{8,10},{9,11},{10,... | collective-permute-start | bytes 207368 | tf_op jit(solution)/shard_map/ppermute | solution.py:320
  20.0 1.3 %collective-permute-start.4 = (bf16[72,240]{1,0:T(8,128)(2,1)S(1)}, bf16[72,240]{1,0:T(8,128)(2,1)S(1)}, u32[]{:S(2)}, u32[]{:S(2)}) collective-permute-start(bf16[72,240]{1,0:T(8,128)(2,1)S(1)} %get-tuple-element.11), channel_id=1, source_target_pairs={{0,1},{1,0},{2,3},{3,2},{4,5},{5,4},{6,7},{7,6},{8,9},{9,8},{10,11... | collective-permute-start | bytes 103688 | tf_op jit(solution)/shard_map/ppermute | solution.py:320
  20.1 1.4 %collective-permute-start.5 = (bf16[72,240]{1,0:T(8,128)(2,1)S(1)}, bf16[72,240]{1,0:T(8,128)(2,1)S(1)}, u32[]{:S(2)}, u32[]{:S(2)}) collective-permute-start(bf16[72,240]{1,0:T(8,128)(2,1)S(1)} %get-tuple-element.12), channel_id=1, source_target_pairs={{0,1},{1,0},{2,3},{3,2},{4,5},{5,4},{6,7},{7,6},{8,9},{9,8},{10,11... | collective-permute-start | bytes 103688 | tf_op jit(solution)/shard_map/ppermute | solution.py:320

commit v21 on v20

--- a/solution.py
+++ b/solution.py
@@ -28,13 +28,16 @@
 
 
 def factors_kernel(
+    n_layer,
     hbm_lengths,
     hbm_hidden,
     hbm_cot,
     hbm_gain,
     hbm_inp,
     hbm_outp,
+    hbm_store,
     packed,
+    far,
     lengths,
     hidden,
     cot,
@@ -67,6 +70,7 @@
     odd = lax.rem(lax.axis_index("store"), 2)
     at_full = pl.multiple_of(odd * half, half)
     at_half = pl.multiple_of((1 - odd) * full, half)
+    slab = store_copies(hbm_store, far, range(2, n_layer), sems, 5 + blocks, n_layer)
     for piece in first:
         piece.wait()
 
@@ -74,6 +78,8 @@
     def _():
         for r in range(1, blocks):
             block_rows(r).start()
+        for piece in slab:
+            piece.start()
 
     whole = dot_nt(outp[...], cot[pl.ds(at_full, full), :])
     for t in range(full // LANES):
@@ -127,20 +133,27 @@
 
     packed[:mid, :] = side_by_side(in_rows(at_full, full)).astype(bf16)
     packed[mid : mid + low, :] = side_by_side(in_rows(at_half, half)).astype(bf16)
+    for piece in slab:
+        piece.wait()
 
 
 def in_hbm(x):
     return pltpu.with_memory_space_constraint(x, pltpu.HBM)
 
 
-def factors(lengths, hidden, cotangent, gain, in_projection, out_projection):
+def factors(n_layer, lengths, hidden, cotangent, gain, in_projection, out_projection, store):
     rows, width = hidden.shape
     blocks = 3
+    far = (store.shape[0] // n_layer * (n_layer - 2), store.shape[1])
+    args = (lengths, hidden, cotangent, gain, in_projection, out_projection, store)
     return pl.pallas_call(
-        factors_kernel,
-        out_shape=jax.ShapeDtypeStruct((rows, 2 * R), bf16),
-        in_specs=[pl.BlockSpec(memory_space=pl.ANY)] * 6,
-        out_specs=pl.BlockSpec(memory_space=pltpu.VMEM),
+        functools.partial(factors_kernel, n_layer),
+        out_shape=[
+            jax.ShapeDtypeStruct((rows, 2 * R), bf16),
+            jax.ShapeDtypeStruct(far, bf16),
+        ],
+        in_specs=[pl.BlockSpec(memory_space=pl.ANY)] * len(args),
+        out_specs=[pl.BlockSpec(memory_space=pltpu.VMEM)] * 2,
         scratch_shapes=[
             pltpu.SMEM(lengths.shape, jnp.int32),
             pltpu.VMEM((blocks, rows // blocks, width), bf16),
@@ -151,23 +164,31 @@
             pltpu.VMEM(in_projection.shape, bf16),
             pltpu.VMEM((rows, 2 * R), f32),
             pltpu.VMEM((-(-rows // LANES) * R, LANES), f32),
-            pltpu.SemaphoreType.DMA((5 + blocks,)),
+            pltpu.SemaphoreType.DMA((5 + blocks + n_layer - 2,)),
         ],
         compiler_params=pltpu.CompilerParams(vmem_limit_bytes=24 * 2**20),
         name="factors",
-    )(*[in_hbm(x) for x in (lengths, hidden, cotangent, gain, in_projection, out_projection)])
-
-
-def fetch_kernel(n_layer, after, store, slab, sems):
-    block = slab.shape[0] // n_layer
+    )(*[in_hbm(x) for x in args])
+
+
+def store_copies(store, slab, places, sems, at, n_layer):
+    block = store.shape[0] // n_layer
     rows = 16 if block % 16 == 0 else 8
     me = lax.axis_index("layer")
     copies = []
-    for k in range(n_layer):
-        at = pl.multiple_of(partner(me, k, n_layer) * block, rows)
-        to = slab.at[pl.ds(k * block, block)]
-        copies.append(pltpu.make_async_copy(store.at[pl.ds(at, block)], to, sems.at[k]))
-        copies[-1].start()
+    for to, k in enumerate(places):
+        start = pl.multiple_of(partner(me, k, n_layer) * block, rows)
+        target = slab.at[pl.ds(to * block, block)]
+        copies.append(
+            pltpu.make_async_copy(store.at[pl.ds(start, block)], target, sems.at[at + to])
+        )
+    return copies
+
+
+def fetch_kernel(n_layer, after, store, near, sems):
+    copies = store_copies(store, near, range(2), sems, 0, n_layer)
+    for copy in copies:
+        copy.start()
     for copy in copies:
         copy.wait()
 
@@ -176,13 +197,13 @@
     rows, features = store.shape
     return pl.pallas_call(
         functools.partial(fetch_kernel, n_layer),
-        out_shape=jax.ShapeDtypeStruct((rows, features), bf16),
+        out_shape=jax.ShapeDtypeStruct((rows // n_layer * 2, features), bf16),
         in_specs=[pl.BlockSpec(memory_space=pl.ANY)] * 2,
         out_specs=pl.BlockSpec(memory_space=pltpu.VMEM),
-        scratch_shapes=[pltpu.SemaphoreType.DMA((n_layer,))],
+        scratch_shapes=[pltpu.SemaphoreType.DMA((2,))],
         compiler_params=pltpu.CompilerParams(vmem_limit_bytes=12 * 2**20),
         cost_estimate=pl.CostEstimate(
-            flops=0, bytes_accessed=2 * rows * features, transcendentals=0
+            flops=0, bytes_accessed=4 * rows * features // n_layer, transcendentals=0
         ),
         name="fetch",
     )(after, in_hbm(store))
@@ -285,7 +306,7 @@
 
 def grads_kernel(n_store, full_groups, k, *refs):
     gathered = refs[:n_store]
-    slab, grads, out, shards = refs[n_store:]
+    slab, _, grads, out, shards = refs[n_store:]
     me_store = lax.axis_index("store")
     for away, block in enumerate(gathered):
         shards[source(me_store, away, n_store)] = block[...]
@@ -320,32 +341,30 @@
     return lax.ppermute(x, axis, pairs)
 
 
-def grads_and_scores(gathered, slab, n_store, n_layer, k):
-    rows, features = slab.shape
-    queries = n_store * gathered[0].shape[0] // S
+def grads_and_scores(gathered, slab, block, at, after):
+    n_store = len(gathered)
+    queries = gathered[0].shape[0] // S
     vmem = pl.BlockSpec(memory_space=pltpu.VMEM)
     return pl.pallas_call(
-        functools.partial(grads_kernel, n_store, queries // n_store // G, k),
+        functools.partial(grads_kernel, n_store, queries // G, at),
         out_shape=[
-            jax.ShapeDtypeStruct((queries, features), bf16),
-            jax.ShapeDtypeStruct((queries, rows // n_layer), bf16),
+            jax.ShapeDtypeStruct((n_store * queries, slab.shape[1]), bf16),
+            jax.ShapeDtypeStruct((n_store * queries, block), bf16),
         ],
-        in_specs=[vmem] * (n_store + 1),
+        in_specs=[vmem] * (n_store + 1) + [pl.BlockSpec(memory_space=pl.ANY)],
         out_specs=[vmem] * 2,
         scratch_shapes=[pltpu.VMEM((n_store,) + gathered[0].shape, bf16)],
         compiler_params=pltpu.CompilerParams(vmem_limit_bytes=24 * 2**20),
         name="grads",
-    )(*gathered, slab)
-
-
-def scores(grads, slab, n_layer, k, pieces=1, after=()):
-    rows, features = slab.shape
-    block = rows // n_layer
-    queries = grads.shape[0]
+    )(*gathered, slab, after)
+
+
+def scores(grads, slab, block, at, kind, pieces=1, after=()):
+    queries, features = grads.shape
     vmem = pl.BlockSpec(memory_space=pltpu.VMEM)
     return pl.pallas_call(
-        functools.partial(scores_kernel, k, skip=len(after)),
-        out_shape=[jax.ShapeDtypeStruct((queries // pieces, block), bf16 if k % 2 else f32)] * pieces,
+        functools.partial(scores_kernel, at, skip=len(after)),
+        out_shape=[jax.ShapeDtypeStruct((queries // pieces, block), kind)] * pieces,
         in_specs=[vmem] * 2 + [pl.BlockSpec(memory_space=pl.ANY)] * len(after),
         out_specs=[vmem] * pieces,
         compiler_params=pltpu.CompilerParams(vmem_limit_bytes=24 * 2**20),
@@ -360,31 +379,36 @@
 
 def on_device(n_store, n_layer, hidden, cotangent, lengths, norm_gain, in_proj, out_proj, store):
     queries, positions, width = hidden.shape[1:]
-    packed = factors(
+    block = store.shape[1] // n_layer
+    packed, far = factors(
+        n_layer,
         lengths,
         hidden.reshape(queries * positions, width),
         cotangent.reshape(queries * positions, cotangent.shape[3]),
         norm_gain,
         in_proj[0],
         out_proj[0],
+        store[0],
     )
     gathered = [packed]
     for away in range(1, n_store):
         pairs = [(source(to, away, n_store), to) for to in range(n_store)]
         gathered.append(lax.ppermute(packed, "store", pairs))
-    slab = fetch(packed, store[0], n_layer)
-    grads, partial = grads_and_scores(gathered, slab, n_store, n_layer, n_layer - 1)
+    near = fetch(packed, store[0], n_layer)
+    last = n_layer - 3
+    grads, partial = grads_and_scores(gathered, far, block, last, near)
     crossed = []
-    for k in reversed(range(2, n_layer, 2)):
-        if k < n_layer - 2:
-            (partial,) = scores(grads, slab, n_layer, k + 1)
+    for at in reversed(range(0, last, 2)):
+        if at + 1 < last:
+            (partial,) = scores(grads, far, block, at + 1, bf16)
         other = swap(partial, "layer", n_layer, 1)
-        (mine,) = scores(grads, slab, n_layer, k)
+        (mine,) = scores(grads, far, block, at, f32)
         joined = (mine + other.astype(f32)).astype(bf16)
-        crossed.append(swap(joined, "layer", n_layer, k))
-    near = [swap(x, "layer", n_layer, 1) for x in scores(grads, slab, n_layer, 1, 2, [joined])]
-    (total,) = scores(grads, slab, n_layer, 0)
-    total = total + jnp.concatenate(near, axis=0).astype(f32)
+        crossed.append(swap(joined, "layer", n_layer, at + 2))
+    halves_of_other = scores(grads, near, block, 1, bf16, 2, [joined])
+    (total,) = scores(grads, near, block, 0, f32)
+    other = [swap(x, "layer", n_layer, 1) for x in halves_of_other]
+    total = total + jnp.concatenate(other, axis=0).astype(f32)
     for x in crossed:
         total = total + x.astype(f32)
     return total.T

time: 23 us -> 23 us (level)
  Pallas kernels: 11.4 us -> 10.2 us
  waiting for transfers between devices: 1.3 us -> 2.5 us
    ppermute x3, waiting for transfers between devices: 0.02 us -> 1.22 us  [on_device(): gathered.append(lax.ppermute(packed, 'store', pairs))]
    pallas_call x1, Pallas kernels: 3.34 us -> 2.15 us  [fetch(): pl.pallas_call(functools.partial(fetch_kernel, n_layer), out_shape=jax.Sh...]
  transfers between devices with their start and end apart: 7 -> 7, of which waited for: 3 -> 5; matrix products, arithmetic and copies ran while one was open for 0% -> 0% of each run, Pallas kernels for 24% -> 19%
where the time goes in v21:
time: 23 us; the launch traced here: 22.8 us
  Pallas kernels  10.2 us (44%)
  starting transfers between devices  9.33 us (41%)
  waiting for transfers between devices  2.5 us (11%)
  other arithmetic  0.7 us (3%)
    ppermute x3, starting transfers between devices, on_device(): gathered.append(lax.ppermute(packed, 'store', pairs))  7.12 us
    pallas_call x1, Pallas kernels, factors(): pl.pallas_call(functools.partial(factors_kernel, n_layer), out_shape=[jax...  4.54 us
    pallas_call x3, Pallas kernels, scores(): pl.pallas_call(functools.partial(scores_kernel, at, skip=len(after)), out...  2.23 us
    ppermute x4, starting transfers between devices, swap(): return lax.ppermute(x, axis, pairs)  2.2 us
    pallas_call x1, Pallas kernels, fetch(): pl.pallas_call(functools.partial(fetch_kernel, n_layer), out_shape=jax.Sh...  2.15 us
    pallas_call x1, Pallas kernels, grads_and_scores(): pl.pallas_call(functools.partial(grads_kernel, n_store, queries // G, at)...  1.3 us
    ppermute x4, waiting for transfers between devices, swap(): return lax.ppermute(x, axis, pairs)  1.28 us
    ppermute x3, waiting for transfers between devices, on_device(): gathered.append(lax.ppermute(packed, 'store', pairs))  1.22 us
  transfers between devices with their start and end apart: 7, of which 5 were waited for; matrix products, arithmetic and copies ran while one was open for 0% of the time, Pallas kernels for 19%

profile of v21, /device:TPU:0, one launch (start us, length us, event | category | flops | bytes accessed | tf_op | source)
XLA Modules:
  0.0 22.8 jit_solution(8197689545415277571)
XLA Ops:
  0.0 4.5 %factors.1 = (bf16[288,128]{1,0:T(8,128)(2,1)S(1)}, bf16[480,4096]{1,0:T(8,128)(2,1)S(1)}) custom-call(s32[36]{0:T(128)} %hbm_lengths.1, bf16[288,8192]{1,0:T(8,128)(2,1)} %bitcast.9, bf16[288,1024]{1,0:T(8,128)(2,1)} %bitcast.11, bf16[1,8192]{1,0:T(2,128)(2,1)} %hbm_gain.1, bf16[64,8192]{1,0:T(8,128)(2,1)} %bitcast.10, bf16[64,1024]{1,0:T(8,128)(2,1)} %bitcast.12, ...), custom_call_target="tpu_custom_call" | custom-call | tf_op jit(solution)/shard_map/factors/pallas_call | solution.py:149
  4.5 3.1 %collective-permute-start.2 = (bf16[288,128]{1,0:T(8,128)(2,1)S(1)}, bf16[288,128]{1,0:T(8,128)(2,1)S(1)}, u32[]{:S(2)}, u32[]{:S(2)}) collective-permute-start(bf16[288,128]{1,0:T(8,128)(2,1)S(1)} %get-tuple-element.11.after.refs_0_), channel_id=1, source_target_pairs={{8,0},{0,4},{12,8},{4,12},{9,1},{1,5},{13,9},{5,13},{10,2},{2,6},{... | collective-permute-start | bytes 221192 | tf_op jit(solution)/shard_map/ppermute | solution.py:396
  7.6 2.5 %collective-permute-start.1 = (bf16[288,128]{1,0:T(8,128)(2,1)S(1)}, bf16[288,128]{1,0:T(8,128)(2,1)S(1)}, u32[]{:S(2)}, u32[]{:S(2)}) collective-permute-start(bf16[288,128]{1,0:T(8,128)(2,1)S(1)} %get-tuple-element.11.after.refs_0_), channel_id=1, source_target_pairs={{12,0},{8,4},{4,8},{0,12},{13,1},{9,5},{5,9},{1,13},{14,2},{10,6},... | collective-permute-start | bytes 221192 | tf_op jit(solution)/shard_map/ppermute | solution.py:396
  10.1 1.6 %collective-permute-start = (bf16[288,128]{1,0:T(8,128)(2,1)S(1)}, bf16[288,128]{1,0:T(8,128)(2,1)S(1)}, u32[]{:S(2)}, u32[]{:S(2)}) collective-permute-start(bf16[288,128]{1,0:T(8,128)(2,1)S(1)} %get-tuple-element.11.after.refs_0_), channel_id=1, source_target_pairs={{4,0},{12,4},{0,8},{8,12},{5,1},{13,5},{1,9},{9,13},{6,2},{14,6},{... | collective-permute-start | bytes 221192 | tf_op jit(solution)/shard_map/ppermute | solution.py:396
  11.7 2.2 %fetch.1.refs_5_.slab = bf16[480,4096]{1,0:T(8,128)(2,1)S(1)} custom-call(bf16[288,128]{1,0:T(8,128)(2,1)S(1)} %get-tuple-element.11.after.refs_0_, bf16[960,4096]{1,0:T(8,128)(2,1)} %bitcast.8), custom_call_target="tpu_custom_call" | custom-call | bytes 3932160 | tf_op jit(solution)/shard_map/fetch/pallas_call | solution.py:198
  13.8 0.0 collective-permute-done.2.refs_3_
  13.8 1.1 %collective-permute-done.1.refs_2_ = bf16[288,128]{1,0:T(8,128)(2,1)S(1)} collective-permute-done((bf16[288,128]{1,0:T(8,128)(2,1)S(1)}, bf16[288,128]{1,0:T(8,128)(2,1)S(1)}, u32[]{:S(2)}, u32[]{:S(2)}) %collective-permute-start.1) | collective-permute-done | bytes 73760 | tf_op jit(solution)/shard_map/ppermute | solution.py:396
  14.9 0.1 collective-permute-done.refs_1_
  15.1 1.3 %grads.1 = (bf16[144,4096]{1,0:T(8,128)(2,1)S(1)}, bf16[144,240]{1,0:T(8,128)(2,1)S(1)}) custom-call(bf16[288,128]{1,0:T(8,128)(2,1)S(1)} %get-tuple-element.11.after.refs_0_, bf16[288,128]{1,0:T(8,128)(2,1)S(1)} %collective-permute-done.refs_1_, bf16[288,128]{1,0:T(8,128)(2,1)S(1)} %collective-permute-done.1.refs_2_, ...), custom_call_target="tpu_custom_call" | custom-call | tf_op jit(solution)/shard_map/grads/pallas_call | solution.py:348
  16.4 0.1 collective-permute-start.3
  16.4 0.7 %scores.4 = f32[144,240]{1,0:T(8,128)S(1)} custom-call(bf16[144,4096]{1,0:T(8,128)(2,1)S(1)} %get-tuple-element.13.grads, bf16[480,4096]{1,0:T(8,128)(2,1)S(1)} %get-tuple-element.12.refs_4_.slab), custom_call_target="tpu_custom_call" | custom-call | flops 283115520 | bytes 3145728 | tf_op jit(solution)/shard_map/scores/pallas_call | solution.py:365
  17.2 0.5 %collective-permute-done.3 = bf16[144,240]{1,0:T(8,128)(2,1)S(1)} collective-permute-done((bf16[144,240]{1,0:T(8,128)(2,1)S(1)}, bf16[144,240]{1,0:T(8,128)(2,1)S(1)}, u32[]{:S(2)}, u32[]{:S(2)}) %collective-permute-start.3) | collective-permute-done | bytes 69152 | tf_op jit(solution)/shard_map/ppermute | solution.py:341
  17.7 1.6 %collective-permute-start.6 = (bf16[144,240]{1,0:T(8,128)(2,1)S(1)}, bf16[144,240]{1,0:T(8,128)(2,1)S(1)}, u32[]{:S(2)}, u32[]{:S(2)}) collective-permute-start(bf16[144,240]{1,0:T(8,128)(2,1)S(1)} %add_convert_fusion.refs_0_), channel_id=1, source_target_pairs={{0,2},{1,3},{2,0},{3,1},{4,6},{5,7},{6,4},{7,5},{8,10},{9,11},{10,... | collective-permute-start | bytes 207368 | tf_op jit(solution)/shard_map/ppermute | solution.py:341
  19.3 0.7 %scores.5 = (bf16[72,240]{1,0:T(8,128)(2,1)S(1)}, bf16[72,240]{1,0:T(8,128)(2,1)S(1)}) custom-call(bf16[144,4096]{1,0:T(8,128)(2,1)S(1)} %get-tuple-element.13.grads, bf16[480,4096]{1,0:T(8,128)(2,1)S(1)} %fetch.1.refs_5_.slab, bf16[144,240]{1,0:T(8,128)(2,1)S(1)} %add_convert_fusion.refs_0_), custom_call_target="tpu_custom_call" | custom-call | flops 283115520 | bytes 3145728 | tf_op jit(solution)/shard_map/scores/pallas_call | solution.py:365
  20.0 0.1 collective-permute-start.4
  20.1 0.5 %collective-permute-start.5 = (bf16[72,240]{1,0:T(8,128)(2,1)S(1)}, bf16[72,240]{1,0:T(8,128)(2,1)S(1)}, u32[]{:S(2)}, u32[]{:S(2)}) collective-permute-start(bf16[72,240]{1,0:T(8,128)(2,1)S(1)} %get-tuple-element.16), channel_id=1, source_target_pairs={{0,1},{1,0},{2,3},{3,2},{4,5},{5,4},{6,7},{7,6},{8,9},{9,8},{10,11... | collective-permute-start | bytes 103688 | tf_op jit(solution)/shard_map/ppermute | solution.py:341
  20.6 0.7 %scores.3 = f32[144,240]{1,0:T(8,128)S(1)} custom-call(bf16[144,4096]{1,0:T(8,128)(2,1)S(1)} %get-tuple-element.13.grads, bf16[480,4096]{1,0:T(8,128)(2,1)S(1)} %fetch.1.refs_5_.slab), custom_call_target="tpu_custom_call" | custom-call | flops 283115520 | bytes 3145728 | tf_op jit(solution)/shard_map/scores/pallas_call | solution.py:365
  21.4 0.0 collective-permute-done.4
  21.4 0.1 collective-permute-done.5
  21.5 0.7 %collective-permute-done.6 = bf16[144,240]{1,0:T(8,128)(2,1)S(1)} collective-permute-done((bf16[144,240]{1,0:T(8,128)(2,1)S(1)}, bf16[144,240]{1,0:T(8,128)(2,1)S(1)}, u32[]{:S(2)}, u32[]{:S(2)}) %collective-permute-start.6) | collective-permute-done | bytes 69152 | tf_op jit(solution)/shard_map/ppermute | solution.py:341
  22.1 0.7 %add_bitcast_fusion = f32[240,144]{0,1:T(8,128)} fusion(bf16[144,240]{1,0:T(8,128)(2,1)S(1)} %collective-permute-done.6, f32[144,240]{1,0:T(8,128)S(1)} %scores.3, bf16[72,240]{1,0:T(8,128)(2,1)S(1)} %collective-permute-done.5, bf16[72,240]{1,0:T(8,128)(2,1)S(1)} %collective-permute-done.4), kind=kLoop, calls=%fused_computation | loop fusion | flops 241920 | bytes 414720 | tf_op jit(solution)/shard_map/transpose | solution.py:414
  (1 shorter events, 0.0 us)
Async XLA Ops:
  4.5 9.3 %collective-permute-start.2 = (bf16[288,128]{1,0:T(8,128)(2,1)S(1)}, bf16[288,128]{1,0:T(8,128)(2,1)S(1)}, u32[]{:S(2)}, u32[]{:S(2)}) collective-permute-start(bf16[288,128]{1,0:T(8,128)(2,1)S(1)} %get-tuple-element.11.after.refs_0_), channel_id=1, source_target_pairs={{8,0},{0,4},{12,8},{4,12},{9,1},{1,5},{13,9},{5,13},{10,2},{2,6},{... | collective-permute-start | bytes 221192 | tf_op jit(solution)/shard_map/ppermute | solution.py:396
  7.6 7.3 %collective-permute-start.1 = (bf16[288,128]{1,0:T(8,128)(2,1)S(1)}, bf16[288,128]{1,0:T(8,128)(2,1)S(1)}, u32[]{:S(2)}, u32[]{:S(2)}) collective-permute-start(bf16[288,128]{1,0:T(8,128)(2,1)S(1)} %get-tuple-element.11.after.refs_0_), channel_id=1, source_target_pairs={{12,0},{8,4},{4,8},{0,12},{13,1},{9,5},{5,9},{1,13},{14,2},{10,6},... | collective-permute-start | bytes 221192 | tf_op jit(solution)/shard_map/ppermute | solution.py:396
  10.1 5.0 %collective-permute-start = (bf16[288,128]{1,0:T(8,128)(2,1)S(1)}, bf16[288,128]{1,0:T(8,128)(2,1)S(1)}, u32[]{:S(2)}, u32[]{:S(2)}) collective-permute-start(bf16[288,128]{1,0:T(8,128)(2,1)S(1)} %get-tuple-element.11.after.refs_0_), channel_id=1, source_target_pairs={{4,0},{12,4},{0,8},{8,12},{5,1},{13,5},{1,9},{9,13},{6,2},{14,6},{... | collective-permute-start | bytes 221192 | tf_op jit(solution)/shard_map/ppermute | solution.py:396
  16.4 1.3 %collective-permute-start.3 = (bf16[144,240]{1,0:T(8,128)(2,1)S(1)}, bf16[144,240]{1,0:T(8,128)(2,1)S(1)}, u32[]{:S(2)}, u32[]{:S(2)}) collective-permute-start(bf16[144,240]{1,0:T(8,128)(2,1)S(1)} %get-tuple-element.14), channel_id=1, source_target_pairs={{0,1},{1,0},{2,3},{3,2},{4,5},{5,4},{6,7},{7,6},{8,9},{9,8},{10,11... | collective-permute-start | bytes 207368 | tf_op jit(solution)/shard_map/ppermute | solution.py:341
  17.7 4.4 %collective-permute-start.6 = (bf16[144,240]{1,0:T(8,128)(2,1)S(1)}, bf16[144,240]{1,0:T(8,128)(2,1)S(1)}, u32[]{:S(2)}, u32[]{:S(2)}) collective-permute-start(bf16[144,240]{1,0:T(8,128)(2,1)S(1)} %add_convert_fusion.refs_0_), channel_id=1, source_target_pairs={{0,2},{1,3},{2,0},{3,1},{4,6},{5,7},{6,4},{7,5},{8,10},{9,11},{10,... | collective-permute-start | bytes 207368 | tf_op jit(solution)/shard_map/ppermute | solution.py:341
  20.0 1.3 %collective-permute-start.4 = (bf16[72,240]{1,0:T(8,128)(2,1)S(1)}, bf16[72,240]{1,0:T(8,128)(2,1)S(1)}, u32[]{:S(2)}, u32[]{:S(2)}) collective-permute-start(bf16[72,240]{1,0:T(8,128)(2,1)S(1)} %get-tuple-element.15), channel_id=1, source_target_pairs={{0,1},{1,0},{2,3},{3,2},{4,5},{5,4},{6,7},{7,6},{8,9},{9,8},{10,11... | collective-permute-start | bytes 103688 | tf_op jit(solution)/shard_map/ppermute | solution.py:341
  20.1 1.4 %collective-permute-start.5 = (bf16[72,240]{1,0:T(8,128)(2,1)S(1)}, bf16[72,240]{1,0:T(8,128)(2,1)S(1)}, u32[]{:S(2)}, u32[]{:S(2)}) collective-permute-start(bf16[72,240]{1,0:T(8,128)(2,1)S(1)} %get-tuple-element.16), channel_id=1, source_target_pairs={{0,1},{1,0},{2,3},{3,2},{4,5},{5,4},{6,7},{7,6},{8,9},{9,8},{10,11... | collective-permute-start | bytes 103688 | tf_op jit(solution)/shard_map/ppermute | solution.py:341

commit v22 on v21

--- a/solution.py
+++ b/solution.py
@@ -143,7 +143,7 @@
 
 def factors(n_layer, lengths, hidden, cotangent, gain, in_projection, out_projection, store):
     rows, width = hidden.shape
-    blocks = 3
+    blocks = 2
     far = (store.shape[0] // n_layer * (n_layer - 2), store.shape[1])
     args = (lengths, hidden, cotangent, gain, in_projection, out_projection, store)
     return pl.pallas_call(

time: 23 us -> 23.1 us (level)
  no operation moved by 1% of the time
where the time goes in v22:
time: 23.1 us; the launch traced here: 22.9 us
  Pallas kernels  10.3 us (45%)
  starting transfers between devices  9.32 us (40%)
  waiting for transfers between devices  2.51 us (11%)
  other arithmetic  0.7 us (3%)
    ppermute x3, starting transfers between devices, on_device(): gathered.append(lax.ppermute(packed, 'store', pairs))  7.13 us
    pallas_call x1, Pallas kernels, factors(): pl.pallas_call(functools.partial(factors_kernel, n_layer), out_shape=[jax...  4.66 us
    pallas_call x3, Pallas kernels, scores(): pl.pallas_call(functools.partial(scores_kernel, at, skip=len(after)), out...  2.24 us
    ppermute x4, starting transfers between devices, swap(): return lax.ppermute(x, axis, pairs)  2.19 us
    pallas_call x1, Pallas kernels, fetch(): pl.pallas_call(functools.partial(fetch_kernel, n_layer), out_shape=jax.Sh...  2.15 us
    pallas_call x1, Pallas kernels, grads_and_scores(): pl.pallas_call(functools.partial(grads_kernel, n_store, queries // G, at)...  1.3 us
    ppermute x4, waiting for transfers between devices, swap(): return lax.ppermute(x, axis, pairs)  1.29 us
    ppermute x3, waiting for transfers between devices, on_device(): gathered.append(lax.ppermute(packed, 'store', pairs))  1.22 us
  transfers between devices with their start and end apart: 7, of which 5 were waited for; matrix products, arithmetic and copies ran while one was open for 0% of the time, Pallas kernels for 19%

profile of v22, /device:TPU:0, one launch (start us, length us, event | category | flops | bytes accessed | tf_op | source)
XLA Modules:
  0.0 22.9 jit_solution(17378528275248868875)
XLA Ops:
  0.0 4.7 %factors.1 = (bf16[288,128]{1,0:T(8,128)(2,1)S(1)}, bf16[480,4096]{1,0:T(8,128)(2,1)S(1)}) custom-call(s32[36]{0:T(128)} %hbm_lengths.1, bf16[288,8192]{1,0:T(8,128)(2,1)} %bitcast.9, bf16[288,1024]{1,0:T(8,128)(2,1)} %bitcast.11, bf16[1,8192]{1,0:T(2,128)(2,1)} %hbm_gain.1, bf16[64,8192]{1,0:T(8,128)(2,1)} %bitcast.10, bf16[64,1024]{1,0:T(8,128)(2,1)} %bitcast.12, ...), custom_call_target="tpu_custom_call" | custom-call | tf_op jit(solution)/shard_map/factors/pallas_call | solution.py:149
  4.7 3.1 %collective-permute-start.2 = (bf16[288,128]{1,0:T(8,128)(2,1)S(1)}, bf16[288,128]{1,0:T(8,128)(2,1)S(1)}, u32[]{:S(2)}, u32[]{:S(2)}) collective-permute-start(bf16[288,128]{1,0:T(8,128)(2,1)S(1)} %get-tuple-element.11.after.refs_0_), channel_id=1, source_target_pairs={{8,0},{0,4},{12,8},{4,12},{9,1},{1,5},{13,9},{5,13},{10,2},{2,6},{... | collective-permute-start | bytes 221192 | tf_op jit(solution)/shard_map/ppermute | solution.py:396
  7.7 2.5 %collective-permute-start.1 = (bf16[288,128]{1,0:T(8,128)(2,1)S(1)}, bf16[288,128]{1,0:T(8,128)(2,1)S(1)}, u32[]{:S(2)}, u32[]{:S(2)}) collective-permute-start(bf16[288,128]{1,0:T(8,128)(2,1)S(1)} %get-tuple-element.11.after.refs_0_), channel_id=1, source_target_pairs={{12,0},{8,4},{4,8},{0,12},{13,1},{9,5},{5,9},{1,13},{14,2},{10,6},... | collective-permute-start | bytes 221192 | tf_op jit(solution)/shard_map/ppermute | solution.py:396
  10.2 1.6 %collective-permute-start = (bf16[288,128]{1,0:T(8,128)(2,1)S(1)}, bf16[288,128]{1,0:T(8,128)(2,1)S(1)}, u32[]{:S(2)}, u32[]{:S(2)}) collective-permute-start(bf16[288,128]{1,0:T(8,128)(2,1)S(1)} %get-tuple-element.11.after.refs_0_), channel_id=1, source_target_pairs={{4,0},{12,4},{0,8},{8,12},{5,1},{13,5},{1,9},{9,13},{6,2},{14,6},{... | collective-permute-start | bytes 221192 | tf_op jit(solution)/shard_map/ppermute | solution.py:396
  11.8 2.2 %fetch.1.refs_5_.slab = bf16[480,4096]{1,0:T(8,128)(2,1)S(1)} custom-call(bf16[288,128]{1,0:T(8,128)(2,1)S(1)} %get-tuple-element.11.after.refs_0_, bf16[960,4096]{1,0:T(8,128)(2,1)} %bitcast.8), custom_call_target="tpu_custom_call" | custom-call | bytes 3932160 | tf_op jit(solution)/shard_map/fetch/pallas_call | solution.py:198
  14.0 0.0 collective-permute-done.2.refs_3_
  14.0 1.1 %collective-permute-done.1.refs_2_ = bf16[288,128]{1,0:T(8,128)(2,1)S(1)} collective-permute-done((bf16[288,128]{1,0:T(8,128)(2,1)S(1)}, bf16[288,128]{1,0:T(8,128)(2,1)S(1)}, u32[]{:S(2)}, u32[]{:S(2)}) %collective-permute-start.1) | collective-permute-done | bytes 73760 | tf_op jit(solution)/shard_map/ppermute | solution.py:396
  15.1 0.1 collective-permute-done.refs_1_
  15.2 1.3 %grads.1 = (bf16[144,4096]{1,0:T(8,128)(2,1)S(1)}, bf16[144,240]{1,0:T(8,128)(2,1)S(1)}) custom-call(bf16[288,128]{1,0:T(8,128)(2,1)S(1)} %get-tuple-element.11.after.refs_0_, bf16[288,128]{1,0:T(8,128)(2,1)S(1)} %collective-permute-done.refs_1_, bf16[288,128]{1,0:T(8,128)(2,1)S(1)} %collective-permute-done.1.refs_2_, ...), custom_call_target="tpu_custom_call" | custom-call | tf_op jit(solution)/shard_map/grads/pallas_call | solution.py:348
  16.5 0.1 collective-permute-start.3
  16.6 0.7 %scores.4 = f32[144,240]{1,0:T(8,128)S(1)} custom-call(bf16[144,4096]{1,0:T(8,128)(2,1)S(1)} %get-tuple-element.13.grads, bf16[480,4096]{1,0:T(8,128)(2,1)S(1)} %get-tuple-element.12.refs_4_.slab), custom_call_target="tpu_custom_call" | custom-call | flops 283115520 | bytes 3145728 | tf_op jit(solution)/shard_map/scores/pallas_call | solution.py:365
  17.3 0.5 %collective-permute-done.3 = bf16[144,240]{1,0:T(8,128)(2,1)S(1)} collective-permute-done((bf16[144,240]{1,0:T(8,128)(2,1)S(1)}, bf16[144,240]{1,0:T(8,128)(2,1)S(1)}, u32[]{:S(2)}, u32[]{:S(2)}) %collective-permute-start.3) | collective-permute-done | bytes 69152 | tf_op jit(solution)/shard_map/ppermute | solution.py:341
  17.8 1.6 %collective-permute-start.6 = (bf16[144,240]{1,0:T(8,128)(2,1)S(1)}, bf16[144,240]{1,0:T(8,128)(2,1)S(1)}, u32[]{:S(2)}, u32[]{:S(2)}) collective-permute-start(bf16[144,240]{1,0:T(8,128)(2,1)S(1)} %add_convert_fusion.refs_0_), channel_id=1, source_target_pairs={{0,2},{1,3},{2,0},{3,1},{4,6},{5,7},{6,4},{7,5},{8,10},{9,11},{10,... | collective-permute-start | bytes 207368 | tf_op jit(solution)/shard_map/ppermute | solution.py:341
  19.4 0.7 %scores.5 = (bf16[72,240]{1,0:T(8,128)(2,1)S(1)}, bf16[72,240]{1,0:T(8,128)(2,1)S(1)}) custom-call(bf16[144,4096]{1,0:T(8,128)(2,1)S(1)} %get-tuple-element.13.grads, bf16[480,4096]{1,0:T(8,128)(2,1)S(1)} %fetch.1.refs_5_.slab, bf16[144,240]{1,0:T(8,128)(2,1)S(1)} %add_convert_fusion.refs_0_), custom_call_target="tpu_custom_call" | custom-call | flops 283115520 | bytes 3145728 | tf_op jit(solution)/shard_map/scores/pallas_call | solution.py:365
  20.1 0.1 collective-permute-start.4
  20.2 0.5 %collective-permute-start.5 = (bf16[72,240]{1,0:T(8,128)(2,1)S(1)}, bf16[72,240]{1,0:T(8,128)(2,1)S(1)}, u32[]{:S(2)}, u32[]{:S(2)}) collective-permute-start(bf16[72,240]{1,0:T(8,128)(2,1)S(1)} %get-tuple-element.16), channel_id=1, source_target_pairs={{0,1},{1,0},{2,3},{3,2},{4,5},{5,4},{6,7},{7,6},{8,9},{9,8},{10,11... | collective-permute-start | bytes 103688 | tf_op jit(solution)/shard_map/ppermute | solution.py:341
  20.7 0.7 %scores.3 = f32[144,240]{1,0:T(8,128)S(1)} custom-call(bf16[144,4096]{1,0:T(8,128)(2,1)S(1)} %get-tuple-element.13.grads, bf16[480,4096]{1,0:T(8,128)(2,1)S(1)} %fetch.1.refs_5_.slab), custom_call_target="tpu_custom_call" | custom-call | flops 283115520 | bytes 3145728 | tf_op jit(solution)/shard_map/scores/pallas_call | solution.py:365
  21.5 0.0 collective-permute-done.4
  21.5 0.1 collective-permute-done.5
  21.6 0.7 %collective-permute-done.6 = bf16[144,240]{1,0:T(8,128)(2,1)S(1)} collective-permute-done((bf16[144,240]{1,0:T(8,128)(2,1)S(1)}, bf16[144,240]{1,0:T(8,128)(2,1)S(1)}, u32[]{:S(2)}, u32[]{:S(2)}) %collective-permute-start.6) | collective-permute-done | bytes 69152 | tf_op jit(solution)/shard_map/ppermute | solution.py:341
  22.3 0.7 %add_bitcast_fusion = f32[240,144]{0,1:T(8,128)} fusion(bf16[144,240]{1,0:T(8,128)(2,1)S(1)} %collective-permute-done.6, f32[144,240]{1,0:T(8,128)S(1)} %scores.3, bf16[72,240]{1,0:T(8,128)(2,1)S(1)} %collective-permute-done.5, bf16[72,240]{1,0:T(8,128)(2,1)S(1)} %collective-permute-done.4), kind=kLoop, calls=%fused_computation | loop fusion | flops 241920 | bytes 414720 | tf_op jit(solution)/shard_map/transpose | solution.py:414
  (1 shorter events, 0.0 us)
Async XLA Ops:
  4.7 9.3 %collective-permute-start.2 = (bf16[288,128]{1,0:T(8,128)(2,1)S(1)}, bf16[288,128]{1,0:T(8,128)(2,1)S(1)}, u32[]{:S(2)}, u32[]{:S(2)}) collective-permute-start(bf16[288,128]{1,0:T(8,128)(2,1)S(1)} %get-tuple-element.11.after.refs_0_), channel_id=1, source_target_pairs={{8,0},{0,4},{12,8},{4,12},{9,1},{1,5},{13,9},{5,13},{10,2},{2,6},{... | collective-permute-start | bytes 221192 | tf_op jit(solution)/shard_map/ppermute | solution.py:396
  7.7 7.3 %collective-permute-start.1 = (bf16[288,128]{1,0:T(8,128)(2,1)S(1)}, bf16[288,128]{1,0:T(8,128)(2,1)S(1)}, u32[]{:S(2)}, u32[]{:S(2)}) collective-permute-start(bf16[288,128]{1,0:T(8,128)(2,1)S(1)} %get-tuple-element.11.after.refs_0_), channel_id=1, source_target_pairs={{12,0},{8,4},{4,8},{0,12},{13,1},{9,5},{5,9},{1,13},{14,2},{10,6},... | collective-permute-start | bytes 221192 | tf_op jit(solution)/shard_map/ppermute | solution.py:396
  10.2 5.0 %collective-permute-start = (bf16[288,128]{1,0:T(8,128)(2,1)S(1)}, bf16[288,128]{1,0:T(8,128)(2,1)S(1)}, u32[]{:S(2)}, u32[]{:S(2)}) collective-permute-start(bf16[288,128]{1,0:T(8,128)(2,1)S(1)} %get-tuple-element.11.after.refs_0_), channel_id=1, source_target_pairs={{4,0},{12,4},{0,8},{8,12},{5,1},{13,5},{1,9},{9,13},{6,2},{14,6},{... | collective-permute-start | bytes 221192 | tf_op jit(solution)/shard_map/ppermute | solution.py:396
  16.5 1.3 %collective-permute-start.3 = (bf16[144,240]{1,0:T(8,128)(2,1)S(1)}, bf16[144,240]{1,0:T(8,128)(2,1)S(1)}, u32[]{:S(2)}, u32[]{:S(2)}) collective-permute-start(bf16[144,240]{1,0:T(8,128)(2,1)S(1)} %get-tuple-element.14), channel_id=1, source_target_pairs={{0,1},{1,0},{2,3},{3,2},{4,5},{5,4},{6,7},{7,6},{8,9},{9,8},{10,11... | collective-permute-start | bytes 207368 | tf_op jit(solution)/shard_map/ppermute | solution.py:341
  17.8 4.4 %collective-permute-start.6 = (bf16[144,240]{1,0:T(8,128)(2,1)S(1)}, bf16[144,240]{1,0:T(8,128)(2,1)S(1)}, u32[]{:S(2)}, u32[]{:S(2)}) collective-permute-start(bf16[144,240]{1,0:T(8,128)(2,1)S(1)} %add_convert_fusion.refs_0_), channel_id=1, source_target_pairs={{0,2},{1,3},{2,0},{3,1},{4,6},{5,7},{6,4},{7,5},{8,10},{9,11},{10,... | collective-permute-start | bytes 207368 | tf_op jit(solution)/shard_map/ppermute | solution.py:341
  20.1 1.3 %collective-permute-start.4 = (bf16[72,240]{1,0:T(8,128)(2,1)S(1)}, bf16[72,240]{1,0:T(8,128)(2,1)S(1)}, u32[]{:S(2)}, u32[]{:S(2)}) collective-permute-start(bf16[72,240]{1,0:T(8,128)(2,1)S(1)} %get-tuple-element.15), channel_id=1, source_target_pairs={{0,1},{1,0},{2,3},{3,2},{4,5},{5,4},{6,7},{7,6},{8,9},{9,8},{10,11... | collective-permute-start | bytes 103688 | tf_op jit(solution)/shard_map/ppermute | solution.py:341
  20.2 1.4 %collective-permute-start.5 = (bf16[72,240]{1,0:T(8,128)(2,1)S(1)}, bf16[72,240]{1,0:T(8,128)(2,1)S(1)}, u32[]{:S(2)}, u32[]{:S(2)}) collective-permute-start(bf16[72,240]{1,0:T(8,128)(2,1)S(1)} %get-tuple-element.16), channel_id=1, source_target_pairs={{0,1},{1,0},{2,3},{3,2},{4,5},{5,4},{6,7},{7,6},{8,9},{9,8},{10,11... | collective-permute-start | bytes 103688 | tf_op jit(solution)/shard_map/ppermute | solution.py:341

commit v23 on v22

--- a/solution.py
+++ b/solution.py
@@ -143,7 +143,7 @@
 
 def factors(n_layer, lengths, hidden, cotangent, gain, in_projection, out_projection, store):
     rows, width = hidden.shape
-    blocks = 2
+    blocks = 6
     far = (store.shape[0] // n_layer * (n_layer - 2), store.shape[1])
     args = (lengths, hidden, cotangent, gain, in_projection, out_projection, store)
     return pl.pallas_call(

time: 23.1 us -> 23.6 us (1.022)
  Pallas kernels: 10.3 us -> 10.9 us
    pallas_call x1, Pallas kernels: 4.66 us -> 5.2 us  [factors(): pl.pallas_call(functools.partial(factors_kernel, n_layer), out_shape=[jax...]
where the time goes in v23:
time: 23.6 us; the launch traced here: 23.5 us
  Pallas kernels  10.9 us (46%)
  starting transfers between devices  9.33 us (40%)
  waiting for transfers between devices  2.51 us (11%)
  other arithmetic  0.7 us (3%)
    ppermute x3, starting transfers between devices, on_device(): gathered.append(lax.ppermute(packed, 'store', pairs))  7.13 us
    pallas_call x1, Pallas kernels, factors(): pl.pallas_call(functools.partial(factors_kernel, n_layer), out_shape=[jax...  5.2 us
    pallas_call x3, Pallas kernels, scores(): pl.pallas_call(functools.partial(scores_kernel, at, skip=len(after)), out...  2.23 us
    ppermute x4, starting transfers between devices, swap(): return lax.ppermute(x, axis, pairs)  2.2 us
    pallas_call x1, Pallas kernels, fetch(): pl.pallas_call(functools.partial(fetch_kernel, n_layer), out_shape=jax.Sh...  2.15 us
    pallas_call x1, Pallas kernels, grads_and_scores(): pl.pallas_call(functools.partial(grads_kernel, n_store, queries // G, at)...  1.3 us
    ppermute x4, waiting for transfers between devices, swap(): return lax.ppermute(x, axis, pairs)  1.29 us
    ppermute x3, waiting for transfers between devices, on_device(): gathered.append(lax.ppermute(packed, 'store', pairs))  1.22 us
  transfers between devices with their start and end apart: 7, of which 5 were waited for; matrix products, arithmetic and copies ran while one was open for 0% of the time, Pallas kernels for 19%

profile of v23, /device:TPU:0, one launch (start us, length us, event | category | flops | bytes accessed | tf_op | source)
XLA Modules:
  0.0 23.5 jit_solution(3590007720847357616)
XLA Ops:
  0.0 5.2 %factors.1 = (bf16[288,128]{1,0:T(8,128)(2,1)S(1)}, bf16[480,4096]{1,0:T(8,128)(2,1)S(1)}) custom-call(s32[36]{0:T(128)} %hbm_lengths.1, bf16[288,8192]{1,0:T(8,128)(2,1)} %bitcast.9, bf16[288,1024]{1,0:T(8,128)(2,1)} %bitcast.11, bf16[1,8192]{1,0:T(2,128)(2,1)} %hbm_gain.1, bf16[64,8192]{1,0:T(8,128)(2,1)} %bitcast.10, bf16[64,1024]{1,0:T(8,128)(2,1)} %bitcast.12, ...), custom_call_target="tpu_custom_call" | custom-call | tf_op jit(solution)/shard_map/factors/pallas_call | solution.py:149
  5.2 3.1 %collective-permute-start.2 = (bf16[288,128]{1,0:T(8,128)(2,1)S(1)}, bf16[288,128]{1,0:T(8,128)(2,1)S(1)}, u32[]{:S(2)}, u32[]{:S(2)}) collective-permute-start(bf16[288,128]{1,0:T(8,128)(2,1)S(1)} %get-tuple-element.11.after.refs_0_), channel_id=1, source_target_pairs={{8,0},{0,4},{12,8},{4,12},{9,1},{1,5},{13,9},{5,13},{10,2},{2,6},{... | collective-permute-start | bytes 221192 | tf_op jit(solution)/shard_map/ppermute | solution.py:396
  8.3 2.5 %collective-permute-start.1 = (bf16[288,128]{1,0:T(8,128)(2,1)S(1)}, bf16[288,128]{1,0:T(8,128)(2,1)S(1)}, u32[]{:S(2)}, u32[]{:S(2)}) collective-permute-start(bf16[288,128]{1,0:T(8,128)(2,1)S(1)} %get-tuple-element.11.after.refs_0_), channel_id=1, source_target_pairs={{12,0},{8,4},{4,8},{0,12},{13,1},{9,5},{5,9},{1,13},{14,2},{10,6},... | collective-permute-start | bytes 221192 | tf_op jit(solution)/shard_map/ppermute | solution.py:396
  10.8 1.6 %collective-permute-start = (bf16[288,128]{1,0:T(8,128)(2,1)S(1)}, bf16[288,128]{1,0:T(8,128)(2,1)S(1)}, u32[]{:S(2)}, u32[]{:S(2)}) collective-permute-start(bf16[288,128]{1,0:T(8,128)(2,1)S(1)} %get-tuple-element.11.after.refs_0_), channel_id=1, source_target_pairs={{4,0},{12,4},{0,8},{8,12},{5,1},{13,5},{1,9},{9,13},{6,2},{14,6},{... | collective-permute-start | bytes 221192 | tf_op jit(solution)/shard_map/ppermute | solution.py:396
  12.3 2.2 %fetch.1.refs_5_.slab = bf16[480,4096]{1,0:T(8,128)(2,1)S(1)} custom-call(bf16[288,128]{1,0:T(8,128)(2,1)S(1)} %get-tuple-element.11.after.refs_0_, bf16[960,4096]{1,0:T(8,128)(2,1)} %bitcast.8), custom_call_target="tpu_custom_call" | custom-call | bytes 3932160 | tf_op jit(solution)/shard_map/fetch/pallas_call | solution.py:198
  14.5 0.0 collective-permute-done.2.refs_3_
  14.5 1.1 %collective-permute-done.1.refs_2_ = bf16[288,128]{1,0:T(8,128)(2,1)S(1)} collective-permute-done((bf16[288,128]{1,0:T(8,128)(2,1)S(1)}, bf16[288,128]{1,0:T(8,128)(2,1)S(1)}, u32[]{:S(2)}, u32[]{:S(2)}) %collective-permute-start.1) | collective-permute-done | bytes 73760 | tf_op jit(solution)/shard_map/ppermute | solution.py:396
  15.6 0.1 collective-permute-done.refs_1_
  15.7 1.3 %grads.1 = (bf16[144,4096]{1,0:T(8,128)(2,1)S(1)}, bf16[144,240]{1,0:T(8,128)(2,1)S(1)}) custom-call(bf16[288,128]{1,0:T(8,128)(2,1)S(1)} %get-tuple-element.11.after.refs_0_, bf16[288,128]{1,0:T(8,128)(2,1)S(1)} %collective-permute-done.refs_1_, bf16[288,128]{1,0:T(8,128)(2,1)S(1)} %collective-permute-done.1.refs_2_, ...), custom_call_target="tpu_custom_call" | custom-call | tf_op jit(solution)/shard_map/grads/pallas_call | solution.py:348
  17.0 0.1 collective-permute-start.3
  17.1 0.7 %scores.4 = f32[144,240]{1,0:T(8,128)S(1)} custom-call(bf16[144,4096]{1,0:T(8,128)(2,1)S(1)} %get-tuple-element.13.grads, bf16[480,4096]{1,0:T(8,128)(2,1)S(1)} %get-tuple-element.12.refs_4_.slab), custom_call_target="tpu_custom_call" | custom-call | flops 283115520 | bytes 3145728 | tf_op jit(solution)/shard_map/scores/pallas_call | solution.py:365
  17.9 0.5 %collective-permute-done.3 = bf16[144,240]{1,0:T(8,128)(2,1)S(1)} collective-permute-done((bf16[144,240]{1,0:T(8,128)(2,1)S(1)}, bf16[144,240]{1,0:T(8,128)(2,1)S(1)}, u32[]{:S(2)}, u32[]{:S(2)}) %collective-permute-start.3) | collective-permute-done | bytes 69152 | tf_op jit(solution)/shard_map/ppermute | solution.py:341
  18.4 1.6 %collective-permute-start.6 = (bf16[144,240]{1,0:T(8,128)(2,1)S(1)}, bf16[144,240]{1,0:T(8,128)(2,1)S(1)}, u32[]{:S(2)}, u32[]{:S(2)}) collective-permute-start(bf16[144,240]{1,0:T(8,128)(2,1)S(1)} %add_convert_fusion.refs_0_), channel_id=1, source_target_pairs={{0,2},{1,3},{2,0},{3,1},{4,6},{5,7},{6,4},{7,5},{8,10},{9,11},{10,... | collective-permute-start | bytes 207368 | tf_op jit(solution)/shard_map/ppermute | solution.py:341
  19.9 0.7 %scores.5 = (bf16[72,240]{1,0:T(8,128)(2,1)S(1)}, bf16[72,240]{1,0:T(8,128)(2,1)S(1)}) custom-call(bf16[144,4096]{1,0:T(8,128)(2,1)S(1)} %get-tuple-element.13.grads, bf16[480,4096]{1,0:T(8,128)(2,1)S(1)} %fetch.1.refs_5_.slab, bf16[144,240]{1,0:T(8,128)(2,1)S(1)} %add_convert_fusion.refs_0_), custom_call_target="tpu_custom_call" | custom-call | flops 283115520 | bytes 3145728 | tf_op jit(solution)/shard_map/scores/pallas_call | solution.py:365
  20.7 0.1 collective-permute-start.4
  20.8 0.5 %collective-permute-start.5 = (bf16[72,240]{1,0:T(8,128)(2,1)S(1)}, bf16[72,240]{1,0:T(8,128)(2,1)S(1)}, u32[]{:S(2)}, u32[]{:S(2)}) collective-permute-start(bf16[72,240]{1,0:T(8,128)(2,1)S(1)} %get-tuple-element.16), channel_id=1, source_target_pairs={{0,1},{1,0},{2,3},{3,2},{4,5},{5,4},{6,7},{7,6},{8,9},{9,8},{10,11... | collective-permute-start | bytes 103688 | tf_op jit(solution)/shard_map/ppermute | solution.py:341
  21.3 0.7 %scores.3 = f32[144,240]{1,0:T(8,128)S(1)} custom-call(bf16[144,4096]{1,0:T(8,128)(2,1)S(1)} %get-tuple-element.13.grads, bf16[480,4096]{1,0:T(8,128)(2,1)S(1)} %fetch.1.refs_5_.slab), custom_call_target="tpu_custom_call" | custom-call | flops 283115520 | bytes 3145728 | tf_op jit(solution)/shard_map/scores/pallas_call | solution.py:365
  22.0 0.0 collective-permute-done.4
  22.0 0.1 collective-permute-done.5
  22.1 0.7 %collective-permute-done.6 = bf16[144,240]{1,0:T(8,128)(2,1)S(1)} collective-permute-done((bf16[144,240]{1,0:T(8,128)(2,1)S(1)}, bf16[144,240]{1,0:T(8,128)(2,1)S(1)}, u32[]{:S(2)}, u32[]{:S(2)}) %collective-permute-start.6) | collective-permute-done | bytes 69152 | tf_op jit(solution)/shard_map/ppermute | solution.py:341
  22.8 0.7 %add_bitcast_fusion = f32[240,144]{0,1:T(8,128)} fusion(bf16[144,240]{1,0:T(8,128)(2,1)S(1)} %collective-permute-done.6, f32[144,240]{1,0:T(8,128)S(1)} %scores.3, bf16[72,240]{1,0:T(8,128)(2,1)S(1)} %collective-permute-done.5, bf16[72,240]{1,0:T(8,128)(2,1)S(1)} %collective-permute-done.4), kind=kLoop, calls=%fused_computation | loop fusion | flops 241920 | bytes 414720 | tf_op jit(solution)/shard_map/transpose | solution.py:414
  (1 shorter events, 0.0 us)
Async XLA Ops:
  5.2 9.3 %collective-permute-start.2 = (bf16[288,128]{1,0:T(8,128)(2,1)S(1)}, bf16[288,128]{1,0:T(8,128)(2,1)S(1)}, u32[]{:S(2)}, u32[]{:S(2)}) collective-permute-start(bf16[288,128]{1,0:T(8,128)(2,1)S(1)} %get-tuple-element.11.after.refs_0_), channel_id=1, source_target_pairs={{8,0},{0,4},{12,8},{4,12},{9,1},{1,5},{13,9},{5,13},{10,2},{2,6},{... | collective-permute-start | bytes 221192 | tf_op jit(solution)/shard_map/ppermute | solution.py:396
  8.3 7.3 %collective-permute-start.1 = (bf16[288,128]{1,0:T(8,128)(2,1)S(1)}, bf16[288,128]{1,0:T(8,128)(2,1)S(1)}, u32[]{:S(2)}, u32[]{:S(2)}) collective-permute-start(bf16[288,128]{1,0:T(8,128)(2,1)S(1)} %get-tuple-element.11.after.refs_0_), channel_id=1, source_target_pairs={{12,0},{8,4},{4,8},{0,12},{13,1},{9,5},{5,9},{1,13},{14,2},{10,6},... | collective-permute-start | bytes 221192 | tf_op jit(solution)/shard_map/ppermute | solution.py:396
  10.8 5.0 %collective-permute-start = (bf16[288,128]{1,0:T(8,128)(2,1)S(1)}, bf16[288,128]{1,0:T(8,128)(2,1)S(1)}, u32[]{:S(2)}, u32[]{:S(2)}) collective-permute-start(bf16[288,128]{1,0:T(8,128)(2,1)S(1)} %get-tuple-element.11.after.refs_0_), channel_id=1, source_target_pairs={{4,0},{12,4},{0,8},{8,12},{5,1},{13,5},{1,9},{9,13},{6,2},{14,6},{... | collective-permute-start | bytes 221192 | tf_op jit(solution)/shard_map/ppermute | solution.py:396
  17.0 1.3 %collective-permute-start.3 = (bf16[144,240]{1,0:T(8,128)(2,1)S(1)}, bf16[144,240]{1,0:T(8,128)(2,1)S(1)}, u32[]{:S(2)}, u32[]{:S(2)}) collective-permute-start(bf16[144,240]{1,0:T(8,128)(2,1)S(1)} %get-tuple-element.14), channel_id=1, source_target_pairs={{0,1},{1,0},{2,3},{3,2},{4,5},{5,4},{6,7},{7,6},{8,9},{9,8},{10,11... | collective-permute-start | bytes 207368 | tf_op jit(solution)/shard_map/ppermute | solution.py:341
  18.4 4.4 %collective-permute-start.6 = (bf16[144,240]{1,0:T(8,128)(2,1)S(1)}, bf16[144,240]{1,0:T(8,128)(2,1)S(1)}, u32[]{:S(2)}, u32[]{:S(2)}) collective-permute-start(bf16[144,240]{1,0:T(8,128)(2,1)S(1)} %add_convert_fusion.refs_0_), channel_id=1, source_target_pairs={{0,2},{1,3},{2,0},{3,1},{4,6},{5,7},{6,4},{7,5},{8,10},{9,11},{10,... | collective-permute-start | bytes 207368 | tf_op jit(solution)/shard_map/ppermute | solution.py:341
  20.7 1.3 %collective-permute-start.4 = (bf16[72,240]{1,0:T(8,128)(2,1)S(1)}, bf16[72,240]{1,0:T(8,128)(2,1)S(1)}, u32[]{:S(2)}, u32[]{:S(2)}) collective-permute-start(bf16[72,240]{1,0:T(8,128)(2,1)S(1)} %get-tuple-element.15), channel_id=1, source_target_pairs={{0,1},{1,0},{2,3},{3,2},{4,5},{5,4},{6,7},{7,6},{8,9},{9,8},{10,11... | collective-permute-start | bytes 103688 | tf_op jit(solution)/shard_map/ppermute | solution.py:341
  20.8 1.4 %collective-permute-start.5 = (bf16[72,240]{1,0:T(8,128)(2,1)S(1)}, bf16[72,240]{1,0:T(8,128)(2,1)S(1)}, u32[]{:S(2)}, u32[]{:S(2)}) collective-permute-start(bf16[72,240]{1,0:T(8,128)(2,1)S(1)} %get-tuple-element.16), channel_id=1, source_target_pairs={{0,1},{1,0},{2,3},{3,2},{4,5},{5,4},{6,7},{7,6},{8,9},{9,8},{10,11... | collective-permute-start | bytes 103688 | tf_op jit(solution)/shard_map/ppermute | solution.py:341

commit v24 on v21

--- a/solution.py
+++ b/solution.py
@@ -185,28 +185,35 @@
     return copies
 
 
-def fetch_kernel(n_layer, after, store, near, sems):
+def fetch_kernel(n_layer, packed, store, near, again, sems):
     copies = store_copies(store, near, range(2), sems, 0, n_layer)
     for copy in copies:
         copy.start()
+    again[...] = packed[...]
     for copy in copies:
         copy.wait()
 
 
-def fetch(after, store, n_layer):
+def fetch(packed, store, n_layer):
     rows, features = store.shape
     return pl.pallas_call(
         functools.partial(fetch_kernel, n_layer),
-        out_shape=jax.ShapeDtypeStruct((rows // n_layer * 2, features), bf16),
-        in_specs=[pl.BlockSpec(memory_space=pl.ANY)] * 2,
-        out_specs=pl.BlockSpec(memory_space=pltpu.VMEM),
+        out_shape=[
+            jax.ShapeDtypeStruct((rows // n_layer * 2, features), bf16),
+            jax.ShapeDtypeStruct(packed.shape, bf16),
+        ],
+        in_specs=[
+            pl.BlockSpec(memory_space=pltpu.VMEM),
+            pl.BlockSpec(memory_space=pl.ANY),
+        ],
+        out_specs=[pl.BlockSpec(memory_space=pltpu.VMEM)] * 2,
         scratch_shapes=[pltpu.SemaphoreType.DMA((2,))],
         compiler_params=pltpu.CompilerParams(vmem_limit_bytes=12 * 2**20),
         cost_estimate=pl.CostEstimate(
             flops=0, bytes_accessed=4 * rows * features // n_layer, transcendentals=0
         ),
         name="fetch",
-    )(after, in_hbm(store))
+    )(packed, in_hbm(store))
 
 
 def spread_out(tile, owner):
@@ -390,11 +397,11 @@
         out_proj[0],
         store[0],
     )
+    near, again = fetch(packed, store[0], n_layer)
     gathered = [packed]
     for away in range(1, n_store):
         pairs = [(source(to, away, n_store), to) for to in range(n_store)]
-        gathered.append(lax.ppermute(packed, "store", pairs))
-    near = fetch(packed, store[0], n_layer)
+        gathered.append(lax.ppermute(again if away == 1 else packed, "store", pairs))
     last = n_layer - 3
     grads, partial = grads_and_scores(gathered, far, block, last, near)
     crossed = []

time: 23 us -> 24.6 us (1.070)
  waiting for transfers between devices: 2.5 us -> 4.06 us
    ppermute x3, waiting for transfers between devices: 1.22 us -> 2.78 us  [on_device(): lax.ppermute(again if away == 1 else packed, 'store', pairs)]
  transfers between devices with their start and end apart: 7 -> 7, of which waited for: 5 -> 5; matrix products, arithmetic and copies ran while one was open for 0% -> 0% of each run, Pallas kernels for 19% -> 18%
where the time goes in v24:
time: 24.6 us; the launch traced here: 24.4 us
  Pallas kernels  10.2 us (41%)
  starting transfers between devices  9.37 us (38%)
  waiting for transfers between devices  4.06 us (17%)
  other arithmetic  0.7 us (3%)
    ppermute x3, starting transfers between devices, on_device(): lax.ppermute(again if away == 1 else packed, 'store', pairs)  7.18 us
    pallas_call x1, Pallas kernels, factors(): pl.pallas_call(functools.partial(factors_kernel, n_layer), out_shape=[jax...  4.54 us
    ppermute x3, waiting for transfers between devices, on_device(): lax.ppermute(again if away == 1 else packed, 'store', pairs)  2.78 us
    pallas_call x3, Pallas kernels, scores(): pl.pallas_call(functools.partial(scores_kernel, at, skip=len(after)), out...  2.23 us
    ppermute x4, starting transfers between devices, swap(): return lax.ppermute(x, axis, pairs)  2.2 us
    pallas_call x1, Pallas kernels, fetch(): pl.pallas_call(functools.partial(fetch_kernel, n_layer), out_shape=[jax.S...  2.16 us
    pallas_call x1, Pallas kernels, grads_and_scores(): pl.pallas_call(functools.partial(grads_kernel, n_store, queries // G, at)...  1.3 us
    ppermute x4, waiting for transfers between devices, swap(): return lax.ppermute(x, axis, pairs)  1.28 us
  transfers between devices with their start and end apart: 7, of which 5 were waited for; matrix products, arithmetic and copies ran while one was open for 0% of the time, Pallas kernels for 18%

profile of v24, /device:TPU:0, one launch (start us, length us, event | category | flops | bytes accessed | tf_op | source)
XLA Modules:
  0.0 24.4 jit_solution(10475589832092130550)
XLA Ops:
  0.0 4.5 %factors.1 = (bf16[288,128]{1,0:T(8,128)(2,1)S(1)}, bf16[480,4096]{1,0:T(8,128)(2,1)S(1)}) custom-call(s32[36]{0:T(128)} %hbm_lengths.1, bf16[288,8192]{1,0:T(8,128)(2,1)} %bitcast.9, bf16[288,1024]{1,0:T(8,128)(2,1)} %bitcast.11, bf16[1,8192]{1,0:T(2,128)(2,1)} %hbm_gain.1, bf16[64,8192]{1,0:T(8,128)(2,1)} %bitcast.10, bf16[64,1024]{1,0:T(8,128)(2,1)} %bitcast.12, ...), custom_call_target="tpu_custom_call" | custom-call | tf_op jit(solution)/shard_map/factors/pallas_call | solution.py:149
  4.5 3.1 %collective-permute-start.2 = (bf16[288,128]{1,0:T(8,128)(2,1)S(1)}, bf16[288,128]{1,0:T(8,128)(2,1)S(1)}, u32[]{:S(2)}, u32[]{:S(2)}) collective-permute-start(bf16[288,128]{1,0:T(8,128)(2,1)S(1)} %get-tuple-element.13.packed.refs_0_), channel_id=1, source_target_pairs={{8,0},{0,4},{12,8},{4,12},{9,1},{1,5},{13,9},{5,13},{10,2},{2,6},{... | collective-permute-start | bytes 221192 | tf_op jit(solution)/shard_map/ppermute | solution.py:404
  7.6 2.5 %collective-permute-start.1 = (bf16[288,128]{1,0:T(8,128)(2,1)S(1)}, bf16[288,128]{1,0:T(8,128)(2,1)S(1)}, u32[]{:S(2)}, u32[]{:S(2)}) collective-permute-start(bf16[288,128]{1,0:T(8,128)(2,1)S(1)} %get-tuple-element.13.packed.refs_0_), channel_id=1, source_target_pairs={{12,0},{8,4},{4,8},{0,12},{13,1},{9,5},{5,9},{1,13},{14,2},{10,6},... | collective-permute-start | bytes 221192 | tf_op jit(solution)/shard_map/ppermute | solution.py:404
  10.1 2.2 %fetch.1 = (bf16[480,4096]{1,0:T(8,128)(2,1)S(1)}, bf16[288,128]{1,0:T(8,128)(2,1)S(1)}) custom-call(bf16[288,128]{1,0:T(8,128)(2,1)S(1)} %get-tuple-element.13.packed.refs_0_, bf16[960,4096]{1,0:T(8,128)(2,1)} %bitcast.8), custom_call_target="tpu_custom_call" | custom-call | bytes 3932160 | tf_op jit(solution)/shard_map/fetch/pallas_call | solution.py:199
  12.3 1.6 %collective-permute-start = (bf16[288,128]{1,0:T(8,128)(2,1)S(1)}, bf16[288,128]{1,0:T(8,128)(2,1)S(1)}, u32[]{:S(2)}, u32[]{:S(2)}) collective-permute-start(bf16[288,128]{1,0:T(8,128)(2,1)S(1)} %get-tuple-element.14), channel_id=1, source_target_pairs={{4,0},{12,4},{0,8},{8,12},{5,1},{13,5},{1,9},{9,13},{6,2},{14,6},{... | collective-permute-start | bytes 221192 | tf_op jit(solution)/shard_map/ppermute | solution.py:404
  13.9 0.0 collective-permute-done.2.refs_3_
  13.9 0.1 collective-permute-done.1.refs_2_
  14.0 2.6 %collective-permute-done.refs_1_ = bf16[288,128]{1,0:T(8,128)(2,1)S(1)} collective-permute-done((bf16[288,128]{1,0:T(8,128)(2,1)S(1)}, bf16[288,128]{1,0:T(8,128)(2,1)S(1)}, u32[]{:S(2)}, u32[]{:S(2)}) %collective-permute-start) | collective-permute-done | bytes 73760 | tf_op jit(solution)/shard_map/ppermute | solution.py:404
  16.7 1.3 %grads.1 = (bf16[144,4096]{1,0:T(8,128)(2,1)S(1)}, bf16[144,240]{1,0:T(8,128)(2,1)S(1)}) custom-call(bf16[288,128]{1,0:T(8,128)(2,1)S(1)} %get-tuple-element.13.packed.refs_0_, bf16[288,128]{1,0:T(8,128)(2,1)S(1)} %collective-permute-done.refs_1_, bf16[288,128]{1,0:T(8,128)(2,1)S(1)} %collective-permute-done.1.refs_2_, ...), custom_call_target="tpu_custom_call" | custom-call | tf_op jit(solution)/shard_map/grads/pallas_call | solution.py:355
  18.0 0.1 collective-permute-start.3
  18.1 0.7 %scores.4 = f32[144,240]{1,0:T(8,128)S(1)} custom-call(bf16[144,4096]{1,0:T(8,128)(2,1)S(1)} %get-tuple-element.17.grads, bf16[480,4096]{1,0:T(8,128)(2,1)S(1)} %get-tuple-element.15.refs_4_.slab), custom_call_target="tpu_custom_call" | custom-call | flops 283115520 | bytes 3145728 | tf_op jit(solution)/shard_map/scores/pallas_call | solution.py:372
  18.8 0.5 %collective-permute-done.3 = bf16[144,240]{1,0:T(8,128)(2,1)S(1)} collective-permute-done((bf16[144,240]{1,0:T(8,128)(2,1)S(1)}, bf16[144,240]{1,0:T(8,128)(2,1)S(1)}, u32[]{:S(2)}, u32[]{:S(2)}) %collective-permute-start.3) | collective-permute-done | bytes 69152 | tf_op jit(solution)/shard_map/ppermute | solution.py:348
  19.3 1.6 %collective-permute-start.6 = (bf16[144,240]{1,0:T(8,128)(2,1)S(1)}, bf16[144,240]{1,0:T(8,128)(2,1)S(1)}, u32[]{:S(2)}, u32[]{:S(2)}) collective-permute-start(bf16[144,240]{1,0:T(8,128)(2,1)S(1)} %add_convert_fusion.refs_0_), channel_id=1, source_target_pairs={{0,2},{1,3},{2,0},{3,1},{4,6},{5,7},{6,4},{7,5},{8,10},{9,11},{10,... | collective-permute-start | bytes 207368 | tf_op jit(solution)/shard_map/ppermute | solution.py:348
  20.9 0.7 %scores.5 = (bf16[72,240]{1,0:T(8,128)(2,1)S(1)}, bf16[72,240]{1,0:T(8,128)(2,1)S(1)}) custom-call(bf16[144,4096]{1,0:T(8,128)(2,1)S(1)} %get-tuple-element.17.grads, bf16[480,4096]{1,0:T(8,128)(2,1)S(1)} %get-tuple-element.16.refs_5_.slab, bf16[144,240]{1,0:T(8,128)(2,1)S(1)} %add_convert_fusion.refs_0_), custom_call_target="tpu_custom_call" | custom-call | flops 283115520 | bytes 3145728 | tf_op jit(solution)/shard_map/scores/pallas_call | solution.py:372
  21.6 0.1 collective-permute-start.4
  21.7 0.5 %collective-permute-start.5 = (bf16[72,240]{1,0:T(8,128)(2,1)S(1)}, bf16[72,240]{1,0:T(8,128)(2,1)S(1)}, u32[]{:S(2)}, u32[]{:S(2)}) collective-permute-start(bf16[72,240]{1,0:T(8,128)(2,1)S(1)} %get-tuple-element.20), channel_id=1, source_target_pairs={{0,1},{1,0},{2,3},{3,2},{4,5},{5,4},{6,7},{7,6},{8,9},{9,8},{10,11... | collective-permute-start | bytes 103688 | tf_op jit(solution)/shard_map/ppermute | solution.py:348
  22.2 0.7 %scores.3 = f32[144,240]{1,0:T(8,128)S(1)} custom-call(bf16[144,4096]{1,0:T(8,128)(2,1)S(1)} %get-tuple-element.17.grads, bf16[480,4096]{1,0:T(8,128)(2,1)S(1)} %get-tuple-element.16.refs_5_.slab), custom_call_target="tpu_custom_call" | custom-call | flops 283115520 | bytes 3145728 | tf_op jit(solution)/shard_map/scores/pallas_call | solution.py:372
  23.0 0.0 collective-permute-done.4
  23.0 0.1 collective-permute-done.5
  23.1 0.7 %collective-permute-done.6 = bf16[144,240]{1,0:T(8,128)(2,1)S(1)} collective-permute-done((bf16[144,240]{1,0:T(8,128)(2,1)S(1)}, bf16[144,240]{1,0:T(8,128)(2,1)S(1)}, u32[]{:S(2)}, u32[]{:S(2)}) %collective-permute-start.6) | collective-permute-done | bytes 69152 | tf_op jit(solution)/shard_map/ppermute | solution.py:348
  23.7 0.7 %add_bitcast_fusion = f32[240,144]{0,1:T(8,128)} fusion(bf16[144,240]{1,0:T(8,128)(2,1)S(1)} %collective-permute-done.6, f32[144,240]{1,0:T(8,128)S(1)} %scores.3, bf16[72,240]{1,0:T(8,128)(2,1)S(1)} %collective-permute-done.5, bf16[72,240]{1,0:T(8,128)(2,1)S(1)} %collective-permute-done.4), kind=kLoop, calls=%fused_computation | loop fusion | flops 241920 | bytes 414720 | tf_op jit(solution)/shard_map/transpose | solution.py:421
  (1 shorter events, 0.0 us)
Async XLA Ops:
  4.5 9.3 %collective-permute-start.2 = (bf16[288,128]{1,0:T(8,128)(2,1)S(1)}, bf16[288,128]{1,0:T(8,128)(2,1)S(1)}, u32[]{:S(2)}, u32[]{:S(2)}) collective-permute-start(bf16[288,128]{1,0:T(8,128)(2,1)S(1)} %get-tuple-element.13.packed.refs_0_), channel_id=1, source_target_pairs={{8,0},{0,4},{12,8},{4,12},{9,1},{1,5},{13,9},{5,13},{10,2},{2,6},{... | collective-permute-start | bytes 221192 | tf_op jit(solution)/shard_map/ppermute | solution.py:404
  7.6 6.4 %collective-permute-start.1 = (bf16[288,128]{1,0:T(8,128)(2,1)S(1)}, bf16[288,128]{1,0:T(8,128)(2,1)S(1)}, u32[]{:S(2)}, u32[]{:S(2)}) collective-permute-start(bf16[288,128]{1,0:T(8,128)(2,1)S(1)} %get-tuple-element.13.packed.refs_0_), channel_id=1, source_target_pairs={{12,0},{8,4},{4,8},{0,12},{13,1},{9,5},{5,9},{1,13},{14,2},{10,6},... | collective-permute-start | bytes 221192 | tf_op jit(solution)/shard_map/ppermute | solution.py:404
  12.3 4.4 %collective-permute-start = (bf16[288,128]{1,0:T(8,128)(2,1)S(1)}, bf16[288,128]{1,0:T(8,128)(2,1)S(1)}, u32[]{:S(2)}, u32[]{:S(2)}) collective-permute-start(bf16[288,128]{1,0:T(8,128)(2,1)S(1)} %get-tuple-element.14), channel_id=1, source_target_pairs={{4,0},{12,4},{0,8},{8,12},{5,1},{13,5},{1,9},{9,13},{6,2},{14,6},{... | collective-permute-start | bytes 221192 | tf_op jit(solution)/shard_map/ppermute | solution.py:404
  18.0 1.3 %collective-permute-start.3 = (bf16[144,240]{1,0:T(8,128)(2,1)S(1)}, bf16[144,240]{1,0:T(8,128)(2,1)S(1)}, u32[]{:S(2)}, u32[]{:S(2)}) collective-permute-start(bf16[144,240]{1,0:T(8,128)(2,1)S(1)} %get-tuple-element.18), channel_id=1, source_target_pairs={{0,1},{1,0},{2,3},{3,2},{4,5},{5,4},{6,7},{7,6},{8,9},{9,8},{10,11... | collective-permute-start | bytes 207368 | tf_op jit(solution)/shard_map/ppermute | solution.py:348
  19.3 4.4 %collective-permute-start.6 = (bf16[144,240]{1,0:T(8,128)(2,1)S(1)}, bf16[144,240]{1,0:T(8,128)(2,1)S(1)}, u32[]{:S(2)}, u32[]{:S(2)}) collective-permute-start(bf16[144,240]{1,0:T(8,128)(2,1)S(1)} %add_convert_fusion.refs_0_), channel_id=1, source_target_pairs={{0,2},{1,3},{2,0},{3,1},{4,6},{5,7},{6,4},{7,5},{8,10},{9,11},{10,... | collective-permute-start | bytes 207368 | tf_op jit(solution)/shard_map/ppermute | solution.py:348
  21.6 1.3 %collective-permute-start.4 = (bf16[72,240]{1,0:T(8,128)(2,1)S(1)}, bf16[72,240]{1,0:T(8,128)(2,1)S(1)}, u32[]{:S(2)}, u32[]{:S(2)}) collective-permute-start(bf16[72,240]{1,0:T(8,128)(2,1)S(1)} %get-tuple-element.19), channel_id=1, source_target_pairs={{0,1},{1,0},{2,3},{3,2},{4,5},{5,4},{6,7},{7,6},{8,9},{9,8},{10,11... | collective-permute-start | bytes 103688 | tf_op jit(solution)/shard_map/ppermute | solution.py:348
  21.7 1.4 %collective-permute-start.5 = (bf16[72,240]{1,0:T(8,128)(2,1)S(1)}, bf16[72,240]{1,0:T(8,128)(2,1)S(1)}, u32[]{:S(2)}, u32[]{:S(2)}) collective-permute-start(bf16[72,240]{1,0:T(8,128)(2,1)S(1)} %get-tuple-element.20), channel_id=1, source_target_pairs={{0,1},{1,0},{2,3},{3,2},{4,5},{5,4},{6,7},{7,6},{8,9},{9,8},{10,11... | collective-permute-start | bytes 103688 | tf_op jit(solution)/shard_map/ppermute | solution.py:348

commit v25 on v21

--- a/solution.py
+++ b/solution.py
@@ -304,11 +304,15 @@
     return place ^ place // 2
 
 
+def shift_order(n):
+    return [2, 1, 3] if n == 4 else list(range(1, n))
+
+
 def grads_kernel(n_store, full_groups, k, *refs):
     gathered = refs[:n_store]
-    slab, _, grads, out, shards = refs[n_store:]
+    slab, _, grads, *outs, shards = refs[n_store:]
     me_store = lax.axis_index("store")
-    for away, block in enumerate(gathered):
+    for away, block in zip([0] + shift_order(n_store), gathered):
         shards[source(me_store, away, n_store)] = block[...]
     four = 4 * (full_groups * G + H)
     if n_store == 4:
@@ -319,7 +323,7 @@
         def _(at):
             build_grads(shards, at * 4, pl.multiple_of(at * four, 16), full_groups, grads)
 
-    scores_kernel(k, grads, slab, out)
+    scores_kernel(k, grads, slab, *outs)
 
 
 def scores_kernel(k, grads, slab, *refs, skip=0):
@@ -349,10 +353,10 @@
         functools.partial(grads_kernel, n_store, queries // G, at),
         out_shape=[
             jax.ShapeDtypeStruct((n_store * queries, slab.shape[1]), bf16),
-            jax.ShapeDtypeStruct((n_store * queries, block), bf16),
-        ],
+        ]
+        + [jax.ShapeDtypeStruct((n_store * queries // 2, block), bf16)] * 2,
         in_specs=[vmem] * (n_store + 1) + [pl.BlockSpec(memory_space=pl.ANY)],
-        out_specs=[vmem] * 2,
+        out_specs=[vmem] * 3,
         scratch_shapes=[pltpu.VMEM((n_store,) + gathered[0].shape, bf16)],
         compiler_params=pltpu.CompilerParams(vmem_limit_bytes=24 * 2**20),
         name="grads",
@@ -391,17 +395,17 @@
         store[0],
     )
     gathered = [packed]
-    for away in range(1, n_store):
+    for away in shift_order(n_store):
         pairs = [(source(to, away, n_store), to) for to in range(n_store)]
         gathered.append(lax.ppermute(packed, "store", pairs))
     near = fetch(packed, store[0], n_layer)
     last = n_layer - 3
-    grads, partial = grads_and_scores(gathered, far, block, last, near)
+    grads, *partial = grads_and_scores(gathered, far, block, last, near)
     crossed = []
     for at in reversed(range(0, last, 2)):
         if at + 1 < last:
-            (partial,) = scores(grads, far, block, at + 1, bf16)
-        other = swap(partial, "layer", n_layer, 1)
+            partial = scores(grads, far, block, at + 1, bf16)
+        other = jnp.concatenate([swap(x, "layer", n_layer, 1) for x in partial], axis=0)
         (mine,) = scores(grads, far, block, at, f32)
         joined = (mine + other.astype(f32)).astype(bf16)
         crossed.append(swap(joined, "layer", n_layer, at + 2))

time: 23 us -> 24.1 us (1.048)
  starting transfers between devices: 9.33 us -> 10.7 us
    ppermute x3, starting transfers between devices: 7.12 us -> 8.02 us  [on_device(): gathered.append(lax.ppermute(packed, 'store', pairs))]
    ppermute x4 -> x5, starting transfers between devices: 2.2 us -> 2.7 us  [swap(): return lax.ppermute(x, axis, pairs)]
    ppermute x4 -> x5, waiting for transfers between devices: 1.28 us -> 1.06 us  [swap(): return lax.ppermute(x, axis, pairs)]
  transfers between devices with their start and end apart: 7 -> 8, of which waited for: 5 -> 4; matrix products, arithmetic and copies ran while one was open for 0% -> 0% of each run, Pallas kernels for 19% -> 18%
where the time goes in v25:
time: 24.1 us; the launch traced here: 24 us
  starting transfers between devices  10.7 us (44%)
  Pallas kernels  10.2 us (42%)
  waiting for transfers between devices  2.27 us (9%)
  other arithmetic  0.71 us (3%)
    ppermute x3, starting transfers between devices, on_device(): gathered.append(lax.ppermute(packed, 'store', pairs))  8.02 us
    pallas_call x1, Pallas kernels, factors(): pl.pallas_call(functools.partial(factors_kernel, n_layer), out_shape=[jax...  4.54 us
    ppermute x5, starting transfers between devices, swap(): return lax.ppermute(x, axis, pairs)  2.7 us
    pallas_call x3, Pallas kernels, scores(): pl.pallas_call(functools.partial(scores_kernel, at, skip=len(after)), out...  2.23 us
    pallas_call x1, Pallas kernels, fetch(): pl.pallas_call(functools.partial(fetch_kernel, n_layer), out_shape=jax.Sh...  2.15 us
    pallas_call x1, Pallas kernels, grads_and_scores(): pl.pallas_call(functools.partial(grads_kernel, n_store, queries // G, at)...  1.3 us
    ppermute x3, waiting for transfers between devices, on_device(): gathered.append(lax.ppermute(packed, 'store', pairs))  1.21 us
    ppermute x5, waiting for transfers between devices, swap(): return lax.ppermute(x, axis, pairs)  1.06 us
  transfers between devices with their start and end apart: 8, of which 4 were waited for; matrix products, arithmetic and copies ran while one was open for 0% of the time, Pallas kernels for 18%

profile of v25, /device:TPU:0, one launch (start us, length us, event | category | flops | bytes accessed | tf_op | source)
XLA Modules:
  0.0 24.0 jit_solution(12613160311326734132)
XLA Ops:
  0.0 4.5 %factors.1 = (bf16[288,128]{1,0:T(8,128)(2,1)S(1)}, bf16[480,4096]{1,0:T(8,128)(2,1)S(1)}) custom-call(s32[36]{0:T(128)} %hbm_lengths.1, bf16[288,8192]{1,0:T(8,128)(2,1)} %bitcast.9, bf16[288,1024]{1,0:T(8,128)(2,1)} %bitcast.11, bf16[1,8192]{1,0:T(2,128)(2,1)} %hbm_gain.1, bf16[64,8192]{1,0:T(8,128)(2,1)} %bitcast.10, bf16[64,1024]{1,0:T(8,128)(2,1)} %bitcast.12, ...), custom_call_target="tpu_custom_call" | custom-call | tf_op jit(solution)/shard_map/factors/pallas_call | solution.py:149
  4.5 3.1 %collective-permute-start.2 = (bf16[288,128]{1,0:T(8,128)(2,1)S(1)}, bf16[288,128]{1,0:T(8,128)(2,1)S(1)}, u32[]{:S(2)}, u32[]{:S(2)}) collective-permute-start(bf16[288,128]{1,0:T(8,128)(2,1)S(1)} %get-tuple-element.12.after.refs_0_), channel_id=1, source_target_pairs={{8,0},{0,4},{12,8},{4,12},{9,1},{1,5},{13,9},{5,13},{10,2},{2,6},{... | collective-permute-start | bytes 221192 | tf_op jit(solution)/shard_map/ppermute | solution.py:400
  7.6 1.1 %collective-permute-start.1 = (bf16[288,128]{1,0:T(8,128)(2,1)S(1)}, bf16[288,128]{1,0:T(8,128)(2,1)S(1)}, u32[]{:S(2)}, u32[]{:S(2)}) collective-permute-start(bf16[288,128]{1,0:T(8,128)(2,1)S(1)} %get-tuple-element.12.after.refs_0_), channel_id=1, source_target_pairs={{4,0},{12,4},{0,8},{8,12},{5,1},{13,5},{1,9},{9,13},{6,2},{14,6},{... | collective-permute-start | bytes 221192 | tf_op jit(solution)/shard_map/ppermute | solution.py:400
  8.7 3.9 %collective-permute-start = (bf16[288,128]{1,0:T(8,128)(2,1)S(1)}, bf16[288,128]{1,0:T(8,128)(2,1)S(1)}, u32[]{:S(2)}, u32[]{:S(2)}) collective-permute-start(bf16[288,128]{1,0:T(8,128)(2,1)S(1)} %get-tuple-element.12.after.refs_0_), channel_id=1, source_target_pairs={{12,0},{8,4},{4,8},{0,12},{13,1},{9,5},{5,9},{1,13},{14,2},{10,6},... | collective-permute-start | bytes 221192 | tf_op jit(solution)/shard_map/ppermute | solution.py:400
  12.6 2.2 %fetch.1.refs_5_.slab = bf16[480,4096]{1,0:T(8,128)(2,1)S(1)} custom-call(bf16[288,128]{1,0:T(8,128)(2,1)S(1)} %get-tuple-element.12.after.refs_0_, bf16[960,4096]{1,0:T(8,128)(2,1)} %bitcast.8), custom_call_target="tpu_custom_call" | custom-call | bytes 3932160 | tf_op jit(solution)/shard_map/fetch/pallas_call | solution.py:198
  14.7 0.0 collective-permute-done.2.refs_3_
  14.7 0.0 collective-permute-done.1.refs_2_
  14.8 1.2 %collective-permute-done.refs_1_ = bf16[288,128]{1,0:T(8,128)(2,1)S(1)} collective-permute-done((bf16[288,128]{1,0:T(8,128)(2,1)S(1)}, bf16[288,128]{1,0:T(8,128)(2,1)S(1)}, u32[]{:S(2)}, u32[]{:S(2)}) %collective-permute-start) | collective-permute-done | bytes 73760 | tf_op jit(solution)/shard_map/ppermute | solution.py:400
  16.0 1.3 %grads.1 = (bf16[144,4096]{1,0:T(8,128)(2,1)S(1)}, bf16[72,240]{1,0:T(8,128)(2,1)S(1)}, bf16[72,240]{1,0:T(8,128)(2,1)S(1)}) custom-call(bf16[288,128]{1,0:T(8,128)(2,1)S(1)} %get-tuple-element.12.after.refs_0_, bf16[288,128]{1,0:T(8,128)(2,1)S(1)} %collective-permute-done.refs_1_, bf16[288,128]{1,0:T(8,128)(2,1)S(1)} %collective-permute-done.1.refs_2_, ...), custom_call_target="tpu_custom_call" | custom-call | tf_op jit(solution)/shard_map/grads/pallas_call | solution.py:352
  17.3 0.1 collective-permute-start.3
  17.3 0.5 %collective-permute-start.4 = (bf16[72,240]{1,0:T(8,128)(2,1)S(1)}, bf16[72,240]{1,0:T(8,128)(2,1)S(1)}, u32[]{:S(2)}, u32[]{:S(2)}) collective-permute-start(bf16[72,240]{1,0:T(8,128)(2,1)S(1)} %get-tuple-element.16), channel_id=1, source_target_pairs={{0,1},{1,0},{2,3},{3,2},{4,5},{5,4},{6,7},{7,6},{8,9},{9,8},{10,11... | collective-permute-start | bytes 103688 | tf_op jit(solution)/shard_map/ppermute | solution.py:345
  17.8 0.7 %scores.4 = f32[144,240]{1,0:T(8,128)S(1)} custom-call(bf16[144,4096]{1,0:T(8,128)(2,1)S(1)} %get-tuple-element.14.grads, bf16[480,4096]{1,0:T(8,128)(2,1)S(1)} %get-tuple-element.13.refs_4_.slab), custom_call_target="tpu_custom_call" | custom-call | flops 283115520 | bytes 3145728 | tf_op jit(solution)/shard_map/scores/pallas_call | solution.py:369
  18.6 0.0 collective-permute-done.3
  18.6 0.1 collective-permute-done.4
  18.7 1.6 %collective-permute-start.7 = (bf16[144,240]{1,0:T(8,128)(2,1)S(1)}, bf16[144,240]{1,0:T(8,128)(2,1)S(1)}, u32[]{:S(2)}, u32[]{:S(2)}) collective-permute-start(bf16[144,240]{1,0:T(8,128)(2,1)S(1)} %add_convert_fusion.refs_0_), channel_id=1, source_target_pairs={{0,2},{1,3},{2,0},{3,1},{4,6},{5,7},{6,4},{7,5},{8,10},{9,11},{10,... | collective-permute-start | bytes 207368 | tf_op jit(solution)/shard_map/ppermute | solution.py:345
  20.3 0.7 %scores.5 = (bf16[72,240]{1,0:T(8,128)(2,1)S(1)}, bf16[72,240]{1,0:T(8,128)(2,1)S(1)}) custom-call(bf16[144,4096]{1,0:T(8,128)(2,1)S(1)} %get-tuple-element.14.grads, bf16[480,4096]{1,0:T(8,128)(2,1)S(1)} %fetch.1.refs_5_.slab, bf16[144,240]{1,0:T(8,128)(2,1)S(1)} %add_convert_fusion.refs_0_), custom_call_target="tpu_custom_call" | custom-call | flops 283115520 | bytes 3145728 | tf_op jit(solution)/shard_map/scores/pallas_call | solution.py:369
  21.0 0.1 collective-permute-start.5
  21.2 0.4 %collective-permute-start.6 = (bf16[72,240]{1,0:T(8,128)(2,1)S(1)}, bf16[72,240]{1,0:T(8,128)(2,1)S(1)}, u32[]{:S(2)}, u32[]{:S(2)}) collective-permute-start(bf16[72,240]{1,0:T(8,128)(2,1)S(1)} %get-tuple-element.18), channel_id=1, source_target_pairs={{0,1},{1,0},{2,3},{3,2},{4,5},{5,4},{6,7},{7,6},{8,9},{9,8},{10,11... | collective-permute-start | bytes 103688 | tf_op jit(solution)/shard_map/ppermute | solution.py:345
  21.6 0.7 %scores.3 = f32[144,240]{1,0:T(8,128)S(1)} custom-call(bf16[144,4096]{1,0:T(8,128)(2,1)S(1)} %get-tuple-element.14.grads, bf16[480,4096]{1,0:T(8,128)(2,1)S(1)} %fetch.1.refs_5_.slab), custom_call_target="tpu_custom_call" | custom-call | flops 283115520 | bytes 3145728 | tf_op jit(solution)/shard_map/scores/pallas_call | solution.py:369
  22.4 0.0 collective-permute-done.5
  22.4 0.1 collective-permute-done.6
  22.5 0.8 %collective-permute-done.7 = bf16[144,240]{1,0:T(8,128)(2,1)S(1)} collective-permute-done((bf16[144,240]{1,0:T(8,128)(2,1)S(1)}, bf16[144,240]{1,0:T(8,128)(2,1)S(1)}, u32[]{:S(2)}, u32[]{:S(2)}) %collective-permute-start.7) | collective-permute-done | bytes 69152 | tf_op jit(solution)/shard_map/ppermute | solution.py:345
  23.3 0.7 %add_bitcast_fusion = f32[240,144]{0,1:T(8,128)} fusion(bf16[144,240]{1,0:T(8,128)(2,1)S(1)} %collective-permute-done.7, f32[144,240]{1,0:T(8,128)S(1)} %scores.3, bf16[72,240]{1,0:T(8,128)(2,1)S(1)} %collective-permute-done.6, bf16[72,240]{1,0:T(8,128)(2,1)S(1)} %collective-permute-done.5), kind=kLoop, calls=%fused_computation | loop fusion | flops 241920 | bytes 414720 | tf_op jit(solution)/shard_map/transpose | solution.py:418
  (1 shorter events, 0.0 us)
Async XLA Ops:
  4.5 10.2 %collective-permute-start.2 = (bf16[288,128]{1,0:T(8,128)(2,1)S(1)}, bf16[288,128]{1,0:T(8,128)(2,1)S(1)}, u32[]{:S(2)}, u32[]{:S(2)}) collective-permute-start(bf16[288,128]{1,0:T(8,128)(2,1)S(1)} %get-tuple-element.12.after.refs_0_), channel_id=1, source_target_pairs={{8,0},{0,4},{12,8},{4,12},{9,1},{1,5},{13,9},{5,13},{10,2},{2,6},{... | collective-permute-start | bytes 221192 | tf_op jit(solution)/shard_map/ppermute | solution.py:400
  7.6 7.1 %collective-permute-start.1 = (bf16[288,128]{1,0:T(8,128)(2,1)S(1)}, bf16[288,128]{1,0:T(8,128)(2,1)S(1)}, u32[]{:S(2)}, u32[]{:S(2)}) collective-permute-start(bf16[288,128]{1,0:T(8,128)(2,1)S(1)} %get-tuple-element.12.after.refs_0_), channel_id=1, source_target_pairs={{4,0},{12,4},{0,8},{8,12},{5,1},{13,5},{1,9},{9,13},{6,2},{14,6},{... | collective-permute-start | bytes 221192 | tf_op jit(solution)/shard_map/ppermute | solution.py:400
  8.7 7.3 %collective-permute-start = (bf16[288,128]{1,0:T(8,128)(2,1)S(1)}, bf16[288,128]{1,0:T(8,128)(2,1)S(1)}, u32[]{:S(2)}, u32[]{:S(2)}) collective-permute-start(bf16[288,128]{1,0:T(8,128)(2,1)S(1)} %get-tuple-element.12.after.refs_0_), channel_id=1, source_target_pairs={{12,0},{8,4},{4,8},{0,12},{13,1},{9,5},{5,9},{1,13},{14,2},{10,6},... | collective-permute-start | bytes 221192 | tf_op jit(solution)/shard_map/ppermute | solution.py:400
  17.3 1.3 %collective-permute-start.3 = (bf16[72,240]{1,0:T(8,128)(2,1)S(1)}, bf16[72,240]{1,0:T(8,128)(2,1)S(1)}, u32[]{:S(2)}, u32[]{:S(2)}) collective-permute-start(bf16[72,240]{1,0:T(8,128)(2,1)S(1)} %get-tuple-element.15), channel_id=1, source_target_pairs={{0,1},{1,0},{2,3},{3,2},{4,5},{5,4},{6,7},{7,6},{8,9},{9,8},{10,11... | collective-permute-start | bytes 103688 | tf_op jit(solution)/shard_map/ppermute | solution.py:345
  17.3 1.4 %collective-permute-start.4 = (bf16[72,240]{1,0:T(8,128)(2,1)S(1)}, bf16[72,240]{1,0:T(8,128)(2,1)S(1)}, u32[]{:S(2)}, u32[]{:S(2)}) collective-permute-start(bf16[72,240]{1,0:T(8,128)(2,1)S(1)} %get-tuple-element.16), channel_id=1, source_target_pairs={{0,1},{1,0},{2,3},{3,2},{4,5},{5,4},{6,7},{7,6},{8,9},{9,8},{10,11... | collective-permute-start | bytes 103688 | tf_op jit(solution)/shard_map/ppermute | solution.py:345
  18.7 4.6 %collective-permute-start.7 = (bf16[144,240]{1,0:T(8,128)(2,1)S(1)}, bf16[144,240]{1,0:T(8,128)(2,1)S(1)}, u32[]{:S(2)}, u32[]{:S(2)}) collective-permute-start(bf16[144,240]{1,0:T(8,128)(2,1)S(1)} %add_convert_fusion.refs_0_), channel_id=1, source_target_pairs={{0,2},{1,3},{2,0},{3,1},{4,6},{5,7},{6,4},{7,5},{8,10},{9,11},{10,... | collective-permute-start | bytes 207368 | tf_op jit(solution)/shard_map/ppermute | solution.py:345
  21.0 1.3 %collective-permute-start.5 = (bf16[72,240]{1,0:T(8,128)(2,1)S(1)}, bf16[72,240]{1,0:T(8,128)(2,1)S(1)}, u32[]{:S(2)}, u32[]{:S(2)}) collective-permute-start(bf16[72,240]{1,0:T(8,128)(2,1)S(1)} %get-tuple-element.17), channel_id=1, source_target_pairs={{0,1},{1,0},{2,3},{3,2},{4,5},{5,4},{6,7},{7,6},{8,9},{9,8},{10,11... | collective-permute-start | bytes 103688 | tf_op jit(solution)/shard_map/ppermute | solution.py:345
  21.2 1.3 %collective-permute-start.6 = (bf16[72,240]{1,0:T(8,128)(2,1)S(1)}, bf16[72,240]{1,0:T(8,128)(2,1)S(1)}, u32[]{:S(2)}, u32[]{:S(2)}) collective-permute-start(bf16[72,240]{1,0:T(8,128)(2,1)S(1)} %get-tuple-element.18), channel_id=1, source_target_pairs={{0,1},{1,0},{2,3},{3,2},{4,5},{5,4},{6,7},{7,6},{8,9},{9,8},{10,11... | collective-permute-start | bytes 103688 | tf_op jit(solution)/shard_map/ppermute | solution.py:345

commit v26 on v21

--- a/solution.py
+++ b/solution.py
@@ -103,6 +103,7 @@
     for piece in then:
         piece.wait()
     weights[...] = inp[...] * gain[...]
+    position = iota((S, R), 0)
 
     @pl.loop(0, blocks)
     def _(r):
@@ -115,24 +116,22 @@
         mean_square = jnp.sum(total, axis=1, keepdims=True) * (1.0 / width)
         factor = product * lax.rsqrt(mean_square + norm_epsilon)
         at = pl.ds(pl.multiple_of(r * step, step), step)
+        live = [
+            jnp.where(position < lengths[r * (step // S) + q], factor[q * S : (q + 1) * S], 0.0)
+            for q in range(step // S)
+        ]
+        factor = jnp.concatenate(live, axis=0)
         in_acc[at, :] = jnp.concatenate([factor, factor], axis=1)
 
-    low_lanes = iota((S, LANES), 1) < R
-    position = iota((S, LANES), 0)
-
-    def in_rows(at, count):
-        factor = in_acc[pl.ds(at, count), :]
-        return [
-            jnp.where(position < lengths[at // S + q], factor[q * S : (q + 1) * S], 0.0)
-            for q in range(count // S)
-        ]
-
-    def side_by_side(tiles):
-        both = zip(tiles[: len(tiles) // 2], tiles[len(tiles) // 2 :])
-        return jnp.concatenate([jnp.where(low_lanes, x, y) for x, y in both], axis=0)
-
-    packed[:mid, :] = side_by_side(in_rows(at_full, full)).astype(bf16)
-    packed[mid : mid + low, :] = side_by_side(in_rows(at_half, half)).astype(bf16)
+    low_lanes = iota((1, LANES), 1) < R
+
+    def side_by_side(at, count):
+        left = in_acc[pl.ds(at, count // 2), :]
+        right = in_acc[pl.ds(at + count // 2, count // 2), :]
+        return jnp.where(low_lanes, left, right).astype(bf16)
+
+    packed[:mid, :] = side_by_side(at_full, full)
+    packed[mid : mid + low, :] = side_by_side(at_half, half)
     for piece in slab:
         piece.wait()
 

time: 23 us -> 23 us (level)
  no operation moved by 1% of the time
where the time goes in v26:
time: 23 us; the launch traced here: 22.8 us
  Pallas kernels  10.2 us (44%)
  starting transfers between devices  9.32 us (41%)
  waiting for transfers between devices  2.51 us (11%)
  other arithmetic  0.7 us (3%)
    ppermute x3, starting transfers between devices, on_device(): gathered.append(lax.ppermute(packed, 'store', pairs))  7.12 us
    pallas_call x1, Pallas kernels, factors(): pl.pallas_call(functools.partial(factors_kernel, n_layer), out_shape=[jax...  4.52 us
    pallas_call x3, Pallas kernels, scores(): pl.pallas_call(functools.partial(scores_kernel, at, skip=len(after)), out...  2.24 us
    ppermute x4, starting transfers between devices, swap(): return lax.ppermute(x, axis, pairs)  2.2 us
    pallas_call x1, Pallas kernels, fetch(): pl.pallas_call(functools.partial(fetch_kernel, n_layer), out_shape=jax.Sh...  2.15 us
    pallas_call x1, Pallas kernels, grads_and_scores(): pl.pallas_call(functools.partial(grads_kernel, n_store, queries // G, at)...  1.3 us
    ppermute x4, waiting for transfers between devices, swap(): return lax.ppermute(x, axis, pairs)  1.28 us
    ppermute x3, waiting for transfers between devices, on_device(): gathered.append(lax.ppermute(packed, 'store', pairs))  1.23 us
  transfers between devices with their start and end apart: 7, of which 5 were waited for; matrix products, arithmetic and copies ran while one was open for 0% of the time, Pallas kernels for 19%

profile of v26, /device:TPU:0, one launch (start us, length us, event | category | flops | bytes accessed | tf_op | source)
XLA Modules:
  0.0 22.8 jit_solution(5794076189576234721)
XLA Ops:
  0.0 4.5 %factors.1 = (bf16[288,128]{1,0:T(8,128)(2,1)S(1)}, bf16[480,4096]{1,0:T(8,128)(2,1)S(1)}) custom-call(s32[36]{0:T(128)} %hbm_lengths.1, bf16[288,8192]{1,0:T(8,128)(2,1)} %bitcast.9, bf16[288,1024]{1,0:T(8,128)(2,1)} %bitcast.11, bf16[1,8192]{1,0:T(2,128)(2,1)} %hbm_gain.1, bf16[64,8192]{1,0:T(8,128)(2,1)} %bitcast.10, bf16[64,1024]{1,0:T(8,128)(2,1)} %bitcast.12, ...), custom_call_target="tpu_custom_call" | custom-call | tf_op jit(solution)/shard_map/factors/pallas_call | solution.py:148
  4.5 3.1 %collective-permute-start.2 = (bf16[288,128]{1,0:T(8,128)(2,1)S(1)}, bf16[288,128]{1,0:T(8,128)(2,1)S(1)}, u32[]{:S(2)}, u32[]{:S(2)}) collective-permute-start(bf16[288,128]{1,0:T(8,128)(2,1)S(1)} %get-tuple-element.11.after.refs_0_), channel_id=1, source_target_pairs={{8,0},{0,4},{12,8},{4,12},{9,1},{1,5},{13,9},{5,13},{10,2},{2,6},{... | collective-permute-start | bytes 221192 | tf_op jit(solution)/shard_map/ppermute | solution.py:395
  7.6 2.5 %collective-permute-start.1 = (bf16[288,128]{1,0:T(8,128)(2,1)S(1)}, bf16[288,128]{1,0:T(8,128)(2,1)S(1)}, u32[]{:S(2)}, u32[]{:S(2)}) collective-permute-start(bf16[288,128]{1,0:T(8,128)(2,1)S(1)} %get-tuple-element.11.after.refs_0_), channel_id=1, source_target_pairs={{12,0},{8,4},{4,8},{0,12},{13,1},{9,5},{5,9},{1,13},{14,2},{10,6},... | collective-permute-start | bytes 221192 | tf_op jit(solution)/shard_map/ppermute | solution.py:395
  10.1 1.6 %collective-permute-start = (bf16[288,128]{1,0:T(8,128)(2,1)S(1)}, bf16[288,128]{1,0:T(8,128)(2,1)S(1)}, u32[]{:S(2)}, u32[]{:S(2)}) collective-permute-start(bf16[288,128]{1,0:T(8,128)(2,1)S(1)} %get-tuple-element.11.after.refs_0_), channel_id=1, source_target_pairs={{4,0},{12,4},{0,8},{8,12},{5,1},{13,5},{1,9},{9,13},{6,2},{14,6},{... | collective-permute-start | bytes 221192 | tf_op jit(solution)/shard_map/ppermute | solution.py:395
  11.7 2.2 %fetch.1.refs_5_.slab = bf16[480,4096]{1,0:T(8,128)(2,1)S(1)} custom-call(bf16[288,128]{1,0:T(8,128)(2,1)S(1)} %get-tuple-element.11.after.refs_0_, bf16[960,4096]{1,0:T(8,128)(2,1)} %bitcast.8), custom_call_target="tpu_custom_call" | custom-call | bytes 3932160 | tf_op jit(solution)/shard_map/fetch/pallas_call | solution.py:197
  13.8 0.0 collective-permute-done.2.refs_3_
  13.8 1.1 %collective-permute-done.1.refs_2_ = bf16[288,128]{1,0:T(8,128)(2,1)S(1)} collective-permute-done((bf16[288,128]{1,0:T(8,128)(2,1)S(1)}, bf16[288,128]{1,0:T(8,128)(2,1)S(1)}, u32[]{:S(2)}, u32[]{:S(2)}) %collective-permute-start.1) | collective-permute-done | bytes 73760 | tf_op jit(solution)/shard_map/ppermute | solution.py:395
  14.9 0.1 collective-permute-done.refs_1_
  15.1 1.3 %grads.1 = (bf16[144,4096]{1,0:T(8,128)(2,1)S(1)}, bf16[144,240]{1,0:T(8,128)(2,1)S(1)}) custom-call(bf16[288,128]{1,0:T(8,128)(2,1)S(1)} %get-tuple-element.11.after.refs_0_, bf16[288,128]{1,0:T(8,128)(2,1)S(1)} %collective-permute-done.refs_1_, bf16[288,128]{1,0:T(8,128)(2,1)S(1)} %collective-permute-done.1.refs_2_, ...), custom_call_target="tpu_custom_call" | custom-call | tf_op jit(solution)/shard_map/grads/pallas_call | solution.py:347
  16.4 0.1 collective-permute-start.3
  16.4 0.7 %scores.4 = f32[144,240]{1,0:T(8,128)S(1)} custom-call(bf16[144,4096]{1,0:T(8,128)(2,1)S(1)} %get-tuple-element.13.grads, bf16[480,4096]{1,0:T(8,128)(2,1)S(1)} %get-tuple-element.12.refs_4_.slab), custom_call_target="tpu_custom_call" | custom-call | flops 283115520 | bytes 3145728 | tf_op jit(solution)/shard_map/scores/pallas_call | solution.py:364
  17.2 0.5 %collective-permute-done.3 = bf16[144,240]{1,0:T(8,128)(2,1)S(1)} collective-permute-done((bf16[144,240]{1,0:T(8,128)(2,1)S(1)}, bf16[144,240]{1,0:T(8,128)(2,1)S(1)}, u32[]{:S(2)}, u32[]{:S(2)}) %collective-permute-start.3) | collective-permute-done | bytes 69152 | tf_op jit(solution)/shard_map/ppermute | solution.py:340
  17.7 1.6 %collective-permute-start.6 = (bf16[144,240]{1,0:T(8,128)(2,1)S(1)}, bf16[144,240]{1,0:T(8,128)(2,1)S(1)}, u32[]{:S(2)}, u32[]{:S(2)}) collective-permute-start(bf16[144,240]{1,0:T(8,128)(2,1)S(1)} %add_convert_fusion.refs_0_), channel_id=1, source_target_pairs={{0,2},{1,3},{2,0},{3,1},{4,6},{5,7},{6,4},{7,5},{8,10},{9,11},{10,... | collective-permute-start | bytes 207368 | tf_op jit(solution)/shard_map/ppermute | solution.py:340
  19.3 0.7 %scores.5 = (bf16[72,240]{1,0:T(8,128)(2,1)S(1)}, bf16[72,240]{1,0:T(8,128)(2,1)S(1)}) custom-call(bf16[144,4096]{1,0:T(8,128)(2,1)S(1)} %get-tuple-element.13.grads, bf16[480,4096]{1,0:T(8,128)(2,1)S(1)} %fetch.1.refs_5_.slab, bf16[144,240]{1,0:T(8,128)(2,1)S(1)} %add_convert_fusion.refs_0_), custom_call_target="tpu_custom_call" | custom-call | flops 283115520 | bytes 3145728 | tf_op jit(solution)/shard_map/scores/pallas_call | solution.py:364
  20.0 0.1 collective-permute-start.4
  20.1 0.5 %collective-permute-start.5 = (bf16[72,240]{1,0:T(8,128)(2,1)S(1)}, bf16[72,240]{1,0:T(8,128)(2,1)S(1)}, u32[]{:S(2)}, u32[]{:S(2)}) collective-permute-start(bf16[72,240]{1,0:T(8,128)(2,1)S(1)} %get-tuple-element.16), channel_id=1, source_target_pairs={{0,1},{1,0},{2,3},{3,2},{4,5},{5,4},{6,7},{7,6},{8,9},{9,8},{10,11... | collective-permute-start | bytes 103688 | tf_op jit(solution)/shard_map/ppermute | solution.py:340
  20.6 0.7 %scores.3 = f32[144,240]{1,0:T(8,128)S(1)} custom-call(bf16[144,4096]{1,0:T(8,128)(2,1)S(1)} %get-tuple-element.13.grads, bf16[480,4096]{1,0:T(8,128)(2,1)S(1)} %fetch.1.refs_5_.slab), custom_call_target="tpu_custom_call" | custom-call | flops 283115520 | bytes 3145728 | tf_op jit(solution)/shard_map/scores/pallas_call | solution.py:364
  21.3 0.0 collective-permute-done.4
  21.4 0.1 collective-permute-done.5
  21.5 0.7 %collective-permute-done.6 = bf16[144,240]{1,0:T(8,128)(2,1)S(1)} collective-permute-done((bf16[144,240]{1,0:T(8,128)(2,1)S(1)}, bf16[144,240]{1,0:T(8,128)(2,1)S(1)}, u32[]{:S(2)}, u32[]{:S(2)}) %collective-permute-start.6) | collective-permute-done | bytes 69152 | tf_op jit(solution)/shard_map/ppermute | solution.py:340
  22.1 0.7 %add_bitcast_fusion = f32[240,144]{0,1:T(8,128)} fusion(bf16[144,240]{1,0:T(8,128)(2,1)S(1)} %collective-permute-done.6, f32[144,240]{1,0:T(8,128)S(1)} %scores.3, bf16[72,240]{1,0:T(8,128)(2,1)S(1)} %collective-permute-done.5, bf16[72,240]{1,0:T(8,128)(2,1)S(1)} %collective-permute-done.4), kind=kLoop, calls=%fused_computation | loop fusion | flops 241920 | bytes 414720 | tf_op jit(solution)/shard_map/transpose | solution.py:413
  (1 shorter events, 0.0 us)
Async XLA Ops:
  4.5 9.3 %collective-permute-start.2 = (bf16[288,128]{1,0:T(8,128)(2,1)S(1)}, bf16[288,128]{1,0:T(8,128)(2,1)S(1)}, u32[]{:S(2)}, u32[]{:S(2)}) collective-permute-start(bf16[288,128]{1,0:T(8,128)(2,1)S(1)} %get-tuple-element.11.after.refs_0_), channel_id=1, source_target_pairs={{8,0},{0,4},{12,8},{4,12},{9,1},{1,5},{13,9},{5,13},{10,2},{2,6},{... | collective-permute-start | bytes 221192 | tf_op jit(solution)/shard_map/ppermute | solution.py:395
  7.6 7.3 %collective-permute-start.1 = (bf16[288,128]{1,0:T(8,128)(2,1)S(1)}, bf16[288,128]{1,0:T(8,128)(2,1)S(1)}, u32[]{:S(2)}, u32[]{:S(2)}) collective-permute-start(bf16[288,128]{1,0:T(8,128)(2,1)S(1)} %get-tuple-element.11.after.refs_0_), channel_id=1, source_target_pairs={{12,0},{8,4},{4,8},{0,12},{13,1},{9,5},{5,9},{1,13},{14,2},{10,6},... | collective-permute-start | bytes 221192 | tf_op jit(solution)/shard_map/ppermute | solution.py:395
  10.1 5.0 %collective-permute-start = (bf16[288,128]{1,0:T(8,128)(2,1)S(1)}, bf16[288,128]{1,0:T(8,128)(2,1)S(1)}, u32[]{:S(2)}, u32[]{:S(2)}) collective-permute-start(bf16[288,128]{1,0:T(8,128)(2,1)S(1)} %get-tuple-element.11.after.refs_0_), channel_id=1, source_target_pairs={{4,0},{12,4},{0,8},{8,12},{5,1},{13,5},{1,9},{9,13},{6,2},{14,6},{... | collective-permute-start | bytes 221192 | tf_op jit(solution)/shard_map/ppermute | solution.py:395
  16.4 1.3 %collective-permute-start.3 = (bf16[144,240]{1,0:T(8,128)(2,1)S(1)}, bf16[144,240]{1,0:T(8,128)(2,1)S(1)}, u32[]{:S(2)}, u32[]{:S(2)}) collective-permute-start(bf16[144,240]{1,0:T(8,128)(2,1)S(1)} %get-tuple-element.14), channel_id=1, source_target_pairs={{0,1},{1,0},{2,3},{3,2},{4,5},{5,4},{6,7},{7,6},{8,9},{9,8},{10,11... | collective-permute-start | bytes 207368 | tf_op jit(solution)/shard_map/ppermute | solution.py:340
  17.7 4.4 %collective-permute-start.6 = (bf16[144,240]{1,0:T(8,128)(2,1)S(1)}, bf16[144,240]{1,0:T(8,128)(2,1)S(1)}, u32[]{:S(2)}, u32[]{:S(2)}) collective-permute-start(bf16[144,240]{1,0:T(8,128)(2,1)S(1)} %add_convert_fusion.refs_0_), channel_id=1, source_target_pairs={{0,2},{1,3},{2,0},{3,1},{4,6},{5,7},{6,4},{7,5},{8,10},{9,11},{10,... | collective-permute-start | bytes 207368 | tf_op jit(solution)/shard_map/ppermute | solution.py:340
  20.0 1.3 %collective-permute-start.4 = (bf16[72,240]{1,0:T(8,128)(2,1)S(1)}, bf16[72,240]{1,0:T(8,128)(2,1)S(1)}, u32[]{:S(2)}, u32[]{:S(2)}) collective-permute-start(bf16[72,240]{1,0:T(8,128)(2,1)S(1)} %get-tuple-element.15), channel_id=1, source_target_pairs={{0,1},{1,0},{2,3},{3,2},{4,5},{5,4},{6,7},{7,6},{8,9},{9,8},{10,11... | collective-permute-start | bytes 103688 | tf_op jit(solution)/shard_map/ppermute | solution.py:340
  20.1 1.4 %collective-permute-start.5 = (bf16[72,240]{1,0:T(8,128)(2,1)S(1)}, bf16[72,240]{1,0:T(8,128)(2,1)S(1)}, u32[]{:S(2)}, u32[]{:S(2)}) collective-permute-start(bf16[72,240]{1,0:T(8,128)(2,1)S(1)} %get-tuple-element.16), channel_id=1, source_target_pairs={{0,1},{1,0},{2,3},{3,2},{4,5},{5,4},{6,7},{7,6},{8,9},{9,8},{10,11... | collective-permute-start | bytes 103688 | tf_op jit(solution)/shard_map/ppermute | solution.py:340

commit v27 on v21

--- a/solution.py
+++ b/solution.py
@@ -300,15 +300,19 @@
 def source(to, away, n):
     if n != 4:
         return (to + away) % n
-    place = ((to ^ to // 2) + away) % n
-    return place ^ place // 2
+    place = (to % 2 * 2 + to // 2 + away) % n
+    return place % 2 * 2 + place // 2
+
+
+def shift_order(n):
+    return [2, 1, 3] if n == 4 else list(range(1, n))
 
 
 def grads_kernel(n_store, full_groups, k, *refs):
     gathered = refs[:n_store]
     slab, _, grads, out, shards = refs[n_store:]
     me_store = lax.axis_index("store")
-    for away, block in enumerate(gathered):
+    for away, block in zip([0] + shift_order(n_store), gathered):
         shards[source(me_store, away, n_store)] = block[...]
     four = 4 * (full_groups * G + H)
     if n_store == 4:
@@ -391,7 +395,7 @@
         store[0],
     )
     gathered = [packed]
-    for away in range(1, n_store):
+    for away in shift_order(n_store):
         pairs = [(source(to, away, n_store), to) for to in range(n_store)]
         gathered.append(lax.ppermute(packed, "store", pairs))
     near = fetch(packed, store[0], n_layer)

time: 23 us -> 23.8 us (1.035)
  waiting for transfers between devices: 2.5 us -> 4.77 us
  starting transfers between devices: 9.33 us -> 7.86 us
    ppermute x3, waiting for transfers between devices: 1.22 us -> 3.49 us  [on_device(): gathered.append(lax.ppermute(packed, 'store', pairs))]
    ppermute x3, starting transfers between devices: 7.12 us -> 5.66 us  [on_device(): gathered.append(lax.ppermute(packed, 'store', pairs))]
  transfers between devices with their start and end apart: 7 -> 7, of which waited for: 5 -> 4; matrix products, arithmetic and copies ran while one was open for 0% -> 0% of each run, Pallas kernels for 19% -> 19%
where the time goes in v27:
time: 23.8 us; the launch traced here: 23.6 us
  Pallas kernels  10.2 us (43%)
  starting transfers between devices  7.86 us (33%)
  waiting for transfers between devices  4.77 us (20%)
  other arithmetic  0.7 us (3%)
    ppermute x3, starting transfers between devices, on_device(): gathered.append(lax.ppermute(packed, 'store', pairs))  5.66 us
    pallas_call x1, Pallas kernels, factors(): pl.pallas_call(functools.partial(factors_kernel, n_layer), out_shape=[jax...  4.54 us
    ppermute x3, waiting for transfers between devices, on_device(): gathered.append(lax.ppermute(packed, 'store', pairs))  3.49 us
    pallas_call x3, Pallas kernels, scores(): pl.pallas_call(functools.partial(scores_kernel, at, skip=len(after)), out...  2.23 us
    ppermute x4, starting transfers between devices, swap(): return lax.ppermute(x, axis, pairs)  2.19 us
    pallas_call x1, Pallas kernels, fetch(): pl.pallas_call(functools.partial(fetch_kernel, n_layer), out_shape=jax.Sh...  2.15 us
    pallas_call x1, Pallas kernels, grads_and_scores(): pl.pallas_call(functools.partial(grads_kernel, n_store, queries // G, at)...  1.3 us
    ppermute x4, waiting for transfers between devices, swap(): return lax.ppermute(x, axis, pairs)  1.29 us
  transfers between devices with their start and end apart: 7, of which 4 were waited for; matrix products, arithmetic and copies ran while one was open for 0% of the time, Pallas kernels for 19%

profile of v27, /device:TPU:0, one launch (start us, length us, event | category | flops | bytes accessed | tf_op | source)
XLA Modules:
  0.0 23.6 jit_solution(1509243947400368504)
XLA Ops:
  0.0 4.5 %factors.1 = (bf16[288,128]{1,0:T(8,128)(2,1)S(1)}, bf16[480,4096]{1,0:T(8,128)(2,1)S(1)}) custom-call(s32[36]{0:T(128)} %hbm_lengths.1, bf16[288,8192]{1,0:T(8,128)(2,1)} %bitcast.9, bf16[288,1024]{1,0:T(8,128)(2,1)} %bitcast.11, bf16[1,8192]{1,0:T(2,128)(2,1)} %hbm_gain.1, bf16[64,8192]{1,0:T(8,128)(2,1)} %bitcast.10, bf16[64,1024]{1,0:T(8,128)(2,1)} %bitcast.12, ...), custom_call_target="tpu_custom_call" | custom-call | tf_op jit(solution)/shard_map/factors/pallas_call | solution.py:149
  4.5 4.1 %collective-permute-start.2 = (bf16[288,128]{1,0:T(8,128)(2,1)S(1)}, bf16[288,128]{1,0:T(8,128)(2,1)S(1)}, u32[]{:S(2)}, u32[]{:S(2)}) collective-permute-start(bf16[288,128]{1,0:T(8,128)(2,1)S(1)} %get-tuple-element.11.after.refs_0_), channel_id=1, source_target_pairs={{12,0},{8,4},{0,8},{4,12},{13,1},{9,5},{1,9},{5,13},{14,2},{10,6},... | collective-permute-start | bytes 221192 | tf_op jit(solution)/shard_map/ppermute | solution.py:400
  8.6 1.1 %collective-permute-start.1 = (bf16[288,128]{1,0:T(8,128)(2,1)S(1)}, bf16[288,128]{1,0:T(8,128)(2,1)S(1)}, u32[]{:S(2)}, u32[]{:S(2)}) collective-permute-start(bf16[288,128]{1,0:T(8,128)(2,1)S(1)} %get-tuple-element.11.after.refs_0_), channel_id=1, source_target_pairs={{8,0},{12,4},{4,8},{0,12},{9,1},{13,5},{5,9},{1,13},{10,2},{14,6},... | collective-permute-start | bytes 221192 | tf_op jit(solution)/shard_map/ppermute | solution.py:400
  9.7 0.5 %collective-permute-start = (bf16[288,128]{1,0:T(8,128)(2,1)S(1)}, bf16[288,128]{1,0:T(8,128)(2,1)S(1)}, u32[]{:S(2)}, u32[]{:S(2)}) collective-permute-start(bf16[288,128]{1,0:T(8,128)(2,1)S(1)} %get-tuple-element.11.after.refs_0_), channel_id=1, source_target_pairs={{4,0},{0,4},{12,8},{8,12},{5,1},{1,5},{13,9},{9,13},{6,2},{2,6},{1... | collective-permute-start | bytes 221192 | tf_op jit(solution)/shard_map/ppermute | solution.py:400
  10.2 2.2 %fetch.1.refs_5_.slab = bf16[480,4096]{1,0:T(8,128)(2,1)S(1)} custom-call(bf16[288,128]{1,0:T(8,128)(2,1)S(1)} %get-tuple-element.11.after.refs_0_, bf16[960,4096]{1,0:T(8,128)(2,1)} %bitcast.8), custom_call_target="tpu_custom_call" | custom-call | bytes 3932160 | tf_op jit(solution)/shard_map/fetch/pallas_call | solution.py:198
  12.4 0.0 collective-permute-done.2.refs_3_
  12.4 3.5 %collective-permute-done.1.refs_2_ = bf16[288,128]{1,0:T(8,128)(2,1)S(1)} collective-permute-done((bf16[288,128]{1,0:T(8,128)(2,1)S(1)}, bf16[288,128]{1,0:T(8,128)(2,1)S(1)}, u32[]{:S(2)}, u32[]{:S(2)}) %collective-permute-start.1) | collective-permute-done | bytes 73760 | tf_op jit(solution)/shard_map/ppermute | solution.py:400
  15.9 0.0 collective-permute-done.refs_1_
  15.9 1.3 %grads.1 = (bf16[144,4096]{1,0:T(8,128)(2,1)S(1)}, bf16[144,240]{1,0:T(8,128)(2,1)S(1)}) custom-call(bf16[288,128]{1,0:T(8,128)(2,1)S(1)} %get-tuple-element.11.after.refs_0_, bf16[288,128]{1,0:T(8,128)(2,1)S(1)} %collective-permute-done.refs_1_, bf16[288,128]{1,0:T(8,128)(2,1)S(1)} %collective-permute-done.1.refs_2_, ...), custom_call_target="tpu_custom_call" | custom-call | tf_op jit(solution)/shard_map/grads/pallas_call | solution.py:352
  17.2 0.1 collective-permute-start.3
  17.3 0.7 %scores.4 = f32[144,240]{1,0:T(8,128)S(1)} custom-call(bf16[144,4096]{1,0:T(8,128)(2,1)S(1)} %get-tuple-element.13.grads, bf16[480,4096]{1,0:T(8,128)(2,1)S(1)} %get-tuple-element.12.refs_4_.slab), custom_call_target="tpu_custom_call" | custom-call | flops 283115520 | bytes 3145728 | tf_op jit(solution)/shard_map/scores/pallas_call | solution.py:369
  18.0 0.5 %collective-permute-done.3 = bf16[144,240]{1,0:T(8,128)(2,1)S(1)} collective-permute-done((bf16[144,240]{1,0:T(8,128)(2,1)S(1)}, bf16[144,240]{1,0:T(8,128)(2,1)S(1)}, u32[]{:S(2)}, u32[]{:S(2)}) %collective-permute-start.3) | collective-permute-done | bytes 69152 | tf_op jit(solution)/shard_map/ppermute | solution.py:345
  18.5 1.6 %collective-permute-start.6 = (bf16[144,240]{1,0:T(8,128)(2,1)S(1)}, bf16[144,240]{1,0:T(8,128)(2,1)S(1)}, u32[]{:S(2)}, u32[]{:S(2)}) collective-permute-start(bf16[144,240]{1,0:T(8,128)(2,1)S(1)} %add_convert_fusion.refs_0_), channel_id=1, source_target_pairs={{0,2},{1,3},{2,0},{3,1},{4,6},{5,7},{6,4},{7,5},{8,10},{9,11},{10,... | collective-permute-start | bytes 207368 | tf_op jit(solution)/shard_map/ppermute | solution.py:345
  20.1 0.7 %scores.5 = (bf16[72,240]{1,0:T(8,128)(2,1)S(1)}, bf16[72,240]{1,0:T(8,128)(2,1)S(1)}) custom-call(bf16[144,4096]{1,0:T(8,128)(2,1)S(1)} %get-tuple-element.13.grads, bf16[480,4096]{1,0:T(8,128)(2,1)S(1)} %fetch.1.refs_5_.slab, bf16[144,240]{1,0:T(8,128)(2,1)S(1)} %add_convert_fusion.refs_0_), custom_call_target="tpu_custom_call" | custom-call | flops 283115520 | bytes 3145728 | tf_op jit(solution)/shard_map/scores/pallas_call | solution.py:369
  20.8 0.1 collective-permute-start.4
  20.9 0.5 %collective-permute-start.5 = (bf16[72,240]{1,0:T(8,128)(2,1)S(1)}, bf16[72,240]{1,0:T(8,128)(2,1)S(1)}, u32[]{:S(2)}, u32[]{:S(2)}) collective-permute-start(bf16[72,240]{1,0:T(8,128)(2,1)S(1)} %get-tuple-element.16), channel_id=1, source_target_pairs={{0,1},{1,0},{2,3},{3,2},{4,5},{5,4},{6,7},{7,6},{8,9},{9,8},{10,11... | collective-permute-start | bytes 103688 | tf_op jit(solution)/shard_map/ppermute | solution.py:345
  21.4 0.7 %scores.3 = f32[144,240]{1,0:T(8,128)S(1)} custom-call(bf16[144,4096]{1,0:T(8,128)(2,1)S(1)} %get-tuple-element.13.grads, bf16[480,4096]{1,0:T(8,128)(2,1)S(1)} %fetch.1.refs_5_.slab), custom_call_target="tpu_custom_call" | custom-call | flops 283115520 | bytes 3145728 | tf_op jit(solution)/shard_map/scores/pallas_call | solution.py:369
  22.2 0.0 collective-permute-done.4
  22.2 0.1 collective-permute-done.5
  22.3 0.7 %collective-permute-done.6 = bf16[144,240]{1,0:T(8,128)(2,1)S(1)} collective-permute-done((bf16[144,240]{1,0:T(8,128)(2,1)S(1)}, bf16[144,240]{1,0:T(8,128)(2,1)S(1)}, u32[]{:S(2)}, u32[]{:S(2)}) %collective-permute-start.6) | collective-permute-done | bytes 69152 | tf_op jit(solution)/shard_map/ppermute | solution.py:345
  22.9 0.7 %add_bitcast_fusion = f32[240,144]{0,1:T(8,128)} fusion(bf16[144,240]{1,0:T(8,128)(2,1)S(1)} %collective-permute-done.6, f32[144,240]{1,0:T(8,128)S(1)} %scores.3, bf16[72,240]{1,0:T(8,128)(2,1)S(1)} %collective-permute-done.5, bf16[72,240]{1,0:T(8,128)(2,1)S(1)} %collective-permute-done.4), kind=kLoop, calls=%fused_computation | loop fusion | flops 241920 | bytes 414720 | tf_op jit(solution)/shard_map/transpose | solution.py:418
  (1 shorter events, 0.0 us)
Async XLA Ops:
  4.5 7.8 %collective-permute-start.2 = (bf16[288,128]{1,0:T(8,128)(2,1)S(1)}, bf16[288,128]{1,0:T(8,128)(2,1)S(1)}, u32[]{:S(2)}, u32[]{:S(2)}) collective-permute-start(bf16[288,128]{1,0:T(8,128)(2,1)S(1)} %get-tuple-element.11.after.refs_0_), channel_id=1, source_target_pairs={{12,0},{8,4},{0,8},{4,12},{13,1},{9,5},{1,9},{5,13},{14,2},{10,6},... | collective-permute-start | bytes 221192 | tf_op jit(solution)/shard_map/ppermute | solution.py:400
  8.6 7.2 %collective-permute-start.1 = (bf16[288,128]{1,0:T(8,128)(2,1)S(1)}, bf16[288,128]{1,0:T(8,128)(2,1)S(1)}, u32[]{:S(2)}, u32[]{:S(2)}) collective-permute-start(bf16[288,128]{1,0:T(8,128)(2,1)S(1)} %get-tuple-element.11.after.refs_0_), channel_id=1, source_target_pairs={{8,0},{12,4},{4,8},{0,12},{9,1},{13,5},{5,9},{1,13},{10,2},{14,6},... | collective-permute-start | bytes 221192 | tf_op jit(solution)/shard_map/ppermute | solution.py:400
  9.7 6.2 %collective-permute-start = (bf16[288,128]{1,0:T(8,128)(2,1)S(1)}, bf16[288,128]{1,0:T(8,128)(2,1)S(1)}, u32[]{:S(2)}, u32[]{:S(2)}) collective-permute-start(bf16[288,128]{1,0:T(8,128)(2,1)S(1)} %get-tuple-element.11.after.refs_0_), channel_id=1, source_target_pairs={{4,0},{0,4},{12,8},{8,12},{5,1},{1,5},{13,9},{9,13},{6,2},{2,6},{1... | collective-permute-start | bytes 221192 | tf_op jit(solution)/shard_map/ppermute | solution.py:400
  17.2 1.3 %collective-permute-start.3 = (bf16[144,240]{1,0:T(8,128)(2,1)S(1)}, bf16[144,240]{1,0:T(8,128)(2,1)S(1)}, u32[]{:S(2)}, u32[]{:S(2)}) collective-permute-start(bf16[144,240]{1,0:T(8,128)(2,1)S(1)} %get-tuple-element.14), channel_id=1, source_target_pairs={{0,1},{1,0},{2,3},{3,2},{4,5},{5,4},{6,7},{7,6},{8,9},{9,8},{10,11... | collective-permute-start | bytes 207368 | tf_op jit(solution)/shard_map/ppermute | solution.py:345
  18.5 4.4 %collective-permute-start.6 = (bf16[144,240]{1,0:T(8,128)(2,1)S(1)}, bf16[144,240]{1,0:T(8,128)(2,1)S(1)}, u32[]{:S(2)}, u32[]{:S(2)}) collective-permute-start(bf16[144,240]{1,0:T(8,128)(2,1)S(1)} %add_convert_fusion.refs_0_), channel_id=1, source_target_pairs={{0,2},{1,3},{2,0},{3,1},{4,6},{5,7},{6,4},{7,5},{8,10},{9,11},{10,... | collective-permute-start | bytes 207368 | tf_op jit(solution)/shard_map/ppermute | solution.py:345
  20.8 1.3 %collective-permute-start.4 = (bf16[72,240]{1,0:T(8,128)(2,1)S(1)}, bf16[72,240]{1,0:T(8,128)(2,1)S(1)}, u32[]{:S(2)}, u32[]{:S(2)}) collective-permute-start(bf16[72,240]{1,0:T(8,128)(2,1)S(1)} %get-tuple-element.15), channel_id=1, source_target_pairs={{0,1},{1,0},{2,3},{3,2},{4,5},{5,4},{6,7},{7,6},{8,9},{9,8},{10,11... | collective-permute-start | bytes 103688 | tf_op jit(solution)/shard_map/ppermute | solution.py:345
  20.9 1.4 %collective-permute-start.5 = (bf16[72,240]{1,0:T(8,128)(2,1)S(1)}, bf16[72,240]{1,0:T(8,128)(2,1)S(1)}, u32[]{:S(2)}, u32[]{:S(2)}) collective-permute-start(bf16[72,240]{1,0:T(8,128)(2,1)S(1)} %get-tuple-element.16), channel_id=1, source_target_pairs={{0,1},{1,0},{2,3},{3,2},{4,5},{5,4},{6,7},{7,6},{8,9},{9,8},{10,11... | collective-permute-start | bytes 103688 | tf_op jit(solution)/shard_map/ppermute | solution.py:345

commit v28 on v21

--- a/solution.py
+++ b/solution.py
@@ -65,7 +65,7 @@
 
     first = [copy(hbm_outp, outp, 0), copy(hbm_cot, cot, 1)]
     then = [copy(hbm_gain, gain, 2), copy(hbm_inp, inp, 3), copy(hbm_lengths, lengths, 4)]
-    for piece in first + then + [block_rows(0)]:
+    for piece in first + then + [block_rows(r) for r in range(blocks)]:
         piece.start()
     odd = lax.rem(lax.axis_index("store"), 2)
     at_full = pl.multiple_of(odd * half, half)
@@ -76,8 +76,6 @@
 
     @pl.when(odd >= 0)
     def _():
-        for r in range(1, blocks):
-            block_rows(r).start()
         for piece in slab:
             piece.start()
 

time: 23 us -> 23 us (level)
  no operation moved by 1% of the time
where the time goes in v28:
time: 23 us; the launch traced here: 22.8 us
  Pallas kernels  10.2 us (44%)
  starting transfers between devices  9.33 us (41%)
  waiting for transfers between devices  2.5 us (11%)
  other arithmetic  0.7 us (3%)
    ppermute x3, starting transfers between devices, on_device(): gathered.append(lax.ppermute(packed, 'store', pairs))  7.12 us
    pallas_call x1, Pallas kernels, factors(): pl.pallas_call(functools.partial(factors_kernel, n_layer), out_shape=[jax...  4.54 us
    pallas_call x3, Pallas kernels, scores(): pl.pallas_call(functools.partial(scores_kernel, at, skip=len(after)), out...  2.23 us
    ppermute x4, starting transfers between devices, swap(): return lax.ppermute(x, axis, pairs)  2.2 us
    pallas_call x1, Pallas kernels, fetch(): pl.pallas_call(functools.partial(fetch_kernel, n_layer), out_shape=jax.Sh...  2.15 us
    pallas_call x1, Pallas kernels, grads_and_scores(): pl.pallas_call(functools.partial(grads_kernel, n_store, queries // G, at)...  1.3 us
    ppermute x4, waiting for transfers between devices, swap(): return lax.ppermute(x, axis, pairs)  1.28 us
    ppermute x3, waiting for transfers between devices, on_device(): gathered.append(lax.ppermute(packed, 'store', pairs))  1.22 us
  transfers between devices with their start and end apart: 7, of which 5 were waited for; matrix products, arithmetic and copies ran while one was open for 0% of the time, Pallas kernels for 19%

profile of v28, /device:TPU:0, one launch (start us, length us, event | category | flops | bytes accessed | tf_op | source)
XLA Modules:
  0.0 22.8 jit_solution(12724059656659504420)
XLA Ops:
  0.0 4.5 %factors.1 = (bf16[288,128]{1,0:T(8,128)(2,1)S(1)}, bf16[480,4096]{1,0:T(8,128)(2,1)S(1)}) custom-call(s32[36]{0:T(128)} %hbm_lengths.1, bf16[288,8192]{1,0:T(8,128)(2,1)} %bitcast.9, bf16[288,1024]{1,0:T(8,128)(2,1)} %bitcast.11, bf16[1,8192]{1,0:T(2,128)(2,1)} %hbm_gain.1, bf16[64,8192]{1,0:T(8,128)(2,1)} %bitcast.10, bf16[64,1024]{1,0:T(8,128)(2,1)} %bitcast.12, ...), custom_call_target="tpu_custom_call" | custom-call | tf_op jit(solution)/shard_map/factors/pallas_call | solution.py:147
  4.5 3.1 %collective-permute-start.2 = (bf16[288,128]{1,0:T(8,128)(2,1)S(1)}, bf16[288,128]{1,0:T(8,128)(2,1)S(1)}, u32[]{:S(2)}, u32[]{:S(2)}) collective-permute-start(bf16[288,128]{1,0:T(8,128)(2,1)S(1)} %get-tuple-element.11.after.refs_0_), channel_id=1, source_target_pairs={{8,0},{0,4},{12,8},{4,12},{9,1},{1,5},{13,9},{5,13},{10,2},{2,6},{... | collective-permute-start | bytes 221192 | tf_op jit(solution)/shard_map/ppermute | solution.py:394
  7.6 2.5 %collective-permute-start.1 = (bf16[288,128]{1,0:T(8,128)(2,1)S(1)}, bf16[288,128]{1,0:T(8,128)(2,1)S(1)}, u32[]{:S(2)}, u32[]{:S(2)}) collective-permute-start(bf16[288,128]{1,0:T(8,128)(2,1)S(1)} %get-tuple-element.11.after.refs_0_), channel_id=1, source_target_pairs={{12,0},{8,4},{4,8},{0,12},{13,1},{9,5},{5,9},{1,13},{14,2},{10,6},... | collective-permute-start | bytes 221192 | tf_op jit(solution)/shard_map/ppermute | solution.py:394
  10.1 1.6 %collective-permute-start = (bf16[288,128]{1,0:T(8,128)(2,1)S(1)}, bf16[288,128]{1,0:T(8,128)(2,1)S(1)}, u32[]{:S(2)}, u32[]{:S(2)}) collective-permute-start(bf16[288,128]{1,0:T(8,128)(2,1)S(1)} %get-tuple-element.11.after.refs_0_), channel_id=1, source_target_pairs={{4,0},{12,4},{0,8},{8,12},{5,1},{13,5},{1,9},{9,13},{6,2},{14,6},{... | collective-permute-start | bytes 221192 | tf_op jit(solution)/shard_map/ppermute | solution.py:394
  11.7 2.2 %fetch.1.refs_5_.slab = bf16[480,4096]{1,0:T(8,128)(2,1)S(1)} custom-call(bf16[288,128]{1,0:T(8,128)(2,1)S(1)} %get-tuple-element.11.after.refs_0_, bf16[960,4096]{1,0:T(8,128)(2,1)} %bitcast.8), custom_call_target="tpu_custom_call" | custom-call | bytes 3932160 | tf_op jit(solution)/shard_map/fetch/pallas_call | solution.py:196
  13.8 0.0 collective-permute-done.2.refs_3_
  13.8 1.1 %collective-permute-done.1.refs_2_ = bf16[288,128]{1,0:T(8,128)(2,1)S(1)} collective-permute-done((bf16[288,128]{1,0:T(8,128)(2,1)S(1)}, bf16[288,128]{1,0:T(8,128)(2,1)S(1)}, u32[]{:S(2)}, u32[]{:S(2)}) %collective-permute-start.1) | collective-permute-done | bytes 73760 | tf_op jit(solution)/shard_map/ppermute | solution.py:394
  14.9 0.1 collective-permute-done.refs_1_
  15.1 1.3 %grads.1 = (bf16[144,4096]{1,0:T(8,128)(2,1)S(1)}, bf16[144,240]{1,0:T(8,128)(2,1)S(1)}) custom-call(bf16[288,128]{1,0:T(8,128)(2,1)S(1)} %get-tuple-element.11.after.refs_0_, bf16[288,128]{1,0:T(8,128)(2,1)S(1)} %collective-permute-done.refs_1_, bf16[288,128]{1,0:T(8,128)(2,1)S(1)} %collective-permute-done.1.refs_2_, ...), custom_call_target="tpu_custom_call" | custom-call | tf_op jit(solution)/shard_map/grads/pallas_call | solution.py:346
  16.4 0.1 collective-permute-start.3
  16.4 0.7 %scores.4 = f32[144,240]{1,0:T(8,128)S(1)} custom-call(bf16[144,4096]{1,0:T(8,128)(2,1)S(1)} %get-tuple-element.13.grads, bf16[480,4096]{1,0:T(8,128)(2,1)S(1)} %get-tuple-element.12.refs_4_.slab), custom_call_target="tpu_custom_call" | custom-call | flops 283115520 | bytes 3145728 | tf_op jit(solution)/shard_map/scores/pallas_call | solution.py:363
  17.2 0.5 %collective-permute-done.3 = bf16[144,240]{1,0:T(8,128)(2,1)S(1)} collective-permute-done((bf16[144,240]{1,0:T(8,128)(2,1)S(1)}, bf16[144,240]{1,0:T(8,128)(2,1)S(1)}, u32[]{:S(2)}, u32[]{:S(2)}) %collective-permute-start.3) | collective-permute-done | bytes 69152 | tf_op jit(solution)/shard_map/ppermute | solution.py:339
  17.7 1.6 %collective-permute-start.6 = (bf16[144,240]{1,0:T(8,128)(2,1)S(1)}, bf16[144,240]{1,0:T(8,128)(2,1)S(1)}, u32[]{:S(2)}, u32[]{:S(2)}) collective-permute-start(bf16[144,240]{1,0:T(8,128)(2,1)S(1)} %add_convert_fusion.refs_0_), channel_id=1, source_target_pairs={{0,2},{1,3},{2,0},{3,1},{4,6},{5,7},{6,4},{7,5},{8,10},{9,11},{10,... | collective-permute-start | bytes 207368 | tf_op jit(solution)/shard_map/ppermute | solution.py:339
  19.3 0.7 %scores.5 = (bf16[72,240]{1,0:T(8,128)(2,1)S(1)}, bf16[72,240]{1,0:T(8,128)(2,1)S(1)}) custom-call(bf16[144,4096]{1,0:T(8,128)(2,1)S(1)} %get-tuple-element.13.grads, bf16[480,4096]{1,0:T(8,128)(2,1)S(1)} %fetch.1.refs_5_.slab, bf16[144,240]{1,0:T(8,128)(2,1)S(1)} %add_convert_fusion.refs_0_), custom_call_target="tpu_custom_call" | custom-call | flops 283115520 | bytes 3145728 | tf_op jit(solution)/shard_map/scores/pallas_call | solution.py:363
  20.0 0.1 collective-permute-start.4
  20.1 0.5 %collective-permute-start.5 = (bf16[72,240]{1,0:T(8,128)(2,1)S(1)}, bf16[72,240]{1,0:T(8,128)(2,1)S(1)}, u32[]{:S(2)}, u32[]{:S(2)}) collective-permute-start(bf16[72,240]{1,0:T(8,128)(2,1)S(1)} %get-tuple-element.16), channel_id=1, source_target_pairs={{0,1},{1,0},{2,3},{3,2},{4,5},{5,4},{6,7},{7,6},{8,9},{9,8},{10,11... | collective-permute-start | bytes 103688 | tf_op jit(solution)/shard_map/ppermute | solution.py:339
  20.6 0.7 %scores.3 = f32[144,240]{1,0:T(8,128)S(1)} custom-call(bf16[144,4096]{1,0:T(8,128)(2,1)S(1)} %get-tuple-element.13.grads, bf16[480,4096]{1,0:T(8,128)(2,1)S(1)} %fetch.1.refs_5_.slab), custom_call_target="tpu_custom_call" | custom-call | flops 283115520 | bytes 3145728 | tf_op jit(solution)/shard_map/scores/pallas_call | solution.py:363
  21.4 0.0 collective-permute-done.4
  21.4 0.1 collective-permute-done.5
  21.5 0.7 %collective-permute-done.6 = bf16[144,240]{1,0:T(8,128)(2,1)S(1)} collective-permute-done((bf16[144,240]{1,0:T(8,128)(2,1)S(1)}, bf16[144,240]{1,0:T(8,128)(2,1)S(1)}, u32[]{:S(2)}, u32[]{:S(2)}) %collective-permute-start.6) | collective-permute-done | bytes 69152 | tf_op jit(solution)/shard_map/ppermute | solution.py:339
  22.1 0.7 %add_bitcast_fusion = f32[240,144]{0,1:T(8,128)} fusion(bf16[144,240]{1,0:T(8,128)(2,1)S(1)} %collective-permute-done.6, f32[144,240]{1,0:T(8,128)S(1)} %scores.3, bf16[72,240]{1,0:T(8,128)(2,1)S(1)} %collective-permute-done.5, bf16[72,240]{1,0:T(8,128)(2,1)S(1)} %collective-permute-done.4), kind=kLoop, calls=%fused_computation | loop fusion | flops 241920 | bytes 414720 | tf_op jit(solution)/shard_map/transpose | solution.py:412
  (1 shorter events, 0.0 us)
Async XLA Ops:
  4.5 9.3 %collective-permute-start.2 = (bf16[288,128]{1,0:T(8,128)(2,1)S(1)}, bf16[288,128]{1,0:T(8,128)(2,1)S(1)}, u32[]{:S(2)}, u32[]{:S(2)}) collective-permute-start(bf16[288,128]{1,0:T(8,128)(2,1)S(1)} %get-tuple-element.11.after.refs_0_), channel_id=1, source_target_pairs={{8,0},{0,4},{12,8},{4,12},{9,1},{1,5},{13,9},{5,13},{10,2},{2,6},{... | collective-permute-start | bytes 221192 | tf_op jit(solution)/shard_map/ppermute | solution.py:394
  7.6 7.3 %collective-permute-start.1 = (bf16[288,128]{1,0:T(8,128)(2,1)S(1)}, bf16[288,128]{1,0:T(8,128)(2,1)S(1)}, u32[]{:S(2)}, u32[]{:S(2)}) collective-permute-start(bf16[288,128]{1,0:T(8,128)(2,1)S(1)} %get-tuple-element.11.after.refs_0_), channel_id=1, source_target_pairs={{12,0},{8,4},{4,8},{0,12},{13,1},{9,5},{5,9},{1,13},{14,2},{10,6},... | collective-permute-start | bytes 221192 | tf_op jit(solution)/shard_map/ppermute | solution.py:394
  10.1 5.0 %collective-permute-start = (bf16[288,128]{1,0:T(8,128)(2,1)S(1)}, bf16[288,128]{1,0:T(8,128)(2,1)S(1)}, u32[]{:S(2)}, u32[]{:S(2)}) collective-permute-start(bf16[288,128]{1,0:T(8,128)(2,1)S(1)} %get-tuple-element.11.after.refs_0_), channel_id=1, source_target_pairs={{4,0},{12,4},{0,8},{8,12},{5,1},{13,5},{1,9},{9,13},{6,2},{14,6},{... | collective-permute-start | bytes 221192 | tf_op jit(solution)/shard_map/ppermute | solution.py:394
  16.4 1.3 %collective-permute-start.3 = (bf16[144,240]{1,0:T(8,128)(2,1)S(1)}, bf16[144,240]{1,0:T(8,128)(2,1)S(1)}, u32[]{:S(2)}, u32[]{:S(2)}) collective-permute-start(bf16[144,240]{1,0:T(8,128)(2,1)S(1)} %get-tuple-element.14), channel_id=1, source_target_pairs={{0,1},{1,0},{2,3},{3,2},{4,5},{5,4},{6,7},{7,6},{8,9},{9,8},{10,11... | collective-permute-start | bytes 207368 | tf_op jit(solution)/shard_map/ppermute | solution.py:339
  17.7 4.4 %collective-permute-start.6 = (bf16[144,240]{1,0:T(8,128)(2,1)S(1)}, bf16[144,240]{1,0:T(8,128)(2,1)S(1)}, u32[]{:S(2)}, u32[]{:S(2)}) collective-permute-start(bf16[144,240]{1,0:T(8,128)(2,1)S(1)} %add_convert_fusion.refs_0_), channel_id=1, source_target_pairs={{0,2},{1,3},{2,0},{3,1},{4,6},{5,7},{6,4},{7,5},{8,10},{9,11},{10,... | collective-permute-start | bytes 207368 | tf_op jit(solution)/shard_map/ppermute | solution.py:339
  20.0 1.3 %collective-permute-start.4 = (bf16[72,240]{1,0:T(8,128)(2,1)S(1)}, bf16[72,240]{1,0:T(8,128)(2,1)S(1)}, u32[]{:S(2)}, u32[]{:S(2)}) collective-permute-start(bf16[72,240]{1,0:T(8,128)(2,1)S(1)} %get-tuple-element.15), channel_id=1, source_target_pairs={{0,1},{1,0},{2,3},{3,2},{4,5},{5,4},{6,7},{7,6},{8,9},{9,8},{10,11... | collective-permute-start | bytes 103688 | tf_op jit(solution)/shard_map/ppermute | solution.py:339
  20.1 1.4 %collective-permute-start.5 = (bf16[72,240]{1,0:T(8,128)(2,1)S(1)}, bf16[72,240]{1,0:T(8,128)(2,1)S(1)}, u32[]{:S(2)}, u32[]{:S(2)}) collective-permute-start(bf16[72,240]{1,0:T(8,128)(2,1)S(1)} %get-tuple-element.16), channel_id=1, source_target_pairs={{0,1},{1,0},{2,3},{3,2},{4,5},{5,4},{6,7},{7,6},{8,9},{9,8},{10,11... | collective-permute-start | bytes 103688 | tf_op jit(solution)/shard_map/ppermute | solution.py:339
